TPU v7x, 32 devices: a whole 2x2x4 slice. The times are simulated.
32 devices in a mesh: section: 4 (over z), dp: 8 (over y, x, core).
Axes of the slice: x: 2, y: 2, z: 4, core: 2. Of those that a mesh axis runs over, the one named last changes fastest.
Arguments:
- clip_inputs: bfloat16 [16, 1280, 768], P('dp'), may hold values from -6 to 6
- out_grad: bfloat16 [16, 1280, 768], P('dp'), may hold values from -6 to 6
- clip_class: int32 [16], P('dp'), may hold values from 0 to 1, as said below
- w_front: bfloat16 [4, 768, 3072], P('section')
- w_back: bfloat16 [4, 1536, 768], P('section'), may hold values from -0.109375 to 0.109375
- norm_gain: float32 [4, 768], P('section'), may hold values from 0.25 to 1.75
- norm_shift: float32 [4, 768], P('section'), may hold values from -3 to 3
- bias_query_value: float32 [2, 1536], replicated, may hold values from -3 to 3
- bias_attn_out: float32 [2, 768], replicated, may hold values from -3 to 3
- bias_up: float32 [2, 3072], replicated, may hold values from -3 to 3
- bias_down: float32 [2, 768], replicated, may hold values from -3 to 3
Outputs:
- activations: bfloat16 [4, 16, 1280, 768], P('section', 'dp')
- input_grads: float32 [4, 16, 1280, 768], P('section', 'dp')
- grad_front: float32 [4, 768, 3072], P('section')
- grad_back: float32 [4, 1536, 768], P('section')
- grad_gain: float32 [4, 768], P('section')
- grad_shift: float32 [4, 768], P('section')
- grad_query_value: float32 [2, 1536], replicated
- grad_attn_out: float32 [2, 768], replicated
- grad_up: float32 [2, 3072], replicated
- grad_down: float32 [2, 768], replicated
Inputs may be any that keep to these rules, and one draw needn't show every extreme that they name: `clip_class`: 1 marks a clip of 1214 tokens, 0 one of 514; the first clip is long and the second short.
All inputs are finite; a program needn't handle non-finite values.
Results may differ from a plain program's by a relative error of at most 0.014.
Values may be sent and summed in bfloat16 or wider, within the bound.
A program may use at most 320 MiB of HBM per device.

v0:
```python
import jax
import jax.numpy as jnp
from jax import lax
from jax.sharding import PartitionSpec as P

HEADS = 12
LONG = 1214
SHORT = 514


EPS = 1e-06


def passed_along(block, axis, distance):
    devices = range(lax.axis_size(axis))
    route = [(i - distance, i) for i in devices if i - distance in devices]
    return lax.ppermute(block, axis, route)


def shortened(value):
    return jax.tree.map(lambda a: a.astype(jnp.bfloat16) if a.dtype == jnp.float32 else a, value)


def layer_norm(hidden_in, scales, offset):
    average = jnp.mean(hidden_in, axis=-1, keepdims=True)
    centred = hidden_in - average
    spread = jnp.mean(centred * centred, axis=-1, keepdims=True)
    return centred * lax.rsqrt(spread + EPS) * scales + offset


def exact_gelu(values):
    return jax.nn.gelu(values, approximate=False)


def contract_rows(left, right):
    return lax.dot_general(
        left, right, (((0,), (0,)), ((), ())), preferred_element_type=jnp.float32
    )


def contract_cols(left, right):
    return lax.dot_general(
        left, right, (((1,), (1,)), ((), ())), preferred_element_type=jnp.float32
    )


def column_sums(values):
    ones_row = jnp.ones((values.shape[0],), values.dtype)
    return jnp.dot(ones_row, values, preferred_element_type=jnp.float32)


def softmax_rows(query_blk, key_heads, key_mask, score_scale):
    scores = (
        jnp.einsum("qhd,khd->hqk", query_blk, key_heads, preferred_element_type=jnp.float32)
        * score_scale
    )
    scores = jnp.where(key_mask[None, None, :], scores, -1e30)
    powered = jnp.exp(scores - jnp.max(scores, axis=-1, keepdims=True))
    return powered / jnp.sum(powered, axis=-1, keepdims=True)


def project_qkv(normed_b, weight_in, bias_pair):
    model_width = normed_b.shape[1]
    full_bias = jnp.concatenate(
        [bias_pair[:model_width], jnp.zeros((model_width,), jnp.float32), bias_pair[model_width:]]
    )
    projected = jnp.dot(
        normed_b, weight_in[:, : 3 * model_width], preferred_element_type=jnp.float32
    )
    return (projected + full_bias).astype(jnp.bfloat16)


def split_heads(qkv_b):
    padded = qkv_b.shape[0]
    model_width = qkv_b.shape[1] // 3
    return [
        qkv_b[:, member * model_width : (member + 1) * model_width].reshape(
            padded, HEADS, model_width // HEADS
        )
        for member in range(3)
    ]


def attention_forward(hidden_in, row_mask, weight_in, scales, offset, bias_pair, bias_attn):
    padded = hidden_in.shape[0]
    model_width = hidden_in.shape[1]
    head_dim = model_width // HEADS
    score_scale = head_dim ** (-0.5)
    normed_b = layer_norm(hidden_in, scales, offset).astype(jnp.bfloat16)
    query_heads, key_heads, value_heads = split_heads(project_qkv(normed_b, weight_in, bias_pair))
    key_mask = row_mask > 0
    halves = query_heads.reshape(2, padded // 2, HEADS, head_dim)

    def one_block(query_blk):
        attn_probs = softmax_rows(query_blk, key_heads, key_mask, score_scale)
        return jnp.einsum(
            "hqk,khd->qhd",
            attn_probs.astype(jnp.bfloat16),
            value_heads,
            preferred_element_type=jnp.float32,
        )

    attended = lax.map(one_block, halves).reshape(padded, model_width).astype(jnp.bfloat16)
    branch = contract_cols(attended, weight_in[:, 3 * model_width :]) + bias_attn
    return (row_mask[:, None] * (hidden_in + branch)).astype(jnp.bfloat16)


def attention_backward(hidden_in, grad_out, row_mask, weight_in, scales, offset, bias_pair):
    padded = hidden_in.shape[0]
    model_width = hidden_in.shape[1]
    hidden_units = weight_in.shape[1]
    head_dim = model_width // HEADS
    score_scale = head_dim ** (-0.5)
    normed, norm_back = jax.vjp(layer_norm, hidden_in, scales, offset)
    normed_b = normed.astype(jnp.bfloat16)
    qkv_b = project_qkv(normed_b, weight_in, bias_pair)
    query_heads, key_heads, value_heads = split_heads(qkv_b)
    key_mask = row_mask > 0
    grad_rows = grad_out * row_mask[:, None]
    grad_b = grad_rows.astype(jnp.bfloat16)
    weight_out_t = weight_in[:, 3 * model_width :]
    grad_attended = jnp.dot(grad_b, weight_out_t, preferred_element_type=jnp.float32).astype(
        jnp.bfloat16
    )
    halves = query_heads.reshape(2, padded // 2, HEADS, head_dim)
    grad_halves = grad_attended.reshape(2, padded // 2, HEADS, head_dim)

    def back_block(loop_state, block_pair):
        query_blk, grad_blk = block_pair
        attn_probs = softmax_rows(query_blk, key_heads, key_mask, score_scale)
        probs_b = attn_probs.astype(jnp.bfloat16)
        attended_blk = jnp.einsum(
            "hqk,khd->qhd", probs_b, value_heads, preferred_element_type=jnp.float32
        )
        grad_probs = jnp.einsum(
            "qhd,khd->hqk", grad_blk, value_heads, preferred_element_type=jnp.float32
        )
        row_dots = jnp.sum(attn_probs * grad_probs, axis=-1, keepdims=True)
        grad_scores = (attn_probs * (grad_probs - row_dots)).astype(jnp.bfloat16)
        grad_query = (
            jnp.einsum("hqk,khd->qhd", grad_scores, key_heads, preferred_element_type=jnp.float32)
            * score_scale
        )
        grad_keys = (
            loop_state[0]
            + jnp.einsum("hqk,qhd->khd", grad_scores, query_blk, preferred_element_type=jnp.float32)
            * score_scale
        )
        grad_values = loop_state[1] + jnp.einsum(
            "hqk,qhd->khd", probs_b, grad_blk, preferred_element_type=jnp.float32
        )
        return ((grad_keys, grad_values), (grad_query, attended_blk))

    zero_heads = jnp.zeros((padded, HEADS, head_dim), jnp.float32)
    (grad_keys, grad_values), (grad_query, attended) = lax.scan(
        back_block, (zero_heads, zero_heads), (halves, grad_halves)
    )
    attended_b = attended.reshape(padded, model_width).astype(jnp.bfloat16)
    grad_weight_out = contract_rows(grad_b, attended_b)
    grad_qkv = jnp.concatenate(
        [
            grad_query.reshape(padded, model_width),
            grad_keys.reshape(padded, model_width),
            grad_values.reshape(padded, model_width),
        ],
        axis=1,
    ).astype(jnp.bfloat16)
    qkv_sums = column_sums(grad_qkv)
    grad_pair = jnp.concatenate([qkv_sums[:model_width], qkv_sums[2 * model_width :]])
    grad_weight_qkv = contract_rows(normed_b, grad_qkv)
    grad_normed = contract_cols(grad_qkv, weight_in[:, : 3 * model_width])
    grad_hidden, grad_scales, grad_offset = norm_back(grad_normed)
    grad_front = jnp.concatenate([grad_weight_qkv, grad_weight_out], axis=1)
    return (
        grad_rows + grad_hidden,
        grad_front,
        jnp.zeros((hidden_units, model_width), jnp.float32),
        grad_scales,
        grad_offset,
        grad_pair,
        jnp.sum(grad_rows, axis=0),
        jnp.zeros((hidden_units,), jnp.float32),
        jnp.zeros((model_width,), jnp.float32),
    )


def mlp_forward(hidden_in, row_mask, weight_in, weight_down, scales, offset, bias_in, bias_out):
    normed_b = layer_norm(hidden_in, scales, offset).astype(jnp.bfloat16)
    pre_act = jnp.dot(normed_b, weight_in, preferred_element_type=jnp.float32) + bias_in
    activated = exact_gelu(pre_act).astype(jnp.bfloat16)
    branch = jnp.dot(activated, weight_down, preferred_element_type=jnp.float32) + bias_out
    return (row_mask[:, None] * (hidden_in + branch)).astype(jnp.bfloat16)


def mlp_backward(hidden_in, grad_out, row_mask, weight_in, weight_down, scales, offset, bias_in):
    model_width = hidden_in.shape[1]
    normed, norm_back = jax.vjp(layer_norm, hidden_in, scales, offset)
    normed_b = normed.astype(jnp.bfloat16)
    pre_act = jnp.dot(normed_b, weight_in, preferred_element_type=jnp.float32) + bias_in
    activated, gelu_back = jax.vjp(exact_gelu, pre_act)
    act_b = activated.astype(jnp.bfloat16)
    grad_rows = grad_out * row_mask[:, None]
    grad_b = grad_rows.astype(jnp.bfloat16)
    grad_down = contract_rows(act_b, grad_b)
    grad_act = contract_cols(grad_b, weight_down)
    grad_pre = gelu_back(grad_act)[0].astype(jnp.bfloat16)
    grad_up = contract_rows(normed_b, grad_pre)
    grad_normed = contract_cols(grad_pre, weight_in)
    grad_hidden, grad_scales, grad_offset = norm_back(grad_normed)
    return (
        grad_rows + grad_hidden,
        grad_up,
        grad_down,
        grad_scales,
        grad_offset,
        jnp.zeros((2 * model_width,), jnp.float32),
        jnp.zeros((model_width,), jnp.float32),
        column_sums(grad_pre),
        jnp.sum(grad_rows, axis=0),
    )


def per_device(
    clip_inputs,
    out_grad,
    clip_class,
    w_front,
    w_back,
    norm_gain,
    norm_shift,
    bias_query_value,
    bias_attn_out,
    bias_up,
    bias_down,
):
    section_id = lax.axis_index("section")
    sections = lax.axis_size("section")
    clip_count, padded, model_width = clip_inputs.shape
    hidden_units = w_front.shape[2]
    half_rows = w_back.shape[1]
    layer_count = bias_up.shape[0]
    layer_id = section_id // 2
    odd_section = section_id % 2
    lengths = SHORT + (LONG - SHORT) * clip_class
    positions = lax.iota(jnp.int32, padded)
    weight_in = w_front[0]
    scales = norm_gain[0]
    offset = norm_shift[0]
    bias_pair = lax.dynamic_index_in_dim(bias_query_value, layer_id, 0, False)
    bias_attn = lax.dynamic_index_in_dim(bias_attn_out, layer_id, 0, False)
    bias_in = lax.dynamic_index_in_dim(bias_up, layer_id, 0, False)
    bias_out = lax.dynamic_index_in_dim(bias_down, layer_id, 0, False)
    received_half = passed_along(w_back, "section", 1)
    weight_down = jnp.concatenate([received_half[0], w_back[0]], axis=0)

    def mask_for(clip_slot):
        length = lax.dynamic_index_in_dim(lengths, clip_slot, 0, False)
        return (positions < length).astype(jnp.float32)

    def attention_step(hidden_in, row_mask):
        return attention_forward(
            hidden_in, row_mask, weight_in, scales, offset, bias_pair, bias_attn
        )

    def feedforward_step(hidden_in, row_mask):
        return mlp_forward(
            hidden_in, row_mask, weight_in, weight_down, scales, offset, bias_in, bias_out
        )

    def resting_step(hidden_in, row_mask):
        return jnp.zeros((padded, model_width), jnp.bfloat16)

    def forward_tick(step_id, loop_state):
        stash, acts, incoming = loop_state
        micro_batch = step_id - section_id
        active = (micro_batch >= 0) & (micro_batch < clip_count)
        clip_slot = jnp.clip(micro_batch, 0, clip_count - 1)
        row_mask = mask_for(clip_slot)
        fresh = (
            lax.dynamic_index_in_dim(clip_inputs, clip_slot, 0, False).astype(jnp.float32)
            * row_mask[:, None]
        ).astype(jnp.bfloat16)
        entering = jnp.where(section_id == 0, fresh, incoming)
        branch_index = jnp.where(active, odd_section, 2)
        leaving = lax.switch(
            branch_index,
            [attention_step, feedforward_step, resting_step],
            entering.astype(jnp.float32),
            row_mask,
        )
        stash = jnp.where(
            active, lax.dynamic_update_index_in_dim(stash, entering, clip_slot, 0), stash
        )
        acts = jnp.where(active, lax.dynamic_update_index_in_dim(acts, leaving, clip_slot, 0), acts)
        incoming = jax.tree.map(
            lambda part, own: part.astype(own.dtype),
            passed_along(shortened(leaving), "section", 1),
            leaving,
        )
        return (stash, acts, incoming)

    empty_acts = jnp.zeros((clip_count, padded, model_width), jnp.bfloat16)
    empty_rows = jnp.zeros((padded, model_width), jnp.bfloat16)
    stash, acts, unused_rows = lax.fori_loop(
        0, clip_count + sections - 1, forward_tick, (empty_acts, empty_acts, empty_rows)
    )

    def attention_grads(hidden_in, grad_out, row_mask):
        return attention_backward(
            hidden_in, grad_out, row_mask, weight_in, scales, offset, bias_pair
        )

    def feedforward_grads(hidden_in, grad_out, row_mask):
        return mlp_backward(
            hidden_in, grad_out, row_mask, weight_in, weight_down, scales, offset, bias_in
        )

    def resting_grads(hidden_in, grad_out, row_mask):
        zero_vec = jnp.zeros((model_width,), jnp.float32)
        return (
            jnp.zeros((padded, model_width), jnp.float32),
            jnp.zeros((model_width, hidden_units), jnp.float32),
            jnp.zeros((hidden_units, model_width), jnp.float32),
            zero_vec,
            zero_vec,
            jnp.zeros((2 * model_width,), jnp.float32),
            zero_vec,
            jnp.zeros((hidden_units,), jnp.float32),
            zero_vec,
        )

    def backward_tick(step_id, loop_state):
        incoming, grad_store, totals = loop_state
        micro_batch = step_id - (sections - 1 - section_id)
        active = (micro_batch >= 0) & (micro_batch < clip_count)
        clip_slot = jnp.clip(micro_batch, 0, clip_count - 1)
        row_mask = mask_for(clip_slot)
        arriving = jnp.where(
            section_id == sections - 1,
            lax.dynamic_index_in_dim(out_grad, clip_slot, 0, False),
            incoming,
        )
        entering = lax.dynamic_index_in_dim(stash, clip_slot, 0, False).astype(jnp.float32)
        branch_index = jnp.where(active, odd_section, 2)
        results = lax.switch(
            branch_index,
            [attention_grads, feedforward_grads, resting_grads],
            entering,
            arriving.astype(jnp.float32),
            row_mask,
        )
        grad_store = jnp.where(
            active,
            lax.dynamic_update_index_in_dim(grad_store, results[0], clip_slot, 0),
            grad_store,
        )
        incoming = passed_along(results[0].astype(jnp.bfloat16), "section", -1)
        totals = tuple((running + adding for running, adding in zip(totals, results[1:])))
        return (incoming, grad_store, totals)

    zero_vec = jnp.zeros((model_width,), jnp.float32)
    start_totals = (
        jnp.zeros((model_width, hidden_units), jnp.float32),
        jnp.zeros((hidden_units, model_width), jnp.float32),
        zero_vec,
        zero_vec,
        jnp.zeros((2 * model_width,), jnp.float32),
        zero_vec,
        jnp.zeros((hidden_units,), jnp.float32),
        zero_vec,
    )
    empty_grads = jnp.zeros((clip_count, padded, model_width), jnp.float32)
    unused_grads, grad_store, totals = lax.fori_loop(
        0, clip_count + sections - 1, backward_tick, (empty_rows, empty_grads, start_totals)
    )
    returned = passed_along(totals[1][:half_rows].astype(jnp.bfloat16), "section", -1).astype(
        jnp.float32
    )
    own_back = jnp.where(odd_section == 1, totals[1][half_rows:], returned)
    section_sums = (
        lax.psum(totals[0].astype(jnp.bfloat16), "dp").astype(jnp.float32),
        lax.psum(own_back.astype(jnp.bfloat16), "dp").astype(jnp.float32),
        lax.psum(totals[2].astype(jnp.bfloat16), "dp").astype(jnp.float32),
        lax.psum(totals[3].astype(jnp.bfloat16), "dp").astype(jnp.float32),
    )
    layer_pick = (lax.iota(jnp.int32, layer_count) == layer_id).astype(jnp.float32)[:, None]
    bias_sums = lax.psum(
        (
            layer_pick * totals[4],
            layer_pick * totals[5],
            layer_pick * totals[6],
            layer_pick * totals[7],
        ),
        ("section", "dp"),
    )
    return (
        acts[None],
        grad_store[None],
        section_sums[0][None],
        section_sums[1][None],
        section_sums[2][None],
        section_sums[3][None],
        bias_sums[0],
        bias_sums[1],
        bias_sums[2],
        bias_sums[3],
    )


def solution(mesh):
    placed = (
        P("dp", None, None),
        P("dp", None, None),
        P("dp"),
        P("section", None, None),
        P("section", None, None),
        P("section", None),
        P("section", None),
        P(),
        P(),
        P(),
        P(),
    )
    return jax.shard_map(
        per_device,
        mesh=mesh,
        in_specs=placed,
        out_specs=(
            P("section", "dp", None, None),
            P("section", "dp", None, None),
            P("section", None, None),
            P("section", None, None),
            P("section", None),
            P("section", None),
            P(),
            P(),
            P(),
            P(),
        ),
        check_vma=False,
    )
```

profile of v0, /device:TPU:0, one launch (start us, length us, event | category | flops | bytes accessed | tf_op | source)
XLA Modules:
  0.0 2812.0 jit_solution(12645978145354024008)
XLA Ops:
  15.8 47.2 %collective-permute-done.2 = bf16[1,1536,768]{2,1,0:T(8,128)(2,1)S(1)} collective-permute-done((bf16[1,1536,768]{2,1,0:T(8,128)(2,1)}, bf16[1,1536,768]{2,1,0:T(8,128)(2,1)S(1)}, u32[]{:S(2)}, u32[]{:S(2)}) %collective-permute-start.2) | collective-permute-done | bytes 2359328 | tf_op jit(solution)/shard_map/ppermute | solution.py:17
  71.6 773.3 %while.80 = (s32[]{:T(128)}, bf16[2,1280,768]{2,1,0:T(8,128)(2,1)}, bf16[2,1280,768]{2,1,0:T(8,128)(2,1)}, bf16[1280,768]{1,0:T(8,128)(2,1)S(1)}, s32[]{:T(128)}...) while((s32[]{:T(128)}, bf16[2,1280,768]{2,1,0:T(8,128)(2,1)}, ...), condition=%wide.region_12.13_spmd.clone, body=%wide.region_0.12_spmd.clone.sunk | while | flops 12362715136 | bytes 219299472 | solution.py:304
  77.5 141.8 %conditional.6 = (bf16[1280,768]{1,0:T(8,128)(2,1)}, bf16[1,1280,768]{2,1,0:T(8,128)(2,1)S(1)}) conditional(s32[]{:T(128)} %clamp.21, (f32[1280]{0:T(1024)S(1)}, f32[1280,768]{1,0:T(8,128)}, f32[1,768]{1,0:T(1,128)}, f32[1,768]{1,0:T(1,128)}, bf16[768,3072]{1,0:T(8,128)(2,1)}, /*index=5*/f32[1536]{0:T(1024)S(1)}, ...), branch_computations={%region_1.7_spmd, %region_8.10_spmd, %region_11.11_spmd} | conditional | flops 12351898624 | bytes 177933808 | solution.py:285
  109.2 99.5 %while.78 = (s32[]{:T(128)}, bf16[2,640,12,64]{1,3,2,0:T(8,128)(2,1)}, pred[1280]{0:T(1024)(128)(4,1)S(1)}, bf16[2,640,12,64]{1,3,2,0:T(8,128)(2,1)}, bf16[1280,...) while((s32[]{:T(128)}, bf16[2,640,12,64]{1,3,2,0:T(8,128)(2,1)}, ...), condition=%wide.region_7.6_spmd, body=%wide.region_4.5_spmd.sunk | while | flops 3863357440 | bytes 88539216 | solution.py:103
  122.2 16.6 fusion.298
  138.9 20.4 bitcast_dynamic-update-slice_fusion.8
  171.7 16.6 fusion.298
  188.3 20.4 bitcast_dynamic-update-slice_fusion.8
  227.5 34.9 %collective-permute-done.1 = bf16[1280,768]{1,0:T(8,128)(2,1)} collective-permute-done((bf16[1280,768]{1,0:T(8,128)(2,1)}, bf16[1280,768]{1,0:T(8,128)(2,1)}, u32[]{:S(2)}, u32[]{:S(2)}) %collective-permute-start.1) | collective-permute-done | bytes 1966112 | tf_op jit(solution)/shard_map/while/body/eval_jaxpr/ppermute | solution.py:17
  269.9 141.6 %conditional.6 = (bf16[1280,768]{1,0:T(8,128)(2,1)}, bf16[1,1280,768]{2,1,0:T(8,128)(2,1)S(1)}) conditional(s32[]{:T(128)} %clamp.21, (f32[1280]{0:T(1024)S(1)}, f32[1280,768]{1,0:T(8,128)}, f32[1,768]{1,0:T(1,128)}, f32[1,768]{1,0:T(1,128)}, bf16[768,3072]{1,0:T(8,128)(2,1)}, /*index=5*/f32[1536]{0:T(1024)S(1)}, ...), branch_computations={%region_1.7_spmd, %region_8.10_spmd, %region_11.11_spmd} | conditional | flops 12351898624 | bytes 177933808 | solution.py:285
  301.6 99.1 %while.78 = (s32[]{:T(128)}, bf16[2,640,12,64]{1,3,2,0:T(8,128)(2,1)}, pred[1280]{0:T(1024)(128)(4,1)S(1)}, bf16[2,640,12,64]{1,3,2,0:T(8,128)(2,1)}, bf16[1280,...) while((s32[]{:T(128)}, bf16[2,640,12,64]{1,3,2,0:T(8,128)(2,1)}, ...), condition=%wide.region_7.6_spmd, body=%wide.region_4.5_spmd.sunk | while | flops 3863357440 | bytes 88539216 | solution.py:103
  314.2 16.6 fusion.298
  330.9 20.4 bitcast_dynamic-update-slice_fusion.8
  363.7 16.6 fusion.298
  380.3 20.4 bitcast_dynamic-update-slice_fusion.8
  419.7 34.3 %collective-permute-done.1 = bf16[1280,768]{1,0:T(8,128)(2,1)} collective-permute-done((bf16[1280,768]{1,0:T(8,128)(2,1)}, bf16[1280,768]{1,0:T(8,128)(2,1)}, u32[]{:S(2)}, u32[]{:S(2)}) %collective-permute-start.1) | collective-permute-done | bytes 1966112 | tf_op jit(solution)/shard_map/while/body/eval_jaxpr/ppermute | solution.py:17
  461.3 18.2 conditional.6
  479.4 62.5 %collective-permute-start.1 = (bf16[1280,768]{1,0:T(8,128)(2,1)}, bf16[1280,768]{1,0:T(8,128)(2,1)}, u32[]{:S(2)}, u32[]{:S(2)}) collective-permute-start(bf16[1280,768]{1,0:T(8,128)(2,1)} %get-tuple-element.1758), channel_id=1, source_target_pairs={{0,8},{8,16},{16,24},{1,9},{9,17},{17,25},{2,10},{10,18},{18,26},{... | collective-permute-start | bytes 5898248 | tf_op jit(solution)/shard_map/while/body/eval_jaxpr/ppermute | solution.py:17
  547.4 33.4 %collective-permute-done.1 = bf16[1280,768]{1,0:T(8,128)(2,1)} collective-permute-done((bf16[1280,768]{1,0:T(8,128)(2,1)}, bf16[1280,768]{1,0:T(8,128)(2,1)}, u32[]{:S(2)}, u32[]{:S(2)}) %collective-permute-start.1) | collective-permute-done | bytes 1966112 | tf_op jit(solution)/shard_map/while/body/eval_jaxpr/ppermute | solution.py:17
  587.9 18.2 conditional.6
  617.7 32.4 %collective-permute-done.1 = bf16[1280,768]{1,0:T(8,128)(2,1)} collective-permute-done((bf16[1280,768]{1,0:T(8,128)(2,1)}, bf16[1280,768]{1,0:T(8,128)(2,1)}, u32[]{:S(2)}, u32[]{:S(2)}) %collective-permute-start.1) | collective-permute-done | bytes 1966112 | tf_op jit(solution)/shard_map/while/body/eval_jaxpr/ppermute | solution.py:17
  657.2 18.2 conditional.6
  675.5 129.5 %collective-permute-start.1 = (bf16[1280,768]{1,0:T(8,128)(2,1)}, bf16[1280,768]{1,0:T(8,128)(2,1)}, u32[]{:S(2)}, u32[]{:S(2)}) collective-permute-start(bf16[1280,768]{1,0:T(8,128)(2,1)} %get-tuple-element.1758), channel_id=1, source_target_pairs={{0,8},{8,16},{16,24},{1,9},{9,17},{17,25},{2,10},{10,18},{18,26},{... | collective-permute-start | bytes 5898248 | tf_op jit(solution)/shard_map/while/body/eval_jaxpr/ppermute | solution.py:17
  810.5 31.5 %collective-permute-done.1 = bf16[1280,768]{1,0:T(8,128)(2,1)} collective-permute-done((bf16[1280,768]{1,0:T(8,128)(2,1)}, bf16[1280,768]{1,0:T(8,128)(2,1)}, u32[]{:S(2)}, u32[]{:S(2)}) %collective-permute-start.1) | collective-permute-done | bytes 1966112 | tf_op jit(solution)/shard_map/while/body/eval_jaxpr/ppermute | solution.py:17
  848.9 1778.4 %while.81 = (s32[]{:T(128)}, bf16[1280,768]{1,0:T(8,128)(2,1)S(1)}, f32[2,1280,768]{2,1,0:T(8,128)}, f32[768,3072]{1,0:T(8,128)}, f32[3072,768]{1,0:T(8,128)}, /...) while((s32[]{:T(128)}, bf16[1280,768]{1,0:T(8,128)(2,1)S(1)}, ...), condition=%wide.region_36.37_spmd.clone, body=%wide.region_13.36_spmd.clone.sunk | while | flops 30580041728 | bytes 723142848 | solution.py:373
  862.6 40.3 %conditional.7 = (f32[1280,768]{1,0:T(8,128)}, f32[768,3072]{1,0:T(8,128)}, f32[3072,768]{1,0:T(8,128)}, f32[768]{0:T(1024)}, f32[768]{0:T(1024)}, /*index=5*/f3...) conditional(s32[]{:T(128)} %clamp.22, (f32[1280]{0:T(1024)S(1)}, ...), branch_computations={%region_14.26_spmd, %region_27.34_spmd, %region_35.35_spmd} | conditional | flops 30565668864 | bytes 626768576 | solution.py:345
  933.4 15.7 collective-permute-done
  958.1 40.4 %conditional.7 = (f32[1280,768]{1,0:T(8,128)}, f32[768,3072]{1,0:T(8,128)}, f32[3072,768]{1,0:T(8,128)}, f32[768]{0:T(1024)}, f32[768]{0:T(1024)}, /*index=5*/f3...) conditional(s32[]{:T(128)} %clamp.22, (f32[1280]{0:T(1024)S(1)}, ...), branch_computations={%region_14.26_spmd, %region_27.34_spmd, %region_35.35_spmd} | conditional | flops 30565668864 | bytes 626768576 | solution.py:345
  1003.5 13.1 select_add_fusion.14
  1034.4 65.0 %collective-permute-done = bf16[1280,768]{1,0:T(8,128)(2,1)S(1)} collective-permute-done((bf16[1280,768]{1,0:T(8,128)(2,1)}, bf16[1280,768]{1,0:T(8,128)(2,1)S(1)}, u32[]{:S(2)}, u32[]{:S(2)}) %collective-permute-start) | collective-permute-done | bytes 1966112 | tf_op jit(solution)/shard_map/while/body/eval_jaxpr/ppermute | solution.py:17
  1108.4 40.4 %conditional.7 = (f32[1280,768]{1,0:T(8,128)}, f32[768,3072]{1,0:T(8,128)}, f32[3072,768]{1,0:T(8,128)}, f32[768]{0:T(1024)}, f32[768]{0:T(1024)}, /*index=5*/f3...) conditional(s32[]{:T(128)} %clamp.22, (f32[1280]{0:T(1024)S(1)}, ...), branch_computations={%region_14.26_spmd, %region_27.34_spmd, %region_35.35_spmd} | conditional | flops 30565668864 | bytes 626768576 | solution.py:345
  1153.8 13.1 select_add_fusion.14
  1184.7 551.4 %collective-permute-done = bf16[1280,768]{1,0:T(8,128)(2,1)S(1)} collective-permute-done((bf16[1280,768]{1,0:T(8,128)(2,1)}, bf16[1280,768]{1,0:T(8,128)(2,1)S(1)}, u32[]{:S(2)}, u32[]{:S(2)}) %collective-permute-start) | collective-permute-done | bytes 1966112 | tf_op jit(solution)/shard_map/while/body/eval_jaxpr/ppermute | solution.py:17
  1745.1 391.3 %conditional.7 = (f32[1280,768]{1,0:T(8,128)}, f32[768,3072]{1,0:T(8,128)}, f32[3072,768]{1,0:T(8,128)}, f32[768]{0:T(1024)}, f32[768]{0:T(1024)}, /*index=5*/f3...) conditional(s32[]{:T(128)} %clamp.22, (f32[1280]{0:T(1024)S(1)}, ...), branch_computations={%region_14.26_spmd, %region_27.34_spmd, %region_35.35_spmd} | conditional | flops 30565668864 | bytes 626768576 | solution.py:345
  1796.5 274.5 %while.79 = (s32[]{:T(128)}, f32[1280,12,64]{0,2,1:T(8,128)}, f32[1280,12,64]{0,2,1:T(8,128)}, bf16[2,640,12,64]{1,3,2,0:T(8,128)(2,1)}, bf16[2,640,12,64]{1,3,2...) while((s32[]{:T(128)}, f32[1280,12,64]{0,2,1:T(8,128)}, ...), condition=%wide.region_21.20_spmd.clone, body=%wide.region_17.19_spmd.clone.sunk | while | flops 10278185984 | bytes 316783328 | solution.py:155
  1796.9 18.3 fusion.291
  1815.3 29.6 %multiply_reduce_fusion.12 = (f32[12,640]{1,0:T(8,128)S(1)}, f32[12,640,1280]{2,1,0:T(8,128)}) fusion(f32[12,640,1280]{2,1,0:T(8,128)} %get-tuple-element.1805, f32[12,640]{1,0:T(8,128)S(1)} %get-tuple-element.1806, bf16[1280,12,64]{0,2,1:T(8,128)(2,1)} %get-tuple-element.1875, bf16[2,640,12,64]{1,3,2,0:T(8,128)(2,1)} %get-tuple-element.1874, ...), kind=kOutput, calls=%fused_computation.27.clone.1 | convolution fusion | flops 1287774720 | bytes 81654272 | tf_op jit(solution)/shard_map/while/body/eval_jaxpr/cond/branch_0_fun/while/body/eval_jaxpr/qhd,khd->hqk/dot_general | solution.py:135
  1844.9 31.8 %multiply_convert_fusion.11 = bf16[12,640,1280]{2,1,0:T(8,128)(2,1)} fusion(f32[12,640,1280]{2,1,0:T(8,128)} %get-tuple-element.1807, f32[12,640]{1,0:T(8,128)S(1)} %get-tuple-element.1808, f32[12,640,1280]{2,1,0:T(8,128)} %get-tuple-element.1805, f32[12,640]{1,0:T(8,128)S(1)} %get-tuple-element.1806), kind=kLoop, calls=%fused_computation.26.clone.1 | loop fusion | flops 39321600 | bytes 98365440 | tf_op jit(solution)/shard_map/while/body/eval_jaxpr/cond/branch_0_fun/while/body/eval_jaxpr/convert_element_type | solution.py:139
  1900.9 15.4 bitcast_add_fusion.5
  1916.3 16.8 bitcast_dynamic-update-slice_fusion.7
  1933.0 18.3 fusion.291
  1951.4 29.6 %multiply_reduce_fusion.12 = (f32[12,640]{1,0:T(8,128)S(1)}, f32[12,640,1280]{2,1,0:T(8,128)}) fusion(f32[12,640,1280]{2,1,0:T(8,128)} %get-tuple-element.1805, f32[12,640]{1,0:T(8,128)S(1)} %get-tuple-element.1806, bf16[1280,12,64]{0,2,1:T(8,128)(2,1)} %get-tuple-element.1875, bf16[2,640,12,64]{1,3,2,0:T(8,128)(2,1)} %get-tuple-element.1874, ...), kind=kOutput, calls=%fused_computation.27.clone.1 | convolution fusion | flops 1287774720 | bytes 81654272 | tf_op jit(solution)/shard_map/while/body/eval_jaxpr/cond/branch_0_fun/while/body/eval_jaxpr/qhd,khd->hqk/dot_general | solution.py:135
  1981.0 31.8 %multiply_convert_fusion.11 = bf16[12,640,1280]{2,1,0:T(8,128)(2,1)} fusion(f32[12,640,1280]{2,1,0:T(8,128)} %get-tuple-element.1807, f32[12,640]{1,0:T(8,128)S(1)} %get-tuple-element.1808, f32[12,640,1280]{2,1,0:T(8,128)} %get-tuple-element.1805, f32[12,640]{1,0:T(8,128)S(1)} %get-tuple-element.1806), kind=kLoop, calls=%fused_computation.26.clone.1 | loop fusion | flops 39321600 | bytes 98365440 | tf_op jit(solution)/shard_map/while/body/eval_jaxpr/cond/branch_0_fun/while/body/eval_jaxpr/convert_element_type | solution.py:139
  2012.8 13.3 bitcast_add_fusion.4
  2038.1 16.0 bitcast_add_fusion.5
  2054.1 16.8 bitcast_dynamic-update-slice_fusion.7
  2141.5 13.1 select_add_fusion.14
  2189.5 391.2 %conditional.7 = (f32[1280,768]{1,0:T(8,128)}, f32[768,3072]{1,0:T(8,128)}, f32[3072,768]{1,0:T(8,128)}, f32[768]{0:T(1024)}, f32[768]{0:T(1024)}, /*index=5*/f3...) conditional(s32[]{:T(128)} %clamp.22, (f32[1280]{0:T(1024)S(1)}, ...), branch_computations={%region_14.26_spmd, %region_27.34_spmd, %region_35.35_spmd} | conditional | flops 30565668864 | bytes 626768576 | solution.py:345
  2240.9 274.5 %while.79 = (s32[]{:T(128)}, f32[1280,12,64]{0,2,1:T(8,128)}, f32[1280,12,64]{0,2,1:T(8,128)}, bf16[2,640,12,64]{1,3,2,0:T(8,128)(2,1)}, bf16[2,640,12,64]{1,3,2...) while((s32[]{:T(128)}, f32[1280,12,64]{0,2,1:T(8,128)}, ...), condition=%wide.region_21.20_spmd.clone, body=%wide.region_17.19_spmd.clone.sunk | while | flops 10278185984 | bytes 316783328 | solution.py:155
  2241.1 18.3 fusion.291
  2259.4 29.6 %multiply_reduce_fusion.12 = (f32[12,640]{1,0:T(8,128)S(1)}, f32[12,640,1280]{2,1,0:T(8,128)}) fusion(f32[12,640,1280]{2,1,0:T(8,128)} %get-tuple-element.1805, f32[12,640]{1,0:T(8,128)S(1)} %get-tuple-element.1806, bf16[1280,12,64]{0,2,1:T(8,128)(2,1)} %get-tuple-element.1875, bf16[2,640,12,64]{1,3,2,0:T(8,128)(2,1)} %get-tuple-element.1874, ...), kind=kOutput, calls=%fused_computation.27.clone.1 | convolution fusion | flops 1287774720 | bytes 81654272 | tf_op jit(solution)/shard_map/while/body/eval_jaxpr/cond/branch_0_fun/while/body/eval_jaxpr/qhd,khd->hqk/dot_general | solution.py:135
  2289.1 31.8 %multiply_convert_fusion.11 = bf16[12,640,1280]{2,1,0:T(8,128)(2,1)} fusion(f32[12,640,1280]{2,1,0:T(8,128)} %get-tuple-element.1807, f32[12,640]{1,0:T(8,128)S(1)} %get-tuple-element.1808, f32[12,640,1280]{2,1,0:T(8,128)} %get-tuple-element.1805, f32[12,640]{1,0:T(8,128)S(1)} %get-tuple-element.1806), kind=kLoop, calls=%fused_computation.26.clone.1 | loop fusion | flops 39321600 | bytes 98365440 | tf_op jit(solution)/shard_map/while/body/eval_jaxpr/cond/branch_0_fun/while/body/eval_jaxpr/convert_element_type | solution.py:139
  2345.0 15.4 bitcast_add_fusion.5
  2360.4 16.8 bitcast_dynamic-update-slice_fusion.7
  2377.2 18.3 fusion.291
  2395.5 29.6 %multiply_reduce_fusion.12 = (f32[12,640]{1,0:T(8,128)S(1)}, f32[12,640,1280]{2,1,0:T(8,128)}) fusion(f32[12,640,1280]{2,1,0:T(8,128)} %get-tuple-element.1805, f32[12,640]{1,0:T(8,128)S(1)} %get-tuple-element.1806, bf16[1280,12,64]{0,2,1:T(8,128)(2,1)} %get-tuple-element.1875, bf16[2,640,12,64]{1,3,2,0:T(8,128)(2,1)} %get-tuple-element.1874, ...), kind=kOutput, calls=%fused_computation.27.clone.1 | convolution fusion | flops 1287774720 | bytes 81654272 | tf_op jit(solution)/shard_map/while/body/eval_jaxpr/cond/branch_0_fun/while/body/eval_jaxpr/qhd,khd->hqk/dot_general | solution.py:135
  2425.1 31.8 %multiply_convert_fusion.11 = bf16[12,640,1280]{2,1,0:T(8,128)(2,1)} fusion(f32[12,640,1280]{2,1,0:T(8,128)} %get-tuple-element.1807, f32[12,640]{1,0:T(8,128)S(1)} %get-tuple-element.1808, f32[12,640,1280]{2,1,0:T(8,128)} %get-tuple-element.1805, f32[12,640]{1,0:T(8,128)S(1)} %get-tuple-element.1806), kind=kLoop, calls=%fused_computation.26.clone.1 | loop fusion | flops 39321600 | bytes 98365440 | tf_op jit(solution)/shard_map/while/body/eval_jaxpr/cond/branch_0_fun/while/body/eval_jaxpr/convert_element_type | solution.py:139
  2457.0 13.3 bitcast_add_fusion.4
  2482.2 16.0 bitcast_add_fusion.5
  2498.3 16.8 bitcast_dynamic-update-slice_fusion.7
  2585.8 13.1 select_add_fusion.14
  2639.2 38.8 %collective-permute-done.3 = bf16[1536,768]{1,0:T(8,128)(2,1)S(1)} collective-permute-done((bf16[1536,768]{1,0:T(8,128)(2,1)}, bf16[1536,768]{1,0:T(8,128)(2,1)S(1)}, u32[]{:S(2)}, u32[]{:S(2)}) %collective-permute-start.3) | collective-permute-done | bytes 2359328 | tf_op jit(solution)/shard_map/ppermute | solution.py:17
  2697.0 39.5 %all-reduce = (f32[2,1536]{1,0:T(2,128)}, f32[2,768]{1,0:T(2,128)}, f32[2,3072]{1,0:T(2,128)}, f32[2,768]{1,0:T(2,128)}) all-reduce(f32[2,1536]{1,0:T(2,128)S(1)} %broadcast_multiply_fusion.5, f32[2,768]{1,0:T(2,128)S(1)} %get-tuple-element.1430, ...), channel_id=1, replica_groups=mesh['section'=4,'dp'=8] {'section','dp'}, use_global_device_ids=true, to_apply=%region_41.42 | all-reduce | flops 12288 | bytes 98304 | tf_op jit(solution)/shard_map/psum | solution.py:387
  2736.5 58.4 %all-reduce.5.cloned.1.call-done = (bf16[1,768,3072]{2,1,0:T(8,128)(2,1)}, bf16[1,1536,768]{2,1,0:T(8,128)(2,1)}) async-done(((bf16[1,768,3072]{2,1,0:T(8,128)(2,1)}, bf16[1,1536,768]{2,1,0:T(8,128)(2,1)}), (bf16[1,768,3072]{2,1,0:T(8,128)(2,1)}, bf16[1,1536,768]{2,1,0:T(8,128)(2,1)})) %all-reduce.5.cloned.1.call-update) | async-done | bytes 7077904 | tf_op jit(solution)/shard_map/psum | solution.py:381
  (680 shorter events, 771.6 us)
Async XLA Ops:
  7.2 2787.7 %all-reduce.5.cloned.1.call-start = ((), (), s32[]{:S(2)}) async-start(), calls=%async_computation | async-start | bytes 14155776 | tf_op jit(solution)/shard_map/psum | solution.py:381
  7.2 55.7 %collective-permute-start.2 = (bf16[1,1536,768]{2,1,0:T(8,128)(2,1)}, bf16[1,1536,768]{2,1,0:T(8,128)(2,1)S(1)}, u32[]{:S(2)}, u32[]{:S(2)}) collective-permute-start(bf16[1,1536,768]{2,1,0:T(8,128)(2,1)} %param.29), channel_id=1, source_target_pairs={{0,8},{8,16},{16,24},{1,9},{9,17},{17,25},{2,10},{10,18},{18,26},{... | collective-permute-start | bytes 7077896 | tf_op jit(solution)/shard_map/ppermute | solution.py:17
  219.3 43.1 %collective-permute-start.1 = (bf16[1280,768]{1,0:T(8,128)(2,1)}, bf16[1280,768]{1,0:T(8,128)(2,1)}, u32[]{:S(2)}, u32[]{:S(2)}) collective-permute-start(bf16[1280,768]{1,0:T(8,128)(2,1)} %get-tuple-element.1758), channel_id=1, source_target_pairs={{0,8},{8,16},{16,24},{1,9},{9,17},{17,25},{2,10},{10,18},{18,26},{... | collective-permute-start | bytes 5898248 | tf_op jit(solution)/shard_map/while/body/eval_jaxpr/ppermute | solution.py:17
  227.5 36.5 %copy-start.66 = (s32[2]{0:T(128)S(1)}, s32[2]{0:T(128)}, u32[]{:S(2)}) copy-start(s32[2]{0:T(128)} %copy-done.65) | copy-start | bytes 28 | tf_op jit(solution)/shard_map/while
  411.5 42.5 %collective-permute-start.1 = (bf16[1280,768]{1,0:T(8,128)(2,1)}, bf16[1280,768]{1,0:T(8,128)(2,1)}, u32[]{:S(2)}, u32[]{:S(2)}) collective-permute-start(bf16[1280,768]{1,0:T(8,128)(2,1)} %get-tuple-element.1758), channel_id=1, source_target_pairs={{0,8},{8,16},{16,24},{1,9},{9,17},{17,25},{2,10},{10,18},{18,26},{... | collective-permute-start | bytes 5898248 | tf_op jit(solution)/shard_map/while/body/eval_jaxpr/ppermute | solution.py:17
  419.7 35.8 %copy-start.66 = (s32[2]{0:T(128)S(1)}, s32[2]{0:T(128)}, u32[]{:S(2)}) copy-start(s32[2]{0:T(128)} %copy-done.65) | copy-start | bytes 28 | tf_op jit(solution)/shard_map/while
  479.4 101.4 %collective-permute-start.1 = (bf16[1280,768]{1,0:T(8,128)(2,1)}, bf16[1280,768]{1,0:T(8,128)(2,1)}, u32[]{:S(2)}, u32[]{:S(2)}) collective-permute-start(bf16[1280,768]{1,0:T(8,128)(2,1)} %get-tuple-element.1758), channel_id=1, source_target_pairs={{0,8},{8,16},{16,24},{1,9},{9,17},{17,25},{2,10},{10,18},{18,26},{... | collective-permute-start | bytes 5898248 | tf_op jit(solution)/shard_map/while/body/eval_jaxpr/ppermute | solution.py:17
  547.4 34.9 %copy-start.66 = (s32[2]{0:T(128)S(1)}, s32[2]{0:T(128)}, u32[]{:S(2)}) copy-start(s32[2]{0:T(128)} %copy-done.65) | copy-start | bytes 28 | tf_op jit(solution)/shard_map/while
  606.1 44.0 %collective-permute-start.1 = (bf16[1280,768]{1,0:T(8,128)(2,1)}, bf16[1280,768]{1,0:T(8,128)(2,1)}, u32[]{:S(2)}, u32[]{:S(2)}) collective-permute-start(bf16[1280,768]{1,0:T(8,128)(2,1)} %get-tuple-element.1758), channel_id=1, source_target_pairs={{0,8},{8,16},{16,24},{1,9},{9,17},{17,25},{2,10},{10,18},{18,26},{... | collective-permute-start | bytes 5898248 | tf_op jit(solution)/shard_map/while/body/eval_jaxpr/ppermute | solution.py:17
  617.7 34.0 %copy-start.66 = (s32[2]{0:T(128)S(1)}, s32[2]{0:T(128)}, u32[]{:S(2)}) copy-start(s32[2]{0:T(128)} %copy-done.65) | copy-start | bytes 28 | tf_op jit(solution)/shard_map/while
  675.5 166.6 %collective-permute-start.1 = (bf16[1280,768]{1,0:T(8,128)(2,1)}, bf16[1280,768]{1,0:T(8,128)(2,1)}, u32[]{:S(2)}, u32[]{:S(2)}) collective-permute-start(bf16[1280,768]{1,0:T(8,128)(2,1)} %get-tuple-element.1758), channel_id=1, source_target_pairs={{0,8},{8,16},{16,24},{1,9},{9,17},{17,25},{2,10},{10,18},{18,26},{... | collective-permute-start | bytes 5898248 | tf_op jit(solution)/shard_map/while/body/eval_jaxpr/ppermute | solution.py:17
  810.5 33.1 %copy-start.66 = (s32[2]{0:T(128)S(1)}, s32[2]{0:T(128)}, u32[]{:S(2)}) copy-start(s32[2]{0:T(128)} %copy-done.65) | copy-start | bytes 28 | tf_op jit(solution)/shard_map/while
  906.5 42.6 %collective-permute-start = (bf16[1280,768]{1,0:T(8,128)(2,1)}, bf16[1280,768]{1,0:T(8,128)(2,1)S(1)}, u32[]{:S(2)}, u32[]{:S(2)}) collective-permute-start(bf16[1280,768]{1,0:T(8,128)(2,1)} %convert_element_type.286), channel_id=1, source_target_pairs={{8,0},{16,8},{24,16},{9,1},{17,9},{25,17},{10,2},{18,10},{26,18},{... | collective-permute-start | bytes 5898248 | tf_op jit(solution)/shard_map/while/body/eval_jaxpr/ppermute | solution.py:17
  925.0 24.1 copy-start.68
  1002.1 97.3 %collective-permute-start = (bf16[1280,768]{1,0:T(8,128)(2,1)}, bf16[1280,768]{1,0:T(8,128)(2,1)S(1)}, u32[]{:S(2)}, u32[]{:S(2)}) collective-permute-start(bf16[1280,768]{1,0:T(8,128)(2,1)} %convert_element_type.286), channel_id=1, source_target_pairs={{8,0},{16,8},{24,16},{9,1},{17,9},{25,17},{10,2},{18,10},{26,18},{... | collective-permute-start | bytes 5898248 | tf_op jit(solution)/shard_map/while/body/eval_jaxpr/ppermute | solution.py:17
  1003.4 13.2 copy-start.37
  1003.4 13.2 copy-start.44
  1003.5 13.2 copy-start.34
  1003.5 13.2 copy-start.41
  1003.5 13.2 copy-start.53
  1003.5 13.2 copy-start.56
  1003.5 13.3 copy-start.47
  1003.5 13.3 copy-start.50
  1023.3 76.1 %copy-start.68 = (s32[2]{0:T(128)S(1)}, s32[2]{0:T(128)}, u32[]{:S(2)}) copy-start(s32[2]{0:T(128)} %copy-done.67) | copy-start | bytes 28 | tf_op jit(solution)/shard_map/while
  1152.4 583.7 %collective-permute-start = (bf16[1280,768]{1,0:T(8,128)(2,1)}, bf16[1280,768]{1,0:T(8,128)(2,1)S(1)}, u32[]{:S(2)}, u32[]{:S(2)}) collective-permute-start(bf16[1280,768]{1,0:T(8,128)(2,1)} %convert_element_type.286), channel_id=1, source_target_pairs={{8,0},{16,8},{24,16},{9,1},{17,9},{25,17},{10,2},{18,10},{26,18},{... | collective-permute-start | bytes 5898248 | tf_op jit(solution)/shard_map/while/body/eval_jaxpr/ppermute | solution.py:17
  1153.7 13.2 copy-start.37
  1153.7 13.2 copy-start.44
  1153.7 13.2 copy-start.34
  1153.7 13.2 copy-start.41
  1153.8 13.2 copy-start.53
  1153.8 13.2 copy-start.56
  1153.8 13.3 copy-start.47
  1153.8 13.3 copy-start.50
  1173.6 562.5 %copy-start.68 = (s32[2]{0:T(128)S(1)}, s32[2]{0:T(128)}, u32[]{:S(2)}) copy-start(s32[2]{0:T(128)} %copy-done.67) | copy-start | bytes 28 | tf_op jit(solution)/shard_map/while
  1745.1 51.4 %copy-start.20 = (f32[1280]{0:T(1024)}, f32[1280]{0:T(1024)S(1)}, u32[]{:S(2)}) copy-start(f32[1280]{0:T(1024)S(1)} %get-tuple-element.999) | copy-start | bytes 15364 | tf_op jit(solution)/shard_map/while/body/eval_jaxpr/cond
  2012.8 13.3 copy-start.13
  2012.8 13.3 copy-start.17
  2140.1 40.1 %collective-permute-start = (bf16[1280,768]{1,0:T(8,128)(2,1)}, bf16[1280,768]{1,0:T(8,128)(2,1)S(1)}, u32[]{:S(2)}, u32[]{:S(2)}) collective-permute-start(bf16[1280,768]{1,0:T(8,128)(2,1)} %convert_element_type.286), channel_id=1, source_target_pairs={{8,0},{16,8},{24,16},{9,1},{17,9},{25,17},{10,2},{18,10},{26,18},{... | collective-permute-start | bytes 5898248 | tf_op jit(solution)/shard_map/while/body/eval_jaxpr/ppermute | solution.py:17
  2141.4 13.2 copy-start.37
  2141.4 13.2 copy-start.44
  2141.4 13.2 copy-start.34
  2141.4 13.2 copy-start.41
  2141.4 13.2 copy-start.53
  2141.4 13.2 copy-start.56
  2141.5 13.3 copy-start.47
  2141.5 13.3 copy-start.50
  2161.2 18.9 copy-start.68
  2189.5 51.4 %copy-start.20 = (f32[1280]{0:T(1024)}, f32[1280]{0:T(1024)S(1)}, u32[]{:S(2)}) copy-start(f32[1280]{0:T(1024)S(1)} %get-tuple-element.999) | copy-start | bytes 15364 | tf_op jit(solution)/shard_map/while/body/eval_jaxpr/cond
  2457.0 13.3 copy-start.13
  2457.0 13.3 copy-start.17
  2584.4 39.2 %collective-permute-start = (bf16[1280,768]{1,0:T(8,128)(2,1)}, bf16[1280,768]{1,0:T(8,128)(2,1)S(1)}, u32[]{:S(2)}, u32[]{:S(2)}) collective-permute-start(bf16[1280,768]{1,0:T(8,128)(2,1)} %convert_element_type.286), channel_id=1, source_target_pairs={{8,0},{16,8},{24,16},{9,1},{17,9},{25,17},{10,2},{18,10},{26,18},{... | collective-permute-start | bytes 5898248 | tf_op jit(solution)/shard_map/while/body/eval_jaxpr/ppermute | solution.py:17
  2585.7 13.2 copy-start.44
  2585.7 13.2 copy-start.34
  2585.7 13.2 copy-start.41
  2585.7 13.2 copy-start.53
  2585.7 13.2 copy-start.56
  2585.7 13.3 copy-start.47
  2585.8 13.3 copy-start.50
  2605.5 18.0 copy-start.68
  2631.3 46.7 %collective-permute-start.3 = (bf16[1536,768]{1,0:T(8,128)(2,1)}, bf16[1536,768]{1,0:T(8,128)(2,1)S(1)}, u32[]{:S(2)}, u32[]{:S(2)}) collective-permute-start(bf16[1536,768]{1,0:T(8,128)(2,1)} %slice.81), channel_id=1, source_target_pairs={{8,0},{16,8},{24,16},{9,1},{17,9},{25,17},{10,2},{18,10},{26,18},{... | collective-permute-start | bytes 7077896 | tf_op jit(solution)/shard_map/ppermute | solution.py:17
  2682.4 14.4 copy-start.55
  2682.4 14.4 copy-start.58
  2682.4 14.5 copy-start.46
  2682.4 14.5 copy-start.39
  (137 other events, 761.2 us)
Sparse Core Ops, SparseCore 0:
  2682.6 112.3 all-reduce.4
where the time goes:
time: 2820 us; the launch traced here: 2810 us
  waiting for transfers between devices  958 us (34%)
  matrix products  715 us (25%)
  other arithmetic  464 us (16%)
  local copies, waits for them, and re-layouts  218 us (8%)
  starting transfers between devices  216 us (8%)
  loops' own time  175 us (6%)
  blocking collectives  52 us (2%)
    ppermute x12, waiting for transfers between devices, passed_along(): return lax.ppermute(block, axis, route)  899 us
    ppermute x12, starting transfers between devices, passed_along(): return lax.ppermute(block, axis, route)  216 us
    convert_element_type x4, other arithmetic, back_block(): grad_scores = (attn_probs * (grad_probs - row_dots)).astype(jnp.bfloat16)  127 us
    sub x8, matrix products, softmax_rows(): powered = jnp.exp(scores - jnp.max(scores, axis=-1, keepdims=True))  123 us
    add x30, other arithmetic, backward_tick(): running + adding  119 us
    dot_general x4, matrix products, back_block(): jnp.einsum('qhd,khd->hqk', grad_blk, value_heads, preferred_element_type=...  119 us
    another operation x5, loops' own time, backward_tick(): lax.switch(branch_index, [attention_grads, feedforward_grads, resting_gra...  109 us
    dot_general x4, matrix products, one_block(): jnp.einsum('hqk,khd->qhd', attn_probs.astype(jnp.bfloat16), value_heads,...  81.6 us
  transfers between devices with their start and end apart: 13, of which 13 were waited for; matrix products, arithmetic and copies ran while one was open for 7% of the time, Pallas kernels for 0%

commit v1 on v0

v1 whole, which is shorter than its diff:
```python
import functools
import math

import jax
import jax.numpy as jnp
from jax import lax
from jax.experimental import pallas as pl
from jax.experimental.pallas import tpu as pltpu
from jax.sharding import PartitionSpec as P

HEADS = 12
LONG = 1214
SHORT = 514
EPS = 1e-06
HEAD_DIM = 64
PAIR = 2 * HEAD_DIM
MASKED = -1e30
F32 = jnp.float32
BF16 = jnp.bfloat16
KERNEL_VMEM = 56 * 2**20


def mm(left, right):
    return jnp.dot(left, right, preferred_element_type=F32)


def contract_rows(left, right):
    return lax.dot_general(left, right, (((0,), (0,)), ((), ())), preferred_element_type=F32)


def contract_cols(left, right):
    return lax.dot_general(left, right, (((1,), (1,)), ((), ())), preferred_element_type=F32)


def lane_ids(shape):
    return lax.broadcasted_iota(jnp.int32, shape, len(shape) - 1)


def three_parts(value):
    high = value.astype(BF16).astype(F32)
    rest = value - high
    middle = rest.astype(BF16).astype(F32)
    return high, middle, rest - middle


def extend_keys(keys_out, values_out, blocks, bias_ref, head):
    aux = HEAD_DIM * (1 - head)
    row = 0
    for key_ref, value_ref in blocks:
        rows = key_ref.shape[0]
        span = slice(row, row + rows)
        lanes = lane_ids((rows, PAIR))
        inside = (lanes // HEAD_DIM) == head
        ones = jnp.where((lanes > aux) & (lanes <= aux + 3), 1.0, 0.0)
        extra = jnp.where(lanes == aux, bias_ref[span, :], ones)
        keys_out[span, :] = jnp.where(inside, key_ref[...].astype(F32), extra).astype(BF16)
        ones = jnp.where((lanes >= aux) & (lanes < aux + 3), 1.0, 0.0)
        values_out[span, :] = jnp.where(inside, value_ref[...].astype(F32), ones).astype(BF16)
        row += rows


def attention_forward_body(
    chunk, query_ref, key_own, value_own, key_far, value_far, bias_ref,
    out_ref, extended_ref, keys, values,
):
    rows = query_ref.shape[0]
    for head in (0, 1):
        extend_keys(
            keys.at[head], values.at[head], ((key_own, value_own), (key_far, value_far)), bias_ref, head
        )
    lanes = lane_ids((chunk, PAIR))
    for start in range(0, rows, chunk):
        span = slice(start, start + chunk)
        outs = []
        for head in (0, 1):
            aux = HEAD_DIM * (1 - head)
            inside = (lanes // HEAD_DIM) == head
            query = query_ref[span, :].astype(F32)
            extended = jnp.where(inside, query, jnp.where(lanes == aux, 1.0, 0.0))
            scores = contract_cols(extended.astype(BF16), keys[head])
            top = jnp.max(scores, axis=1, keepdims=True)
            powered = jnp.exp(scores - top).astype(BF16)
            summed = mm(powered, values[head])
            total = summed[:, aux : aux + 1]
            outs.append(summed / total)
            high, middle, low = three_parts(-(top + jnp.log(total)))
            extended = jnp.where(lanes == aux + 1, high, extended)
            extended = jnp.where(lanes == aux + 2, middle, extended)
            extended = jnp.where(lanes == aux + 3, low, extended)
            extended_ref[head, span, :] = extended.astype(BF16)
        out_ref[span, :] = jnp.where(lanes < HEAD_DIM, outs[0], outs[1])


def attention_forward(qkv, kv_far, key_bias):
    rows, width = qkv.shape[0], qkv.shape[1] // 3
    pairs = width // PAIR

    def block(base):
        return pl.BlockSpec((rows, PAIR), lambda p: (0, base + p))

    return pl.pallas_call(
        functools.partial(attention_forward_body, rows // 2),
        grid=(pairs,),
        in_specs=[
            block(0), block(pairs), block(2 * pairs), block(0), block(pairs),
            pl.BlockSpec((2 * rows, 1), lambda p: (0, 0)),
        ],
        out_specs=[block(0), pl.BlockSpec((2, rows, PAIR), lambda p: (p, 0, 0))],
        out_shape=[
            jax.ShapeDtypeStruct((rows, width), F32),
            jax.ShapeDtypeStruct((2 * pairs, rows, PAIR), BF16),
        ],
        scratch_shapes=[pltpu.VMEM((2, 2 * rows, PAIR), BF16)] * 2,
        compiler_params=pltpu.CompilerParams(vmem_limit_bytes=KERNEL_VMEM),
        cost_estimate=pl.CostEstimate(
            flops=16 * rows * rows * 2 * width * 2, bytes_accessed=12 * rows * width,
            transcendentals=2 * rows * rows * 2 * pairs,
        ),
        name="attention_forward",
    )(qkv, qkv, qkv, kv_far, kv_far, key_bias)


def attention_backward_body(
    chunks, extended_ref, key_own, value_own, key_far, value_far, bias_ref, grad_ref, out_ref,
    grad_query, grad_key_own, grad_value_own, grad_key_far, grad_value_far,
    keys, values, key_sums, value_sums,
):
    rows = extended_ref.shape[1]
    for head in (0, 1):
        extend_keys(
            keys.at[head], values.at[head], ((key_own, value_own), (key_far, value_far)), bias_ref, head
        )
    for start, size in chunks:
        span = slice(start, start + size)
        lanes = lane_ids((size, PAIR))
        parts = []
        for head in (0, 1):
            aux = HEAD_DIM * (1 - head)
            inside = (lanes // HEAD_DIM) == head
            query = extended_ref[head, span, :]
            grad = jnp.where(inside, grad_ref[span, :].astype(F32), 0.0)
            dots = jnp.sum(grad * out_ref[span, :], axis=1, keepdims=True)
            high, middle, low = three_parts(-dots)
            grad = jnp.where(lanes == aux, high, grad)
            grad = jnp.where(lanes == aux + 1, middle, grad)
            grad = jnp.where(lanes == aux + 2, low, grad)
            probs = jnp.exp(contract_cols(query, keys[head]))
            shifted = contract_cols(grad.astype(BF16), values[head])
            grad_scores = (probs * shifted).astype(BF16)
            parts.append(mm(grad_scores, keys[head]) * HEAD_DIM**-0.5)
            to_values = mm(grad.T.astype(BF16), probs.astype(BF16)).T
            to_keys = mm(query.astype(F32).T.astype(BF16), grad_scores).T
            if start == 0:
                key_sums[head] = to_keys
                value_sums[head] = to_values
            else:
                key_sums[head] += to_keys
                value_sums[head] += to_values
        grad_query[span, :] = jnp.where(lanes < HEAD_DIM, parts[0], parts[1]).astype(BF16)
    lanes = lane_ids((rows, PAIR))
    for part, (to_key, to_value) in enumerate(
        ((grad_key_own, grad_value_own), (grad_key_far, grad_value_far))
    ):
        span = slice(part * rows, (part + 1) * rows)
        first = lanes < HEAD_DIM
        to_key[...] = jnp.where(first, key_sums[0, span, :], key_sums[1, span, :]).astype(BF16)
        to_value[...] = jnp.where(first, value_sums[0, span, :], value_sums[1, span, :]).astype(BF16)


def attention_backward(extended, qkv, kv_far, key_bias, grad, out):
    rows, width = out.shape
    pairs = width // PAIR

    def block(base):
        return pl.BlockSpec((rows, PAIR), lambda p: (0, base + p))

    shape = jax.ShapeDtypeStruct((rows, width), BF16)
    return pl.pallas_call(
        functools.partial(attention_backward_body, ((0, rows),)),
        grid=(pairs,),
        in_specs=[
            pl.BlockSpec((2, rows, PAIR), lambda p: (p, 0, 0)),
            block(pairs), block(2 * pairs), block(0), block(pairs),
            pl.BlockSpec((2 * rows, 1), lambda p: (0, 0)),
            block(0), block(0),
        ],
        out_specs=[block(0)] * 5,
        out_shape=[shape] * 5,
        scratch_shapes=[pltpu.VMEM((2, 2 * rows, PAIR), BF16)] * 2
        + [pltpu.VMEM((2, 2 * rows, PAIR), F32)] * 2,
        compiler_params=pltpu.CompilerParams(vmem_limit_bytes=KERNEL_VMEM),
        cost_estimate=pl.CostEstimate(
            flops=40 * rows * rows * 2 * width * 2, bytes_accessed=24 * rows * width,
            transcendentals=2 * rows * rows * 2 * pairs,
        ),
        name="attention_backward",
    )(extended, qkv, qkv, kv_far, kv_far, key_bias, grad, out)


def norm_parts(hidden):
    average = jnp.mean(hidden, axis=-1, keepdims=True)
    centred = hidden - average
    inverse = lax.rsqrt(jnp.mean(centred * centred, axis=-1, keepdims=True) + EPS)
    return centred * inverse, inverse


def norm_backward(hidden, grad_normed, gain):
    unit, inverse = norm_parts(hidden)
    scaled = grad_normed * gain
    first = jnp.mean(scaled, axis=-1, keepdims=True)
    second = jnp.mean(scaled * unit, axis=-1, keepdims=True)
    grad_hidden = inverse * (scaled - first - unit * second)
    return grad_hidden, jnp.sum(grad_normed * unit, axis=0), jnp.sum(grad_normed, axis=0)


def gelu_and_slope(pre):
    size = jnp.abs(pre) * (0.5**0.5)
    density = jnp.exp(-0.5 * pre * pre)
    t = 1.0 / (1.0 + 0.3275911 * size)
    series = t * (0.254829592 + t * (-0.284496736 + t * (1.421413741 + t * (-1.453152027 + t * 1.061405429))))
    tail = 0.5 * series * density
    below = jnp.where(pre < 0, tail, 1.0 - tail)
    return pre * below, below + pre * density * (1.0 / math.sqrt(2.0 * math.pi))


def swap(block, bit):
    count = lax.axis_size("dp")
    return lax.ppermute(block, "dp", [(i, i ^ bit) for i in range(count)])


def spread_over_sections(piece, source, section):
    result = piece
    for step, last in ((1, lax.axis_size("section") - 1), (-1, 0)):
        carried = piece
        for at in range(source, last, step):
            carried = lax.ppermute(carried, "section", [(at, at + step)])
            result = jnp.where(section == at + step, carried, result)
    return result


def rows_from(array, start, size):
    return lax.dynamic_slice_in_dim(array, start, size, 0)


def gather_rows(weight, source, place):
    rows = weight.shape[0]
    half, part = rows // 2, rows // 4
    mine = rows_from(weight, place.core * half + place.parity * part, part)
    mine = spread_over_sections(mine, source, place.section)
    from_x = swap(mine[: part // 2], place.x_bit)
    from_y = swap(mine[part // 2 :], place.y_bit)
    near = jnp.concatenate([from_x, from_y], axis=0)
    first = jnp.where(place.parity == 0, mine, near)
    second = jnp.where(place.parity == 0, near, mine)
    own = jnp.concatenate([first, second], axis=0)
    other = swap(own, 1)
    return jnp.concatenate(
        [jnp.where(place.core == 0, own, other), jnp.where(place.core == 0, other, own)], axis=0
    )


def add(a, b):
    return (a.astype(F32) + b.astype(F32)).astype(BF16)


def scatter_rows(grad, place):
    half = grad.shape[0] // 2
    kept = rows_from(grad, place.core * half, half)
    given = rows_from(grad, (1 - place.core) * half, half)
    kept = add(kept, swap(given, 1))
    columns = kept.shape[1] // 2
    lanes = []
    for lane, bits in enumerate((place.bits, place.bits[::-1])):
        block = kept[:, lane * columns : (lane + 1) * columns]
        for bit in bits:
            size = block.shape[0] // 2
            high = (place.dp // bit) % 2
            given = rows_from(block, (1 - high) * size, size)
            block = add(rows_from(block, high * size, size), swap(given, bit))
        lanes.append(block)
    return jnp.stack(lanes)


def to_section(block, target, section):
    count = lax.axis_size("section")
    total = jnp.where(section == target, block.astype(F32), 0.0)
    for source in range(count):
        if source != target:
            total = total + lax.ppermute(block, "section", [(source, target)]).astype(F32)
    return total


def gather_scattered(lanes, place):
    out = []
    for lane, bits in enumerate((place.bits, place.bits[::-1])):
        block = lanes[lane]
        for bit in bits[::-1]:
            high = (place.dp // bit) % 2
            far = swap(block, bit)
            block = jnp.concatenate(
                [jnp.where(high == 0, block, far), jnp.where(high == 0, far, block)], axis=0
            )
        out.append(block)
    own = jnp.concatenate(out, axis=1)
    far = swap(own, 1)
    return jnp.concatenate(
        [jnp.where(place.core == 0, own, far), jnp.where(place.core == 0, far, own)], axis=0
    ).astype(F32)


def deliver(block, target):
    sections, count = lax.axis_size("section"), lax.axis_size("dp")
    pieces = []
    for slot in (0, 1):
        for core in (0, 1):
            route = [
                (z * count + d, target * count + (d - core + z // 2))
                for z in range(slot, sections, 2)
                for d in range(core, count, 2)
            ]
            pieces.append(lax.ppermute(block, ("section", "dp"), route))
    return pieces


class Place:
    def __init__(self):
        self.section = lax.axis_index("section")
        self.dp = lax.axis_index("dp")
        count = lax.axis_size("dp")
        self.core = self.dp % 2
        self.bits = [1 << i for i in range(1, count.bit_length() - 1)]
        self.x_bit, self.y_bit = self.bits[0], self.bits[-1]
        self.parity = ((self.dp // self.x_bit) + (self.dp // self.y_bit)) % 2


def per_device(
    clip_inputs, out_grad, clip_class, w_front, w_back, norm_gain, norm_shift,
    bias_query_value, bias_attn_out, bias_up, bias_down,
):
    place = Place()
    sections = lax.axis_size("section")
    padded, width = clip_inputs.shape[1:]
    rows = -(-LONG // 32) * 16
    core, section = place.core, place.section

    owner, slot = section // 2, section % 2
    mine = jnp.stack([lax.dynamic_index_in_dim(a, slot, 0, False) for a in (clip_inputs, out_grad)])
    far = swap(lax.dynamic_slice_in_dim(mine, (1 - core) * rows, rows, 1), 1)
    near = lax.dynamic_slice_in_dim(mine, core * rows, rows, 1)
    clip_pair = jnp.where(core == owner, near, far)
    own_class = lax.dynamic_index_in_dim(clip_class, slot, 0, False).astype(F32)
    own_class = jnp.broadcast_to(own_class, (8, 128))
    clip_kind = jnp.where(core == owner, own_class, swap(own_class, 1))[0, 0]
    length = SHORT + (LONG - SHORT) * clip_kind
    positions = jnp.arange(rows, dtype=jnp.int32)
    own_rows = (positions + core * rows).astype(F32) < length
    far_rows = (positions + (1 - core) * rows).astype(F32) < length
    row_mask = own_rows.astype(F32)[:, None]
    key_bias = jnp.where(jnp.concatenate([own_rows, far_rows]), 0.0, MASKED)[:, None]

    gains = lax.all_gather(norm_gain[0], "section")
    shifts = lax.all_gather(norm_shift[0], "section")
    fronts = [gather_rows(w_front[0], s, place) for s in range(sections)]
    downs = [
        jnp.concatenate([gather_rows(w_back[0], s - 1, place), gather_rows(w_back[0], s, place)], axis=0)
        if s % 2
        else None
        for s in range(sections)
    ]

    hidden = (clip_pair[0].astype(F32) * row_mask).astype(BF16)
    saved, delivered = [], []
    for s in range(sections):
        layer = s // 2
        entering = hidden.astype(F32)
        unit, _ = norm_parts(entering)
        normed = (unit * gains[s] + shifts[s]).astype(BF16)
        if s % 2 == 0:
            pair = bias_query_value[layer]
            bias = jnp.concatenate([pair[:width], jnp.zeros((width,), F32), pair[width:]])
            scale = jnp.where(jnp.arange(3 * width) < width, HEAD_DIM**-0.5, 1.0)
            qkv = ((mm(normed, fronts[s][:, : 3 * width]) + bias).astype(BF16) * scale).astype(BF16)
            kv_far = swap(qkv[:, width:], 1)
            attended, extended = attention_forward(qkv, kv_far, key_bias)
            attended_b = attended.astype(BF16)
            branch = contract_cols(attended_b, fronts[s][:, 3 * width :]) + bias_attn_out[layer]
            saved.append((hidden, normed, qkv, kv_far, attended, attended_b, extended))
        else:
            pre = mm(normed, fronts[s]) + bias_up[layer]
            act, slope = gelu_and_slope(pre)
            act, slope = act.astype(BF16), slope.astype(BF16)
            branch = mm(act, downs[s]) + bias_down[layer]
            saved.append((hidden, normed, act, slope))
        hidden = (row_mask * (entering + branch)).astype(BF16)
        delivered.append(deliver(hidden, s))

    incoming = clip_pair[1]
    sent_grads = [None] * sections
    front_total = jnp.zeros((), F32)
    back_total = jnp.zeros((), F32)
    grad_gain, grad_shift = [None] * sections, [None] * sections
    grad_pairs, grad_outs, grad_ups, grad_downs = [], [], [], []
    for s in reversed(range(sections)):
        grad_rows = row_mask * incoming.astype(F32)
        grad_b = grad_rows.astype(BF16)
        front = fronts[s]
        if s % 2 == 0:
            entered, normed, qkv, kv_far, attended, attended_b, extended = saved[s]
            grad_attended = mm(grad_b, front[:, 3 * width :]).astype(BF16)
            to_query, to_key, to_value, key_far, value_far = attention_backward(
                extended, qkv, kv_far, key_bias, grad_attended, attended
            )
            back = swap(jnp.stack([key_far, value_far]), 1)
            grad_qkv = jnp.concatenate([to_query, add(to_key, back[0]), add(to_value, back[1])], axis=1)
            sums = jnp.sum(grad_qkv.astype(F32), axis=0)
            grad_pairs.insert(0, jnp.concatenate([sums[:width], sums[2 * width :]]))
            grad_outs.insert(0, jnp.sum(grad_rows, axis=0))
            grad_front = jnp.concatenate(
                [contract_rows(normed, grad_qkv).astype(BF16), contract_rows(grad_b, attended_b).astype(BF16)],
                axis=1,
            )
            grad_normed = contract_cols(grad_qkv, front[:, : 3 * width])
        else:
            entered, normed, act, slope = saved[s]
            grad_act = contract_cols(grad_b, downs[s])
            grad_pre = (grad_act * slope.astype(F32)).astype(BF16)
            grad_down = contract_rows(act, grad_b).astype(BF16)
            grad_front = contract_rows(normed, grad_pre).astype(BF16)
            grad_ups.insert(0, jnp.sum(grad_pre.astype(F32), axis=0))
            grad_downs.insert(0, jnp.sum(grad_rows, axis=0))
            grad_normed = contract_cols(grad_pre, front)
            half = grad_down.shape[0] // 2
            for target, piece in ((s - 1, grad_down[:half]), (s, grad_down[half:])):
                back_total = back_total + to_section(scatter_rows(piece, place), target, section)
        front_total = front_total + to_section(scatter_rows(grad_front, place), s, section)
        grad_hidden, grad_gain[s], grad_shift[s] = norm_backward(entered.astype(F32), grad_normed, gains[s])
        incoming = (grad_rows + grad_hidden).astype(BF16)
        sent_grads[s] = deliver(incoming, s)

    def assemble(pieces, kind):
        clips = []
        for slot_id in (0, 1):
            halves = []
            for half in (0, 1):
                choice = pieces[0][2 * slot_id + half]
                for s in range(1, sections):
                    choice = jnp.where(section == s, pieces[s][2 * slot_id + half], choice)
                halves.append(choice.astype(kind))
            halves.append(jnp.zeros((padded - 2 * rows, width), kind))
            clips.append(jnp.concatenate(halves, axis=0))
        return jnp.stack(clips)[None]

    small = lax.psum(
        jnp.concatenate(
            [v.reshape(-1) for v in grad_gain + grad_shift + grad_pairs + grad_outs + grad_ups + grad_downs]
        ),
        ("section", "dp"),
    )
    parts, place_at = [], 0
    layers, hidden_units = bias_up.shape
    for count, size in (
        (sections, width), (sections, width), (layers, 2 * width), (layers, width),
        (layers, hidden_units), (layers, width),
    ):
        parts.append(small[place_at : place_at + count * size].reshape(count, size))
        place_at += count * size
    return (
        assemble(delivered, BF16),
        assemble(sent_grads, F32),
        gather_scattered(front_total.astype(BF16), place)[None],
        gather_scattered(back_total.astype(BF16), place)[None],
        lax.dynamic_slice_in_dim(parts[0], section, 1, 0),
        lax.dynamic_slice_in_dim(parts[1], section, 1, 0),
        *parts[2:],
    )


def solution(mesh):
    placed = (
        P("dp", None, None), P("dp", None, None), P("dp"),
        P("section", None, None), P("section", None, None), P("section", None), P("section", None),
        P(), P(), P(), P(),
    )
    return jax.shard_map(
        per_device,
        mesh=mesh,
        in_specs=placed,
        out_specs=(
            P("section", "dp", None, None), P("section", "dp", None, None),
            P("section", None, None), P("section", None, None), P("section", None), P("section", None),
            P(), P(), P(), P(),
        ),
        check_vma=False,
    )
```

time: 2820 us -> 1290 us (0.46)
  matrix products: 715 us -> 140 us
  waiting for transfers between devices: 958 us -> 413 us
  other arithmetic: 464 us -> 127 us
  starting transfers between devices: 216 us -> 393 us
  loops' own time: 175 us -> 0 us
  local copies, waits for them, and re-layouts: 218 us -> 54.6 us
  Pallas kernels: 0 us -> 95.2 us
    ppermute x12 -> x160, waiting for transfers between devices: 899 us -> 317 us  [the longest x80 187 us: swap(): return lax.ppermute(block, 'dp', [(i, i ^ bit) for i in range(count)])]
    dot_general x36 -> x8, matrix products: 539 us -> 46 us  [mm(): return jnp.dot(left, right, preferred_element_type=F32)]
    ppermute x12 -> x160, starting transfers between devices: 216 us -> 393 us  [the longest x80 156 us: swap(): return lax.ppermute(block, 'dp', [(i, i ^ bit) for i in range(count)])]
    convert_element_type x37 -> x39, other arithmetic: 210 us -> 34.4 us  [the longest x26 13.2 us: add(): return (a.astype(F32) + b.astype(F32)).astype(BF16)]
    another operation x16 -> x0, loops' own time: 175 us -> none  [the longest x5 109 us: backward_tick(): lax.switch(branch_index, [attention_grads, feedforward_grads, resting_gra...]
    sub x8 -> x0, matrix products: 123 us -> none  [softmax_rows(): powered = jnp.exp(scores - jnp.max(scores, axis=-1, keepdims=True))]
    add x31 -> x0, other arithmetic: 120 us -> none  [the longest x30 119 us: backward_tick(): running + adding]
    pallas_call x0 -> x4, Pallas kernels: none -> 95.2 us  [the longest x2 55.9 us: attention_backward(): pl.pallas_call(functools.partial(attention_backward_body, ((0, rows),)),...]
  transfers between devices with their start and end apart: 13 -> 161, of which waited for: 13 -> 56; matrix products, arithmetic and copies ran while one was open for 7% -> 23% of each run, Pallas kernels for 0% -> 7%
where the time goes in v1:
time: 1290 us; the launch traced here: 1270 us
  waiting for transfers between devices  413 us (32%)
  starting transfers between devices  393 us (30%)
  matrix products  140 us (11%)
  other arithmetic  127 us (10%)
  Pallas kernels  95.2 us (7%)
  local copies, waits for them, and re-layouts  54.6 us (4%)
  blocking collectives  32 us (2%)
  between operations  19.9 us (2%)
    ppermute x80, waiting for transfers between devices, swap(): return lax.ppermute(block, 'dp', [(i, i ^ bit) for i in range(count)])  187 us
    ppermute x80, starting transfers between devices, swap(): return lax.ppermute(block, 'dp', [(i, i ^ bit) for i in range(count)])  156 us
    psum x1, waiting for transfers between devices, per_device(): lax.psum(jnp.concatenate([v.reshape(-1) for v in grad_gain + grad_shift +...  95.9 us
    ppermute x24, starting transfers between devices, to_section(): lax.ppermute(block, 'section', [(source, target)]).astype(F32)  88.7 us
    ppermute x24, starting transfers between devices, spread_over_sections(): carried = lax.ppermute(carried, 'section', [(at, at + step)])  83.8 us
    ppermute x24, waiting for transfers between devices, spread_over_sections(): carried = lax.ppermute(carried, 'section', [(at, at + step)])  76.8 us
    ppermute x32, starting transfers between devices, deliver(): pieces.append(lax.ppermute(block, ('section', 'dp'), route))  64.7 us
    dot_general x8, matrix products, contract_cols(): lax.dot_general(left, right, (((1,), (1,)), ((), ())), preferred_element_...  60.1 us
  transfers between devices with their start and end apart: 161, of which 56 were waited for; matrix products, arithmetic and copies ran while one was open for 23% of the time, Pallas kernels for 7%

profile of v1, /device:TPU:0, one launch (start us, length us, event | category | flops | bytes accessed | tf_op | source)
XLA Modules:
  0.0 1273.8 jit_solution(9890774156947520259)
XLA Ops:
  9.2 5.0 collective-permute-start.15
  15.6 6.0 collective-permute-start.22
  26.2 18.6 %all-gather = f32[4,1,768]{2,1,0:T(1,128)S(1)} all-gather(f32[1,1,768]{2,1,0:T(1,128)} %bitcast.172), channel_id=1, replica_groups=mesh['section'=4,'dp'=8] {'section'}, dimensions={0}, use_global_device_ids=true | all-gather | bytes 15360 | tf_op jit(solution)/shard_map/all_gather | solution.py:361
  45.4 13.4 %all-gather.1 = f32[4,1,768]{2,1,0:T(1,128)S(1)} all-gather(f32[1,1,768]{2,1,0:T(1,128)} %bitcast.173), channel_id=1, replica_groups=mesh['section'=4,'dp'=8] {'section'}, dimensions={0}, use_global_device_ids=true | all-gather | bytes 15360 | tf_op jit(solution)/shard_map/all_gather | solution.py:362
  77.7 9.4 collective-permute-start.42
  97.5 8.6 collective-permute-done.41
  106.1 12.1 collective-permute-done.48
  124.6 6.0 collective-permute-done.18
  150.5 5.2 collective-permute-done.49
  165.7 38.8 %collective-permute-start.36 = (bf16[192,3072]{1,0:T(8,128)(2,1)S(1)}, bf16[192,3072]{1,0:T(8,128)(2,1)S(1)}, u32[]{:S(2)}, u32[]{:S(2)}) collective-permute-start(bf16[192,3072]{1,0:T(8,128)(2,1)S(1)} %collective-permute-done.35), channel_id=1, source_target_pairs={{8,0},{9,1},{10,2},{11,3},{12,4},{13,5},{14,6},{15,7}} | collective-permute-start | bytes 3538952 | tf_op jit(solution)/shard_map/ppermute | solution.py:236
  213.0 14.4 %collective-permute-done.9 = bf16[192,3072]{1,0:T(8,128)(2,1)S(1)} collective-permute-done((bf16[192,3072]{1,0:T(8,128)(2,1)}, bf16[192,3072]{1,0:T(8,128)(2,1)S(1)}, u32[]{:S(2)}, u32[]{:S(2)}) %collective-permute-start.9) | collective-permute-done | bytes 1179680 | tf_op jit(solution)/shard_map/ppermute | solution.py:236
  229.2 23.4 %collective-permute-done.28 = bf16[192,3072]{1,0:T(8,128)(2,1)S(1)} collective-permute-done((bf16[192,3072]{1,0:T(8,128)(2,1)S(1)}, bf16[192,3072]{1,0:T(8,128)(2,1)S(1)}, u32[]{:S(2)}, u32[]{:S(2)}) %collective-permute-start.28) | collective-permute-done | bytes 1179680 | tf_op jit(solution)/shard_map/ppermute | solution.py:236
  252.7 18.2 %collective-permute-done.36 = bf16[192,3072]{1,0:T(8,128)(2,1)S(1)} collective-permute-done((bf16[192,3072]{1,0:T(8,128)(2,1)S(1)}, bf16[192,3072]{1,0:T(8,128)(2,1)S(1)}, u32[]{:S(2)}, u32[]{:S(2)}) %collective-permute-start.36) | collective-permute-done | bytes 1179680 | tf_op jit(solution)/shard_map/ppermute | solution.py:236
  279.5 10.2 collective-permute-done.5
  296.1 5.2 collective-permute-start.38
  305.4 15.9 %collective-permute-done.30 = bf16[96,3072]{1,0:T(8,128)(2,1)S(1)} collective-permute-done((bf16[96,3072]{1,0:T(8,128)(2,1)S(1)}, bf16[96,3072]{1,0:T(8,128)(2,1)S(1)}, u32[]{:S(2)}, u32[]{:S(2)}) %collective-permute-start.30) | collective-permute-done | bytes 589856 | tf_op jit(solution)/shard_map/ppermute | solution.py:228
  321.6 7.9 collective-permute-done.31
  334.8 5.8 collective-permute-start.39
  349.5 8.0 broadcast_select_fusion.1
  357.5 19.7 %attention_forward.2 = (f32[608,768]{1,0:T(8,128)}, bf16[12,608,128]{2,1,0:T(8,128)(2,1)}) custom-call(bf16[608,2304]{1,0:T(8,128)(2,1)} %copy-done.69, bf16[608,2304]{1,0:T(8,128)(2,1)} %copy-done.69, bf16[608,2304]{1,0:T(8,128)(2,1)} %copy-done.69, bf16[608,1536]{1,0:T(8,128)(2,1)} %collective-permute-done.8.key_far.value_far, ...), custom_call_target="tpu_custom_call" | custom-call | flops 18169724928 | bytes 5603328 | tf_op jit(solution)/shard_map/attention_forward/pallas_call | solution.py:101
  382.8 11.7 multiply_convert_fusion.3
  394.5 6.8 convert_reduce_fusion.5
  425.4 12.8 %collective-permute-start.54 = (bf16[608,768]{1,0:T(8,128)(2,1)}, bf16[608,768]{1,0:T(8,128)(2,1)}, u32[]{:S(2)}, u32[]{:S(2)}) collective-permute-start(bf16[608,768]{1,0:T(8,128)(2,1)} %get-tuple-element.201), channel_id=1, source_target_pairs={{0,8},{2,10},{4,12},{6,14},{16,9},{18,11},{20,13},{22,15}} | collective-permute-start | bytes 2801672 | tf_op jit(solution)/shard_map/ppermute | solution.py:321
  438.2 19.6 %attention_forward.3 = (f32[608,768]{1,0:T(8,128)}, bf16[12,608,128]{2,1,0:T(8,128)(2,1)}) custom-call(bf16[608,2304]{1,0:T(8,128)(2,1)} %copy-done.70, bf16[608,2304]{1,0:T(8,128)(2,1)} %copy-done.70, bf16[608,2304]{1,0:T(8,128)(2,1)} %copy-done.70, bf16[608,1536]{1,0:T(8,128)(2,1)} %collective-permute-done.33.key_far.value_far, ...), custom_call_target="tpu_custom_call" | custom-call | flops 18169724928 | bytes 5603328 | tf_op jit(solution)/shard_map/attention_forward/pallas_call | solution.py:101
  461.4 10.9 multiply_convert_fusion.2
  472.4 17.1 %convert_reduce_fusion = (f32[3072]{0:T(1024)}, bf16[608,3072]{1,0:T(8,128)(2,1)S(1)}) fusion(f32[608,3072]{1,0:T(8,128)} %get-tuple-element.205, f32[3072]{0:T(1024)S(1)} %bitcast.171, bf16[768,768]{1,0:T(8,128)(2,1)S(1)} %copy-done.82, bf16[768,768]{1,0:T(8,128)(2,1)S(1)} %copy-done.80, bf16[768,768]{1,0:T(8,128)(2,1)S(1)} %copy-done.79, ...), kind=kOutput, calls=%fused_computation.17 | convolution fusion | flops 2945209344 | bytes 16887808 | tf_op jit(solution)/shard_map/dot_general | solution.py:32
  498.3 27.9 %attention_backward.2 = (bf16[608,768]{1,0:T(8,128)(2,1)}, bf16[608,768]{1,0:T(8,128)(2,1)}, bf16[608,768]{1,0:T(8,128)(2,1)}, bf16[608,768]{1,0:T(8,128)(2,1)}, bf16[608,768]{1,0:T(8,128)(2,1)}) custom-call(bf16[12,608,128]{2,1,0:T(8,128)(2,1)} %get-tuple-element.26.extended_ref, bf16[608,2304]{1,0:T(8,128)(2,1)} %copy-done.70, ...), custom_call_target="tpu_custom_call" | custom-call | flops 45424312320 | bytes 11206656 | tf_op jit(solution)/shard_map/attention_backward/pallas_call | solution.py:178
  526.2 5.3 fusion.91
  550.1 7.1 collective-permute-start.53
  569.1 41.0 %collective-permute-start.69 = (bf16[2,608,768]{2,1,0:T(8,128)(2,1)S(1)}, bf16[2,608,768]{2,1,0:T(8,128)(2,1)S(1)}, u32[]{:S(2)}, u32[]{:S(2)}) collective-permute-start(bf16[2,608,768]{2,1,0:T(8,128)(2,1)S(1)} %pad_maximum_fusion.14), channel_id=1, source_target_pairs={{0,1},{1,0},{2,3},{3,2},{4,5},{5,4},{6,7},{7,6},{8,9},{9,8},{10,11... | collective-permute-start | bytes 5603336 | tf_op jit(solution)/shard_map/ppermute | solution.py:228
  610.5 5.6 collective-permute-start.123
  616.1 5.7 collective-permute-start.131
  649.6 14.4 %collective-permute-start.128 = (bf16[2,192,384]{2,1,0:T(8,128)(2,1)}, bf16[2,192,384]{2,1,0:T(8,128)(2,1)}, u32[]{:S(2)}, u32[]{:S(2)}) collective-permute-start(bf16[2,192,384]{2,1,0:T(8,128)(2,1)} %pad_maximum_fusion.32), channel_id=1, source_target_pairs={{0,16},{1,17},{2,18},{3,19},{4,20},{5,21},{6,22},{7,23}} | collective-permute-start | bytes 884744 | tf_op jit(solution)/shard_map/ppermute | solution.py:289
  677.9 17.7 %convert_reduce_fusion.1 = (f32[3072]{0:T(1024)S(1)}, bf16[608,3072]{1,0:T(8,128)(2,1)S(1)}) fusion(f32[608,3072]{1,0:T(8,128)} %get-tuple-element.199, f32[3072]{0:T(1024)S(1)} %bitcast.169, bf16[768,768]{1,0:T(8,128)(2,1)S(1)} %copy-done.78, bf16[768,768]{1,0:T(8,128)(2,1)S(1)} %copy-done.76, bf16[768,768]{1,0:T(8,128)(2,1)S(1)} %copy-done.74, ...), kind=kOutput, calls=%fused_computation.18 | convolution fusion | flops 2945209344 | bytes 16886144 | tf_op jit(solution)/shard_map/dot_general | solution.py:32
  702.2 6.5 convolution_convert_fusion.2
  716.8 27.9 %attention_backward.3 = (bf16[608,768]{1,0:T(8,128)(2,1)}, bf16[608,768]{1,0:T(8,128)(2,1)}, bf16[608,768]{1,0:T(8,128)(2,1)}, bf16[608,768]{1,0:T(8,128)(2,1)}, bf16[608,768]{1,0:T(8,128)(2,1)}) custom-call(bf16[12,608,128]{2,1,0:T(8,128)(2,1)} %get-tuple-element.32.extended_ref, bf16[608,2304]{1,0:T(8,128)(2,1)} %copy-done.69, ...), custom_call_target="tpu_custom_call" | custom-call | flops 45424312320 | bytes 11206656 | tf_op jit(solution)/shard_map/attention_backward/pallas_call | solution.py:178
  766.0 6.2 collective-permute-done.87
  779.2 5.0 collective-permute-done.88
  830.2 5.6 fusion.82
  835.8 5.1 convolution_convert_fusion.4
  851.0 8.3 collective-permute-start.146
  865.3 5.3 collective-permute-start.154
  870.6 95.9 %all-reduce.2.cloned.1.call-done = f32[18432]{0:T(1024)} async-done(((f32[18432]{0:T(1024)}), f32[18432]{0:T(1024)}) %all-reduce.2.cloned.1.call-update) | async-done | bytes 73744 | tf_op jit(solution)/shard_map/psum | solution.py:453
  1004.4 10.1 collective-permute-done.95
  1018.0 10.9 collective-permute-done.103
  1031.3 7.4 collective-permute-done.96
  1040.2 6.5 collective-permute-done.98
  1048.5 5.6 collective-permute-done.104
  1056.1 4.8 collective-permute-done.106
  1060.8 10.6 collective-permute-start.91
  1074.0 8.5 collective-permute-done.111
  1083.9 10.7 collective-permute-done.113
  1105.2 8.9 collective-permute-start.99
  1114.1 4.8 collective-permute-start.107
  1124.5 8.3 collective-permute-start.109
  1135.4 6.6 collective-permute-start.117
  1145.3 8.1 collective-permute-start.68
  1154.2 31.9 %collective-permute-done.116 = bf16[2,96,1536]{2,1,0:T(8,128)(2,1)S(1)} collective-permute-done((bf16[2,96,1536]{2,1,0:T(8,128)(2,1)S(1)}, bf16[2,96,1536]{2,1,0:T(8,128)(2,1)S(1)}, u32[]{:S(2)}, u32[]{:S(2)}) %collective-permute-start.116) | collective-permute-done | bytes 589856 | tf_op jit(solution)/shard_map/ppermute | solution.py:289
  1190.9 6.5 collective-permute-start.70
  1198.9 12.7 collective-permute-done.85
  1224.7 6.4 collective-permute-done.119
  1232.8 6.5 collective-permute-start.159
  1250.6 11.2 select_bitcast_fusion.1
  1261.8 5.0 maximum_convert_fusion
  (873 shorter events, 440.9 us)
Async XLA Ops:
  7.2 959.3 %all-reduce.2.cloned.1.call-start = ((), (), s32[]{:S(2)}) async-start(), calls=%async_computation | async-start | bytes 147456 | tf_op jit(solution)/shard_map/psum | solution.py:453
  9.2 63.9 %collective-permute-start.15 = (bf16[384,768]{1,0:T(8,128)(2,1)}, bf16[384,768]{1,0:T(8,128)(2,1)S(1)}, u32[]{:S(2)}, u32[]{:S(2)}) collective-permute-start(bf16[384,768]{1,0:T(8,128)(2,1)} %dynamic-slice_bitcast_fusion.1), channel_id=1, source_target_pairs={{0,8},{1,9},{2,10},{3,11},{4,12},{5,13},{6,14},{7,15}} | collective-permute-start | bytes 1769480 | tf_op jit(solution)/shard_map/ppermute | solution.py:236
  14.1 60.5 %collective-permute-start.46 = (bf16[384,768]{1,0:T(8,128)(2,1)}, bf16[384,768]{1,0:T(8,128)(2,1)}, u32[]{:S(2)}, u32[]{:S(2)}) collective-permute-start(bf16[384,768]{1,0:T(8,128)(2,1)} %dynamic-slice_bitcast_fusion.1), channel_id=1, source_target_pairs={{24,16},{25,17},{26,18},{27,19},{28,20},{29,21},{30,22},{31,23}} | collective-permute-start | bytes 1769480 | tf_op jit(solution)/shard_map/ppermute | solution.py:236
  15.6 62.1 %collective-permute-start.22 = (bf16[384,768]{1,0:T(8,128)(2,1)}, bf16[384,768]{1,0:T(8,128)(2,1)}, u32[]{:S(2)}, u32[]{:S(2)}) collective-permute-start(bf16[384,768]{1,0:T(8,128)(2,1)} %dynamic-slice_bitcast_fusion.1), channel_id=1, source_target_pairs={{8,16},{9,17},{10,18},{11,19},{12,20},{13,21},{14,22},{15,23}} | collective-permute-start | bytes 1769480 | tf_op jit(solution)/shard_map/ppermute | solution.py:236
  21.6 65.5 %collective-permute-start.40 = (bf16[384,768]{1,0:T(8,128)(2,1)}, bf16[384,768]{1,0:T(8,128)(2,1)}, u32[]{:S(2)}, u32[]{:S(2)}) collective-permute-start(bf16[384,768]{1,0:T(8,128)(2,1)} %dynamic-slice_bitcast_fusion.1), channel_id=1, source_target_pairs={{16,8},{17,9},{18,10},{19,11},{20,12},{21,13},{22,14},{23,15}} | collective-permute-start | bytes 1769480 | tf_op jit(solution)/shard_map/ppermute | solution.py:236
  25.0 46.8 %collective-permute-start = (f32[8,128]{1,0:T(8,128)S(1)}, f32[8,128]{1,0:T(8,128)S(1)}, u32[]{:S(2)}, u32[]{:S(2)}) collective-permute-start(f32[8,128]{1,0:T(8,128)S(1)} %broadcast_in_dim.38), channel_id=1, source_target_pairs={{0,1},{1,0},{2,3},{3,2},{4,5},{5,4},{6,7},{7,6},{8,9},{9,8},{10,11... | collective-permute-start | bytes 12296 | tf_op jit(solution)/shard_map/ppermute | solution.py:228
  89.9 28.3 %collective-permute-start.48 = (bf16[384,768]{1,0:T(8,128)(2,1)}, bf16[384,768]{1,0:T(8,128)(2,1)S(1)}, u32[]{:S(2)}, u32[]{:S(2)}) collective-permute-start(bf16[384,768]{1,0:T(8,128)(2,1)} %collective-permute-done.47), channel_id=1, source_target_pairs={{8,0},{9,1},{10,2},{11,3},{12,4},{13,5},{14,6},{15,7}} | collective-permute-start | bytes 1769480 | tf_op jit(solution)/shard_map/ppermute | solution.py:236
  92.1 31.9 %collective-permute-start.34 = (bf16[192,3072]{1,0:T(8,128)(2,1)}, bf16[192,3072]{1,0:T(8,128)(2,1)S(1)}, u32[]{:S(2)}, u32[]{:S(2)}) collective-permute-start(bf16[192,3072]{1,0:T(8,128)(2,1)} %dynamic-slice_bitcast_fusion), channel_id=1, source_target_pairs={{24,16},{25,17},{26,18},{27,19},{28,20},{29,21},{30,22},{31,23}} | collective-permute-start | bytes 3538952 | tf_op jit(solution)/shard_map/ppermute | solution.py:236
  92.8 45.4 %collective-permute-start.2 = (bf16[192,3072]{1,0:T(8,128)(2,1)}, bf16[192,3072]{1,0:T(8,128)(2,1)S(1)}, u32[]{:S(2)}, u32[]{:S(2)}) collective-permute-start(bf16[192,3072]{1,0:T(8,128)(2,1)} %dynamic-slice_bitcast_fusion), channel_id=1, source_target_pairs={{0,8},{1,9},{2,10},{3,11},{4,12},{5,13},{6,14},{7,15}} | collective-permute-start | bytes 3538952 | tf_op jit(solution)/shard_map/ppermute | solution.py:236
  106.1 37.5 %collective-permute-start.1 = (bf16[2,608,768]{2,1,0:T(8,128)(2,1)S(1)}, bf16[2,608,768]{2,1,0:T(8,128)(2,1)S(1)}, u32[]{:S(2)}, u32[]{:S(2)}) collective-permute-start(bf16[2,608,768]{2,1,0:T(8,128)(2,1)S(1)} %copy-done.59), channel_id=1, source_target_pairs={{0,1},{1,0},{2,3},{3,2},{4,5},{5,4},{6,7},{7,6},{8,9},{9,8},{10,11... | collective-permute-start | bytes 5603336 | tf_op jit(solution)/shard_map/ppermute | solution.py:228
  140.3 23.3 %collective-permute-start.35 = (bf16[192,3072]{1,0:T(8,128)(2,1)S(1)}, bf16[192,3072]{1,0:T(8,128)(2,1)S(1)}, u32[]{:S(2)}, u32[]{:S(2)}) collective-permute-start(bf16[192,3072]{1,0:T(8,128)(2,1)S(1)} %collective-permute-done.34), channel_id=1, source_target_pairs={{16,8},{17,9},{18,10},{19,11},{20,12},{21,13},{22,14},{23,15}} | collective-permute-start | bytes 3538952 | tf_op jit(solution)/shard_map/ppermute | solution.py:236
  141.2 23.2 %collective-permute-start.3 = (bf16[192,3072]{1,0:T(8,128)(2,1)S(1)}, bf16[192,3072]{1,0:T(8,128)(2,1)S(1)}, u32[]{:S(2)}, u32[]{:S(2)}) collective-permute-start(bf16[192,3072]{1,0:T(8,128)(2,1)S(1)} %collective-permute-done.2), channel_id=1, source_target_pairs={{8,16},{9,17},{10,18},{11,19},{12,20},{13,21},{14,22},{15,23}} | collective-permute-start | bytes 3538952 | tf_op jit(solution)/shard_map/ppermute | solution.py:236
  143.7 22.1 %collective-permute-start.20 = (bf16[768,768]{1,0:T(8,128)(2,1)S(1)}, bf16[768,768]{1,0:T(8,128)(2,1)S(1)}, u32[]{:S(2)}, u32[]{:S(2)}) collective-permute-start(bf16[768,768]{1,0:T(8,128)(2,1)S(1)} %pad_maximum_fusion.18), channel_id=1, source_target_pairs={{0,1},{1,0},{2,3},{3,2},{4,5},{5,4},{6,7},{7,6},{8,9},{9,8},{10,11... | collective-permute-start | bytes 3538952 | tf_op jit(solution)/shard_map/ppermute | solution.py:228
  145.0 59.5 %collective-permute-start.26 = (bf16[768,768]{1,0:T(8,128)(2,1)S(1)}, bf16[768,768]{1,0:T(8,128)(2,1)S(1)}, u32[]{:S(2)}, u32[]{:S(2)}) collective-permute-start(bf16[768,768]{1,0:T(8,128)(2,1)S(1)} %pad_maximum_fusion.19), channel_id=1, source_target_pairs={{0,1},{1,0},{2,3},{3,2},{4,5},{5,4},{6,7},{7,6},{8,9},{9,8},{10,11... | collective-permute-start | bytes 3538952 | tf_op jit(solution)/shard_map/ppermute | solution.py:228
  162.4 65.0 %collective-permute-start.9 = (bf16[192,3072]{1,0:T(8,128)(2,1)}, bf16[192,3072]{1,0:T(8,128)(2,1)S(1)}, u32[]{:S(2)}, u32[]{:S(2)}) collective-permute-start(bf16[192,3072]{1,0:T(8,128)(2,1)} %dynamic-slice_bitcast_fusion), channel_id=1, source_target_pairs={{8,0},{9,1},{10,2},{11,3},{12,4},{13,5},{14,6},{15,7}} | collective-permute-start | bytes 3538952 | tf_op jit(solution)/shard_map/ppermute | solution.py:236
  163.7 65.6 %collective-permute-start.11 = (bf16[192,3072]{1,0:T(8,128)(2,1)S(1)}, bf16[192,3072]{1,0:T(8,128)(2,1)S(1)}, u32[]{:S(2)}, u32[]{:S(2)}) collective-permute-start(bf16[192,3072]{1,0:T(8,128)(2,1)S(1)} %collective-permute-done.10), channel_id=1, source_target_pairs={{16,24},{17,25},{18,26},{19,27},{20,28},{21,29},{22,30},{23,31}} | collective-permute-start | bytes 3538952 | tf_op jit(solution)/shard_map/ppermute | solution.py:236
  164.4 88.3 %collective-permute-start.28 = (bf16[192,3072]{1,0:T(8,128)(2,1)S(1)}, bf16[192,3072]{1,0:T(8,128)(2,1)S(1)}, u32[]{:S(2)}, u32[]{:S(2)}) collective-permute-start(bf16[192,3072]{1,0:T(8,128)(2,1)S(1)} %collective-permute-done.27), channel_id=1, source_target_pairs={{8,0},{9,1},{10,2},{11,3},{12,4},{13,5},{14,6},{15,7}} | collective-permute-start | bytes 3538952 | tf_op jit(solution)/shard_map/ppermute | solution.py:236
  165.7 105.1 %collective-permute-start.36 = (bf16[192,3072]{1,0:T(8,128)(2,1)S(1)}, bf16[192,3072]{1,0:T(8,128)(2,1)S(1)}, u32[]{:S(2)}, u32[]{:S(2)}) collective-permute-start(bf16[192,3072]{1,0:T(8,128)(2,1)S(1)} %collective-permute-done.35), channel_id=1, source_target_pairs={{8,0},{9,1},{10,2},{11,3},{12,4},{13,5},{14,6},{15,7}} | collective-permute-start | bytes 3538952 | tf_op jit(solution)/shard_map/ppermute | solution.py:236
  204.6 66.3 %collective-permute-start.4 = (bf16[192,3072]{1,0:T(8,128)(2,1)S(1)}, bf16[192,3072]{1,0:T(8,128)(2,1)S(1)}, u32[]{:S(2)}, u32[]{:S(2)}) collective-permute-start(bf16[192,3072]{1,0:T(8,128)(2,1)S(1)} %collective-permute-done.3), channel_id=1, source_target_pairs={{16,24},{17,25},{18,26},{19,27},{20,28},{21,29},{22,30},{23,31}} | collective-permute-start | bytes 3538952 | tf_op jit(solution)/shard_map/ppermute | solution.py:236
  227.4 185.8 %collective-permute-start.45 = (bf16[768,768]{1,0:T(8,128)(2,1)}, bf16[768,768]{1,0:T(8,128)(2,1)}, u32[]{:S(2)}, u32[]{:S(2)}) collective-permute-start(bf16[768,768]{1,0:T(8,128)(2,1)} %pad_maximum_fusion.20), channel_id=1, source_target_pairs={{0,1},{1,0},{2,3},{3,2},{4,5},{5,4},{6,7},{7,6},{8,9},{9,8},{10,11... | collective-permute-start | bytes 3538952 | tf_op jit(solution)/shard_map/ppermute | solution.py:228
  276.6 24.7 %collective-permute-start.6 = (bf16[96,3072]{1,0:T(8,128)(2,1)S(1)}, bf16[96,3072]{1,0:T(8,128)(2,1)S(1)}, u32[]{:S(2)}, u32[]{:S(2)}) collective-permute-start(bf16[96,3072]{1,0:T(8,128)(2,1)S(1)} %get-tuple-element.149), channel_id=1, source_target_pairs={{0,4},{1,5},{2,6},{3,7},{4,0},{5,1},{6,2},{7,3},{8,12},{9,13},{10,... | collective-permute-start | bytes 1769480 | tf_op jit(solution)/shard_map/ppermute | solution.py:228
  278.8 24.7 %collective-permute-start.13 = (bf16[96,3072]{1,0:T(8,128)(2,1)S(1)}, bf16[96,3072]{1,0:T(8,128)(2,1)S(1)}, u32[]{:S(2)}, u32[]{:S(2)}) collective-permute-start(bf16[96,3072]{1,0:T(8,128)(2,1)S(1)} %get-tuple-element.147), channel_id=1, source_target_pairs={{0,4},{1,5},{2,6},{3,7},{4,0},{5,1},{6,2},{7,3},{8,12},{9,13},{10,... | collective-permute-start | bytes 1769480 | tf_op jit(solution)/shard_map/ppermute | solution.py:228
  289.7 40.1 %collective-permute-start.37 = (bf16[96,3072]{1,0:T(8,128)(2,1)S(1)}, bf16[96,3072]{1,0:T(8,128)(2,1)S(1)}, u32[]{:S(2)}, u32[]{:S(2)}) collective-permute-start(bf16[96,3072]{1,0:T(8,128)(2,1)S(1)} %get-tuple-element.136), channel_id=1, source_target_pairs={{0,2},{1,3},{2,0},{3,1},{4,6},{5,7},{6,4},{7,5},{8,10},{9,11},{10,... | collective-permute-start | bytes 1769480 | tf_op jit(solution)/shard_map/ppermute | solution.py:228
  296.1 38.4 %collective-permute-start.38 = (bf16[96,3072]{1,0:T(8,128)(2,1)S(1)}, bf16[96,3072]{1,0:T(8,128)(2,1)S(1)}, u32[]{:S(2)}, u32[]{:S(2)}) collective-permute-start(bf16[96,3072]{1,0:T(8,128)(2,1)S(1)} %get-tuple-element.135), channel_id=1, source_target_pairs={{0,4},{1,5},{2,6},{3,7},{4,0},{5,1},{6,2},{7,3},{8,12},{9,13},{10,... | collective-permute-start | bytes 1769480 | tf_op jit(solution)/shard_map/ppermute | solution.py:228
  303.5 25.9 %collective-permute-start.31 = (bf16[96,3072]{1,0:T(8,128)(2,1)S(1)}, bf16[96,3072]{1,0:T(8,128)(2,1)S(1)}, u32[]{:S(2)}, u32[]{:S(2)}) collective-permute-start(bf16[96,3072]{1,0:T(8,128)(2,1)S(1)} %get-tuple-element.141), channel_id=1, source_target_pairs={{0,4},{1,5},{2,6},{3,7},{4,0},{5,1},{6,2},{7,3},{8,12},{9,13},{10,... | collective-permute-start | bytes 1769480 | tf_op jit(solution)/shard_map/ppermute | solution.py:228
  419.6 116.6 %collective-permute-start.62 = (bf16[608,768]{1,0:T(8,128)(2,1)}, bf16[608,768]{1,0:T(8,128)(2,1)}, u32[]{:S(2)}, u32[]{:S(2)}) collective-permute-start(bf16[608,768]{1,0:T(8,128)(2,1)} %get-tuple-element.201), channel_id=1, source_target_pairs={{8,8},{10,10},{12,12},{14,14},{24,9},{26,11},{28,13},{30,15}} | collective-permute-start | bytes 2801672 | tf_op jit(solution)/shard_map/ppermute | solution.py:321
  421.2 121.9 %collective-permute-start.63 = (bf16[608,768]{1,0:T(8,128)(2,1)}, bf16[608,768]{1,0:T(8,128)(2,1)}, u32[]{:S(2)}, u32[]{:S(2)}) collective-permute-start(bf16[608,768]{1,0:T(8,128)(2,1)} %get-tuple-element.197), channel_id=1, source_target_pairs={{8,0},{10,2},{12,4},{14,6},{24,1},{26,3},{28,5},{30,7}} | collective-permute-start | bytes 2801672 | tf_op jit(solution)/shard_map/ppermute | solution.py:321
  422.5 121.8 %collective-permute-start.66 = (bf16[608,768]{1,0:T(8,128)(2,1)}, bf16[608,768]{1,0:T(8,128)(2,1)}, u32[]{:S(2)}, u32[]{:S(2)}) collective-permute-start(bf16[608,768]{1,0:T(8,128)(2,1)} %get-tuple-element.201), channel_id=1, source_target_pairs={{9,8},{11,10},{13,12},{15,14},{25,9},{27,11},{29,13},{31,15}} | collective-permute-start | bytes 2801672 | tf_op jit(solution)/shard_map/ppermute | solution.py:321
  424.1 121.0 %collective-permute-start.67 = (bf16[608,768]{1,0:T(8,128)(2,1)}, bf16[608,768]{1,0:T(8,128)(2,1)}, u32[]{:S(2)}, u32[]{:S(2)}) collective-permute-start(bf16[608,768]{1,0:T(8,128)(2,1)} %get-tuple-element.197), channel_id=1, source_target_pairs={{9,0},{11,2},{13,4},{15,6},{25,1},{27,3},{29,5},{31,7}} | collective-permute-start | bytes 2801672 | tf_op jit(solution)/shard_map/ppermute | solution.py:321
  425.4 120.5 %collective-permute-start.54 = (bf16[608,768]{1,0:T(8,128)(2,1)}, bf16[608,768]{1,0:T(8,128)(2,1)}, u32[]{:S(2)}, u32[]{:S(2)}) collective-permute-start(bf16[608,768]{1,0:T(8,128)(2,1)} %get-tuple-element.201), channel_id=1, source_target_pairs={{0,8},{2,10},{4,12},{6,14},{16,9},{18,11},{20,13},{22,15}} | collective-permute-start | bytes 2801672 | tf_op jit(solution)/shard_map/ppermute | solution.py:321
  559.7 50.7 %collective-permute-start.58 = (bf16[608,768]{1,0:T(8,128)(2,1)}, bf16[608,768]{1,0:T(8,128)(2,1)S(1)}, u32[]{:S(2)}, u32[]{:S(2)}) collective-permute-start(bf16[608,768]{1,0:T(8,128)(2,1)} %get-tuple-element.201), channel_id=1, source_target_pairs={{1,8},{3,10},{5,12},{7,14},{17,9},{19,11},{21,13},{23,15}} | collective-permute-start | bytes 2801672 | tf_op jit(solution)/shard_map/ppermute | solution.py:321
  560.4 55.7 %collective-permute-start.59 = (bf16[608,768]{1,0:T(8,128)(2,1)}, bf16[608,768]{1,0:T(8,128)(2,1)S(1)}, u32[]{:S(2)}, u32[]{:S(2)}) collective-permute-start(bf16[608,768]{1,0:T(8,128)(2,1)} %get-tuple-element.197), channel_id=1, source_target_pairs={{1,0},{3,2},{5,4},{7,6},{17,1},{19,3},{21,5},{23,7}} | collective-permute-start | bytes 2801672 | tf_op jit(solution)/shard_map/ppermute | solution.py:321
  561.8 60.1 %collective-permute-start.56 = (bf16[608,768]{1,0:T(8,128)(2,1)S(1)}, bf16[608,768]{1,0:T(8,128)(2,1)S(1)}, u32[]{:S(2)}, u32[]{:S(2)}) collective-permute-start(bf16[608,768]{1,0:T(8,128)(2,1)S(1)} %fusion.91), channel_id=1, source_target_pairs={{1,24},{3,26},{5,28},{7,30},{17,25},{19,27},{21,29},{23,31}} | collective-permute-start | bytes 2801672 | tf_op jit(solution)/shard_map/ppermute | solution.py:321
  562.5 59.7 %collective-permute-start.57 = (bf16[608,768]{1,0:T(8,128)(2,1)S(1)}, bf16[608,768]{1,0:T(8,128)(2,1)S(1)}, u32[]{:S(2)}, u32[]{:S(2)}) collective-permute-start(bf16[608,768]{1,0:T(8,128)(2,1)S(1)} %get-tuple-element.203), channel_id=1, source_target_pairs={{1,16},{3,18},{5,20},{7,22},{17,17},{19,19},{21,21},{23,23}} | collective-permute-start | bytes 2801672 | tf_op jit(solution)/shard_map/ppermute | solution.py:321
  569.1 99.0 %collective-permute-start.69 = (bf16[2,608,768]{2,1,0:T(8,128)(2,1)S(1)}, bf16[2,608,768]{2,1,0:T(8,128)(2,1)S(1)}, u32[]{:S(2)}, u32[]{:S(2)}) collective-permute-start(bf16[2,608,768]{2,1,0:T(8,128)(2,1)S(1)} %pad_maximum_fusion.14), channel_id=1, source_target_pairs={{0,1},{1,0},{2,3},{3,2},{4,5},{5,4},{6,7},{7,6},{8,9},{9,8},{10,11... | collective-permute-start | bytes 5603336 | tf_op jit(solution)/shard_map/ppermute | solution.py:228
  621.9 137.6 %collective-permute-start.86 = (bf16[384,3072]{1,0:T(8,128)(2,1)}, bf16[384,3072]{1,0:T(8,128)(2,1)}, u32[]{:S(2)}, u32[]{:S(2)}) collective-permute-start(bf16[384,3072]{1,0:T(8,128)(2,1)} %constant_dynamic-slice_fusion.39), channel_id=1, source_target_pairs={{0,1},{1,0},{2,3},{3,2},{4,5},{5,4},{6,7},{7,6},{8,9},{9,8},{10,11... | collective-permute-start | bytes 7077896 | tf_op jit(solution)/shard_map/ppermute | solution.py:228
  649.6 195.6 %collective-permute-start.128 = (bf16[2,192,384]{2,1,0:T(8,128)(2,1)}, bf16[2,192,384]{2,1,0:T(8,128)(2,1)}, u32[]{:S(2)}, u32[]{:S(2)}) collective-permute-start(bf16[2,192,384]{2,1,0:T(8,128)(2,1)} %pad_maximum_fusion.32), channel_id=1, source_target_pairs={{0,16},{1,17},{2,18},{3,19},{4,20},{5,21},{6,22},{7,23}} | collective-permute-start | bytes 884744 | tf_op jit(solution)/shard_map/ppermute | solution.py:289
  664.0 181.9 %collective-permute-start.129 = (bf16[2,192,384]{2,1,0:T(8,128)(2,1)}, bf16[2,192,384]{2,1,0:T(8,128)(2,1)}, u32[]{:S(2)}, u32[]{:S(2)}) collective-permute-start(bf16[2,192,384]{2,1,0:T(8,128)(2,1)} %pad_maximum_fusion.32), channel_id=1, source_target_pairs={{8,16},{9,17},{10,18},{11,19},{12,20},{13,21},{14,22},{15,23}} | collective-permute-start | bytes 884744 | tf_op jit(solution)/shard_map/ppermute | solution.py:289
  665.5 181.1 %collective-permute-start.130 = (bf16[2,192,384]{2,1,0:T(8,128)(2,1)}, bf16[2,192,384]{2,1,0:T(8,128)(2,1)}, u32[]{:S(2)}, u32[]{:S(2)}) collective-permute-start(bf16[2,192,384]{2,1,0:T(8,128)(2,1)} %pad_maximum_fusion.32), channel_id=1, source_target_pairs={{24,16},{25,17},{26,18},{27,19},{28,20},{29,21},{30,22},{31,23}} | collective-permute-start | bytes 884744 | tf_op jit(solution)/shard_map/ppermute | solution.py:289
  800.1 26.7 %collective-permute-start.72 = (bf16[2,608,768]{2,1,0:T(8,128)(2,1)S(1)}, bf16[2,608,768]{2,1,0:T(8,128)(2,1)S(1)}, u32[]{:S(2)}, u32[]{:S(2)}) collective-permute-start(bf16[2,608,768]{2,1,0:T(8,128)(2,1)S(1)} %pad_maximum_fusion.15), channel_id=1, source_target_pairs={{0,1},{1,0},{2,3},{3,2},{4,5},{5,4},{6,7},{7,6},{8,9},{9,8},{10,11... | collective-permute-start | bytes 5603336 | tf_op jit(solution)/shard_map/ppermute | solution.py:228
  822.2 25.7 %collective-permute-start.136 = (bf16[2,192,384]{2,1,0:T(8,128)(2,1)}, bf16[2,192,384]{2,1,0:T(8,128)(2,1)S(1)}, u32[]{:S(2)}, u32[]{:S(2)}) collective-permute-start(bf16[2,192,384]{2,1,0:T(8,128)(2,1)} %pad_maximum_fusion.33), channel_id=1, source_target_pairs={{0,24},{1,25},{2,26},{3,27},{4,28},{5,29},{6,30},{7,31}} | collective-permute-start | bytes 884744 | tf_op jit(solution)/shard_map/ppermute | solution.py:289
  826.8 166.0 %collective-permute-start.94 = (bf16[384,3072]{1,0:T(8,128)(2,1)}, bf16[384,3072]{1,0:T(8,128)(2,1)}, u32[]{:S(2)}, u32[]{:S(2)}) collective-permute-start(bf16[384,3072]{1,0:T(8,128)(2,1)} %fusion.22), channel_id=1, source_target_pairs={{0,1},{1,0},{2,3},{3,2},{4,5},{5,4},{6,7},{7,6},{8,9},{9,8},{10,11... | collective-permute-start | bytes 7077896 | tf_op jit(solution)/shard_map/ppermute | solution.py:228
  851.0 118.8 %collective-permute-start.146 = (bf16[2,192,384]{2,1,0:T(8,128)(2,1)}, bf16[2,192,384]{2,1,0:T(8,128)(2,1)S(1)}, u32[]{:S(2)}, u32[]{:S(2)}) collective-permute-start(bf16[2,192,384]{2,1,0:T(8,128)(2,1)} %pad_maximum_fusion.34), channel_id=1, source_target_pairs={{24,0},{25,1},{26,2},{27,3},{28,4},{29,5},{30,6},{31,7}} | collective-permute-start | bytes 884744 | tf_op jit(solution)/shard_map/ppermute | solution.py:289
  859.4 112.0 %collective-permute-start.152 = (bf16[2,192,384]{2,1,0:T(8,128)(2,1)}, bf16[2,192,384]{2,1,0:T(8,128)(2,1)S(1)}, u32[]{:S(2)}, u32[]{:S(2)}) collective-permute-start(bf16[2,192,384]{2,1,0:T(8,128)(2,1)} %pad_maximum_fusion.35), channel_id=1, source_target_pairs={{0,8},{1,9},{2,10},{3,11},{4,12},{5,13},{6,14},{7,15}} | collective-permute-start | bytes 884744 | tf_op jit(solution)/shard_map/ppermute | solution.py:289
  864.6 107.9 %collective-permute-start.153 = (bf16[2,192,384]{2,1,0:T(8,128)(2,1)}, bf16[2,192,384]{2,1,0:T(8,128)(2,1)S(1)}, u32[]{:S(2)}, u32[]{:S(2)}) collective-permute-start(bf16[2,192,384]{2,1,0:T(8,128)(2,1)} %pad_maximum_fusion.35), channel_id=1, source_target_pairs={{16,8},{17,9},{18,10},{19,11},{20,12},{21,13},{22,14},{23,15}} | collective-permute-start | bytes 884744 | tf_op jit(solution)/shard_map/ppermute | solution.py:289
  865.3 108.0 %collective-permute-start.154 = (bf16[2,192,384]{2,1,0:T(8,128)(2,1)}, bf16[2,192,384]{2,1,0:T(8,128)(2,1)}, u32[]{:S(2)}, u32[]{:S(2)}) collective-permute-start(bf16[2,192,384]{2,1,0:T(8,128)(2,1)} %pad_maximum_fusion.35), channel_id=1, source_target_pairs={{24,8},{25,9},{26,10},{27,11},{28,12},{29,13},{30,14},{31,15}} | collective-permute-start | bytes 884744 | tf_op jit(solution)/shard_map/ppermute | solution.py:289
  969.8 125.8 %collective-permute-start.78 = (bf16[608,768]{1,0:T(8,128)(2,1)}, bf16[608,768]{1,0:T(8,128)(2,1)}, u32[]{:S(2)}, u32[]{:S(2)}) collective-permute-start(bf16[608,768]{1,0:T(8,128)(2,1)} %fusion.54), channel_id=1, source_target_pairs={{8,24},{10,26},{12,28},{14,30},{24,25},{26,27},{28,29},{30,31}} | collective-permute-start | bytes 2801672 | tf_op jit(solution)/shard_map/ppermute | solution.py:321
  971.4 25.6 %collective-permute-start.102 = (bf16[384,3072]{1,0:T(8,128)(2,1)}, bf16[384,3072]{1,0:T(8,128)(2,1)}, u32[]{:S(2)}, u32[]{:S(2)}) collective-permute-start(bf16[384,3072]{1,0:T(8,128)(2,1)} %constant_dynamic-slice_fusion.30), channel_id=1, source_target_pairs={{0,1},{1,0},{2,3},{3,2},{4,5},{5,4},{6,7},{7,6},{8,9},{9,8},{10,11... | collective-permute-start | bytes 7077896 | tf_op jit(solution)/shard_map/ppermute | solution.py:228
  989.8 106.5 %collective-permute-start.80 = (bf16[608,768]{1,0:T(8,128)(2,1)}, bf16[608,768]{1,0:T(8,128)(2,1)S(1)}, u32[]{:S(2)}, u32[]{:S(2)}) collective-permute-start(bf16[608,768]{1,0:T(8,128)(2,1)} %copy-done.31), channel_id=1, source_target_pairs={{8,8},{10,10},{12,12},{14,14},{24,9},{26,11},{28,13},{30,15}} | collective-permute-start | bytes 2801672 | tf_op jit(solution)/shard_map/ppermute | solution.py:321
  990.6 106.4 %collective-permute-start.79 = (bf16[608,768]{1,0:T(8,128)(2,1)}, bf16[608,768]{1,0:T(8,128)(2,1)S(1)}, u32[]{:S(2)}, u32[]{:S(2)}) collective-permute-start(bf16[608,768]{1,0:T(8,128)(2,1)} %copy-done.28), channel_id=1, source_target_pairs={{8,16},{10,18},{12,20},{14,22},{24,17},{26,19},{28,21},{30,23}} | collective-permute-start | bytes 2801672 | tf_op jit(solution)/shard_map/ppermute | solution.py:321
  1029.0 42.6 %collective-permute-start.110 = (bf16[384,3072]{1,0:T(8,128)(2,1)S(1)}, bf16[384,3072]{1,0:T(8,128)(2,1)S(1)}, u32[]{:S(2)}, u32[]{:S(2)}) collective-permute-start(bf16[384,3072]{1,0:T(8,128)(2,1)S(1)} %copy-done.52), channel_id=1, source_target_pairs={{0,1},{1,0},{2,3},{3,2},{4,5},{5,4},{6,7},{7,6},{8,9},{9,8},{10,11... | collective-permute-start | bytes 7077896 | tf_op jit(solution)/shard_map/ppermute | solution.py:228
  1060.8 37.5 %collective-permute-start.91 = (bf16[2,96,1536]{2,1,0:T(8,128)(2,1)S(1)}, bf16[2,96,1536]{2,1,0:T(8,128)(2,1)S(1)}, u32[]{:S(2)}, u32[]{:S(2)}) collective-permute-start(bf16[2,96,1536]{2,1,0:T(8,128)(2,1)S(1)} %copy-done.97), channel_id=1, source_target_pairs={{0,24},{1,25},{2,26},{3,27},{4,28},{5,29},{6,30},{7,31}} | collective-permute-start | bytes 1769480 | tf_op jit(solution)/shard_map/ppermute | solution.py:289
  1097.1 26.7 %collective-permute-start.81 = (bf16[608,768]{1,0:T(8,128)(2,1)S(1)}, bf16[608,768]{1,0:T(8,128)(2,1)S(1)}, u32[]{:S(2)}, u32[]{:S(2)}) collective-permute-start(bf16[608,768]{1,0:T(8,128)(2,1)S(1)} %copy-done.89), channel_id=1, source_target_pairs={{8,0},{10,2},{12,4},{14,6},{24,1},{26,3},{28,5},{30,7}} | collective-permute-start | bytes 2801672 | tf_op jit(solution)/shard_map/ppermute | solution.py:321
  1102.4 22.1 %collective-permute-start.100 = (bf16[2,96,1536]{2,1,0:T(8,128)(2,1)S(1)}, bf16[2,96,1536]{2,1,0:T(8,128)(2,1)S(1)}, u32[]{:S(2)}, u32[]{:S(2)}) collective-permute-start(bf16[2,96,1536]{2,1,0:T(8,128)(2,1)S(1)} %pad_maximum_fusion.27), channel_id=1, source_target_pairs={{8,16},{9,17},{10,18},{11,19},{12,20},{13,21},{14,22},{15,23}} | collective-permute-start | bytes 1769480 | tf_op jit(solution)/shard_map/ppermute | solution.py:289
  1103.1 29.7 %collective-permute-start.101 = (bf16[2,96,1536]{2,1,0:T(8,128)(2,1)S(1)}, bf16[2,96,1536]{2,1,0:T(8,128)(2,1)S(1)}, u32[]{:S(2)}, u32[]{:S(2)}) collective-permute-start(bf16[2,96,1536]{2,1,0:T(8,128)(2,1)S(1)} %pad_maximum_fusion.27), channel_id=1, source_target_pairs={{24,16},{25,17},{26,18},{27,19},{28,20},{29,21},{30,22},{31,23}} | collective-permute-start | bytes 1769480 | tf_op jit(solution)/shard_map/ppermute | solution.py:289
  1105.2 28.9 %collective-permute-start.99 = (bf16[2,96,1536]{2,1,0:T(8,128)(2,1)S(1)}, bf16[2,96,1536]{2,1,0:T(8,128)(2,1)S(1)}, u32[]{:S(2)}, u32[]{:S(2)}) collective-permute-start(bf16[2,96,1536]{2,1,0:T(8,128)(2,1)S(1)} %pad_maximum_fusion.27), channel_id=1, source_target_pairs={{0,16},{1,17},{2,18},{3,19},{4,20},{5,21},{6,22},{7,23}} | collective-permute-start | bytes 1769480 | tf_op jit(solution)/shard_map/ppermute | solution.py:289
  1134.1 51.9 %collective-permute-start.116 = (bf16[2,96,1536]{2,1,0:T(8,128)(2,1)S(1)}, bf16[2,96,1536]{2,1,0:T(8,128)(2,1)S(1)}, u32[]{:S(2)}, u32[]{:S(2)}) collective-permute-start(bf16[2,96,1536]{2,1,0:T(8,128)(2,1)S(1)} %pad_maximum_fusion.29), channel_id=1, source_target_pairs={{16,0},{17,1},{18,2},{19,3},{20,4},{21,5},{22,6},{23,7}} | collective-permute-start | bytes 1769480 | tf_op jit(solution)/shard_map/ppermute | solution.py:289
  1135.4 51.3 %collective-permute-start.117 = (bf16[2,96,1536]{2,1,0:T(8,128)(2,1)S(1)}, bf16[2,96,1536]{2,1,0:T(8,128)(2,1)S(1)}, u32[]{:S(2)}, u32[]{:S(2)}) collective-permute-start(bf16[2,96,1536]{2,1,0:T(8,128)(2,1)S(1)} %pad_maximum_fusion.29), channel_id=1, source_target_pairs={{24,0},{25,1},{26,2},{27,3},{28,4},{29,5},{30,6},{31,7}} | collective-permute-start | bytes 1769480 | tf_op jit(solution)/shard_map/ppermute | solution.py:289
  1144.4 45.1 %collective-permute-start.82 = (bf16[608,768]{1,0:T(8,128)(2,1)}, bf16[608,768]{1,0:T(8,128)(2,1)S(1)}, u32[]{:S(2)}, u32[]{:S(2)}) collective-permute-start(bf16[608,768]{1,0:T(8,128)(2,1)} %fusion.54), channel_id=1, source_target_pairs={{9,24},{11,26},{13,28},{15,30},{25,25},{27,27},{29,29},{31,31}} | collective-permute-start | bytes 2801672 | tf_op jit(solution)/shard_map/ppermute | solution.py:321
  1145.3 75.4 %collective-permute-start.68 = (bf16[608,768]{1,0:T(8,128)(2,1)}, bf16[608,768]{1,0:T(8,128)(2,1)S(1)}, u32[]{:S(2)}, u32[]{:S(2)}) collective-permute-start(bf16[608,768]{1,0:T(8,128)(2,1)} %fusion.54), channel_id=1, source_target_pairs={{0,24},{2,26},{4,28},{6,30},{16,25},{18,27},{20,29},{22,31}} | collective-permute-start | bytes 2801672 | tf_op jit(solution)/shard_map/ppermute | solution.py:321
  1153.4 37.4 %collective-permute-start.84 = (bf16[608,768]{1,0:T(8,128)(2,1)S(1)}, bf16[608,768]{1,0:T(8,128)(2,1)S(1)}, u32[]{:S(2)}, u32[]{:S(2)}) collective-permute-start(bf16[608,768]{1,0:T(8,128)(2,1)S(1)} %copy-done.34), channel_id=1, source_target_pairs={{9,8},{11,10},{13,12},{15,14},{25,9},{27,11},{29,13},{31,15}} | collective-permute-start | bytes 2801672 | tf_op jit(solution)/shard_map/ppermute | solution.py:321
  1186.8 24.9 %collective-permute-start.85 = (bf16[608,768]{1,0:T(8,128)(2,1)S(1)}, bf16[608,768]{1,0:T(8,128)(2,1)S(1)}, u32[]{:S(2)}, u32[]{:S(2)}) collective-permute-start(bf16[608,768]{1,0:T(8,128)(2,1)S(1)} %copy-done.89), channel_id=1, source_target_pairs={{9,0},{11,2},{13,4},{15,6},{25,1},{27,3},{29,5},{31,7}} | collective-permute-start | bytes 2801672 | tf_op jit(solution)/shard_map/ppermute | solution.py:321
  1189.5 31.9 %collective-permute-start.71 = (bf16[608,768]{1,0:T(8,128)(2,1)S(1)}, bf16[608,768]{1,0:T(8,128)(2,1)S(1)}, u32[]{:S(2)}, u32[]{:S(2)}) collective-permute-start(bf16[608,768]{1,0:T(8,128)(2,1)S(1)} %copy-done.34), channel_id=1, source_target_pairs={{0,8},{2,10},{4,12},{6,14},{16,9},{18,11},{20,13},{22,15}} | collective-permute-start | bytes 2801672 | tf_op jit(solution)/shard_map/ppermute | solution.py:321
  1190.9 31.2 %collective-permute-start.70 = (bf16[608,768]{1,0:T(8,128)(2,1)S(1)}, bf16[608,768]{1,0:T(8,128)(2,1)S(1)}, u32[]{:S(2)}, u32[]{:S(2)}) collective-permute-start(bf16[608,768]{1,0:T(8,128)(2,1)S(1)} %copy-done.30), channel_id=1, source_target_pairs={{0,16},{2,18},{4,20},{6,22},{16,17},{18,19},{20,21},{22,23}} | collective-permute-start | bytes 2801672 | tf_op jit(solution)/shard_map/ppermute | solution.py:321
  (252 other events, 6615.3 us)
Sparse Core Ops, SparseCore 0:
  841.9 124.5 all-reduce.1

commit v2 on v1

--- a/solution.py
+++ b/solution.py
@@ -228,120 +228,517 @@
     return lax.ppermute(block, "dp", [(i, i ^ bit) for i in range(count)])
 
 
-def spread_over_sections(piece, source, section):
-    result = piece
-    for step, last in ((1, lax.axis_size("section") - 1), (-1, 0)):
-        carried = piece
-        for at in range(source, last, step):
-            carried = lax.ppermute(carried, "section", [(at, at + step)])
-            result = jnp.where(section == at + step, carried, result)
-    return result
-
-
-def rows_from(array, start, size):
-    return lax.dynamic_slice_in_dim(array, start, size, 0)
-
-
-def gather_rows(weight, source, place):
-    rows = weight.shape[0]
-    half, part = rows // 2, rows // 4
-    mine = rows_from(weight, place.core * half + place.parity * part, part)
-    mine = spread_over_sections(mine, source, place.section)
-    from_x = swap(mine[: part // 2], place.x_bit)
-    from_y = swap(mine[part // 2 :], place.y_bit)
-    near = jnp.concatenate([from_x, from_y], axis=0)
-    first = jnp.where(place.parity == 0, mine, near)
-    second = jnp.where(place.parity == 0, near, mine)
-    own = jnp.concatenate([first, second], axis=0)
-    other = swap(own, 1)
-    return jnp.concatenate(
-        [jnp.where(place.core == 0, own, other), jnp.where(place.core == 0, other, own)], axis=0
-    )
-
-
 def add(a, b):
     return (a.astype(F32) + b.astype(F32)).astype(BF16)
 
 
-def scatter_rows(grad, place):
-    half = grad.shape[0] // 2
-    kept = rows_from(grad, place.core * half, half)
-    given = rows_from(grad, (1 - place.core) * half, half)
-    kept = add(kept, swap(given, 1))
-    columns = kept.shape[1] // 2
-    lanes = []
-    for lane, bits in enumerate((place.bits, place.bits[::-1])):
-        block = kept[:, lane * columns : (lane + 1) * columns]
-        for bit in bits:
-            size = block.shape[0] // 2
-            high = (place.dp // bit) % 2
-            given = rows_from(block, (1 - high) * size, size)
-            block = add(rows_from(block, high * size, size), swap(given, bit))
-        lanes.append(block)
-    return jnp.stack(lanes)
-
-
-def to_section(block, target, section):
-    count = lax.axis_size("section")
-    total = jnp.where(section == target, block.astype(F32), 0.0)
-    for source in range(count):
-        if source != target:
-            total = total + lax.ppermute(block, "section", [(source, target)]).astype(F32)
-    return total
-
-
-def gather_scattered(lanes, place):
-    out = []
-    for lane, bits in enumerate((place.bits, place.bits[::-1])):
-        block = lanes[lane]
-        for bit in bits[::-1]:
-            high = (place.dp // bit) % 2
-            far = swap(block, bit)
-            block = jnp.concatenate(
-                [jnp.where(high == 0, block, far), jnp.where(high == 0, far, block)], axis=0
-            )
-        out.append(block)
-    own = jnp.concatenate(out, axis=1)
-    far = swap(own, 1)
-    return jnp.concatenate(
-        [jnp.where(place.core == 0, own, far), jnp.where(place.core == 0, far, own)], axis=0
-    ).astype(F32)
-
-
-def deliver(block, target):
-    sections, count = lax.axis_size("section"), lax.axis_size("dp")
-    pieces = []
-    for slot in (0, 1):
-        for core in (0, 1):
-            route = [
-                (z * count + d, target * count + (d - core + z // 2))
-                for z in range(slot, sections, 2)
-                for d in range(core, count, 2)
-            ]
-            pieces.append(lax.ppermute(block, ("section", "dp"), route))
-    return pieces
-
-
-class Place:
+class Spot:
     def __init__(self):
-        self.section = lax.axis_index("section")
-        self.dp = lax.axis_index("dp")
-        count = lax.axis_size("dp")
-        self.core = self.dp % 2
-        self.bits = [1 << i for i in range(1, count.bit_length() - 1)]
-        self.x_bit, self.y_bit = self.bits[0], self.bits[-1]
-        self.parity = ((self.dp // self.x_bit) + (self.dp // self.y_bit)) % 2
+        self.z, self.sections = lax.axis_index("section"), lax.axis_size("section")
+        self.d, self.count = lax.axis_index("dp"), lax.axis_size("dp")
+        self.x_bit, self.y_bit = 2, 2 * math.isqrt(self.count // 2)
+        self.core = self.d % 2
+        self.xb, self.yb = (self.d // self.x_bit) % 2, (self.d // self.y_bit) % 2
+        self.c, self.c_x = self.yb * 2 + self.xb, self.yb * 2 + 1 - self.xb
+        self.c_y, self.c_d = (1 - self.yb) * 2 + self.xb, (1 - self.yb) * 2 + 1 - self.xb
+        self.mate, self.x, self.y = (self.flipped(b) for b in (1, self.x_bit, self.y_bit))
+        self.above, self.below = {"section": self.z + 1}, {"section": self.z - 1}
+        self.spare_bits = [
+            1 << i for i in range(self.count.bit_length() - 1) if 1 << i not in (1, self.x_bit, self.y_bit)
+        ]
+
+    def flipped(self, bit):
+        return {"dp": self.d + bit * (1 - 2 * ((self.d // bit) % 2))}
+
+    def greet(self):
+        barrier = pltpu.get_barrier_semaphore()
+        devices = [self.x, self.y]
+        for step in range(self.sections):
+            for core in (0, 1):
+                if step or core:
+                    devices.append({
+                        "section": (self.z + step) % self.sections,
+                        "dp": self.d - self.core + (self.core + core) % 2,
+                    })
+        for device in devices:
+            pl.semaphore_signal(barrier, inc=1, device_id=device, device_id_type=pl.DeviceIdType.MESH)
+        pl.semaphore_wait(barrier, len(devices))
+
+
+def remote(src, dst, send, recv, device):
+    return pltpu.make_async_remote_copy(
+        src_ref=src, dst_ref=dst, send_sem=send, recv_sem=recv,
+        device_id=device, device_id_type=pl.DeviceIdType.MESH,
+    )
+
+
+class PlaneGather:
+    SENDS, RECEIVES = 9, 9
+
+    def __init__(self, spot, dst, send, recv):
+        self.spot, self.dst, self.send, self.recv = spot, dst, send, recv
+
+    def blocks(self, core, chip, half=None):
+        at = core * 8 + chip * 2
+        return pl.ds(at, 2) if half is None else pl.ds(at + half, 1)
+
+    def copies(self, own=None):
+        s, k = self.spot, self.spot.core
+        plan = {
+            "x": (self.blocks(k, s.c), s.x), "y": (self.blocks(k, s.c), s.y),
+            "m": (self.blocks(k, s.c), s.mate),
+            "xy": (self.blocks(k, s.c_x, 0), s.y), "yx": (self.blocks(k, s.c_y, 1), s.x),
+            "mx": (self.blocks(k, s.c_x), s.mate), "my": (self.blocks(k, s.c_y), s.mate),
+            "md0": (self.blocks(k, s.c_d, 0), s.mate), "md1": (self.blocks(k, s.c_d, 1), s.mate),
+        }
+        out = {}
+        for index, (name, (rows, device)) in enumerate(plan.items()):
+            src = own if own is not None and name in ("x", "y", "m") else self.dst.at[rows]
+            out[name] = remote(src, self.dst.at[rows], self.send.at[index], self.recv.at[index], device)
+        return out
+
+    def arrivals(self):
+        s, k = self.spot, self.spot.core
+        plan = {
+            "x": self.blocks(k, s.c_x), "y": self.blocks(k, s.c_y), "m": self.blocks(1 - k, s.c),
+            "xy": self.blocks(k, s.c_d, 0), "yx": self.blocks(k, s.c_d, 1),
+            "mx": self.blocks(1 - k, s.c_x), "my": self.blocks(1 - k, s.c_y),
+            "md0": self.blocks(1 - k, s.c_d, 0), "md1": self.blocks(1 - k, s.c_d, 1),
+        }
+        return {
+            name: remote(self.dst.at[rows], self.dst.at[rows], self.send.at[i], self.recv.at[i], s.mate)
+            for i, (name, rows) in enumerate(plan.items())
+        }
+
+    def begin(self, own):
+        copies = self.copies(own)
+        for name in ("x", "y", "m"):
+            copies[name].start()
+
+    def second(self):
+        copies, arrivals = self.copies(), self.arrivals()
+        arrivals["x"].wait_recv()
+        copies["xy"].start()
+        copies["mx"].start()
+        arrivals["y"].wait_recv()
+        copies["yx"].start()
+        copies["my"].start()
+
+    def third(self):
+        copies, arrivals = self.copies(), self.arrivals()
+        for name, after in (("xy", "md0"), ("yx", "md1")):
+            arrivals[name].wait_recv()
+            copies[after].start()
+
+    def finish(self):
+        copies, arrivals = self.copies(), self.arrivals()
+        for name in copies:
+            copies[name].wait_send()
+        for name in ("m", "mx", "my", "md0", "md1"):
+            arrivals[name].wait_recv()
+
+
+class WeightGather(PlaneGather):
+    def __init__(self, spot, src, dst, source, send, recv):
+        super().__init__(spot, dst, send, recv)
+        self.src, self.source = src, source
+        self.own = self.blocks(spot.core, spot.c)
+
+    def along(self, src):
+        s = self.spot
+        return (
+            remote(src.at[self.own], self.dst.at[self.own], self.send.at[9], self.recv.at[9], s.above),
+            remote(src.at[self.own], self.dst.at[self.own], self.send.at[10], self.recv.at[9], s.below),
+            pltpu.make_async_copy(src.at[self.own], self.dst.at[self.own], self.send.at[11]),
+        )
+
+    def open(self):
+        z, source = self.spot.z, self.source
+        up, down, stay = self.along(self.src)
+        @pl.when(z == source)
+        def _():
+            if source + 1 < self.spot.sections:
+                up.start()
+            if source:
+                down.start()
+            stay.start()
+            self.begin(self.src.at[self.own])
+
+    def first(self):
+        z, source, last = self.spot.z, self.source, self.spot.sections - 1
+        up, down, _ = self.along(self.dst)
+        @pl.when(z != source)
+        def _():
+            up.wait_recv()
+            if source < last - 1:
+                pl.when((z > source) & (z < last))(up.start)
+            if source > 1:
+                pl.when((z < source) & (z > 0))(down.start)
+            self.begin(self.dst.at[self.own])
+
+    def finish(self):
+        z, source, last = self.spot.z, self.source, self.spot.sections - 1
+        up, down, stay = self.along(self.src)
+        if source < last:
+            pl.when((z >= source) & (z < last))(up.wait_send)
+        if source:
+            pl.when((z <= source) & (z > 0))(down.wait_send)
+        pl.when(z == source)(stay.wait)
+        super().finish()
+
+
+def gather_weights_body(front, back, norms, *refs):
+    fronts, downs, norm_all = refs[:4], refs[4:6], refs[6]
+    send, recv, norm_send, norm_recv = refs[7:]
+    spot = Spot()
+    spot.greet()
+    norm_copies = [
+        remote(
+            norms, norm_all.at[spot.z], norm_send.at[step], norm_recv.at[step],
+            {"section": (spot.z + step) % spot.sections},
+        )
+        for step in range(1, spot.sections)
+    ]
+    kept = pltpu.make_async_copy(norms, norm_all.at[spot.z], norm_send.at[0])
+    for copy in norm_copies + [kept]:
+        copy.start()
+    jobs = []
+    for layer in range(2):
+        low, high = downs[layer].at[pl.ds(0, 16)], downs[layer].at[pl.ds(16, 16)]
+        jobs += [(front, fronts[2 * layer], 2 * layer), (front, fronts[2 * layer + 1], 2 * layer + 1)]
+        jobs += [(back, low, 2 * layer), (back, high, 2 * layer + 1)]
+    gathers = [WeightGather(spot, a, b, s, send.at[i], recv.at[i]) for i, (a, b, s) in enumerate(jobs)]
+    for gather in gathers:
+        gather.open()
+    for i in range(len(gathers) + 2):
+        if i < len(gathers):
+            gathers[i].first()
+        if 0 <= i - 1 < len(gathers):
+            gathers[i - 1].second()
+        if i >= 2:
+            gathers[i - 2].third()
+    for gather in gathers:
+        gather.finish()
+    kept.wait()
+    for step, copy in enumerate(norm_copies, 1):
+        copy.wait_send()
+        block = norm_all.at[(spot.z + spot.sections - step) % spot.sections]
+        remote(block, block, norm_send.at[step], norm_recv.at[step], spot.mate).wait_recv()
+
+
+def gather_weights(front, back, norms):
+    sections = lax.axis_size("section")
+    blocks = lambda a, n: (n, a.shape[0] // 16, a.shape[1])
+    front_b, back_b = front.reshape(blocks(front, 16)), back.reshape(blocks(back, 16))
+    full = jax.ShapeDtypeStruct(front_b.shape, BF16)
+    down = jax.ShapeDtypeStruct((32,) + back_b.shape[1:], BF16)
+    hbm = pl.BlockSpec(memory_space=pl.ANY)
+    out = pl.pallas_call(
+        gather_weights_body,
+        in_specs=[hbm] * 3, out_specs=[hbm] * 7,
+        out_shape=[full] * 4 + [down] * 2 + [jax.ShapeDtypeStruct((sections,) + norms.shape, F32)],
+        scratch_shapes=[
+            pltpu.SemaphoreType.DMA((8, 12)), pltpu.SemaphoreType.DMA((8, 10)),
+            pltpu.SemaphoreType.DMA((sections,)), pltpu.SemaphoreType.DMA((sections,)),
+        ],
+        compiler_params=pltpu.CompilerParams(collective_id=0, has_side_effects=True),
+        name="gather_weights",
+    )(front_b, back_b, norms)
+    fronts = [a.reshape(front.shape) for a in out[:4]]
+    downs = [a.reshape(2 * back.shape[0], back.shape[1]) for a in out[4:6]]
+    return fronts, downs, out[6]
+
+
+class Deliver:
+    def __init__(self, spot, src, dst, target, send, recv, core_rows):
+        self.spot, self.src, self.dst, self.target, self.send, self.recv = spot, src, dst, target, send, recv
+        self.rows = core_rows
+        self.owner, self.slot = spot.z // 2, spot.z % 2
+        self.home = (spot.z == target) & (spot.core == self.owner)
+
+    def place(self, slot, core):
+        return self.dst.at[slot, pl.ds(pl.multiple_of(core * self.rows, 16), self.rows)]
+
+    def copies(self):
+        s, spot = self, self.spot
+        spot_at = s.place(s.slot, spot.core)
+        away = remote(
+            s.src, spot_at, s.send.at[0], s.recv.at[s.slot * 2 + spot.core],
+            {"section": s.target, "dp": spot.d - spot.core + s.owner},
+        )
+        return away, pltpu.make_async_copy(s.src, spot_at, s.send.at[1])
+
+    def start(self):
+        away, stay = self.copies()
+        pl.when(self.home)(stay.start)
+        pl.when(jnp.logical_not(self.home))(away.start)
+
+    def finish(self):
+        away, stay = self.copies()
+        pl.when(self.home)(stay.wait)
+        pl.when(jnp.logical_not(self.home))(away.wait_send)
+        spot = self.spot
+        for slot in (0, 1):
+            for core in (0, 1):
+                here = (spot.core * 2 + slot == spot.z) & (spot.core == core)
+                block = self.place(slot, core)
+                landing = remote(block, block, self.send.at[0], self.recv.at[slot * 2 + core], spot.mate)
+                pl.when((spot.z == self.target) & jnp.logical_not(here))(landing.wait_recv)
+
+
+def add_into(target, *others):
+    blocks, rows, _ = target.shape
+    def step(i, carry):
+        b, r = i // (rows // 16), pl.ds(pl.multiple_of((i % (rows // 16)) * 16, 16), 16)
+        total = target[b, r, :].astype(F32)
+        for other in others:
+            total = total + other[b, r, :].astype(F32)
+        target[b, r, :] = total.astype(BF16)
+        return carry
+    lax.fori_loop(0, blocks * (rows // 16), step, 0)
+
+
+class ScatterSum:
+    SEMS = 9
+
+    def __init__(self, spot, src, target, bufs, send, recv):
+        self.spot, self.src, self.target, self.send, self.recv = spot, src, target, send, recv
+        self.half, self.from_mate, self.in_x, self.in_y, self.in_yx, self.in_xy, self.from_z = bufs
+
+    @staticmethod
+    def scratch(block_rows, columns):
+        return [
+            pltpu.VMEM((n, block_rows, columns), BF16) for n in (8, 8, 2, 2, 1, 1, 4)
+        ]
+
+    def mate_copies(self):
+        s, spot = self, self.spot
+        return (
+            pltpu.make_async_copy(s.src.at[pl.ds(spot.core * 8, 8)], s.half, s.send.at[0]),
+            remote(s.src.at[pl.ds((1 - spot.core) * 8, 8)], s.from_mate, s.send.at[1], s.recv.at[1], spot.mate),
+        )
+
+    def start(self):
+        for copy in self.mate_copies():
+            copy.start()
+
+    def block(self, chip, half):
+        return self.half.at[pl.ds(chip * 2 + half, 1)]
+
+    def first_copies(self):
+        s, spot = self, self.spot
+        first, second = pl.ds(0, 1), pl.ds(1, 1)
+        return (
+            remote(s.block(spot.c_x, 0), s.in_x.at[first], s.send.at[2], s.recv.at[2], spot.x),
+            remote(s.block(spot.c_d, 0), s.in_x.at[second], s.send.at[3], s.recv.at[3], spot.x),
+            remote(s.block(spot.c_y, 1), s.in_y.at[first], s.send.at[4], s.recv.at[4], spot.y),
+            remote(s.block(spot.c_d, 1), s.in_y.at[second], s.send.at[5], s.recv.at[5], spot.y),
+        )
+
+    def second_copies(self):
+        s, spot = self, self.spot
+        return (
+            remote(s.block(spot.c_y, 0), s.in_xy, s.send.at[6], s.recv.at[6], spot.y),
+            remote(s.block(spot.c_x, 1), s.in_yx, s.send.at[7], s.recv.at[7], spot.x),
+        )
+
+    def first(self):
+        for copy in self.mate_copies():
+            copy.wait()
+        add_into(self.half, self.from_mate)
+        for copy in self.first_copies():
+            copy.start()
+
+    def second(self):
+        s, spot = self, self.spot
+        for copy in self.first_copies():
+            copy.wait_recv()
+        first, other = pl.ds(0, 1), pl.ds(1, 1)
+        add_into(s.block(spot.c_y, 0), s.in_x.at[other])
+        add_into(s.block(spot.c_x, 1), s.in_y.at[other])
+        for copy in self.second_copies():
+            copy.start()
+        add_into(s.block(spot.c, 0), s.in_x.at[first])
+        add_into(s.block(spot.c, 1), s.in_y.at[first])
+
+    def third(self):
+        s, spot = self, self.spot
+        for copy in self.second_copies():
+            copy.wait_recv()
+        add_into(s.block(spot.c, 0), s.in_xy)
+        add_into(s.block(spot.c, 1), s.in_yx)
+
+    def own(self):
+        return self.half.at[pl.ds(self.spot.c * 2, 2)]
+
+    def along(self):
+        s, spot = self, self.spot
+        down = remote(s.own(), s.from_z.at[pl.ds(0, 2)], s.send.at[8], s.recv.at[8], spot.below)
+        up = remote(s.own(), s.from_z.at[pl.ds(2, 2)], s.send.at[8], s.recv.at[0], spot.above)
+        return up, down
+
+    def pass_on(self, z):
+        up, down = self.along()
+        last = self.spot.sections - 1
+
+        @pl.when(self.spot.z == z)
+        def _():
+            if z >= self.target and z < last:
+                down.wait_recv()
+                add_into(self.own(), self.from_z.at[pl.ds(0, 2)])
+            if z <= self.target and z > 0:
+                up.wait_recv()
+                add_into(self.own(), self.from_z.at[pl.ds(2, 2)])
+            if z > self.target:
+                down.start()
+            if z < self.target:
+                up.start()
+
+    def fourth(self):
+        for z in range(self.spot.sections):
+            self.pass_on(z)
+
+    def finish(self):
+        for copy in self.first_copies() + self.second_copies():
+            copy.wait_send()
+        up, down = self.along()
+        pl.when(self.spot.z != self.target)(up.wait_send)
+
+
+def collect_body(rows, n_small, *refs):
+    sections = lax.axis_size("section")
+    take = lambda n: tuple(refs_list.pop(0) for _ in range(n))
+    refs_list = list(refs)
+    acts, grads, fronts, backs, (small,) = take(sections), take(sections), take(sections), take(sections), take(1)
+    acts_out, grads_out, front_out, back_out, small_out = take(5)
+    zeros, sums, arriving = take(3)
+    front_bufs = [take(7) for _ in range(sections)]
+    back_bufs = [take(7) for _ in range(sections)]
+    send, recv, dsend, drecv, asend, arecv, ssend, srecv, psem = take(9)
+    spot = Spot()
+    spot.greet()
+    scatters = {}
+    for s in range(sections):
+        scatters["front", s] = ScatterSum(spot, fronts[s], s, front_bufs[s], send.at[s], recv.at[s])
+        scatters["back", s] = ScatterSum(spot, backs[s], s, back_bufs[s], send.at[sections + s], recv.at[sections + s])
+    order = []
+    for s in reversed(range(sections)):
+        order.append(scatters["front", s])
+        if s % 2:
+            order += [scatters["back", s - 1], scatters["back", s]]
+    delivers = [Deliver(spot, a, acts_out, s, dsend.at[s], drecv.at[s], rows) for s, a in enumerate(acts)]
+    delivers += [
+        Deliver(spot, a, grads_out, s, dsend.at[sections + s], drecv.at[sections + s], rows)
+        for s, a in enumerate(grads)
+    ]
+    for scatter in order:
+        scatter.start()
+    for deliver in delivers:
+        deliver.start()
+    zeros[...] = jnp.zeros_like(zeros)
+    pad = acts_out.shape[1] - 2 * rows
+    pads = [
+        pltpu.make_async_copy(zeros, acts_out.at[slot, pl.ds(2 * rows, pad)], psem.at[slot]) for slot in (0, 1)
+    ]
+    for copy in pads:
+        copy.start()
+    sums[0] = small[...]
+    partners = [spot.mate, spot.x, spot.y] + [
+        {"section": spot.z + bit * (1 - 2 * ((spot.z // bit) % 2))}
+        for bit in (1 << i for i in range((sections - 1).bit_length()))
+    ]
+
+    def small_step(i):
+        copy = remote(sums.at[i], arriving.at[i], ssend.at[i], srecv.at[i], partners[i])
+        copy.start()
+        copy.wait()
+        sums[i + 1] = sums[i] + arriving[i]
+
+    count = len(order)
+    for i in range(count + 3):
+        if i < count:
+            order[i].first()
+        if 0 <= i - 1 < count:
+            order[i - 1].second()
+        if 0 <= i - 2 < count:
+            order[i - 2].third()
+        if 0 <= i - 3 < count:
+            order[i - 3].fourth()
+        if i < len(partners):
+            small_step(i)
+    small_out[...] = sums[len(partners)]
+    gathers = [
+        PlaneGather(spot, out, asend.at[i], arecv.at[i]) for i, out in enumerate((front_out, back_out))
+    ]
+    stays = []
+    for i, (gather, kind) in enumerate(zip(gathers, ("front", "back"))):
+        for s in range(sections):
+            own = scatters[kind, s].own()
+            stay = pltpu.make_async_copy(own, gather.dst.at[gather.blocks(spot.core, spot.c)], psem.at[2 + i])
+
+            @pl.when(spot.z == s)
+            def _(gather=gather, own=own, stay=stay):
+                stay.start()
+                gather.begin(own)
+        stays.append(stay)
+    for gather in gathers:
+        gather.second()
+    for gather in gathers:
+        gather.third()
+    for gather in gathers:
+        gather.finish()
+    for copy in stays + pads:
+        copy.wait()
+    for deliver in delivers:
+        deliver.finish()
+    for scatter in order:
+        scatter.finish()
+
+
+def collect(acts, grads, fronts, backs, small, padded):
+    sections = lax.axis_size("section")
+    rows, width = acts[0].shape
+    blocked = lambda a: a.reshape(16, a.shape[0] // 16, a.shape[1])
+    fronts, backs = [blocked(a) for a in fronts], [blocked(a) for a in backs]
+    hbm, vmem = pl.BlockSpec(memory_space=pl.ANY), pl.BlockSpec(memory_space=pltpu.VMEM)
+    steps = 3 + (sections - 1).bit_length()
+    sems = pltpu.SemaphoreType.DMA
+    out = pl.pallas_call(
+        functools.partial(collect_body, rows, small.shape[0]),
+        in_specs=[hbm] * (4 * sections) + [vmem],
+        out_specs=[hbm] * 4 + [vmem],
+        out_shape=[
+            jax.ShapeDtypeStruct((2, padded, width), BF16), jax.ShapeDtypeStruct((2, 2 * rows, width), BF16),
+            jax.ShapeDtypeStruct(fronts[0].shape, BF16), jax.ShapeDtypeStruct(backs[0].shape, BF16),
+            jax.ShapeDtypeStruct(small.shape, F32),
+        ],
+        scratch_shapes=[
+            pltpu.VMEM((padded - 2 * rows, width), BF16),
+            pltpu.VMEM((steps + 1,) + small.shape, F32), pltpu.VMEM((steps,) + small.shape, F32),
+        ]
+        + ScatterSum.scratch(*fronts[0].shape[1:]) * sections
+        + ScatterSum.scratch(*backs[0].shape[1:]) * sections
+        + [
+            sems((2 * sections, 9)), sems((2 * sections, 9)), sems((2 * sections, 2)), sems((2 * sections, 4)),
+            sems((2, 9)), sems((2, 9)), sems((steps,)), sems((steps,)), sems((4,)),
+        ],
+        compiler_params=pltpu.CompilerParams(
+            collective_id=1, has_side_effects=True, vmem_limit_bytes=62 * 2**20
+        ),
+        name="collect",
+    )(*acts, *grads, *fronts, *backs, small)
+    return out[0], out[1], out[2].reshape(-1, fronts[0].shape[2]), out[3].reshape(-1, backs[0].shape[2]), out[4]
 
 
 def per_device(
     clip_inputs, out_grad, clip_class, w_front, w_back, norm_gain, norm_shift,
     bias_query_value, bias_attn_out, bias_up, bias_down,
 ):
-    place = Place()
+    spot = Spot()
     sections = lax.axis_size("section")
     padded, width = clip_inputs.shape[1:]
     rows = -(-LONG // 32) * 16
-    core, section = place.core, place.section
+    core, section = spot.core, spot.z
 
     owner, slot = section // 2, section % 2
     mine = jnp.stack([lax.dynamic_index_in_dim(a, slot, 0, False) for a in (clip_inputs, out_grad)])
@@ -358,15 +755,9 @@
     row_mask = own_rows.astype(F32)[:, None]
     key_bias = jnp.where(jnp.concatenate([own_rows, far_rows]), 0.0, MASKED)[:, None]
 
-    gains = lax.all_gather(norm_gain[0], "section")
-    shifts = lax.all_gather(norm_shift[0], "section")
-    fronts = [gather_rows(w_front[0], s, place) for s in range(sections)]
-    downs = [
-        jnp.concatenate([gather_rows(w_back[0], s - 1, place), gather_rows(w_back[0], s, place)], axis=0)
-        if s % 2
-        else None
-        for s in range(sections)
-    ]
+    norms = jnp.concatenate([norm_gain, norm_shift, jnp.zeros((6, width), F32)], axis=0)
+    fronts, downs, norm_all = gather_weights(w_front[0], w_back[0], norms)
+    gains, shifts = norm_all[:, 0], norm_all[:, 1]
 
     hidden = (clip_pair[0].astype(F32) * row_mask).astype(BF16)
     saved, delivered = [], []
@@ -389,15 +780,14 @@
             pre = mm(normed, fronts[s]) + bias_up[layer]
             act, slope = gelu_and_slope(pre)
             act, slope = act.astype(BF16), slope.astype(BF16)
-            branch = mm(act, downs[s]) + bias_down[layer]
+            branch = mm(act, downs[layer]) + bias_down[layer]
             saved.append((hidden, normed, act, slope))
         hidden = (row_mask * (entering + branch)).astype(BF16)
-        delivered.append(deliver(hidden, s))
+        delivered.append(hidden)
 
     incoming = clip_pair[1]
     sent_grads = [None] * sections
-    front_total = jnp.zeros((), F32)
-    back_total = jnp.zeros((), F32)
+    grad_fronts, grad_backs = [None] * sections, [None] * sections
     grad_gain, grad_shift = [None] * sections, [None] * sections
     grad_pairs, grad_outs, grad_ups, grad_downs = [], [], [], []
     for s in reversed(range(sections)):
@@ -415,47 +805,37 @@
             sums = jnp.sum(grad_qkv.astype(F32), axis=0)
             grad_pairs.insert(0, jnp.concatenate([sums[:width], sums[2 * width :]]))
             grad_outs.insert(0, jnp.sum(grad_rows, axis=0))
-            grad_front = jnp.concatenate(
+            grad_fronts[s] = jnp.concatenate(
                 [contract_rows(normed, grad_qkv).astype(BF16), contract_rows(grad_b, attended_b).astype(BF16)],
                 axis=1,
             )
             grad_normed = contract_cols(grad_qkv, front[:, : 3 * width])
         else:
             entered, normed, act, slope = saved[s]
-            grad_act = contract_cols(grad_b, downs[s])
+            grad_act = contract_cols(grad_b, downs[s // 2])
             grad_pre = (grad_act * slope.astype(F32)).astype(BF16)
             grad_down = contract_rows(act, grad_b).astype(BF16)
-            grad_front = contract_rows(normed, grad_pre).astype(BF16)
+            grad_fronts[s] = contract_rows(normed, grad_pre).astype(BF16)
             grad_ups.insert(0, jnp.sum(grad_pre.astype(F32), axis=0))
             grad_downs.insert(0, jnp.sum(grad_rows, axis=0))
             grad_normed = contract_cols(grad_pre, front)
             half = grad_down.shape[0] // 2
-            for target, piece in ((s - 1, grad_down[:half]), (s, grad_down[half:])):
-                back_total = back_total + to_section(scatter_rows(piece, place), target, section)
-        front_total = front_total + to_section(scatter_rows(grad_front, place), s, section)
+            grad_backs[s - 1], grad_backs[s] = grad_down[:half], grad_down[half:]
         grad_hidden, grad_gain[s], grad_shift[s] = norm_backward(entered.astype(F32), grad_normed, gains[s])
         incoming = (grad_rows + grad_hidden).astype(BF16)
-        sent_grads[s] = deliver(incoming, s)
-
-    def assemble(pieces, kind):
-        clips = []
-        for slot_id in (0, 1):
-            halves = []
-            for half in (0, 1):
-                choice = pieces[0][2 * slot_id + half]
-                for s in range(1, sections):
-                    choice = jnp.where(section == s, pieces[s][2 * slot_id + half], choice)
-                halves.append(choice.astype(kind))
-            halves.append(jnp.zeros((padded - 2 * rows, width), kind))
-            clips.append(jnp.concatenate(halves, axis=0))
-        return jnp.stack(clips)[None]
-
-    small = lax.psum(
-        jnp.concatenate(
-            [v.reshape(-1) for v in grad_gain + grad_shift + grad_pairs + grad_outs + grad_ups + grad_downs]
-        ),
-        ("section", "dp"),
+        sent_grads[s] = incoming
+
+    small = jnp.concatenate(
+        [v.reshape(-1) for v in grad_gain + grad_shift + grad_pairs + grad_outs + grad_ups + grad_downs]
     )
+    acts_out, grads_out, front_out, back_out, small = collect(
+        delivered, sent_grads, grad_fronts, grad_backs, small.reshape(-1, 128), padded
+    )
+    small = small.reshape(-1)
+    for bit in spot.spare_bits:
+        small = small + swap(small, bit)
+        front_out, back_out = add(front_out, swap(front_out, bit)), add(back_out, swap(back_out, bit))
+    grads_out = jnp.pad(grads_out.astype(F32), ((0, 0), (0, padded - 2 * rows), (0, 0)))
     parts, place_at = [], 0
     layers, hidden_units = bias_up.shape
     for count, size in (
@@ -465,10 +845,10 @@
         parts.append(small[place_at : place_at + count * size].reshape(count, size))
         place_at += count * size
     return (
-        assemble(delivered, BF16),
-        assemble(sent_grads, F32),
-        gather_scattered(front_total.astype(BF16), place)[None],
-        gather_scattered(back_total.astype(BF16), place)[None],
+        acts_out[None],
+        grads_out[None],
+        front_out.astype(F32)[None],
+        back_out.astype(F32)[None],
         lax.dynamic_slice_in_dim(parts[0], section, 1, 0),
         lax.dynamic_slice_in_dim(parts[1], section, 1, 0),
         *parts[2:],

time: 1290 us -> 810 us (0.63)
  Pallas kernels: 95.2 us -> 597 us
  waiting for transfers between devices: 413 us -> 5.58 us
  starting transfers between devices: 393 us -> 2.76 us
  other arithmetic: 127 us -> 38.2 us
  blocking collectives: 32 us -> 0 us
  local copies, waits for them, and re-layouts: 54.6 us -> 34.7 us
  matrix products: 140 us -> 122 us
  between operations: 19.9 us -> 3.79 us
    pallas_call x0 -> x2, Pallas kernels: none -> 502 us  [the longest x1 332 us: collect(): pl.pallas_call(functools.partial(collect_body, rows, small.shape[0]), in_...]
    ppermute x80 -> x0, starting transfers between devices: 237 us -> none  [the longest x24 88.7 us: to_section(): lax.ppermute(block, 'section', [(source, target)]).astype(F32)]
    ppermute x80 -> x6, waiting for transfers between devices: 187 us -> 5.58 us  [swap(): return lax.ppermute(block, 'dp', [(i, i ^ bit) for i in range(count)])]
    ppermute x80 -> x6, starting transfers between devices: 156 us -> 2.76 us  [swap(): return lax.ppermute(block, 'dp', [(i, i ^ bit) for i in range(count)])]
    ppermute x80 -> x0, waiting for transfers between devices: 130 us -> none  [the longest x24 76.8 us: spread_over_sections(): carried = lax.ppermute(carried, 'section', [(at, at + step)])]
    psum x1 -> x0, waiting for transfers between devices: 95.9 us -> none  [per_device(): lax.psum(jnp.concatenate([v.reshape(-1) for v in grad_gain + grad_shift +...]
    select_n x27 -> x0, other arithmetic: 36.9 us -> none  [the longest x7 22.1 us: gather_rows(): jnp.where(place.core == 0, own, other)]
    all_gather x2 -> x0, blocking collectives: 32 us -> none  [the longest x1 18.6 us: per_device(): gains = lax.all_gather(norm_gain[0], 'section')]
  transfers between devices with their start and end apart: 161 -> 6, of which waited for: 56 -> 2; matrix products, arithmetic and copies ran while one was open for 23% -> 5% of each run, Pallas kernels for 7% -> 21%
where the time goes in v2:
time: 810 us; the launch traced here: 804 us
  Pallas kernels  597 us (74%)
  matrix products  122 us (15%)
  other arithmetic  38.2 us (5%)
  local copies, waits for them, and re-layouts  34.7 us (4%)
    pallas_call x1, Pallas kernels, collect(): pl.pallas_call(functools.partial(collect_body, rows, small.shape[0]), in_...  332 us
    pallas_call x1, Pallas kernels, gather_weights(): pl.pallas_call(gather_weights_body, in_specs=[hbm] * 3, out_specs=[hbm] *...  170 us
    pallas_call x2, Pallas kernels, attention_backward(): pl.pallas_call(functools.partial(attention_backward_body, ((0, rows),)),...  55.7 us
    dot_general x8, matrix products, mm(): return jnp.dot(left, right, preferred_element_type=F32)  44.7 us
    dot_general x8, matrix products, contract_cols(): lax.dot_general(left, right, (((1,), (1,)), ((), ())), preferred_element_...  42.5 us
    pallas_call x2, Pallas kernels, attention_forward(): pl.pallas_call(functools.partial(attention_forward_body, rows // 2), grid...  39.5 us
    dot_general x8, matrix products, contract_rows(): lax.dot_general(left, right, (((0,), (0,)), ((), ())), preferred_element_...  34.5 us
  transfers between devices with their start and end apart: 6, of which 2 were waited for; matrix products, arithmetic and copies ran while one was open for 5% of the time, Pallas kernels for 21%

profile of v2, /device:TPU:0, one launch (start us, length us, event | category | flops | bytes accessed | tf_op | source)
XLA Modules:
  0.0 804.1 jit_solution(11990445962999092365)
XLA Ops:
  0.7 2.4 constant_dynamic-slice_fusion.2
  3.3 1.1 copy-done
  6.9 0.7 maximum_maximum_fusion.norms
  7.6 170.4 %gather_weights.1 = (bf16[16,48,3072]{2,1,0:T(8,128)(2,1)}, bf16[16,48,3072]{2,1,0:T(8,128)(2,1)}, bf16[16,48,3072]{2,1,0:T(8,128)(2,1)}, bf16[16,48,3072]{2,1,0...) custom-call(bf16[16,48,3072]{2,1,0:T(8,128)(2,1)} %bitcast.121, ...), custom_call_target="tpu_custom_call" | custom-call | tf_op jit(solution)/shard_map/gather_weights/pallas_call | solution.py:436
  178.1 1.0 slice_reduce_fusion.2
  180.4 2.1 fusion.94
  182.8 1.2 fusion.81
  184.6 2.6 fusion.12.query_ref.key_own.value_own
  187.2 1.5 copy-done.12
  188.7 1.4 slice.236
  190.1 0.9 collective-permute-start.2
  192.2 0.9 broadcast_select_fusion.bias_ref
  193.1 1.8 collective-permute-done.2.key_far.value_far
  194.9 19.9 %attention_forward.2 = (f32[608,768]{1,0:T(8,128)}, bf16[12,608,128]{2,1,0:T(8,128)(2,1)}) custom-call(bf16[608,2304]{1,0:T(8,128)(2,1)} %copy-done.12, bf16[608,2304]{1,0:T(8,128)(2,1)} %copy-done.12, bf16[608,2304]{1,0:T(8,128)(2,1)} %copy-done.12, bf16[608,1536]{1,0:T(8,128)(2,1)} %collective-permute-done.2.key_far.value_far, ...), custom_call_target="tpu_custom_call" | custom-call | flops 18169724928 | bytes 5603328 | tf_op jit(solution)/shard_map/attention_forward/pallas_call | solution.py:101
  214.8 3.1 convert_reduce_fusion.6
  218.4 12.5 %multiply_convert_fusion.3 = (bf16[608,3072]{1,0:T(8,128)(2,1)S(1)}, f32[608,3072]{1,0:T(8,128)}) fusion(f32[3072]{0:T(1024)S(1)} %bitcast.132, bf16[768,3072]{1,0:T(8,128)(2,1)} %bitcast.142, bf16[608,768]{1,0:T(8,128)(2,1)S(1)} %get-tuple-element.117.refs_0_, f32[768]{0:T(1024)S(1)} %get-tuple-element.84, f32[768]{0:T(1024)S(1)} %get-tuple-element.85, ...), kind=kOutput, calls=%fused_computation.21 | convolution fusion | flops 2914664448 | bytes 16882432 | tf_op jit(solution)/shard_map/dot_general | solution.py:24
  230.9 3.2 convert_reduce_fusion.5
  234.7 2.6 fusion.13.query_ref.key_own.value_own
  237.3 1.6 copy-done.13
  238.9 1.4 slice.239
  240.7 3.8 collective-permute-done.3.key_far.value_far
  244.5 19.6 %attention_forward.3 = (f32[608,768]{1,0:T(8,128)}, bf16[12,608,128]{2,1,0:T(8,128)(2,1)}) custom-call(bf16[608,2304]{1,0:T(8,128)(2,1)} %copy-done.13, bf16[608,2304]{1,0:T(8,128)(2,1)} %copy-done.13, bf16[608,2304]{1,0:T(8,128)(2,1)} %copy-done.13, bf16[608,1536]{1,0:T(8,128)(2,1)} %collective-permute-done.3.key_far.value_far, ...), custom_call_target="tpu_custom_call" | custom-call | flops 18169724928 | bytes 5603328 | tf_op jit(solution)/shard_map/attention_forward/pallas_call | solution.py:101
  264.1 3.1 convert_reduce_fusion.4
  267.6 12.8 %multiply_convert_fusion.2 = (bf16[608,3072]{1,0:T(8,128)(2,1)}, f32[608,3072]{1,0:T(8,128)}) fusion(f32[3072]{0:T(1024)S(1)} %bitcast.134, bf16[768,3072]{1,0:T(8,128)(2,1)} %bitcast.166, bf16[608,768]{1,0:T(8,128)(2,1)S(1)} %get-tuple-element.123.refs_2_, f32[768]{0:T(1024)S(1)} %get-tuple-element.81, f32[768]{0:T(1024)S(1)} %get-tuple-element.80, ...), kind=kOutput, calls=%fused_computation.20 | convolution fusion | flops 2914664448 | bytes 16882432 | tf_op jit(solution)/shard_map/dot_general | solution.py:24
  280.4 12.3 %convert_reduce_fusion = (f32[3072]{0:T(1024)}, bf16[608,3072]{1,0:T(8,128)(2,1)S(1)}) fusion(f32[608,3072]{1,0:T(8,128)} %get-tuple-element.125, f32[3072]{0:T(1024)S(1)} %bitcast.135, bf16[3072,768]{1,0:T(8,128)(2,1)S(1)} %bitcast.162, f32[608]{0:T(1024)S(1)} %get-tuple-element.137, bf16[2,608,768]{2,1,0:T(8,128)(2,1)S(1)} %fusion.94), kind=kOutput, calls=%fused_computation.16 | convolution fusion | flops 2926334976 | bytes 16887808 | tf_op jit(solution)/shard_map/dot_general | solution.py:32
  292.7 4.0 fusion.51
  296.7 0.9 fusion.50.refs_7_
  297.6 3.5 convolution_convert_fusion.9.grad_ref
  301.1 27.9 %attention_backward.2 = (bf16[608,768]{1,0:T(8,128)(2,1)}, bf16[608,768]{1,0:T(8,128)(2,1)}, bf16[608,768]{1,0:T(8,128)(2,1)}, bf16[608,768]{1,0:T(8,128)(2,1)}, bf16[608,768]{1,0:T(8,128)(2,1)}) custom-call(bf16[12,608,128]{2,1,0:T(8,128)(2,1)} %get-tuple-element.45.extended_ref, bf16[608,2304]{1,0:T(8,128)(2,1)} %copy-done.13, ...), custom_call_target="tpu_custom_call" | custom-call | flops 45424312320 | bytes 11206656 | tf_op jit(solution)/shard_map/attention_backward/pallas_call | solution.py:178
  329.0 1.8 pad_maximum_fusion.4
  331.6 4.3 convolution_convert_fusion
  335.9 2.7 fusion.142
  338.6 2.3 convolution_convert_fusion.6
  341.0 0.9 copy-done.69
  341.9 6.4 convolution_convert_fusion.2
  348.4 4.0 fusion.91.refs_3_
  354.2 2.8 fusion.60
  357.1 5.0 convolution_convert_fusion.4
  362.1 0.9 fusion.59.refs_6_
  363.0 1.1 copy-done.64
  364.1 5.8 convolution_convert_fusion.1
  370.0 10.4 %convert_reduce_fusion.1 = (f32[3072]{0:T(1024)S(1)}, bf16[608,3072]{1,0:T(8,128)(2,1)S(1)}) fusion(f32[608,3072]{1,0:T(8,128)S(1)} %bitcast.171, f32[3072]{0:T(1024)S(1)} %bitcast.133, bf16[3072,768]{1,0:T(8,128)(2,1)S(1)} %bitcast.151, bf16[608,768]{1,0:T(8,128)(2,1)S(1)} %fusion.59.refs_6_, f32[608]{0:T(1024)S(1)} %get-tuple-element.137), kind=kOutput, calls=%fused_computation.17 | convolution fusion | flops 2926334976 | bytes 16886144 | tf_op jit(solution)/shard_map/dot_general | solution.py:32
  380.5 3.5 fusion.69
  384.1 1.0 fusion.68.refs_5_
  385.0 3.5 convolution_convert_fusion.8.grad_ref
  388.6 1.3 convolution_convert_fusion.7
  389.9 27.9 %attention_backward.3 = (bf16[608,768]{1,0:T(8,128)(2,1)}, bf16[608,768]{1,0:T(8,128)(2,1)}, bf16[608,768]{1,0:T(8,128)(2,1)}, bf16[608,768]{1,0:T(8,128)(2,1)}, bf16[608,768]{1,0:T(8,128)(2,1)}) custom-call(bf16[12,608,128]{2,1,0:T(8,128)(2,1)} %get-tuple-element.51.extended_ref, bf16[608,2304]{1,0:T(8,128)(2,1)} %copy-done.12, ...), custom_call_target="tpu_custom_call" | custom-call | flops 45424312320 | bytes 11206656 | tf_op jit(solution)/shard_map/attention_backward/pallas_call | solution.py:178
  417.8 1.8 pad_maximum_fusion.5
  420.3 4.4 pad_maximum_fusion.1
  424.8 2.7 fusion.143
  427.5 1.0 copy-done.67
  428.5 6.0 convolution_convert_fusion.3
  436.4 3.4 fusion.78
  439.8 3.3 convolution_convert_fusion.5
  443.5 2.8 pad_maximum_fusion
  446.3 1.8 fusion.77.refs_4_
  448.1 331.7 %collect.1 = (bf16[2,1280,768]{2,1,0:T(8,128)(2,1)}, bf16[2,1216,768]{2,1,0:T(8,128)(2,1)}, bf16[16,48,3072]{2,1,0:T(8,128)(2,1)}, bf16[16,96,768]{2,1,0:T(8,128)(2,1)}, f32[144,128]{1,0:T(8,128)}) custom-call(bf16[608,768]{1,0:T(8,128)(2,1)} %copy-done.2, bf16[608,768]{1,0:T(8,128)(2,1)} %copy-done.4, bf16[608,768]{1,0:T(8,128)(2,1)} %copy-done.5, ...), custom_call_target="tpu_custom_call" | custom-call | tf_op jit(solution)/shard_map/collect/pallas_call | solution.py:706
  779.8 0.7 fusion.145
  780.6 0.8 slice.232
  781.3 0.7 fusion.144
  782.1 7.5 bitcast_convert_fusion
  789.6 3.8 bitcast_convert_fusion.1
  793.4 2.5 bitcast_convert_fusion.2
  799.6 4.3 copy.51
  (268 shorter events, 15.3 us)
Async XLA Ops:
  3.1 3.8 copy-start.57
  3.1 3.8 copy-start.58
  5.0 175.3 %collective-permute-start.1 = (bf16[2,608,768]{2,1,0:T(8,128)(2,1)S(1)}, bf16[2,608,768]{2,1,0:T(8,128)(2,1)}, u32[]{:S(2)}, u32[]{:S(2)}) collective-permute-start(bf16[2,608,768]{2,1,0:T(8,128)(2,1)S(1)} %fusion.92), channel_id=1, source_target_pairs={{0,1},{1,0},{2,3},{3,2},{4,5},{5,4},{6,7},{7,6},{8,9},{9,8},{10,11... | collective-permute-start | bytes 5603336 | tf_op jit(solution)/shard_map/ppermute | solution.py:228
  6.7 172.4 %collective-permute-start = (f32[8,128]{1,0:T(8,128)S(1)}, f32[8,128]{1,0:T(8,128)S(1)}, u32[]{:S(2)}, u32[]{:S(2)}) collective-permute-start(f32[8,128]{1,0:T(8,128)S(1)} %broadcast_in_dim.29), channel_id=1, source_target_pairs={{0,1},{1,0},{2,3},{3,2},{4,5},{5,4},{6,7},{7,6},{8,9},{9,8},{10,11... | collective-permute-start | bytes 12296 | tf_op jit(solution)/shard_map/ppermute | solution.py:228
  7.6 170.4 %copy-start.42 = (f32[2,1536]{1,0:T(2,128)S(1)}, f32[2,1536]{1,0:T(2,128)}, u32[]{:S(2)}) copy-start(f32[2,1536]{1,0:T(2,128)} %param.18) | copy-start | bytes 36868
  179.0 5.0 copy-start.29
  179.0 5.0 copy-start.48
  179.0 39.3 %copy-start.31 = (f32[768]{0:T(1024)}, f32[768]{0:T(1024)S(1)}, u32[]{:S(2)}) copy-start(f32[768]{0:T(1024)S(1)} %get-tuple-element.85) | copy-start | bytes 9220
  179.0 39.3 %copy-start.50 = (f32[768]{0:T(1024)}, f32[768]{0:T(1024)S(1)}, u32[]{:S(2)}) copy-start(f32[768]{0:T(1024)S(1)} %get-tuple-element.84) | copy-start | bytes 9220
  179.1 55.6 %copy-start.33 = (f32[768]{0:T(1024)}, f32[768]{0:T(1024)S(1)}, u32[]{:S(2)}) copy-start(f32[768]{0:T(1024)S(1)} %get-tuple-element.83) | copy-start | bytes 9220
  179.1 55.6 %copy-start.52 = (f32[768]{0:T(1024)}, f32[768]{0:T(1024)S(1)}, u32[]{:S(2)}) copy-start(f32[768]{0:T(1024)S(1)} %get-tuple-element.82) | copy-start | bytes 9220
  180.3 4.2 copy-start.59
  182.8 4.4 copy-start.22
  190.1 4.7 collective-permute-start.2
  191.7 26.6 %copy-start.44 = (f32[1,3072]{1,0:T(1,128)}, f32[1,3072]{1,0:T(1,128)S(1)}, u32[]{:S(2)}) copy-start(f32[1,3072]{1,0:T(1,128)S(1)} %get-tuple-element.113) | copy-start | bytes 36868
  214.8 16.1 %slice-start.6 = ((s8[4718592]{0:T(1024)(128)(4,1)}), s8[4194304]{0:T(1024)(128)(4,1)S(1)}, s32[]{:S(2)}) async-start(s8[4718592]{0:T(1024)(128)(4,1)} %bitcast.146), calls=%async_computation.6 | async-start | bytes 8388608
  214.8 19.9 %slice-start.10 = ((s8[4718592]{0:T(1024)(128)(4,1)}), s8[4194304]{0:T(1024)(128)(4,1)S(1)}, s32[]{:S(2)}) async-start(s8[4718592]{0:T(1024)(128)(4,1)} %bitcast.154), calls=%async_computation.10 | async-start | bytes 8388608
  217.9 13.0 %copy-start.2 = (bf16[608,768]{1,0:T(8,128)(2,1)}, bf16[608,768]{1,0:T(8,128)(2,1)S(1)}, u32[]{:S(2)}) copy-start(bf16[608,768]{1,0:T(8,128)(2,1)S(1)} %get-tuple-element.117.refs_0_) | copy-start | bytes 2801668
  217.9 13.0 %copy-start.24 = (f32[608]{0:T(1024)}, f32[608]{0:T(1024)S(1)}, u32[]{:S(2)}) copy-start(f32[608]{0:T(1024)S(1)} %broadcast_multiply_fusion.10) | copy-start | bytes 7300
  218.3 12.6 %copy-start.38 = (f32[608]{0:T(1024)}, f32[608]{0:T(1024)S(1)}, u32[]{:S(2)}) copy-start(f32[608]{0:T(1024)S(1)} %add_rsqrt_fusion.2) | copy-start | bytes 7300
  218.4 12.6 %slice-start.7 = ((s8[4718592]{0:T(1024)(128)(4,1)}), s8[524288]{0:T(1024)(128)(4,1)S(1)}, s32[]{:S(2)}) async-start(s8[4718592]{0:T(1024)(128)(4,1)} %bitcast.146), calls=%async_computation.7 | async-start | bytes 1048576
  218.4 16.3 %slice-start.11 = ((s8[4718592]{0:T(1024)(128)(4,1)}), s8[524288]{0:T(1024)(128)(4,1)S(1)}, s32[]{:S(2)}) async-start(s8[4718592]{0:T(1024)(128)(4,1)} %bitcast.154), calls=%async_computation.11 | async-start | bytes 1048576
  234.2 127.9 %copy-start.4 = (bf16[608,768]{1,0:T(8,128)(2,1)}, bf16[608,768]{1,0:T(8,128)(2,1)S(1)}, u32[]{:S(2)}) copy-start(bf16[608,768]{1,0:T(8,128)(2,1)S(1)} %get-tuple-element.121.refs_1_) | copy-start | bytes 2801668
  240.3 4.2 collective-permute-start.3
  264.1 16.3 %slice-start.14 = ((s8[4718592]{0:T(1024)(128)(4,1)}), s8[4194304]{0:T(1024)(128)(4,1)S(1)}, s32[]{:S(2)}) async-start(s8[4718592]{0:T(1024)(128)(4,1)} %bitcast.160), calls=%async_computation.14 | async-start | bytes 8388608
  267.1 81.2 %copy-start.5 = (bf16[608,768]{1,0:T(8,128)(2,1)}, bf16[608,768]{1,0:T(8,128)(2,1)S(1)}, u32[]{:S(2)}) copy-start(bf16[608,768]{1,0:T(8,128)(2,1)S(1)} %get-tuple-element.123.refs_2_) | copy-start | bytes 2801668
  267.6 12.8 %slice-start.15 = ((s8[4718592]{0:T(1024)(128)(4,1)}), s8[524288]{0:T(1024)(128)(4,1)S(1)}, s32[]{:S(2)}) async-start(s8[4718592]{0:T(1024)(128)(4,1)} %bitcast.160), calls=%async_computation.15 | async-start | bytes 1048576
  267.6 25.1 %slice-start.18 = ((s8[4718592]{0:T(1024)(128)(4,1)}), s8[4194304]{0:T(1024)(128)(4,1)S(1)}, s32[]{:S(2)}) async-start(s8[4718592]{0:T(1024)(128)(4,1)} %bitcast.167), calls=%async_computation.18 | async-start | bytes 8388608
  280.4 12.3 %slice-start.19 = ((s8[4718592]{0:T(1024)(128)(4,1)}), s8[524288]{0:T(1024)(128)(4,1)S(1)}, s32[]{:S(2)}) async-start(s8[4718592]{0:T(1024)(128)(4,1)} %bitcast.167), calls=%async_computation.19 | async-start | bytes 1048576
  292.7 4.0 copy-start.68
  297.6 138.7 %copy-start.6 = (bf16[608,768]{1,0:T(8,128)(2,1)}, bf16[608,768]{1,0:T(8,128)(2,1)S(1)}, u32[]{:S(2)}) copy-start(bf16[608,768]{1,0:T(8,128)(2,1)S(1)} %fusion.50.refs_7_) | copy-start | bytes 2801668
  330.8 21.7 %collective-permute-start.4 = (bf16[2,608,768]{2,1,0:T(8,128)(2,1)S(1)}, bf16[2,608,768]{2,1,0:T(8,128)(2,1)S(1)}, u32[]{:S(2)}, u32[]{:S(2)}) collective-permute-start(bf16[2,608,768]{2,1,0:T(8,128)(2,1)S(1)} %pad_maximum_fusion.4), channel_id=1, source_target_pairs={{0,1},{1,0},{2,3},{3,2},{4,5},{5,4},{6,7},{7,6},{8,9},{9,8},{10,11... | collective-permute-start | bytes 5603336 | tf_op jit(solution)/shard_map/ppermute | solution.py:228
  335.9 12.4 %slice-start.16 = ((s8[4718592]{0:T(1024)(128)(4,1)}), s8[4194304]{0:T(1024)(128)(4,1)S(1)}, s32[]{:S(2)}) async-start(s8[4718592]{0:T(1024)(128)(4,1)} %bitcast.163), calls=%async_computation.16 | async-start | bytes 8388608
  341.9 6.4 copy-start.54
  341.9 6.5 slice-start.17
  341.9 12.3 %slice-start.12 = ((s8[4718592]{0:T(1024)(128)(4,1)}), s8[4194304]{0:T(1024)(128)(4,1)S(1)}, s32[]{:S(2)}) async-start(s8[4718592]{0:T(1024)(128)(4,1)} %bitcast.157), calls=%async_computation.12 | async-start | bytes 8388608
  348.3 4.1 copy-start.16
  348.4 4.1 copy-start.17
  348.4 5.8 slice-start.13
  357.0 12.9 %slice-start.8 = ((s8[4718592]{0:T(1024)(128)(4,1)}), s8[4194304]{0:T(1024)(128)(4,1)S(1)}, s32[]{:S(2)}) async-start(s8[4718592]{0:T(1024)(128)(4,1)} %bitcast.149), calls=%async_computation.8 | async-start | bytes 8388608
  357.0 12.9 %slice-start.20 = ((s8[7471104]{0:T(1024)(128)(4,1)}), s8[4194304]{0:T(1024)(128)(4,1)S(1)}, s32[]{:S(2)}) async-start(s8[7471104]{0:T(1024)(128)(4,1)} %bitcast.170), calls=%async_computation.20 | async-start | bytes 8388608
  362.1 7.9 slice-start.9
  362.1 7.8 slice-start.21
  364.1 72.2 %copy-start.7 = (bf16[608,768]{1,0:T(8,128)(2,1)}, bf16[608,768]{1,0:T(8,128)(2,1)S(1)}, u32[]{:S(2)}) copy-start(bf16[608,768]{1,0:T(8,128)(2,1)S(1)} %fusion.59.refs_6_) | copy-start | bytes 2801668
  364.1 5.8 copy-start.45
  364.1 16.3 %slice-start.4 = ((s8[4718592]{0:T(1024)(128)(4,1)}), s8[4194304]{0:T(1024)(128)(4,1)S(1)}, s32[]{:S(2)}) async-start(s8[4718592]{0:T(1024)(128)(4,1)} %bitcast.143), calls=%async_computation.4 | async-start | bytes 8388608
  369.9 10.5 %copy-start.3 = (bf16[608,768]{1,0:T(8,128)(2,1)S(1)}, bf16[608,768]{1,0:T(8,128)(2,1)}, u32[]{:S(2)}) copy-start(bf16[608,768]{1,0:T(8,128)(2,1)} %copy-done.2) | copy-start | bytes 2801668
  370.0 10.5 %copy-start.25 = (f32[608]{0:T(1024)S(1)}, f32[608]{0:T(1024)}, u32[]{:S(2)}) copy-start(f32[608]{0:T(1024)} %copy-done.24) | copy-start | bytes 7300
  370.0 10.5 %copy-start.32 = (f32[768]{0:T(1024)S(1)}, f32[768]{0:T(1024)}, u32[]{:S(2)}) copy-start(f32[768]{0:T(1024)} %copy-done.31) | copy-start | bytes 9220
  370.0 10.5 %copy-start.39 = (f32[608]{0:T(1024)S(1)}, f32[608]{0:T(1024)}, u32[]{:S(2)}) copy-start(f32[608]{0:T(1024)} %copy-done.38) | copy-start | bytes 7300
  370.0 10.5 %slice-start.5 = ((s8[4718592]{0:T(1024)(128)(4,1)}), s8[524288]{0:T(1024)(128)(4,1)S(1)}, s32[]{:S(2)}) async-start(s8[4718592]{0:T(1024)(128)(4,1)} %bitcast.143), calls=%async_computation.5 | async-start | bytes 1048576
  380.4 3.6 copy-start.66
  385.0 61.3 %copy-start.8 = (bf16[608,768]{1,0:T(8,128)(2,1)}, bf16[608,768]{1,0:T(8,128)(2,1)S(1)}, u32[]{:S(2)}) copy-start(bf16[608,768]{1,0:T(8,128)(2,1)S(1)} %fusion.68.refs_5_) | copy-start | bytes 2801668
  417.8 7.0 slice-start
  419.6 5.2 slice-start.1
  419.6 15.0 %collective-permute-start.5 = (bf16[2,608,768]{2,1,0:T(8,128)(2,1)S(1)}, bf16[2,608,768]{2,1,0:T(8,128)(2,1)S(1)}, u32[]{:S(2)}, u32[]{:S(2)}) collective-permute-start(bf16[2,608,768]{2,1,0:T(8,128)(2,1)S(1)} %pad_maximum_fusion.5), channel_id=1, source_target_pairs={{0,1},{1,0},{2,3},{3,2},{4,5},{5,4},{6,7},{7,6},{8,9},{9,8},{10,11... | collective-permute-start | bytes 5603336 | tf_op jit(solution)/shard_map/ppermute | solution.py:228
  424.8 3.8 copy-start.67
  424.8 11.6 %slice-start.2 = ((s8[4718592]{0:T(1024)(128)(4,1)}), s8[4194304]{0:T(1024)(128)(4,1)S(1)}, s32[]{:S(2)}) async-start(s8[4718592]{0:T(1024)(128)(4,1)} %bitcast.139), calls=%async_computation.2 | async-start | bytes 8388608
  428.5 6.1 copy-start.18
  428.5 6.1 copy-start.19
  428.5 7.8 slice-start.3
  439.8 3.6 copy-start.37
  782.0 7.5 copy-start.9
  789.6 3.8 copy-start.11
  (34 other events, 78.0 us)

commit v3 on v2

--- a/solution.py
+++ b/solution.py
@@ -30,197 +30,6 @@
 
 def contract_cols(left, right):
     return lax.dot_general(left, right, (((1,), (1,)), ((), ())), preferred_element_type=F32)
-
-
-def lane_ids(shape):
-    return lax.broadcasted_iota(jnp.int32, shape, len(shape) - 1)
-
-
-def three_parts(value):
-    high = value.astype(BF16).astype(F32)
-    rest = value - high
-    middle = rest.astype(BF16).astype(F32)
-    return high, middle, rest - middle
-
-
-def extend_keys(keys_out, values_out, blocks, bias_ref, head):
-    aux = HEAD_DIM * (1 - head)
-    row = 0
-    for key_ref, value_ref in blocks:
-        rows = key_ref.shape[0]
-        span = slice(row, row + rows)
-        lanes = lane_ids((rows, PAIR))
-        inside = (lanes // HEAD_DIM) == head
-        ones = jnp.where((lanes > aux) & (lanes <= aux + 3), 1.0, 0.0)
-        extra = jnp.where(lanes == aux, bias_ref[span, :], ones)
-        keys_out[span, :] = jnp.where(inside, key_ref[...].astype(F32), extra).astype(BF16)
-        ones = jnp.where((lanes >= aux) & (lanes < aux + 3), 1.0, 0.0)
-        values_out[span, :] = jnp.where(inside, value_ref[...].astype(F32), ones).astype(BF16)
-        row += rows
-
-
-def attention_forward_body(
-    chunk, query_ref, key_own, value_own, key_far, value_far, bias_ref,
-    out_ref, extended_ref, keys, values,
-):
-    rows = query_ref.shape[0]
-    for head in (0, 1):
-        extend_keys(
-            keys.at[head], values.at[head], ((key_own, value_own), (key_far, value_far)), bias_ref, head
-        )
-    lanes = lane_ids((chunk, PAIR))
-    for start in range(0, rows, chunk):
-        span = slice(start, start + chunk)
-        outs = []
-        for head in (0, 1):
-            aux = HEAD_DIM * (1 - head)
-            inside = (lanes // HEAD_DIM) == head
-            query = query_ref[span, :].astype(F32)
-            extended = jnp.where(inside, query, jnp.where(lanes == aux, 1.0, 0.0))
-            scores = contract_cols(extended.astype(BF16), keys[head])
-            top = jnp.max(scores, axis=1, keepdims=True)
-            powered = jnp.exp(scores - top).astype(BF16)
-            summed = mm(powered, values[head])
-            total = summed[:, aux : aux + 1]
-            outs.append(summed / total)
-            high, middle, low = three_parts(-(top + jnp.log(total)))
-            extended = jnp.where(lanes == aux + 1, high, extended)
-            extended = jnp.where(lanes == aux + 2, middle, extended)
-            extended = jnp.where(lanes == aux + 3, low, extended)
-            extended_ref[head, span, :] = extended.astype(BF16)
-        out_ref[span, :] = jnp.where(lanes < HEAD_DIM, outs[0], outs[1])
-
-
-def attention_forward(qkv, kv_far, key_bias):
-    rows, width = qkv.shape[0], qkv.shape[1] // 3
-    pairs = width // PAIR
-
-    def block(base):
-        return pl.BlockSpec((rows, PAIR), lambda p: (0, base + p))
-
-    return pl.pallas_call(
-        functools.partial(attention_forward_body, rows // 2),
-        grid=(pairs,),
-        in_specs=[
-            block(0), block(pairs), block(2 * pairs), block(0), block(pairs),
-            pl.BlockSpec((2 * rows, 1), lambda p: (0, 0)),
-        ],
-        out_specs=[block(0), pl.BlockSpec((2, rows, PAIR), lambda p: (p, 0, 0))],
-        out_shape=[
-            jax.ShapeDtypeStruct((rows, width), F32),
-            jax.ShapeDtypeStruct((2 * pairs, rows, PAIR), BF16),
-        ],
-        scratch_shapes=[pltpu.VMEM((2, 2 * rows, PAIR), BF16)] * 2,
-        compiler_params=pltpu.CompilerParams(vmem_limit_bytes=KERNEL_VMEM),
-        cost_estimate=pl.CostEstimate(
-            flops=16 * rows * rows * 2 * width * 2, bytes_accessed=12 * rows * width,
-            transcendentals=2 * rows * rows * 2 * pairs,
-        ),
-        name="attention_forward",
-    )(qkv, qkv, qkv, kv_far, kv_far, key_bias)
-
-
-def attention_backward_body(
-    chunks, extended_ref, key_own, value_own, key_far, value_far, bias_ref, grad_ref, out_ref,
-    grad_query, grad_key_own, grad_value_own, grad_key_far, grad_value_far,
-    keys, values, key_sums, value_sums,
-):
-    rows = extended_ref.shape[1]
-    for head in (0, 1):
-        extend_keys(
-            keys.at[head], values.at[head], ((key_own, value_own), (key_far, value_far)), bias_ref, head
-        )
-    for start, size in chunks:
-        span = slice(start, start + size)
-        lanes = lane_ids((size, PAIR))
-        parts = []
-        for head in (0, 1):
-            aux = HEAD_DIM * (1 - head)
-            inside = (lanes // HEAD_DIM) == head
-            query = extended_ref[head, span, :]
-            grad = jnp.where(inside, grad_ref[span, :].astype(F32), 0.0)
-            dots = jnp.sum(grad * out_ref[span, :], axis=1, keepdims=True)
-            high, middle, low = three_parts(-dots)
-            grad = jnp.where(lanes == aux, high, grad)
-            grad = jnp.where(lanes == aux + 1, middle, grad)
-            grad = jnp.where(lanes == aux + 2, low, grad)
-            probs = jnp.exp(contract_cols(query, keys[head]))
-            shifted = contract_cols(grad.astype(BF16), values[head])
-            grad_scores = (probs * shifted).astype(BF16)
-            parts.append(mm(grad_scores, keys[head]) * HEAD_DIM**-0.5)
-            to_values = mm(grad.T.astype(BF16), probs.astype(BF16)).T
-            to_keys = mm(query.astype(F32).T.astype(BF16), grad_scores).T
-            if start == 0:
-                key_sums[head] = to_keys
-                value_sums[head] = to_values
-            else:
-                key_sums[head] += to_keys
-                value_sums[head] += to_values
-        grad_query[span, :] = jnp.where(lanes < HEAD_DIM, parts[0], parts[1]).astype(BF16)
-    lanes = lane_ids((rows, PAIR))
-    for part, (to_key, to_value) in enumerate(
-        ((grad_key_own, grad_value_own), (grad_key_far, grad_value_far))
-    ):
-        span = slice(part * rows, (part + 1) * rows)
-        first = lanes < HEAD_DIM
-        to_key[...] = jnp.where(first, key_sums[0, span, :], key_sums[1, span, :]).astype(BF16)
-        to_value[...] = jnp.where(first, value_sums[0, span, :], value_sums[1, span, :]).astype(BF16)
-
-
-def attention_backward(extended, qkv, kv_far, key_bias, grad, out):
-    rows, width = out.shape
-    pairs = width // PAIR
-
-    def block(base):
-        return pl.BlockSpec((rows, PAIR), lambda p: (0, base + p))
-
-    shape = jax.ShapeDtypeStruct((rows, width), BF16)
-    return pl.pallas_call(
-        functools.partial(attention_backward_body, ((0, rows),)),
-        grid=(pairs,),
-        in_specs=[
-            pl.BlockSpec((2, rows, PAIR), lambda p: (p, 0, 0)),
-            block(pairs), block(2 * pairs), block(0), block(pairs),
-            pl.BlockSpec((2 * rows, 1), lambda p: (0, 0)),
-            block(0), block(0),
-        ],
-        out_specs=[block(0)] * 5,
-        out_shape=[shape] * 5,
-        scratch_shapes=[pltpu.VMEM((2, 2 * rows, PAIR), BF16)] * 2
-        + [pltpu.VMEM((2, 2 * rows, PAIR), F32)] * 2,
-        compiler_params=pltpu.CompilerParams(vmem_limit_bytes=KERNEL_VMEM),
-        cost_estimate=pl.CostEstimate(
-            flops=40 * rows * rows * 2 * width * 2, bytes_accessed=24 * rows * width,
-            transcendentals=2 * rows * rows * 2 * pairs,
-        ),
-        name="attention_backward",
-    )(extended, qkv, qkv, kv_far, kv_far, key_bias, grad, out)
-
-
-def norm_parts(hidden):
-    average = jnp.mean(hidden, axis=-1, keepdims=True)
-    centred = hidden - average
-    inverse = lax.rsqrt(jnp.mean(centred * centred, axis=-1, keepdims=True) + EPS)
-    return centred * inverse, inverse
-
-
-def norm_backward(hidden, grad_normed, gain):
-    unit, inverse = norm_parts(hidden)
-    scaled = grad_normed * gain
-    first = jnp.mean(scaled, axis=-1, keepdims=True)
-    second = jnp.mean(scaled * unit, axis=-1, keepdims=True)
-    grad_hidden = inverse * (scaled - first - unit * second)
-    return grad_hidden, jnp.sum(grad_normed * unit, axis=0), jnp.sum(grad_normed, axis=0)
-
-
-def gelu_and_slope(pre):
-    size = jnp.abs(pre) * (0.5**0.5)
-    density = jnp.exp(-0.5 * pre * pre)
-    t = 1.0 / (1.0 + 0.3275911 * size)
-    series = t * (0.254829592 + t * (-0.284496736 + t * (1.421413741 + t * (-1.453152027 + t * 1.061405429))))
-    tail = 0.5 * series * density
-    below = jnp.where(pre < 0, tail, 1.0 - tail)
-    return pre * below, below + pre * density * (1.0 / math.sqrt(2.0 * math.pi))
 
 
 def swap(block, bit):
@@ -249,6 +58,11 @@
 
     def flipped(self, bit):
         return {"dp": self.d + bit * (1 - 2 * ((self.d // bit) % 2))}
+
+    def greet_mate(self):
+        barrier = pltpu.get_barrier_semaphore()
+        pl.semaphore_signal(barrier, inc=1, device_id=self.mate, device_id_type=pl.DeviceIdType.MESH)
+        pl.semaphore_wait(barrier, 1)
 
     def greet(self):
         barrier = pltpu.get_barrier_semaphore()
@@ -609,7 +423,8 @@
     sections = lax.axis_size("section")
     take = lambda n: tuple(refs_list.pop(0) for _ in range(n))
     refs_list = list(refs)
-    acts, grads, fronts, backs, (small,) = take(sections), take(sections), take(sections), take(sections), take(1)
+    acts, grads, fronts, downs, (small,) = take(sections), take(sections), take(sections), take(sections // 2), take(1)
+    backs = [downs[s // 2].at[pl.ds(16 * (s % 2), 16)] for s in range(sections)]
     acts_out, grads_out, front_out, back_out, small_out = take(5)
     zeros, sums, arriving = take(3)
     front_bufs = [take(7) for _ in range(sections)]
@@ -695,21 +510,20 @@
         scatter.finish()
 
 
-def collect(acts, grads, fronts, backs, small, padded):
+def collect(acts, grads, fronts, downs, small, padded):
     sections = lax.axis_size("section")
     rows, width = acts[0].shape
-    blocked = lambda a: a.reshape(16, a.shape[0] // 16, a.shape[1])
-    fronts, backs = [blocked(a) for a in fronts], [blocked(a) for a in backs]
+    back_shape = (16,) + downs[0].shape[1:]
     hbm, vmem = pl.BlockSpec(memory_space=pl.ANY), pl.BlockSpec(memory_space=pltpu.VMEM)
     steps = 3 + (sections - 1).bit_length()
     sems = pltpu.SemaphoreType.DMA
     out = pl.pallas_call(
         functools.partial(collect_body, rows, small.shape[0]),
-        in_specs=[hbm] * (4 * sections) + [vmem],
+        in_specs=[hbm] * (3 * sections + sections // 2) + [vmem],
         out_specs=[hbm] * 4 + [vmem],
         out_shape=[
             jax.ShapeDtypeStruct((2, padded, width), BF16), jax.ShapeDtypeStruct((2, 2 * rows, width), BF16),
-            jax.ShapeDtypeStruct(fronts[0].shape, BF16), jax.ShapeDtypeStruct(backs[0].shape, BF16),
+            jax.ShapeDtypeStruct(fronts[0].shape, BF16), jax.ShapeDtypeStruct(back_shape, BF16),
             jax.ShapeDtypeStruct(small.shape, F32),
         ],
         scratch_shapes=[
@@ -717,7 +531,7 @@
             pltpu.VMEM((steps + 1,) + small.shape, F32), pltpu.VMEM((steps,) + small.shape, F32),
         ]
         + ScatterSum.scratch(*fronts[0].shape[1:]) * sections
-        + ScatterSum.scratch(*backs[0].shape[1:]) * sections
+        + ScatterSum.scratch(*back_shape[1:]) * sections
         + [
             sems((2 * sections, 9)), sems((2 * sections, 9)), sems((2 * sections, 2)), sems((2 * sections, 4)),
             sems((2, 9)), sems((2, 9)), sems((steps,)), sems((steps,)), sems((4,)),
@@ -726,8 +540,467 @@
             collective_id=1, has_side_effects=True, vmem_limit_bytes=62 * 2**20
         ),
         name="collect",
-    )(*acts, *grads, *fronts, *backs, small)
-    return out[0], out[1], out[2].reshape(-1, fronts[0].shape[2]), out[3].reshape(-1, backs[0].shape[2]), out[4]
+    )(*acts, *grads, *fronts, *downs, small)
+    return out[0], out[1], out[2].reshape(-1, fronts[0].shape[2]), out[3].reshape(-1, back_shape[2]), out[4]
+
+
+def norm_rows(hidden):
+    average = jnp.mean(hidden, axis=-1, keepdims=True)
+    centred = hidden - average
+    inverse = lax.rsqrt(jnp.mean(centred * centred, axis=-1, keepdims=True) + EPS)
+    return centred * inverse, inverse
+
+
+def norm_backward(hidden, grad_normed, gain):
+    unit, inverse = norm_rows(hidden)
+    scaled = grad_normed * gain
+    first = jnp.mean(scaled, axis=-1, keepdims=True)
+    second = jnp.mean(scaled * unit, axis=-1, keepdims=True)
+    return (
+        inverse * (scaled - first - unit * second),
+        jnp.sum(grad_normed * unit, axis=0, keepdims=True),
+        jnp.sum(grad_normed, axis=0, keepdims=True),
+    )
+
+
+def gelu_and_slope(pre):
+    density = jnp.exp(-0.5 * pre * pre)
+    t = 1.0 / (1.0 + (0.3275911 * 0.5**0.5) * jnp.abs(pre))
+    series = t * (0.127414796 + t * (-0.142248368 + t * (0.7107068705 + t * (-0.7265760135 + t * 0.5307027145))))
+    tail = series * density
+    below = jnp.where(pre < 0, tail, 1.0 - tail)
+    return pre * below, below + pre * density * (1.0 / math.sqrt(2.0 * math.pi))
+
+
+def pairs_of(block):
+    return [block[:, p * PAIR : (p + 1) * PAIR] for p in range(block.shape[1] // PAIR)]
+
+
+def joined(ref, lead=()):
+    return jnp.concatenate([ref[lead + (p,)] for p in range(ref.shape[len(lead)])], axis=1)
+
+
+def whole(shape):
+    return pl.BlockSpec(shape, lambda i: (0,) * len(shape))
+
+
+def swap_with_mate(spot, src, dst, send, recv):
+    return remote(src, dst, send, recv, spot.mate)
+
+
+def ff_forward_body(
+    hidden_ref, mask_ref, gain_ref, shift_ref, up_ref, bias_up_ref, down_ref, bias_down_ref,
+    act_ref, slope_ref, normed_out, out_ref, normed, total,
+):
+    step, last = pl.program_id(0), pl.num_programs(0) - 1
+
+    @pl.when(step == 0)
+    def _():
+        unit, _ = norm_rows(hidden_ref[...].astype(F32))
+        normed[...] = (unit * gain_ref[...] + shift_ref[...]).astype(BF16)
+        normed_out[...] = normed[...]
+
+    rows = normed.shape[0]
+    for span in (slice(0, rows // 2), slice(rows // 2, rows)):
+        pre = mm(normed[span, :], up_ref[...]) + bias_up_ref[...]
+        act, slope = gelu_and_slope(pre)
+        act_ref[span, :] = act.astype(BF16)
+        slope_ref[span, :] = slope.astype(BF16)
+        part = mm(act.astype(BF16), down_ref[...])
+        total[span, :] = jnp.where(step == 0, part, total[span, :] + part)
+
+    @pl.when(step == last)
+    def _():
+        hidden = hidden_ref[...].astype(F32)
+        out_ref[...] = (mask_ref[...] * (hidden + total[...] + bias_down_ref[...])).astype(BF16)
+
+
+def ff_forward(hidden, mask, gain, shift, up, bias_up, down, bias_down):
+    rows, width = hidden.shape
+    units = up.shape[1]
+    size = width
+    columns = pl.BlockSpec((rows, size), lambda i: (0, i))
+    return pl.pallas_call(
+        ff_forward_body,
+        grid=(units // size,),
+        in_specs=[
+            whole((rows, width)), whole((rows, 1)), whole((1, width)), whole((1, width)),
+            pl.BlockSpec((width, size), lambda i: (0, i)), pl.BlockSpec((1, size), lambda i: (0, i)),
+            pl.BlockSpec((size, width), lambda i: (i, 0)), whole((1, width)),
+        ],
+        out_specs=[columns, columns, whole((rows, width)), whole((rows, width))],
+        out_shape=[
+            jax.ShapeDtypeStruct((rows, units), BF16), jax.ShapeDtypeStruct((rows, units), BF16),
+            jax.ShapeDtypeStruct((rows, width), BF16), jax.ShapeDtypeStruct((rows, width), BF16),
+        ],
+        scratch_shapes=[pltpu.VMEM((rows, width), BF16), pltpu.VMEM((rows, width), F32)],
+        compiler_params=pltpu.CompilerParams(vmem_limit_bytes=KERNEL_VMEM),
+        name="ff_forward",
+    )(hidden, mask, gain, shift, up, bias_up, down, bias_down)
+
+
+def ff_backward_body(
+    incoming_ref, mask_ref, hidden_ref, normed_ref, act_ref, slope_ref, up_ref, down_ref, gain_ref,
+    up_grad, down_grad, out_ref, gain_grad, shift_grad, up_bias_grad, down_bias_grad,
+    grad, normed_t, total,
+):
+    step, last = pl.program_id(0), pl.num_programs(0) - 1
+
+    @pl.when(step == 0)
+    def _():
+        grad_rows = mask_ref[...] * incoming_ref[...].astype(F32)
+        grad[...] = grad_rows.astype(BF16)
+        down_bias_grad[...] = jnp.sum(grad_rows, axis=0, keepdims=True)
+        normed_t[...] = normed_ref[...].astype(F32).T.astype(BF16)
+
+    grad_pre = (contract_cols(grad[...], down_ref[...]) * slope_ref[...].astype(F32)).astype(BF16)
+    down_grad[...] = contract_rows(act_ref[...], grad[...]).astype(BF16).reshape(down_grad.shape)
+    up_bias_grad[...] = jnp.sum(grad_pre.astype(F32), axis=0, keepdims=True)
+    up_grad[...] = mm(normed_t[...], grad_pre).astype(BF16).reshape(up_grad.shape)
+    part = contract_cols(grad_pre, up_ref[...])
+    total[...] = jnp.where(step == 0, part, total[...] + part)
+
+    @pl.when(step == last)
+    def _():
+        grad_hidden, gain_grad[...], shift_grad[...] = norm_backward(
+            hidden_ref[...].astype(F32), total[...], gain_ref[...]
+        )
+        out_ref[...] = (grad[...].astype(F32) + grad_hidden).astype(BF16)
+
+
+def ff_backward(incoming, mask, hidden, normed, act, slope, up, down, gain):
+    rows, width = hidden.shape
+    units, size = up.shape[1], width
+    columns = pl.BlockSpec((rows, size), lambda i: (0, i))
+    vector = jax.ShapeDtypeStruct((1, width), F32)
+    return pl.pallas_call(
+        ff_backward_body,
+        grid=(units // size,),
+        in_specs=[
+            whole((rows, width)), whole((rows, 1)), whole((rows, width)), whole((rows, width)), columns, columns,
+            pl.BlockSpec((width, size), lambda i: (0, i)), pl.BlockSpec((size, width), lambda i: (i, 0)),
+            whole((1, width)),
+        ],
+        out_specs=[
+            pl.BlockSpec((16, width // 16, size), lambda i: (0, 0, i)),
+            pl.BlockSpec((size * 32 // units, units // 32, width), lambda i: (i, 0, 0)),
+            whole((rows, width)), whole((1, width)), whole((1, width)),
+            pl.BlockSpec((1, size), lambda i: (0, i)), whole((1, width)),
+        ],
+        out_shape=[
+            jax.ShapeDtypeStruct((16, width // 16, units), BF16), jax.ShapeDtypeStruct((32, units // 32, width), BF16),
+            jax.ShapeDtypeStruct((rows, width), BF16), vector, vector,
+            jax.ShapeDtypeStruct((1, units), F32), vector,
+        ],
+        scratch_shapes=[
+            pltpu.VMEM((rows, width), BF16), pltpu.VMEM((width, rows), BF16), pltpu.VMEM((rows, width), F32),
+        ],
+        compiler_params=pltpu.CompilerParams(vmem_limit_bytes=KERNEL_VMEM),
+        name="ff_backward",
+    )(incoming, mask, hidden, normed, act, slope, up, down, gain)
+
+
+def lane_ids(shape):
+    return lax.broadcasted_iota(jnp.int32, shape, len(shape) - 1)
+
+
+def three_parts(value):
+    high = value.astype(BF16).astype(F32)
+    rest = value - high
+    middle = rest.astype(BF16).astype(F32)
+    return high, middle, rest - middle
+
+
+def extend_keys(keys_out, values_out, blocks, bias_ref, head):
+    aux = HEAD_DIM * (1 - head)
+    row = 0
+    for key, value in blocks:
+        rows = key.shape[0]
+        span = slice(row, row + rows)
+        lanes = lane_ids((rows, PAIR))
+        inside = (lanes // HEAD_DIM) == head
+        ones = jnp.where((lanes > aux) & (lanes <= aux + 3), 1.0, 0.0)
+        extra = jnp.where(lanes == aux, bias_ref[span, :], ones)
+        keys_out[span, :] = jnp.where(inside, key.astype(F32), extra).astype(BF16)
+        ones = jnp.where((lanes >= aux) & (lanes < aux + 3), 1.0, 0.0)
+        values_out[span, :] = jnp.where(inside, value.astype(F32), ones).astype(BF16)
+        row += rows
+
+
+def pair_forward(query_of, keys, values, rows, chunk, save):
+    lanes = lane_ids((chunk, PAIR))
+    units = [(start, head) for start in range(0, rows, chunk) for head in (0, 1)]
+
+    def extended(start, head):
+        aux = HEAD_DIM * (1 - head)
+        inside = (lanes // HEAD_DIM) == head
+        query = query_of(slice(start, start + chunk)).astype(F32)
+        return jnp.where(inside, query, jnp.where(lanes == aux, 1.0, 0.0))
+
+    def scores(start, head):
+        return contract_cols(extended(start, head).astype(BF16), keys[head])
+
+    ahead = [scores(*unit) for unit in units[:2]]
+    for index, (start, head) in enumerate(units):
+        now = ahead.pop(0)
+        if index + 2 < len(units):
+            ahead.append(scores(*units[index + 2]))
+        aux = HEAD_DIM * (1 - head)
+        top = jnp.max(now, axis=1, keepdims=True)
+        summed = mm(jnp.exp(now - top).astype(BF16), values[head])
+        total = summed[:, aux : aux + 1]
+        query = extended(start, head)
+        for lane, part in enumerate(three_parts(-(top + jnp.log(total))), aux + 1):
+            query = jnp.where(lanes == lane, part, query)
+        save(head, slice(start, start + chunk), query.astype(BF16), summed / total)
+
+
+def attention_forward_body(
+    hidden_ref, mask_ref, gain_ref, shift_ref, weight_ref, bias_ref, key_bias_ref, out_bias_ref,
+    normed_out, key_out, value_out, key_far_out, value_far_out, extended_out, attended_out, out_ref,
+    normed, own, far, attended, keys, values, send, recv,
+):
+    step, last = pl.program_id(0), pl.num_programs(0) - 1
+    rows, width = normed.shape
+    pairs = width // PAIR
+    spot = Spot()
+
+    def swaps():
+        return [swap_with_mate(spot, own.at[j], far.at[j], send.at[j], recv.at[j]) for j in (0, 1)]
+
+    @pl.when(step == 0)
+    def _():
+        spot.greet_mate()
+        unit, _ = norm_rows(hidden_ref[...].astype(F32))
+        normed[...] = (unit * gain_ref[...] + shift_ref[...]).astype(BF16)
+        normed_out[...] = normed[...]
+
+    for j, scale in ((0, 1.0), (1, 1.0), (2, HEAD_DIM**-0.5)):
+        @pl.when(step == j)
+        def _(j=j, scale=scale):
+            block = (mm(normed[...], weight_ref[...]) + bias_ref[...]).astype(BF16)
+            if scale != 1.0:
+                block = (block.astype(F32) * scale).astype(BF16)
+            for p, part in enumerate(pairs_of(block)):
+                own[j, p] = part
+            if j < 2:
+                swaps()[j].start()
+            else:
+                for copy in swaps():
+                    copy.wait()
+
+    @pl.when((step >= 3) & (step < 3 + pairs))
+    def _():
+        p = step - 3
+        for head in (0, 1):
+            extend_keys(
+                keys.at[head], values.at[head], [(own[0, p], own[1, p]), (far[0, p], far[1, p])],
+                key_bias_ref, head,
+            )
+        for j, out in enumerate((key_out, value_out)):
+            out[0] = own[j, p]
+        for j, out in enumerate((key_far_out, value_far_out)):
+            out[0] = far[j, p]
+        lanes = lane_ids((rows // 2, PAIR))
+        firsts = {}
+
+        def save(head, span, query, out):
+            extended_out[head, span, :] = query
+            if head == 0:
+                firsts[span.start] = out
+            else:
+                both = jnp.where(lanes < HEAD_DIM, firsts[span.start], out)
+                attended_out[0, span, :] = both
+                attended[p, span, :] = both.astype(BF16)
+
+        pair_forward(lambda span: own[2, p, span, :], keys, values, rows, rows // 2, save)
+
+    @pl.when(step == last)
+    def _():
+        branch = contract_cols(joined(attended), weight_ref[...]) + out_bias_ref[...]
+        out_ref[...] = (mask_ref[...] * (hidden_ref[...].astype(F32) + branch)).astype(BF16)
+
+
+def attention_forward(hidden, mask, gain, shift, weight, bias, key_bias, out_bias, collective_id):
+    rows, width = hidden.shape
+    pairs = width // PAIR
+    pair = lambda i: jnp.clip(i - 3, 0, pairs - 1)
+    part = lambda i: jnp.where(i < 3, (i + 1) % 3, 3)
+    block = pl.BlockSpec((1, rows, PAIR), lambda i: (pair(i), 0, 0))
+    saved = jax.ShapeDtypeStruct((pairs, rows, PAIR), BF16)
+    full = jax.ShapeDtypeStruct((rows, width), BF16)
+    return pl.pallas_call(
+        attention_forward_body,
+        grid=(pairs + 4,),
+        in_specs=[
+            whole((rows, width)), whole((rows, 1)), whole((1, width)), whole((1, width)),
+            pl.BlockSpec((width, width), lambda i: (0, part(i))),
+            pl.BlockSpec((1, width), lambda i: (0, jnp.minimum(part(i), 2))),
+            whole((2 * rows, 1)), whole((1, width)),
+        ],
+        out_specs=[whole((rows, width))] + [block] * 4
+        + [pl.BlockSpec((2, rows, PAIR), lambda i: (pair(i), 0, 0)), block, whole((rows, width))],
+        out_shape=[full] + [saved] * 4 + [
+            jax.ShapeDtypeStruct((2 * pairs, rows, PAIR), BF16),
+            jax.ShapeDtypeStruct((pairs, rows, PAIR), F32), full,
+        ],
+        scratch_shapes=[
+            pltpu.VMEM((rows, width), BF16), pltpu.VMEM((3, pairs, rows, PAIR), BF16),
+            pltpu.VMEM((2, pairs, rows, PAIR), BF16), pltpu.VMEM((pairs, rows, PAIR), BF16),
+            pltpu.VMEM((2, 2 * rows, PAIR), BF16), pltpu.VMEM((2, 2 * rows, PAIR), BF16),
+            pltpu.SemaphoreType.DMA((2,)), pltpu.SemaphoreType.DMA((2,)),
+        ],
+        compiler_params=pltpu.CompilerParams(
+            vmem_limit_bytes=KERNEL_VMEM, collective_id=collective_id, has_side_effects=True
+        ),
+        name="attention_forward",
+    )(hidden, mask, gain, shift, weight, bias, key_bias, out_bias)
+
+
+def pair_backward(query_of, grad_of, out_of, keys, values, key_sums, value_sums, rows, save):
+    lanes = lane_ids((rows, PAIR))
+    parts = []
+    for head in (0, 1):
+        aux = HEAD_DIM * (1 - head)
+        inside = (lanes // HEAD_DIM) == head
+        query = query_of(head)
+        grad = jnp.where(inside, grad_of().astype(F32), 0.0)
+        dots = jnp.sum(grad * out_of(), axis=1, keepdims=True)
+        for lane, part in enumerate(three_parts(-dots), aux):
+            grad = jnp.where(lanes == lane, part, grad)
+        probs = jnp.exp(contract_cols(query, keys[head]))
+        shifted = contract_cols(grad.astype(BF16), values[head])
+        grad_scores = (probs * shifted).astype(BF16)
+        parts.append(mm(grad_scores, keys[head]) * HEAD_DIM**-0.5)
+        value_sums[head] = mm(grad.T.astype(BF16), probs.astype(BF16)).T
+        key_sums[head] = mm(query.astype(F32).T.astype(BF16), grad_scores).T
+    save(jnp.where(lanes < HEAD_DIM, parts[0], parts[1]).astype(BF16))
+
+
+def attention_backward_body(
+    incoming_ref, mask_ref, hidden_ref, normed_ref, key_ref, value_ref, key_far_ref, value_far_ref,
+    extended_ref, attended_ref, weight_ref, gain_ref, key_bias_ref,
+    weight_grad, out_ref, gain_grad, shift_grad, query_bias_grad, value_bias_grad, out_bias_grad,
+    grad, grad_out, attended, normed_t, total, grads, sent, arrived, keys, values, key_sums, value_sums,
+    send, recv,
+):
+    step, last = pl.program_id(0), pl.num_programs(0) - 1
+    rows, width = grad.shape
+    pairs = width // PAIR
+    spot = Spot()
+
+    def swap_of(p):
+        return swap_with_mate(spot, sent.at[p], arrived.at[p], send.at[p], recv.at[p])
+
+    @pl.when(step == 0)
+    def _():
+        spot.greet_mate()
+        grad_rows = mask_ref[...] * incoming_ref[...].astype(F32)
+        grad[...] = grad_rows.astype(BF16)
+        out_bias_grad[...] = jnp.sum(grad_rows, axis=0, keepdims=True)
+        for p, part in enumerate(pairs_of(mm(grad[...], weight_ref[...]).astype(BF16))):
+            grad_out[p] = part
+
+    @pl.when(step < pairs)
+    def _():
+        p = step
+        for head in (0, 1):
+            extend_keys(
+                keys.at[head], values.at[head],
+                [(key_ref[0], value_ref[0]), (key_far_ref[0], value_far_ref[0])], key_bias_ref, head,
+            )
+        attended[p] = attended_ref[0].astype(BF16)
+
+        def save(value):
+            grads[0, p] = value
+
+        pair_backward(
+            lambda head: extended_ref[head], lambda: grad_out[p], lambda: attended_ref[0],
+            keys, values, key_sums, value_sums, rows, save,
+        )
+        first = lane_ids((rows, PAIR)) < HEAD_DIM
+        for j, sums in enumerate((key_sums, value_sums)):
+            grads[1 + j, p] = jnp.where(first, sums[0, :rows, :], sums[1, :rows, :]).astype(BF16)
+            sent[p, j] = jnp.where(first, sums[0, rows:, :], sums[1, rows:, :]).astype(BF16)
+        swap_of(p).start()
+
+    @pl.when(step == pairs)
+    def _():
+        normed_t[...] = normed_ref[...].astype(F32).T.astype(BF16)
+        for p in range(pairs):
+            swap_of(p).wait()
+            for j in (0, 1):
+                grads[1 + j, p] = (grads[1 + j, p].astype(F32) + arrived[p, j].astype(F32)).astype(BF16)
+
+    @pl.when((step >= pairs) & (step < last))
+    def _():
+        j = step - pairs
+        part = joined(grads, (j,))
+        sums = jnp.sum(part.astype(F32), axis=0, keepdims=True)
+
+        @pl.when(j == 0)
+        def _():
+            query_bias_grad[...] = sums
+
+        @pl.when(j == 2)
+        def _():
+            value_bias_grad[...] = sums
+
+        weight_grad[...] = mm(normed_t[...], part).astype(BF16).reshape(weight_grad.shape)
+        product = contract_cols(part, weight_ref[...])
+        total[...] = jnp.where(j == 0, product, total[...] + product)
+
+    @pl.when(step == last)
+    def _():
+        weight_grad[...] = contract_rows(grad[...], joined(attended)).astype(BF16).reshape(weight_grad.shape)
+        grad_hidden, gain_grad[...], shift_grad[...] = norm_backward(
+            hidden_ref[...].astype(F32), total[...], gain_ref[...]
+        )
+        out_ref[...] = (grad[...].astype(F32) + grad_hidden).astype(BF16)
+
+
+def attention_backward(
+    incoming, mask, hidden, normed, key, value, key_far, value_far, extended, attended, weight, gain, key_bias,
+    collective_id,
+):
+    rows, width = hidden.shape
+    pairs = width // PAIR
+    pair = lambda i: jnp.minimum(i, pairs - 1)
+    block = pl.BlockSpec((1, rows, PAIR), lambda i: (pair(i), 0, 0))
+    vector = jax.ShapeDtypeStruct((1, width), F32)
+    return pl.pallas_call(
+        attention_backward_body,
+        grid=(pairs + 4,),
+        in_specs=[whole((rows, width)), whole((rows, 1)), whole((rows, width)), whole((rows, width))]
+        + [block] * 4
+        + [
+            pl.BlockSpec((2, rows, PAIR), lambda i: (pair(i), 0, 0)), block,
+            pl.BlockSpec((width, width), lambda i: (0, jnp.where(i < pairs, 3, jnp.minimum(i - pairs, 2)))),
+            whole((1, width)), whole((2 * rows, 1)),
+        ],
+        out_specs=[
+            pl.BlockSpec((16, width // 16, width), lambda i: (0, 0, jnp.maximum(i - pairs, 0))),
+            whole((rows, width)),
+        ] + [whole((1, width))] * 5,
+        out_shape=[
+            jax.ShapeDtypeStruct((16, width // 16, 4 * width), BF16), jax.ShapeDtypeStruct((rows, width), BF16),
+        ] + [vector] * 5,
+        scratch_shapes=[
+            pltpu.VMEM((rows, width), BF16), pltpu.VMEM((pairs, rows, PAIR), BF16),
+            pltpu.VMEM((pairs, rows, PAIR), BF16), pltpu.VMEM((width, rows), BF16),
+            pltpu.VMEM((rows, width), F32), pltpu.VMEM((3, pairs, rows, PAIR), BF16),
+            pltpu.VMEM((pairs, 2, rows, PAIR), BF16), pltpu.VMEM((pairs, 2, rows, PAIR), BF16),
+            pltpu.VMEM((2, 2 * rows, PAIR), BF16), pltpu.VMEM((2, 2 * rows, PAIR), BF16),
+            pltpu.VMEM((2, 2 * rows, PAIR), F32), pltpu.VMEM((2, 2 * rows, PAIR), F32),
+            pltpu.SemaphoreType.DMA((pairs,)), pltpu.SemaphoreType.DMA((pairs,)),
+        ],
+        compiler_params=pltpu.CompilerParams(
+            vmem_limit_bytes=KERNEL_VMEM, collective_id=collective_id, has_side_effects=True
+        ),
+        name="attention_backward",
+    )(
+        incoming, mask, hidden, normed, key, value, key_far, value_far, extended, attended, weight, gain, key_bias
+    )
 
 
 def per_device(
@@ -760,76 +1033,54 @@
     gains, shifts = norm_all[:, 0], norm_all[:, 1]
 
     hidden = (clip_pair[0].astype(F32) * row_mask).astype(BF16)
+    row = lambda a: a.reshape(1, -1)
     saved, delivered = [], []
     for s in range(sections):
         layer = s // 2
-        entering = hidden.astype(F32)
-        unit, _ = norm_parts(entering)
-        normed = (unit * gains[s] + shifts[s]).astype(BF16)
+        gain, shift = row(gains[s]), row(shifts[s])
         if s % 2 == 0:
             pair = bias_query_value[layer]
             bias = jnp.concatenate([pair[:width], jnp.zeros((width,), F32), pair[width:]])
-            scale = jnp.where(jnp.arange(3 * width) < width, HEAD_DIM**-0.5, 1.0)
-            qkv = ((mm(normed, fronts[s][:, : 3 * width]) + bias).astype(BF16) * scale).astype(BF16)
-            kv_far = swap(qkv[:, width:], 1)
-            attended, extended = attention_forward(qkv, kv_far, key_bias)
-            attended_b = attended.astype(BF16)
-            branch = contract_cols(attended_b, fronts[s][:, 3 * width :]) + bias_attn_out[layer]
-            saved.append((hidden, normed, qkv, kv_far, attended, attended_b, extended))
+            *kept, leaving = attention_forward(
+                hidden, row_mask, gain, shift, fronts[s], row(bias), key_bias, row(bias_attn_out[layer]), 2 + s
+            )
         else:
-            pre = mm(normed, fronts[s]) + bias_up[layer]
-            act, slope = gelu_and_slope(pre)
-            act, slope = act.astype(BF16), slope.astype(BF16)
-            branch = mm(act, downs[layer]) + bias_down[layer]
-            saved.append((hidden, normed, act, slope))
-        hidden = (row_mask * (entering + branch)).astype(BF16)
-        delivered.append(hidden)
+            *kept, leaving = ff_forward(
+                hidden, row_mask, gain, shift, fronts[s], row(bias_up[layer]), downs[layer], row(bias_down[layer])
+            )
+        saved.append((hidden, *kept))
+        hidden = leaving
+        delivered.append(leaving)
 
     incoming = clip_pair[1]
-    sent_grads = [None] * sections
-    grad_fronts, grad_backs = [None] * sections, [None] * sections
+    sent_grads, grad_fronts, grad_downs = [None] * sections, [None] * sections, [None] * 2
     grad_gain, grad_shift = [None] * sections, [None] * sections
-    grad_pairs, grad_outs, grad_ups, grad_downs = [], [], [], []
+    query_sums, value_sums, out_sums, up_sums, down_sums = ([None] * 2 for _ in range(5))
     for s in reversed(range(sections)):
-        grad_rows = row_mask * incoming.astype(F32)
-        grad_b = grad_rows.astype(BF16)
-        front = fronts[s]
+        layer, gain = s // 2, row(gains[s])
         if s % 2 == 0:
-            entered, normed, qkv, kv_far, attended, attended_b, extended = saved[s]
-            grad_attended = mm(grad_b, front[:, 3 * width :]).astype(BF16)
-            to_query, to_key, to_value, key_far, value_far = attention_backward(
-                extended, qkv, kv_far, key_bias, grad_attended, attended
+            entered, normed, key, value, key_far, value_far, extended, attended = saved[s]
+            (
+                grad_fronts[s], incoming, grad_gain[s], grad_shift[s],
+                query_sums[layer], value_sums[layer], out_sums[layer],
+            ) = attention_backward(
+                incoming, row_mask, entered, normed, key, value, key_far, value_far, extended, attended,
+                fronts[s], gain, key_bias, 3 + s,
             )
-            back = swap(jnp.stack([key_far, value_far]), 1)
-            grad_qkv = jnp.concatenate([to_query, add(to_key, back[0]), add(to_value, back[1])], axis=1)
-            sums = jnp.sum(grad_qkv.astype(F32), axis=0)
-            grad_pairs.insert(0, jnp.concatenate([sums[:width], sums[2 * width :]]))
-            grad_outs.insert(0, jnp.sum(grad_rows, axis=0))
-            grad_fronts[s] = jnp.concatenate(
-                [contract_rows(normed, grad_qkv).astype(BF16), contract_rows(grad_b, attended_b).astype(BF16)],
-                axis=1,
-            )
-            grad_normed = contract_cols(grad_qkv, front[:, : 3 * width])
         else:
-            entered, normed, act, slope = saved[s]
-            grad_act = contract_cols(grad_b, downs[s // 2])
-            grad_pre = (grad_act * slope.astype(F32)).astype(BF16)
-            grad_down = contract_rows(act, grad_b).astype(BF16)
-            grad_fronts[s] = contract_rows(normed, grad_pre).astype(BF16)
-            grad_ups.insert(0, jnp.sum(grad_pre.astype(F32), axis=0))
-            grad_downs.insert(0, jnp.sum(grad_rows, axis=0))
-            grad_normed = contract_cols(grad_pre, front)
-            half = grad_down.shape[0] // 2
-            grad_backs[s - 1], grad_backs[s] = grad_down[:half], grad_down[half:]
-        grad_hidden, grad_gain[s], grad_shift[s] = norm_backward(entered.astype(F32), grad_normed, gains[s])
-        incoming = (grad_rows + grad_hidden).astype(BF16)
+            entered, act, slope, normed = saved[s]
+            (
+                grad_fronts[s], grad_downs[layer], incoming, grad_gain[s], grad_shift[s],
+                up_sums[layer], down_sums[layer],
+            ) = ff_backward(incoming, row_mask, entered, normed, act, slope, fronts[s], downs[layer], gain)
         sent_grads[s] = incoming
 
+    pair_sums = [jnp.concatenate([q, v], axis=1) for q, v in zip(query_sums, value_sums)]
     small = jnp.concatenate(
-        [v.reshape(-1) for v in grad_gain + grad_shift + grad_pairs + grad_outs + grad_ups + grad_downs]
+        [v.reshape(-1) for v in grad_gain + grad_shift + pair_sums + out_sums + up_sums + down_sums]
     )
     acts_out, grads_out, front_out, back_out, small = collect(
-        delivered, sent_grads, grad_fronts, grad_backs, small.reshape(-1, 128), padded
+        delivered, sent_grads, grad_fronts, grad_downs, small.reshape(-1, 128), padded
     )
     small = small.reshape(-1)
     for bit in spot.spare_bits:

time: 810 us -> 774 us (0.956)
  Pallas kernels: 597 us -> 721 us
  matrix products: 122 us -> 0 us
  other arithmetic: 38.2 us -> 23.1 us
  local copies, waits for them, and re-layouts: 34.7 us -> 22 us
    pallas_call x4 -> x8, Pallas kernels: 95.2 us -> 219 us  [the longest x2 82.4 us: attention_backward(): pl.pallas_call(attention_backward_body, grid=(pairs + 4,), in_specs=[whol...]
    dot_general x24 -> x0, matrix products: 122 us -> none  [the longest x8 44.7 us: mm(): return jnp.dot(left, right, preferred_element_type=F32)]
    unnamed x202 -> x66, local copies, waits for them, and re-layouts: 15.1 us -> 6.35 us
  transfers between devices with their start and end apart: 6 -> 2, of which waited for: 2 -> 0; matrix products, arithmetic and copies ran while one was open for 5% -> 1% of each run, Pallas kernels for 21% -> 22%
where the time goes in v3:
time: 774 us; the launch traced here: 770 us
  Pallas kernels  721 us (93%)
  other arithmetic  23.1 us (3%)
  local copies, waits for them, and re-layouts  22 us (3%)
    pallas_call x1, Pallas kernels, collect(): pl.pallas_call(functools.partial(collect_body, rows, small.shape[0]), in_...  332 us
    pallas_call x1, Pallas kernels, gather_weights(): pl.pallas_call(gather_weights_body, in_specs=[hbm] * 3, out_specs=[hbm] *...  170 us
    pallas_call x2, Pallas kernels, attention_backward(): pl.pallas_call(attention_backward_body, grid=(pairs + 4,), in_specs=[whol...  82.4 us
    pallas_call x2, Pallas kernels, ff_backward(): pl.pallas_call(ff_backward_body, grid=(units // size,), in_specs=[whole((...  52.8 us
    pallas_call x2, Pallas kernels, attention_forward(): pl.pallas_call(attention_forward_body, grid=(pairs + 4,), in_specs=[whole...  51.7 us
    pallas_call x2, Pallas kernels, ff_forward(): pl.pallas_call(ff_forward_body, grid=(units // size,), in_specs=[whole((r...  32.4 us
  transfers between devices with their start and end apart: 2, of which 0 were waited for; matrix products, arithmetic and copies ran while one was open for 1% of the time, Pallas kernels for 22%

profile of v3, /device:TPU:0, one launch (start us, length us, event | category | flops | bytes accessed | tf_op | source)
XLA Modules:
  0.0 770.2 jit_solution(8659406802379111200)
XLA Ops:
  0.7 2.4 constant_dynamic-slice_fusion.2
  3.1 0.0 copy-start
  3.1 0.0 copy-start.22
  3.1 0.0 copy-start.20
  3.1 0.0 copy-start.21
  3.1 1.2 copy-done
  4.3 1.4 fusion
  5.7 0.5 collective-permute-start
  6.2 0.6 dynamic_slice.27
  7.5 0.1 collective-permute-start.1
  7.6 0.1 pad.20.clone
  7.7 0.7 maximum_maximum_fusion.norms
  8.4 170.4 %gather_weights.1 = (bf16[16,48,3072]{2,1,0:T(8,128)(2,1)}, bf16[16,48,3072]{2,1,0:T(8,128)(2,1)}, bf16[16,48,3072]{2,1,0:T(8,128)(2,1)}, bf16[16,48,3072]{2,1,0...) custom-call(bf16[16,48,3072]{2,1,0:T(8,128)(2,1)} %bitcast.63, ...), custom_call_target="tpu_custom_call" | custom-call | tf_op jit(solution)/shard_map/gather_weights/pallas_call | solution.py:250
  178.8 1.5 slice_bitcast_fusion.2
  180.3 0.6 fusion.12
  180.9 0.6 fusion.11
  181.6 0.6 fusion.10
  182.2 0.6 reshape.212.bias_ref
  182.8 0.6 reshape.216.bias_ref
  183.4 0.0 collective-permute-done.1
  183.5 0.5 slice.144
  184.6 0.1 pad_add_fusion
  184.7 0.3 copy.23
  185.0 0.8 fusion.4.mask_ref
  185.8 0.9 broadcast_select_fusion.key_bias_ref
  186.7 0.0 collective-permute-done
  186.7 1.6 fusion.2
  188.3 1.0 slice_bitcast_fusion.incoming_ref
  189.3 1.2 fusion.3.hidden_ref
  190.5 26.1 %attention_forward.2 = (bf16[608,768]{1,0:T(8,128)(2,1)}, bf16[6,608,128]{2,1,0:T(8,128)(2,1)}, bf16[6,608,128]{2,1,0:T(8,128)(2,1)}, bf16[6,608,128]{2,1,0:T(8,...) custom-call(bf16[608,768]{1,0:T(8,128)(2,1)} %fusion.3.hidden_ref, ...), custom_call_target="tpu_custom_call" | custom-call | tf_op jit(solution)/shard_map/attention_forward/pallas_call | solution.py:832
  216.6 16.2 %ff_forward.2 = (bf16[608,3072]{1,0:T(8,128)(2,1)}, bf16[608,3072]{1,0:T(8,128)(2,1)}, bf16[608,768]{1,0:T(8,128)(2,1)}, bf16[608,768]{1,0:T(8,128)(2,1)}) custom-call(bf16[608,768]{1,0:T(8,128)(2,1)} %get-tuple-element.76.hidden_ref.refs_0_, f32[608,1]{1,0:T(8,128)} %fusion.4.mask_ref, f32[1,768]{1,0:T(1,128)} %get-tuple-element.147.gain_ref, ...), custom_call_target="tpu_custom_call" | custom-call | tf_op jit(solution)/shard_map/ff_forward/pallas_call | solution.py:623
  232.8 25.6 %attention_forward.3 = (bf16[608,768]{1,0:T(8,128)(2,1)}, bf16[6,608,128]{2,1,0:T(8,128)(2,1)}, bf16[6,608,128]{2,1,0:T(8,128)(2,1)}, bf16[6,608,128]{2,1,0:T(8,...) custom-call(bf16[608,768]{1,0:T(8,128)(2,1)} %get-tuple-element.79.h, ...), custom_call_target="tpu_custom_call" | custom-call | tf_op jit(solution)/shard_map/attention_forward/pallas_call | solution.py:832
  258.4 16.2 %ff_forward.3 = (bf16[608,3072]{1,0:T(8,128)(2,1)}, bf16[608,3072]{1,0:T(8,128)(2,1)}, bf16[608,768]{1,0:T(8,128)(2,1)}, bf16[608,768]{1,0:T(8,128)(2,1)}) custom-call(bf16[608,768]{1,0:T(8,128)(2,1)} %get-tuple-element.81.hidden_ref.refs_2_, f32[608,1]{1,0:T(8,128)} %fusion.4.mask_ref, f32[1,768]{1,0:T(1,128)} %get-tuple-element.143.gain_ref, ...), custom_call_target="tpu_custom_call" | custom-call | tf_op jit(solution)/shard_map/ff_forward/pallas_call | solution.py:623
  274.7 31.3 %ff_backward.2 = (bf16[16,48,3072]{2,1,0:T(8,128)(2,1)}, bf16[32,96,768]{2,1,0:T(8,128)(2,1)}, bf16[608,768]{1,0:T(8,128)(2,1)}, f32[1,768]{1,0:T(1,128)}, f32[1...) custom-call(bf16[608,768]{1,0:T(8,128)(2,1)} %slice_bitcast_fusion.incoming_ref, f32[608,1]{1,0:T(8,128)} %fusion.4.mask_ref, ...), custom_call_target="tpu_custom_call" | custom-call | tf_op jit(solution)/shard_map/ff_backward/pallas_call | solution.py:676
  306.0 41.2 %attention_backward.2 = (bf16[16,48,3072]{2,1,0:T(8,128)(2,1)}, bf16[608,768]{1,0:T(8,128)(2,1)}, f32[1,768]{1,0:T(1,128)}, f32[1,768]{1,0:T(1,128)}, f32[1,768]...) custom-call(bf16[608,768]{1,0:T(8,128)(2,1)} %get-tuple-element.88.incoming_ref.refs_7_, f32[608,1]{1,0:T(8,128)} %fusion.4.mask_ref, ...), custom_call_target="tpu_custom_call" | custom-call | tf_op jit(solution)/shard_map/attention_backward/pallas_call | solution.py:971
  347.2 21.5 %ff_backward.3 = (bf16[16,48,3072]{2,1,0:T(8,128)(2,1)}, bf16[32,96,768]{2,1,0:T(8,128)(2,1)}, bf16[608,768]{1,0:T(8,128)(2,1)}, f32[1,768]{1,0:T(1,128)}, f32[1...) custom-call(bf16[608,768]{1,0:T(8,128)(2,1)} %get-tuple-element.96.incoming_ref.refs_6_, ...), custom_call_target="tpu_custom_call" | custom-call | tf_op jit(solution)/shard_map/ff_backward/pallas_call | solution.py:676
  368.8 0.0 copy-start.19
  368.8 0.0 copy-start.13
  368.8 0.0 copy-start.18
  368.8 0.0 copy-start.12
  368.9 0.0 copy-start.6
  368.9 0.0 copy-start.5
  368.9 41.1 %attention_backward.3 = (bf16[16,48,3072]{2,1,0:T(8,128)(2,1)}, bf16[608,768]{1,0:T(8,128)(2,1)}, f32[1,768]{1,0:T(1,128)}, f32[1,768]{1,0:T(1,128)}, f32[1,768]...) custom-call(bf16[608,768]{1,0:T(8,128)(2,1)} %get-tuple-element.100.incoming_ref.refs_5_, f32[608,1]{1,0:T(8,128)} %fusion.4.mask_ref, ...), custom_call_target="tpu_custom_call" | custom-call | tf_op jit(solution)/shard_map/attention_backward/pallas_call | solution.py:971
  410.1 0.7 reduce.4
  410.9 0.7 reduce.8
  411.7 0.7 reduce.14
  412.5 0.7 maximum_reduce_fusion
  413.4 0.0 copy-start.2
  413.4 0.6 copy-done.2
  414.1 331.7 %collect.1 = (bf16[2,1280,768]{2,1,0:T(8,128)(2,1)}, bf16[2,1216,768]{2,1,0:T(8,128)(2,1)}, bf16[16,48,3072]{2,1,0:T(8,128)(2,1)}, bf16[16,96,768]{2,1,0:T(8,128)(2,1)}, f32[144,128]{1,0:T(8,128)}) custom-call(bf16[608,768]{1,0:T(8,128)(2,1)} %get-tuple-element.76.hidden_ref.refs_0_, bf16[608,768]{1,0:T(8,128)(2,1)} %get-tuple-element.79.hidden_ref.refs_1_, ...), custom_call_target="tpu_custom_call" | custom-call | tf_op jit(solution)/shard_map/collect/pallas_call | solution.py:520
  745.8 0.0 slice-start
  745.8 0.9 fusion.9
  746.7 0.9 fusion.8
  747.6 0.8 slice.180
  748.3 5.9 bitcast_convert_fusion.1
  754.3 5.0 bitcast_convert_fusion
  759.3 2.5 bitcast_convert_fusion.2
  761.9 0.6 constant_dynamic-slice_fusion.1
  762.5 0.6 constant_dynamic-slice_fusion
  763.1 0.6 reshape.238
  763.7 0.6 reshape.239
  764.3 0.6 reshape.240
  764.9 0.6 reshape.241
  765.5 4.3 copy.41
  (76 shorter events, 0.4 us)
Async XLA Ops:
  3.1 1.3 copy-start
  3.1 3.2 copy-start.22
  3.1 4.6 copy-start.20
  3.1 4.6 copy-start.21
  5.7 174.6 %copy-start.4 = (f32[2,1536]{1,0:T(2,128)S(1)}, f32[2,1536]{1,0:T(2,128)}, u32[]{:S(2)}) copy-start(f32[2,1536]{1,0:T(2,128)} %param.18) | copy-start | bytes 36868
  5.7 174.6 %copy-start.7 = (f32[2,768]{1,0:T(2,128)S(1)}, f32[2,768]{1,0:T(2,128)}, u32[]{:S(2)}) copy-start(f32[2,768]{1,0:T(2,128)} %param.19) | copy-start | bytes 18436
  5.7 175.2 %copy-start.8 = (f32[2,768]{1,0:T(2,128)S(1)}, f32[2,768]{1,0:T(2,128)}, u32[]{:S(2)}) copy-start(f32[2,768]{1,0:T(2,128)} %param.21) | copy-start | bytes 18436
  5.7 175.8 %copy-start.3 = (f32[2,3072]{1,0:T(2,128)S(1)}, f32[2,3072]{1,0:T(2,128)}, u32[]{:S(2)}) copy-start(f32[2,3072]{1,0:T(2,128)} %param.20) | copy-start | bytes 73732
  5.7 181.0 %collective-permute-start = (bf16[2,608,768]{2,1,0:T(8,128)(2,1)}, bf16[2,608,768]{2,1,0:T(8,128)(2,1)}, u32[]{:S(2)}, u32[]{:S(2)}) collective-permute-start(bf16[2,608,768]{2,1,0:T(8,128)(2,1)} %fusion), channel_id=1, source_target_pairs={{0,1},{1,0},{2,3},{3,2},{4,5},{5,4},{6,7},{7,6},{8,9},{9,8},{10,11... | collective-permute-start | bytes 5603336 | tf_op jit(solution)/shard_map/ppermute | solution.py:37
  7.5 176.0 %collective-permute-start.1 = (f32[8,128]{1,0:T(8,128)S(1)}, f32[8,128]{1,0:T(8,128)S(1)}, u32[]{:S(2)}, u32[]{:S(2)}) collective-permute-start(f32[8,128]{1,0:T(8,128)S(1)} %broadcast_in_dim.27), channel_id=1, source_target_pairs={{0,1},{1,0},{2,3},{3,2},{4,5},{5,4},{6,7},{7,6},{8,9},{9,8},{10,11... | collective-permute-start | bytes 12296 | tf_op jit(solution)/shard_map/ppermute | solution.py:37
  368.8 42.0 %copy-start.19 = (f32[1,768]{1,0:T(1,128)S(1)}, f32[1,768]{1,0:T(1,128)}, u32[]{:S(2)}) copy-start(f32[1,768]{1,0:T(1,128)} %get-tuple-element.116) | copy-start | bytes 9220
  368.8 42.0 %copy-start.16 = (f32[1,768]{1,0:T(1,128)S(1)}, f32[1,768]{1,0:T(1,128)}, u32[]{:S(2)}) copy-start(f32[1,768]{1,0:T(1,128)} %get-tuple-element.117) | copy-start | bytes 9220
  368.8 42.0 %copy-start.13 = (f32[1,768]{1,0:T(1,128)S(1)}, f32[1,768]{1,0:T(1,128)}, u32[]{:S(2)}) copy-start(f32[1,768]{1,0:T(1,128)} %get-tuple-element.118) | copy-start | bytes 9220
  368.8 42.8 %copy-start.18 = (f32[1,768]{1,0:T(1,128)S(1)}, f32[1,768]{1,0:T(1,128)}, u32[]{:S(2)}) copy-start(f32[1,768]{1,0:T(1,128)} %get-tuple-element.120) | copy-start | bytes 9220
  368.8 42.8 %copy-start.15 = (f32[1,768]{1,0:T(1,128)S(1)}, f32[1,768]{1,0:T(1,128)}, u32[]{:S(2)}) copy-start(f32[1,768]{1,0:T(1,128)} %get-tuple-element.121) | copy-start | bytes 9220
  368.8 42.8 %copy-start.12 = (f32[1,768]{1,0:T(1,128)S(1)}, f32[1,768]{1,0:T(1,128)}, u32[]{:S(2)}) copy-start(f32[1,768]{1,0:T(1,128)} %get-tuple-element.122) | copy-start | bytes 9220
  368.8 43.5 %copy-start.14 = (f32[1,768]{1,0:T(1,128)S(1)}, f32[1,768]{1,0:T(1,128)}, u32[]{:S(2)}) copy-start(f32[1,768]{1,0:T(1,128)} %get-tuple-element.128) | copy-start | bytes 9220
  368.9 43.5 %copy-start.17 = (f32[1,768]{1,0:T(1,128)S(1)}, f32[1,768]{1,0:T(1,128)}, u32[]{:S(2)}) copy-start(f32[1,768]{1,0:T(1,128)} %get-tuple-element.131) | copy-start | bytes 9220
  368.9 43.5 %copy-start.11 = (f32[1,768]{1,0:T(1,128)S(1)}, f32[1,768]{1,0:T(1,128)}, u32[]{:S(2)}) copy-start(f32[1,768]{1,0:T(1,128)} %get-tuple-element.132) | copy-start | bytes 9220
  368.9 44.4 %copy-start.9 = (f32[1,768]{1,0:T(1,128)S(1)}, f32[1,768]{1,0:T(1,128)}, u32[]{:S(2)}) copy-start(f32[1,768]{1,0:T(1,128)} %get-tuple-element.125) | copy-start | bytes 9220
  368.9 44.4 %copy-start.10 = (f32[1,768]{1,0:T(1,128)S(1)}, f32[1,768]{1,0:T(1,128)}, u32[]{:S(2)}) copy-start(f32[1,768]{1,0:T(1,128)} %get-tuple-element.126) | copy-start | bytes 9220
  368.9 44.5 %copy-start.6 = (f32[1,3072]{1,0:T(1,128)S(1)}, f32[1,3072]{1,0:T(1,128)}, u32[]{:S(2)}) copy-start(f32[1,3072]{1,0:T(1,128)} %get-tuple-element.129) | copy-start | bytes 36868
  368.9 44.5 %copy-start.5 = (f32[1,3072]{1,0:T(1,128)S(1)}, f32[1,3072]{1,0:T(1,128)}, u32[]{:S(2)}) copy-start(f32[1,3072]{1,0:T(1,128)} %get-tuple-element.130) | copy-start | bytes 36868
  413.4 0.6 copy-start.2
  745.8 8.5 %slice-start = ((s8[4718592]{0:T(1024)(128)(4,1)}), s8[4194304]{0:T(1024)(128)(4,1)S(1)}, s32[]{:S(2)}) async-start(s8[4718592]{0:T(1024)(128)(4,1)} %bitcast.60), calls=%async_computation | async-start | bytes 8388608
  748.3 6.0 slice-start.1
  754.3 5.1 copy-start.1

commit v4 on v3

--- a/solution.py
+++ b/solution.py
@@ -152,135 +152,184 @@
             arrivals[name].wait_recv()
 
 
-class WeightGather(PlaneGather):
-    def __init__(self, spot, src, dst, source, send, recv):
-        super().__init__(spot, dst, send, recv)
-        self.src, self.source = src, source
-        self.own = self.blocks(spot.core, spot.c)
-
-    def along(self, src):
-        s = self.spot
+class SpreadHop:
+    def __init__(self, spot, own, source, hop, send, recv, ways="both"):
+        self.spot, self.own, self.send, self.recv = spot, own, send, recv
+        self.up_from = source + hop - 1 if source + hop < spot.sections and ways != "down" else None
+        self.down_from = source - hop + 1 if source - hop >= 0 and ways != "up" else None
+
+    def copies(self):
+        s, spot = self, self.spot
         return (
-            remote(src.at[self.own], self.dst.at[self.own], self.send.at[9], self.recv.at[9], s.above),
-            remote(src.at[self.own], self.dst.at[self.own], self.send.at[10], self.recv.at[9], s.below),
-            pltpu.make_async_copy(src.at[self.own], self.dst.at[self.own], self.send.at[11]),
+            remote(s.own, s.own, s.send.at[0], s.recv, spot.above),
+            remote(s.own, s.own, s.send.at[1], s.recv, spot.below),
         )
 
-    def open(self):
-        z, source = self.spot.z, self.source
-        up, down, stay = self.along(self.src)
-        @pl.when(z == source)
-        def _():
-            if source + 1 < self.spot.sections:
-                up.start()
-            if source:
-                down.start()
-            stay.start()
-            self.begin(self.src.at[self.own])
-
-    def first(self):
-        z, source, last = self.spot.z, self.source, self.spot.sections - 1
-        up, down, _ = self.along(self.dst)
-        @pl.when(z != source)
-        def _():
-            up.wait_recv()
-            if source < last - 1:
-                pl.when((z > source) & (z < last))(up.start)
-            if source > 1:
-                pl.when((z < source) & (z > 0))(down.start)
-            self.begin(self.dst.at[self.own])
+    def start(self, upwards=True, downwards=True):
+        up, down = self.copies()
+        if upwards and self.up_from is not None:
+            pl.when(self.spot.z == self.up_from)(up.start)
+        if downwards and self.down_from is not None:
+            pl.when(self.spot.z == self.down_from)(down.start)
+
+    def arrive(self):
+        up, _ = self.copies()
+        if self.up_from is not None:
+            pl.when(self.spot.z == self.up_from + 1)(up.wait_recv)
+        if self.down_from is not None:
+            pl.when(self.spot.z == self.down_from - 1)(up.wait_recv)
+
+    def leave(self):
+        up, down = self.copies()
+        if self.up_from is not None:
+            pl.when(self.spot.z == self.up_from)(up.wait_send)
+        if self.down_from is not None:
+            pl.when(self.spot.z == self.down_from)(down.wait_send)
 
     def finish(self):
-        z, source, last = self.spot.z, self.source, self.spot.sections - 1
-        up, down, stay = self.along(self.src)
-        if source < last:
-            pl.when((z >= source) & (z < last))(up.wait_send)
-        if source:
-            pl.when((z <= source) & (z > 0))(down.wait_send)
-        pl.when(z == source)(stay.wait)
-        super().finish()
-
-
-def gather_weights_body(front, back, norms, *refs):
-    fronts, downs, norm_all = refs[:4], refs[4:6], refs[6]
-    send, recv, norm_send, norm_recv = refs[7:]
+        self.arrive()
+        self.leave()
+
+
+def hops_from(source, sections):
+    return max(source, sections - 1 - source)
+
+
+COLUMN_CHUNKS = 4
+BEGUN = (
+    ("front", 1, 2, "both"), ("back", 0, 1, "both"), ("back", 1, 1, "both"), ("front", 2, 1, "down"),
+    ("front", 3, 1, "both"), ("back", 2, 1, "both"), ("back", 3, 1, "both"),
+)
+
+
+def first_weights_body(*refs):
+    refs_list = list(refs)
+    take = lambda n: [refs_list.pop(0) for _ in range(n)]
+    own_in, norms, _ = take(1)[0], take(1)[0], take(len(BEGUN))
+    front, norm_all, owns = take(1)[0], take(1)[0], take(len(BEGUN))
+    own, own_sem, norm_send, norm_recv, zsend, zrecv, psend, precv, stay_sem, bsend, brecv = take(11)
     spot = Spot()
+    load = pltpu.make_async_copy(own_in, own, own_sem)
+    load.start()
+    load.wait()
     spot.greet()
-    norm_copies = [
-        remote(
-            norms, norm_all.at[spot.z], norm_send.at[step], norm_recv.at[step],
-            {"section": (spot.z + step) % spot.sections},
+    size = own.shape[2] // COLUMN_CHUNKS
+    hops, gathers, stays = [], [], []
+    for j in range(COLUMN_CHUNKS):
+        at = pl.ds((j + 1) % COLUMN_CHUNKS * size, size)
+        piece = own.at[:, :, at]
+        hops.append([SpreadHop(spot, piece, 0, hop, zsend.at[j, hop - 1], zrecv.at[j, hop - 1]) for hop in (1, 2, 3)])
+        gathers.append(PlaneGather(spot, front.at[:, :, at], psend.at[j], precv.at[j]))
+        stays.append(
+            pltpu.make_async_copy(piece, gathers[j].dst.at[gathers[j].blocks(spot.core, spot.c)], stay_sem.at[j])
         )
-        for step in range(1, spot.sections)
-    ]
-    kept = pltpu.make_async_copy(norms, norm_all.at[spot.z], norm_send.at[0])
-    for copy in norm_copies + [kept]:
-        copy.start()
-    jobs = []
-    for layer in range(2):
-        low, high = downs[layer].at[pl.ds(0, 16)], downs[layer].at[pl.ds(16, 16)]
-        jobs += [(front, fronts[2 * layer], 2 * layer), (front, fronts[2 * layer + 1], 2 * layer + 1)]
-        jobs += [(back, low, 2 * layer), (back, high, 2 * layer + 1)]
-    gathers = [WeightGather(spot, a, b, s, send.at[i], recv.at[i]) for i, (a, b, s) in enumerate(jobs)]
+        hops[j][0].start()
+        if j == 0:
+            norm_copies = [
+                remote(
+                    norms, norm_all.at[spot.z], norm_send.at[step], norm_recv.at[step],
+                    {"section": (spot.z + step) % spot.sections},
+                )
+                for step in range(1, spot.sections)
+            ]
+            norm_copies.append(pltpu.make_async_copy(norms, norm_all.at[spot.z], norm_send.at[0]))
+            for copy in norm_copies:
+                copy.start()
+    begun, count = [], 0
+    for held, (_, source, made, ways) in zip(owns, BEGUN):
+        begun.append([
+            SpreadHop(
+                spot, held, source, hop + 1, bsend.at[count + hop], brecv.at[count + hop], "both" if hop else ways
+            )
+            for hop in range(made)
+        ])
+        count += made
+    for chain in begun:
+        chain[0].start(upwards=False)
+    begun[5][0].start(downwards=False)
+    for j in range(COLUMN_CHUNKS):
+        for hop in range(3):
+            hops[j][hop].arrive()
+            if hop < 2:
+                hops[j][hop + 1].start()
+        gathers[j].begin(own.at[:, :, pl.ds((j + 1) % COLUMN_CHUNKS * size, size)])
+        stays[j].start()
+    for chain in begun[:5] + begun[6:]:
+        chain[0].start(downwards=False)
+    for j in range(COLUMN_CHUNKS):
+        gathers[j].second()
+    begun[0][0].arrive()
+    begun[0][1].start()
     for gather in gathers:
-        gather.open()
-    for i in range(len(gathers) + 2):
-        if i < len(gathers):
-            gathers[i].first()
-        if 0 <= i - 1 < len(gathers):
-            gathers[i - 1].second()
-        if i >= 2:
-            gathers[i - 2].third()
-    for gather in gathers:
-        gather.finish()
-    kept.wait()
-    for step, copy in enumerate(norm_copies, 1):
+        gather.third()
+    for chain in begun[1:]:
+        chain[0].arrive()
+    begun[0][1].arrive()
+    for chain in begun:
+        for hop in chain:
+            hop.leave()
+    for j in range(COLUMN_CHUNKS):
+        for hop in hops[j]:
+            hop.leave()
+        gathers[j].finish()
+        stays[j].wait()
+    norm_copies[-1].wait()
+    for step, copy in enumerate(norm_copies[:-1], 1):
         copy.wait_send()
         block = norm_all.at[(spot.z + spot.sections - step) % spot.sections]
         remote(block, block, norm_send.at[step], norm_recv.at[step], spot.mate).wait_recv()
 
 
-def gather_weights(front, back, norms):
+def first_weights(front, back, norms):
     sections = lax.axis_size("section")
-    blocks = lambda a, n: (n, a.shape[0] // 16, a.shape[1])
-    front_b, back_b = front.reshape(blocks(front, 16)), back.reshape(blocks(back, 16))
-    full = jax.ShapeDtypeStruct(front_b.shape, BF16)
-    down = jax.ShapeDtypeStruct((32,) + back_b.shape[1:], BF16)
-    hbm = pl.BlockSpec(memory_space=pl.ANY)
+    spot = Spot()
+    at = spot.core * 8 + spot.c * 2
+    owns = {}
+    for kind, weight in (("front", front), ("back", back)):
+        blocks = weight.reshape(16, weight.shape[0] // 16, weight.shape[1])
+        owns[kind] = lax.dynamic_slice_in_dim(blocks, at, 2, 0)
+    hbm = hbm_spec()
+    sems = pltpu.SemaphoreType.DMA
+    begun = [owns[kind] for kind, _, _, _ in BEGUN]
+    made = sum(hops for _, _, hops, _ in BEGUN)
+    shape = lambda a: jax.ShapeDtypeStruct(a.shape, a.dtype)
+    full = jax.ShapeDtypeStruct((16,) + owns["front"].shape[1:], BF16)
     out = pl.pallas_call(
-        gather_weights_body,
-        in_specs=[hbm] * 3, out_specs=[hbm] * 7,
-        out_shape=[full] * 4 + [down] * 2 + [jax.ShapeDtypeStruct((sections,) + norms.shape, F32)],
+        first_weights_body,
+        in_specs=[hbm] * (2 + len(begun)), out_specs=[hbm] * (2 + len(begun)),
+        out_shape=[full, jax.ShapeDtypeStruct((sections,) + norms.shape, F32)] + [shape(a) for a in begun],
         scratch_shapes=[
-            pltpu.SemaphoreType.DMA((8, 12)), pltpu.SemaphoreType.DMA((8, 10)),
-            pltpu.SemaphoreType.DMA((sections,)), pltpu.SemaphoreType.DMA((sections,)),
+            pltpu.VMEM(owns["front"].shape, BF16), sems, sems((sections,)), sems((sections,)),
+            sems((COLUMN_CHUNKS, 3, 2)), sems((COLUMN_CHUNKS, 3)), sems((COLUMN_CHUNKS, 9)), sems((COLUMN_CHUNKS, 9)),
+            sems((COLUMN_CHUNKS,)), sems((made, 2)), sems((made,)),
         ],
+        input_output_aliases={2 + i: 2 + i for i in range(len(begun))},
         compiler_params=pltpu.CompilerParams(collective_id=0, has_side_effects=True),
-        name="gather_weights",
-    )(front_b, back_b, norms)
-    fronts = [a.reshape(front.shape) for a in out[:4]]
-    downs = [a.reshape(2 * back.shape[0], back.shape[1]) for a in out[4:6]]
-    return fronts, downs, out[6]
+        name="first_weights",
+    )(owns["front"], norms, *begun)
+    return out[0], out[1], {(kind, source): held for (kind, source, _, _), held in zip(BEGUN, out[2:])}
 
 
 class Deliver:
-    def __init__(self, spot, src, dst, target, send, recv, core_rows):
+    def __init__(self, spot, src, dst, target, send, recv, start=0, size=None):
         self.spot, self.src, self.dst, self.target, self.send, self.recv = spot, src, dst, target, send, recv
-        self.rows = core_rows
+        self.rows, self.start_row = src.shape[0], start
+        self.size = size or src.shape[0]
         self.owner, self.slot = spot.z // 2, spot.z % 2
         self.home = (spot.z == target) & (spot.core == self.owner)
 
     def place(self, slot, core):
-        return self.dst.at[slot, pl.ds(pl.multiple_of(core * self.rows, 16), self.rows)]
+        at = pl.multiple_of(core * self.rows + self.start_row, 16)
+        return self.dst.at[slot, pl.ds(at, self.size)]
 
     def copies(self):
         s, spot = self, self.spot
-        spot_at = s.place(s.slot, spot.core)
+        spot_at, src = s.place(s.slot, spot.core), s.src.at[pl.ds(s.start_row, s.size)]
         away = remote(
-            s.src, spot_at, s.send.at[0], s.recv.at[s.slot * 2 + spot.core],
+            src, spot_at, s.send.at[0], s.recv.at[s.slot * 2 + spot.core],
             {"section": s.target, "dp": spot.d - spot.core + s.owner},
         )
-        return away, pltpu.make_async_copy(s.src, spot_at, s.send.at[1])
+        return away, pltpu.make_async_copy(src, spot_at, s.send.at[1])
 
     def start(self):
         away, stay = self.copies()
@@ -300,30 +349,251 @@
                 pl.when((spot.z == self.target) & jnp.logical_not(here))(landing.wait_recv)
 
 
+class Guest:
+    def __init__(self, inputs=(), outputs=(), scratch=(), aliases=(), plan=None):
+        self.inputs, self.outputs, self.scratch = list(inputs), list(outputs), list(scratch)
+        self.aliases, self.plan = list(aliases), plan
+
+
+def hbm_spec():
+    return pl.BlockSpec(memory_space=pl.ANY)
+
+
+def vmem_spec():
+    return pl.BlockSpec(memory_space=pltpu.VMEM)
+
+
+def hosted(body, grid, operands, results, scratch, guests, collective_id, name, vmem=KERNEL_VMEM):
+    guest_in = [pair for g in guests for pair in g.inputs]
+    guest_out = [pair for g in guests for pair in g.outputs]
+    guest_scratch = [s for g in guests for s in g.scratch]
+    aliases, at_in, at_out = {}, len(operands), len(results)
+    for g in guests:
+        for i, o in g.aliases:
+            aliases[at_in + i] = at_out + o
+        at_in, at_out = at_in + len(g.inputs), at_out + len(g.outputs)
+
+    def kernel(*refs):
+        refs = list(refs)
+        take = lambda n: [refs.pop(0) for _ in range(n)]
+        ins, gins = take(len(operands)), take(len(guest_in))
+        outs, gouts = take(len(results)), take(len(guest_out))
+        held, gheld = take(len(scratch)), take(len(guest_scratch))
+        spot, step = Spot(), pl.program_id(0)
+        pl.when(step == 0)(spot.greet)
+        hooks = {}
+        for g in guests:
+            parts = [[r.pop(0) for _ in range(n)] for r, n in (
+                (gins, len(g.inputs)), (gouts, len(g.outputs)), (gheld, len(g.scratch))
+            )]
+            for at, actions in g.plan(spot, *parts).items():
+                hooks.setdefault(at, []).extend(actions)
+
+        def run(actions):
+            for action in actions:
+                action()
+
+        for at in sorted(k for k in hooks if k != "end"):
+            pl.when(step == at)(functools.partial(run, hooks[at]))
+        body(spot, *ins, *outs, *held)
+        if "end" in hooks:
+            pl.when(step == grid - 1)(functools.partial(run, hooks["end"]))
+
+    out = pl.pallas_call(
+        kernel,
+        grid=(grid,),
+        in_specs=[s for _, s in operands + guest_in],
+        out_specs=[s for _, s in results + guest_out],
+        out_shape=[s for s, _ in results + guest_out],
+        scratch_shapes=list(scratch) + guest_scratch,
+        input_output_aliases=aliases,
+        compiler_params=pltpu.CompilerParams(
+            vmem_limit_bytes=vmem, collective_id=collective_id, has_side_effects=True
+        ),
+        name=name,
+    )(*[a for a, _ in operands + guest_in])
+    own, rest, per_guest = out[: len(results)], list(out[len(results) :]), []
+    for g in guests:
+        per_guest.append([rest.pop(0) for _ in g.outputs])
+    return own, per_guest
+
+
+def deliver_guest(pieces, home, steps):
+    sems = pltpu.SemaphoreType.DMA
+    count = len(pieces)
+
+    def plan(spot, ins, outs, held):
+        send, recv = held
+        hooks = {}
+        for i, (_, target, first, size) in enumerate(pieces):
+            blocks = size // 16
+            for step in range(steps):
+                low, high = blocks * step // steps, blocks * (step + 1) // steps
+                if high > low:
+                    part = Deliver(
+                        spot, ins[i], outs[0], target, send.at[i], recv.at[i], first + 16 * low, 16 * (high - low)
+                    )
+                    hooks.setdefault(step, []).append(part.start)
+            every = Deliver(spot, ins[i], outs[0], target, send.at[i], recv.at[i], first, size)
+            hooks.setdefault("end", []).append(every.finish)
+        return hooks
+
+    return Guest(
+        [(piece[0], hbm_spec()) for piece in pieces] + [(home, hbm_spec())],
+        [(jax.ShapeDtypeStruct(home.shape, home.dtype), hbm_spec())],
+        [sems((count, 2)), sems((count, 4))],
+        [(count, 0)], plan,
+    )
+
+
+def plane_gather_guest(parts, shapes, stages):
+    sems = pltpu.SemaphoreType.DMA
+
+    def plan(spot, ins, outs, held):
+        send, recv, stay_sem = held
+        hooks = {}
+        for i, (_, result, first) in enumerate(parts):
+            job = PlaneGather(spot, outs[result].at[pl.ds(first, 16)], send.at[i], recv.at[i])
+            stay = pltpu.make_async_copy(ins[i], job.dst.at[job.blocks(spot.core, spot.c)], stay_sem.at[i])
+            actions = (functools.partial(job.begin, ins[i]), job.second, job.third)
+            for at, action in zip(stages[i], actions):
+                hooks.setdefault(at, []).append(action)
+            hooks.setdefault(stages[i][0], []).append(stay.start)
+            hooks.setdefault("end", []).extend([job.finish, stay.wait])
+        return hooks
+
+    return Guest(
+        [(a, vmem_spec()) for a, _, _ in parts],
+        [(jax.ShapeDtypeStruct(shape, BF16), hbm_spec()) for shape in shapes],
+        [sems((len(parts), 9)), sems((len(parts), 9)), sems((len(parts),))],
+        (), plan,
+    )
+
+
+def spread_gather_guest(jobs, shape):
+    sems = pltpu.SemaphoreType.DMA
+    made = sum(len(job[2]) for job in jobs)
+
+    def plan(spot, ins, outs, held):
+        hsend, hrecv, send, recv, stay_sem = held
+        hooks, count = {}, 0
+        for i, (_, source, hop_steps, stages, first) in enumerate(jobs):
+            own, before = outs[i], None
+            for back, at in enumerate(hop_steps):
+                hop = SpreadHop(
+                    spot, own, source, hops_from(source, spot.sections) - len(hop_steps) + 1 + back,
+                    hsend.at[count], hrecv.at[count],
+                )
+                count += 1
+                if before is not None:
+                    hooks.setdefault(at, []).append(before.arrive)
+                hooks.setdefault(at, []).append(hop.start)
+                hooks.setdefault("end", []).append(hop.leave)
+                before = hop
+            job = PlaneGather(spot, outs[-1].at[pl.ds(first, 16)], send.at[i], recv.at[i])
+            stay = pltpu.make_async_copy(own, job.dst.at[job.blocks(spot.core, spot.c)], stay_sem.at[i])
+            hooks.setdefault(stages[0], []).extend([before.arrive, functools.partial(job.begin, own), stay.start])
+            hooks.setdefault(stages[1], []).append(job.second)
+            hooks.setdefault(stages[2], []).append(job.third)
+            hooks.setdefault("end", []).extend([job.finish, stay.wait])
+        return hooks
+
+    return Guest(
+        [(job[0], hbm_spec()) for job in jobs],
+        [(jax.ShapeDtypeStruct(job[0].shape, BF16), hbm_spec()) for job in jobs]
+        + [(jax.ShapeDtypeStruct(shape, BF16), hbm_spec())],
+        [sems((made, 2)), sems((made,)), sems((len(jobs), 9)), sems((len(jobs), 9)), sems((len(jobs),))],
+        [(i, i) for i in range(len(jobs))], plan,
+    )
+
+
+def spread_hop_guest(arrays, jobs, start=0):
+    sems = pltpu.SemaphoreType.DMA
+
+    def plan(spot, ins, outs, held):
+        send, recv = held
+        hops = [
+            SpreadHop(spot, outs[i], source, hop, send.at[n], recv.at[n], ways)
+            for n, (i, source, hop, ways) in enumerate(jobs)
+        ]
+        return {start: [h.start for h in hops], "end": [h.finish for h in hops]}
+
+    return Guest(
+        [(a, hbm_spec()) for a in arrays],
+        [(jax.ShapeDtypeStruct(a.shape, a.dtype), hbm_spec()) for a in arrays],
+        [sems((len(jobs), 2)), sems((len(jobs),))],
+        [(i, i) for i in range(len(arrays))], plan,
+    )
+
+
+def plane_sum_guest(jobs, stages):
+    sems = pltpu.SemaphoreType.DMA
+    shapes = [(a.shape[1], a.shape[2]) for a, _ in jobs]
+    arrays = []
+    for a, _ in jobs:
+        if not any(a is b for b in arrays):
+            arrays.append(a)
+    index = [next(i for i, b in enumerate(arrays) if b is a) for a, _ in jobs]
+
+    def plan(spot, ins, outs, held):
+        send, recv = held[-2:]
+        hooks = {}
+        for i, (_, first) in enumerate(jobs):
+            src = ins[index[i]].at[pl.ds(first, 16)]
+            job = PlaneSum(spot, src, held[6 * i : 6 * i + 6], send.at[i], recv.at[i])
+            actions = (job.start, job.first, job.second, functools.partial(job.third, outs[i]))
+            for at, action in zip(stages[i], actions):
+                hooks.setdefault(at, []).append(action)
+            hooks.setdefault("end", []).append(job.finish)
+        return hooks
+
+    return Guest(
+        [(a, hbm_spec()) for a in arrays],
+        [(jax.ShapeDtypeStruct((2,) + s, BF16), vmem_spec()) for s in shapes],
+        [b for s in shapes for b in PlaneSum.scratch(*s)] + [sems((len(jobs), 8)), sems((len(jobs), 8))],
+        (), plan,
+    )
+
+
+def section_hop_guest(jobs, start=0):
+    sems = pltpu.SemaphoreType.DMA
+
+    def plan(spot, ins, outs, held):
+        send, recv = held[-2:]
+        hops = [
+            SectionHop(spot, ins[i], outs[i], held[i], target, hop, send.at[i], recv.at[i])
+            for i, (_, target, hop) in enumerate(jobs)
+        ]
+        return {start: [h.start for h in hops], "end": [h.finish for h in hops]}
+
+    return Guest(
+        [(a, vmem_spec()) for a, _, _ in jobs],
+        [(jax.ShapeDtypeStruct(a.shape, BF16), vmem_spec()) for a, _, _ in jobs],
+        [pltpu.VMEM((2 * a.shape[0],) + a.shape[1:], BF16) for a, _, _ in jobs]
+        + [sems((len(jobs),)), sems((len(jobs), 2))],
+        (), plan,
+    )
+
+
 def add_into(target, *others):
-    blocks, rows, _ = target.shape
-    def step(i, carry):
-        b, r = i // (rows // 16), pl.ds(pl.multiple_of((i % (rows // 16)) * 16, 16), 16)
-        total = target[b, r, :].astype(F32)
+    def step(b, carry):
+        total = target[b].astype(F32)
         for other in others:
-            total = total + other[b, r, :].astype(F32)
-        target[b, r, :] = total.astype(BF16)
+            total = total + other[b].astype(F32)
+        target[b] = total.astype(BF16)
         return carry
-    lax.fori_loop(0, blocks * (rows // 16), step, 0)
-
-
-class ScatterSum:
-    SEMS = 9
-
-    def __init__(self, spot, src, target, bufs, send, recv):
-        self.spot, self.src, self.target, self.send, self.recv = spot, src, target, send, recv
-        self.half, self.from_mate, self.in_x, self.in_y, self.in_yx, self.in_xy, self.from_z = bufs
+
+    lax.fori_loop(0, target.shape[0], step, 0)
+
+
+class PlaneSum:
+    def __init__(self, spot, src, bufs, send, recv):
+        self.spot, self.src, self.send, self.recv = spot, src, send, recv
+        self.half, self.from_mate, self.in_x, self.in_y, self.in_yx, self.in_xy = bufs
 
     @staticmethod
     def scratch(block_rows, columns):
-        return [
-            pltpu.VMEM((n, block_rows, columns), BF16) for n in (8, 8, 2, 2, 1, 1, 4)
-        ]
+        return [pltpu.VMEM((n, block_rows, columns), BF16) for n in (8, 8, 2, 2, 1, 1)]
 
     def mate_copies(self):
         s, spot = self, self.spot
@@ -372,91 +642,106 @@
         add_into(s.block(spot.c_x, 1), s.in_y.at[other])
         for copy in self.second_copies():
             copy.start()
-        add_into(s.block(spot.c, 0), s.in_x.at[first])
-        add_into(s.block(spot.c, 1), s.in_y.at[first])
-
-    def third(self):
+
+    def third(self, out):
         s, spot = self, self.spot
         for copy in self.second_copies():
             copy.wait_recv()
-        add_into(s.block(spot.c, 0), s.in_xy)
-        add_into(s.block(spot.c, 1), s.in_yx)
-
-    def own(self):
-        return self.half.at[pl.ds(self.spot.c * 2, 2)]
-
-    def along(self):
-        s, spot = self, self.spot
-        down = remote(s.own(), s.from_z.at[pl.ds(0, 2)], s.send.at[8], s.recv.at[8], spot.below)
-        up = remote(s.own(), s.from_z.at[pl.ds(2, 2)], s.send.at[8], s.recv.at[0], spot.above)
-        return up, down
-
-    def pass_on(self, z):
-        up, down = self.along()
-        last = self.spot.sections - 1
-
-        @pl.when(self.spot.z == z)
-        def _():
-            if z >= self.target and z < last:
-                down.wait_recv()
-                add_into(self.own(), self.from_z.at[pl.ds(0, 2)])
-            if z <= self.target and z > 0:
-                up.wait_recv()
-                add_into(self.own(), self.from_z.at[pl.ds(2, 2)])
-            if z > self.target:
-                down.start()
-            if z < self.target:
-                up.start()
-
-    def fourth(self):
-        for z in range(self.spot.sections):
-            self.pass_on(z)
+        first = pl.ds(0, 1)
+        add_into(s.block(spot.c, 0), s.in_x.at[first], s.in_xy)
+        add_into(s.block(spot.c, 1), s.in_y.at[first], s.in_yx)
+        out[...] = s.half[pl.ds(spot.c * 2, 2)]
 
     def finish(self):
         for copy in self.first_copies() + self.second_copies():
             copy.wait_send()
-        up, down = self.along()
-        pl.when(self.spot.z != self.target)(up.wait_send)
-
-
-def collect_body(rows, n_small, *refs):
+
+
+class SectionHop:
+    def __init__(self, spot, src, total, bufs, target, hop, send, recv):
+        self.spot, self.src, self.total, self.bufs, self.send, self.recv = spot, src, total, bufs, send, recv
+        last = spot.sections - 1
+        self.below = hop - 1 if hop <= target else None
+        self.above = last - hop + 1 if last - hop >= target else None
+
+    def copies(self):
+        s, spot, n = self, self.spot, self.src.shape[0]
+        up = remote(s.src, s.bufs.at[pl.ds(n, n)], s.send, s.recv.at[1], spot.above)
+        down = remote(s.src, s.bufs.at[pl.ds(0, n)], s.send, s.recv.at[0], spot.below)
+        return up, down
+
+    def start(self):
+        up, down = self.copies()
+        if self.below is not None:
+            pl.when(self.spot.z == self.below)(up.start)
+        if self.above is not None:
+            pl.when(self.spot.z == self.above)(down.start)
+        self.total[...] = self.src[...]
+
+    def finish(self):
+        up, down = self.copies()
+        n = self.src.shape[0]
+        if self.below is not None:
+            pl.when(self.spot.z == self.below)(up.wait_send)
+
+            @pl.when(self.spot.z == self.below + 1)
+            def _():
+                up.wait_recv()
+                add_into(self.total, self.bufs.at[pl.ds(n, n)])
+        if self.above is not None:
+            pl.when(self.spot.z == self.above)(down.wait_send)
+
+            @pl.when(self.spot.z == self.above - 1)
+            def _():
+                down.wait_recv()
+                add_into(self.total, self.bufs.at[pl.ds(0, n)])
+
+
+LEFT = (("front", 3, 2), ("back", 3, 2), ("front", 2, 1), ("back", 2, 2), ("front", 1, 0), ("back", 0, 0), ("back", 1, 0))
+
+
+def collect_body(*refs):
     sections = lax.axis_size("section")
-    take = lambda n: tuple(refs_list.pop(0) for _ in range(n))
     refs_list = list(refs)
-    acts, grads, fronts, downs, (small,) = take(sections), take(sections), take(sections), take(sections // 2), take(1)
-    backs = [downs[s // 2].at[pl.ds(16 * (s % 2), 16)] for s in range(sections)]
-    acts_out, grads_out, front_out, back_out, small_out = take(5)
-    zeros, sums, arriving = take(3)
-    front_bufs = [take(7) for _ in range(sections)]
-    back_bufs = [take(7) for _ in range(sections)]
-    send, recv, dsend, drecv, asend, arecv, ssend, srecv, psem = take(9)
+    take = lambda n: [refs_list.pop(0) for _ in range(n)]
+    last, second, first_front = take(3)
+    parts = take(len(LEFT))
+    small, _ = take(2)
+    home, front_out, back_out, small_out = take(4)
+    plane_bufs, own, (sums, arriving) = take(6), take(1)[0], take(2)
+    psend, precv, dsend, drecv, asend, arecv, ssend, srecv, stay_sem, zsend, zrecv = take(11)
+    hop_refs = refs_list
     spot = Spot()
     spot.greet()
-    scatters = {}
-    for s in range(sections):
-        scatters["front", s] = ScatterSum(spot, fronts[s], s, front_bufs[s], send.at[s], recv.at[s])
-        scatters["back", s] = ScatterSum(spot, backs[s], s, back_bufs[s], send.at[sections + s], recv.at[sections + s])
-    order = []
-    for s in reversed(range(sections)):
-        order.append(scatters["front", s])
-        if s % 2:
-            order += [scatters["back", s - 1], scatters["back", s]]
-    delivers = [Deliver(spot, a, acts_out, s, dsend.at[s], drecv.at[s], rows) for s, a in enumerate(acts)]
-    delivers += [
-        Deliver(spot, a, grads_out, s, dsend.at[sections + s], drecv.at[sections + s], rows)
-        for s, a in enumerate(grads)
+    delivers = [
+        Deliver(spot, piece, home, target, dsend.at[target // 2], drecv.at[target // 2], *rows)
+        for piece, target, rows in ((last, 0, ()), (second, 2, (192, second.shape[0] - 192)))
     ]
-    for scatter in order:
-        scatter.start()
-    for deliver in delivers:
-        deliver.start()
-    zeros[...] = jnp.zeros_like(zeros)
-    pad = acts_out.shape[1] - 2 * rows
-    pads = [
-        pltpu.make_async_copy(zeros, acts_out.at[slot, pl.ds(2 * rows, pad)], psem.at[slot]) for slot in (0, 1)
-    ]
-    for copy in pads:
-        copy.start()
+    plane = PlaneSum(spot, first_front, plane_bufs, psend, precv)
+    count = 0
+
+    def chain(src, target, done):
+        nonlocal count
+        hops = []
+        for hop in range(done + 1, max(target, sections - 1 - target) + 1):
+            total, bufs = hop_refs.pop(0), hop_refs.pop(0)
+            hops.append(SectionHop(spot, src, total, bufs, target, hop, zsend.at[count], zrecv.at[count]))
+            src, count = total, count + 1
+        return hops, src
+
+    chains = [chain(part, target, done) for part, (_, target, done) in zip(parts, LEFT)]
+    first_chains = [chain(own.at[pl.ds(i, 1)], 0, 0) for i in (0, 1)]
+
+    def turn(which, i):
+        for hops, _ in which:
+            if 0 < i <= len(hops):
+                hops[i - 1].finish()
+        for hops, _ in which:
+            if i < len(hops):
+                hops[i].start()
+
+    plane.start()
+    turn(chains, 0)
     sums[0] = small[...]
     partners = [spot.mate, spot.x, spot.y] + [
         {"section": spot.z + bit * (1 - 2 * ((spot.z // bit) % 2))}
@@ -469,79 +754,102 @@
         copy.wait()
         sums[i + 1] = sums[i] + arriving[i]
 
-    count = len(order)
-    for i in range(count + 3):
-        if i < count:
-            order[i].first()
-        if 0 <= i - 1 < count:
-            order[i - 1].second()
-        if 0 <= i - 2 < count:
-            order[i - 2].third()
-        if 0 <= i - 3 < count:
-            order[i - 3].fourth()
-        if i < len(partners):
-            small_step(i)
+    small_step(0)
+    plane.first()
+    for deliver in delivers:
+        deliver.start()
+    turn(chains, 1)
+    for i in range(1, len(partners)):
+        small_step(i)
     small_out[...] = sums[len(partners)]
+    plane.second()
+    turn(chains, 2)
+    plane.third(own)
+    turn(first_chains[:1], 0)
+    turn(first_chains[1:], 0)
+    turn(chains, 3)
     gathers = [
         PlaneGather(spot, out, asend.at[i], arecv.at[i]) for i, out in enumerate((front_out, back_out))
     ]
+    ends = {(kind, target): end for (kind, target, _), (_, end) in zip(LEFT, chains)}
     stays = []
-    for i, (gather, kind) in enumerate(zip(gathers, ("front", "back"))):
-        for s in range(sections):
-            own = scatters[kind, s].own()
-            stay = pltpu.make_async_copy(own, gather.dst.at[gather.blocks(spot.core, spot.c)], psem.at[2 + i])
-
-            @pl.when(spot.z == s)
-            def _(gather=gather, own=own, stay=stay):
-                stay.start()
-                gather.begin(own)
-        stays.append(stay)
-    for gather in gathers:
-        gather.second()
-    for gather in gathers:
-        gather.third()
+
+    def begin(i, kind):
+        gather = gathers[i]
+        for z in range(sections):
+            blocks = gather.blocks(spot.core, spot.c)
+            if kind == "front" and z == 0:
+                pieces = [
+                    (end, gather.dst.at[gather.blocks(spot.core, spot.c, half)], stay_sem.at[half])
+                    for half, (_, end) in enumerate(first_chains)
+                ]
+            else:
+                pieces = [(ends[kind, z], gather.dst.at[blocks], stay_sem.at[2 + i])]
+            copies = [pltpu.make_async_copy(*piece) for piece in pieces]
+
+            @pl.when(spot.z == z)
+            def _(gather=gather, copies=copies):
+                for copy in copies:
+                    copy.start()
+                for copy in copies:
+                    copy.wait()
+                gather.begin(gather.dst.at[gather.blocks(spot.core, spot.c)])
+
+    begin(1, "back")
+    turn(first_chains[:1], 1)
+    turn(first_chains[1:], 1)
+    gathers[1].second()
+    turn(first_chains[:1], 2)
+    turn(first_chains[1:], 2)
+    gathers[1].third()
+    turn(first_chains[:1], 3)
+    turn(first_chains[1:], 3)
+    begin(0, "front")
+    gathers[0].second()
+    gathers[0].third()
     for gather in gathers:
         gather.finish()
-    for copy in stays + pads:
-        copy.wait()
     for deliver in delivers:
         deliver.finish()
-    for scatter in order:
-        scatter.finish()
-
-
-def collect(acts, grads, fronts, downs, small, padded):
+    plane.finish()
+
+
+def collect(last, second, home, first_front, parts, small):
     sections = lax.axis_size("section")
-    rows, width = acts[0].shape
-    back_shape = (16,) + downs[0].shape[1:]
-    hbm, vmem = pl.BlockSpec(memory_space=pl.ANY), pl.BlockSpec(memory_space=pltpu.VMEM)
+    hbm, vmem = hbm_spec(), vmem_spec()
     steps = 3 + (sections - 1).bit_length()
     sems = pltpu.SemaphoreType.DMA
-    out = pl.pallas_call(
-        functools.partial(collect_body, rows, small.shape[0]),
-        in_specs=[hbm] * (3 * sections + sections // 2) + [vmem],
-        out_specs=[hbm] * 4 + [vmem],
+    front_shape = first_front.shape
+    back_shape = (16,) + parts[1].shape[1:]
+    hop_scratch, hops = [], 0
+    jobs = [(p.shape, target, done) for p, (_, target, done) in zip(parts, LEFT)]
+    for shape, target, done in jobs + [((1,) + front_shape[1:], 0, 0)] * 2:
+        for _ in range(done, max(target, sections - 1 - target)):
+            hop_scratch += [pltpu.VMEM(shape, BF16), pltpu.VMEM((2 * shape[0],) + shape[1:], BF16)]
+            hops += 1
+    return pl.pallas_call(
+        collect_body,
+        in_specs=[hbm] * 3 + [vmem] * (len(parts) + 1) + [hbm],
+        out_specs=[hbm] * 3 + [vmem],
         out_shape=[
-            jax.ShapeDtypeStruct((2, padded, width), BF16), jax.ShapeDtypeStruct((2, 2 * rows, width), BF16),
-            jax.ShapeDtypeStruct(fronts[0].shape, BF16), jax.ShapeDtypeStruct(back_shape, BF16),
-            jax.ShapeDtypeStruct(small.shape, F32),
+            jax.ShapeDtypeStruct(home.shape, BF16), jax.ShapeDtypeStruct(front_shape, BF16),
+            jax.ShapeDtypeStruct(back_shape, BF16), jax.ShapeDtypeStruct(small.shape, F32),
         ],
-        scratch_shapes=[
-            pltpu.VMEM((padded - 2 * rows, width), BF16),
+        scratch_shapes=PlaneSum.scratch(*front_shape[1:])
+        + [
+            pltpu.VMEM((2,) + front_shape[1:], BF16),
             pltpu.VMEM((steps + 1,) + small.shape, F32), pltpu.VMEM((steps,) + small.shape, F32),
+            sems((8,)), sems((8,)), sems((2, 2)), sems((2, 4)),
+            sems((2, 9)), sems((2, 9)), sems((steps,)), sems((steps,)), sems((4,)),
+            sems((hops,)), sems((hops, 2)),
         ]
-        + ScatterSum.scratch(*fronts[0].shape[1:]) * sections
-        + ScatterSum.scratch(*back_shape[1:]) * sections
-        + [
-            sems((2 * sections, 9)), sems((2 * sections, 9)), sems((2 * sections, 2)), sems((2 * sections, 4)),
-            sems((2, 9)), sems((2, 9)), sems((steps,)), sems((steps,)), sems((4,)),
-        ],
+        + hop_scratch,
+        input_output_aliases={4 + len(parts): 0},
         compiler_params=pltpu.CompilerParams(
-            collective_id=1, has_side_effects=True, vmem_limit_bytes=62 * 2**20
+            collective_id=1, has_side_effects=True, vmem_limit_bytes=KERNEL_VMEM
         ),
         name="collect",
-    )(*acts, *grads, *fronts, *downs, small)
-    return out[0], out[1], out[2].reshape(-1, fronts[0].shape[2]), out[3].reshape(-1, back_shape[2]), out[4]
+    )(last, second, first_front, *parts, small, home)
 
 
 def norm_rows(hidden):
@@ -589,7 +897,7 @@
 
 
 def ff_forward_body(
-    hidden_ref, mask_ref, gain_ref, shift_ref, up_ref, bias_up_ref, down_ref, bias_down_ref,
+    spot, hidden_ref, mask_ref, gain_ref, shift_ref, up_ref, bias_up_ref, down_ref, bias_down_ref,
     act_ref, slope_ref, normed_out, out_ref, normed, total,
 ):
     step, last = pl.program_id(0), pl.num_programs(0) - 1
@@ -615,32 +923,30 @@
         out_ref[...] = (mask_ref[...] * (hidden + total[...] + bias_down_ref[...])).astype(BF16)
 
 
-def ff_forward(hidden, mask, gain, shift, up, bias_up, down, bias_down):
+def ff_forward(hidden, mask, gain, shift, up, bias_up, down, bias_down, guests, collective_id):
     rows, width = hidden.shape
     units = up.shape[1]
     size = width
     columns = pl.BlockSpec((rows, size), lambda i: (0, i))
-    return pl.pallas_call(
-        ff_forward_body,
-        grid=(units // size,),
-        in_specs=[
+    in_specs = ([
             whole((rows, width)), whole((rows, 1)), whole((1, width)), whole((1, width)),
             pl.BlockSpec((width, size), lambda i: (0, i)), pl.BlockSpec((1, size), lambda i: (0, i)),
             pl.BlockSpec((size, width), lambda i: (i, 0)), whole((1, width)),
-        ],
-        out_specs=[columns, columns, whole((rows, width)), whole((rows, width))],
-        out_shape=[
+        ])
+    out_specs = ([columns, columns, whole((rows, width)), whole((rows, width))])
+    out_shape = ([
             jax.ShapeDtypeStruct((rows, units), BF16), jax.ShapeDtypeStruct((rows, units), BF16),
             jax.ShapeDtypeStruct((rows, width), BF16), jax.ShapeDtypeStruct((rows, width), BF16),
-        ],
-        scratch_shapes=[pltpu.VMEM((rows, width), BF16), pltpu.VMEM((rows, width), F32)],
-        compiler_params=pltpu.CompilerParams(vmem_limit_bytes=KERNEL_VMEM),
-        name="ff_forward",
-    )(hidden, mask, gain, shift, up, bias_up, down, bias_down)
+        ])
+    scratch = ([pltpu.VMEM((rows, width), BF16), pltpu.VMEM((rows, width), F32)])
+    return hosted(
+        ff_forward_body, units // size, list(zip((hidden, mask, gain, shift, up, bias_up, down, bias_down), in_specs)), list(zip(out_shape, out_specs)), scratch,
+        guests, collective_id, "ff_forward",
+    )
 
 
 def ff_backward_body(
-    incoming_ref, mask_ref, hidden_ref, normed_ref, act_ref, slope_ref, up_ref, down_ref, gain_ref,
+    spot, incoming_ref, mask_ref, hidden_ref, normed_ref, act_ref, slope_ref, up_ref, down_ref, gain_ref,
     up_grad, down_grad, out_ref, gain_grad, shift_grad, up_bias_grad, down_bias_grad,
     grad, normed_t, total,
 ):
@@ -668,36 +974,34 @@
         out_ref[...] = (grad[...].astype(F32) + grad_hidden).astype(BF16)
 
 
-def ff_backward(incoming, mask, hidden, normed, act, slope, up, down, gain):
+def ff_backward(incoming, mask, hidden, normed, act, slope, up, down, gain, guests, collective_id):
     rows, width = hidden.shape
     units, size = up.shape[1], width
     columns = pl.BlockSpec((rows, size), lambda i: (0, i))
     vector = jax.ShapeDtypeStruct((1, width), F32)
-    return pl.pallas_call(
-        ff_backward_body,
-        grid=(units // size,),
-        in_specs=[
+    in_specs = ([
             whole((rows, width)), whole((rows, 1)), whole((rows, width)), whole((rows, width)), columns, columns,
             pl.BlockSpec((width, size), lambda i: (0, i)), pl.BlockSpec((size, width), lambda i: (i, 0)),
             whole((1, width)),
-        ],
-        out_specs=[
+        ])
+    out_specs = ([
             pl.BlockSpec((16, width // 16, size), lambda i: (0, 0, i)),
             pl.BlockSpec((size * 32 // units, units // 32, width), lambda i: (i, 0, 0)),
             whole((rows, width)), whole((1, width)), whole((1, width)),
             pl.BlockSpec((1, size), lambda i: (0, i)), whole((1, width)),
-        ],
-        out_shape=[
+        ])
+    out_shape = ([
             jax.ShapeDtypeStruct((16, width // 16, units), BF16), jax.ShapeDtypeStruct((32, units // 32, width), BF16),
             jax.ShapeDtypeStruct((rows, width), BF16), vector, vector,
             jax.ShapeDtypeStruct((1, units), F32), vector,
-        ],
-        scratch_shapes=[
+        ])
+    scratch = ([
             pltpu.VMEM((rows, width), BF16), pltpu.VMEM((width, rows), BF16), pltpu.VMEM((rows, width), F32),
-        ],
-        compiler_params=pltpu.CompilerParams(vmem_limit_bytes=KERNEL_VMEM),
-        name="ff_backward",
-    )(incoming, mask, hidden, normed, act, slope, up, down, gain)
+        ])
+    return hosted(
+        ff_backward_body, units // size, list(zip((incoming, mask, hidden, normed, act, slope, up, down, gain), in_specs)), list(zip(out_shape, out_specs)), scratch,
+        guests, collective_id, "ff_backward",
+    )
 
 
 def lane_ids(shape):
@@ -756,21 +1060,19 @@
 
 
 def attention_forward_body(
-    hidden_ref, mask_ref, gain_ref, shift_ref, weight_ref, bias_ref, key_bias_ref, out_bias_ref,
+    spot, hidden_ref, mask_ref, gain_ref, shift_ref, weight_ref, bias_ref, key_bias_ref, out_bias_ref,
     normed_out, key_out, value_out, key_far_out, value_far_out, extended_out, attended_out, out_ref,
     normed, own, far, attended, keys, values, send, recv,
 ):
     step, last = pl.program_id(0), pl.num_programs(0) - 1
     rows, width = normed.shape
     pairs = width // PAIR
-    spot = Spot()
 
     def swaps():
         return [swap_with_mate(spot, own.at[j], far.at[j], send.at[j], recv.at[j]) for j in (0, 1)]
 
     @pl.when(step == 0)
     def _():
-        spot.greet_mate()
         unit, _ = norm_rows(hidden_ref[...].astype(F32))
         normed[...] = (unit * gain_ref[...] + shift_ref[...]).astype(BF16)
         normed_out[...] = normed[...]
@@ -821,7 +1123,9 @@
         out_ref[...] = (mask_ref[...] * (hidden_ref[...].astype(F32) + branch)).astype(BF16)
 
 
-def attention_forward(hidden, mask, gain, shift, weight, bias, key_bias, out_bias, collective_id):
+def attention_forward(
+    hidden, mask, gain, shift, weight, bias, key_bias, out_bias, guests, collective_id
+):
     rows, width = hidden.shape
     pairs = width // PAIR
     pair = lambda i: jnp.clip(i - 3, 0, pairs - 1)
@@ -829,32 +1133,28 @@
     block = pl.BlockSpec((1, rows, PAIR), lambda i: (pair(i), 0, 0))
     saved = jax.ShapeDtypeStruct((pairs, rows, PAIR), BF16)
     full = jax.ShapeDtypeStruct((rows, width), BF16)
-    return pl.pallas_call(
-        attention_forward_body,
-        grid=(pairs + 4,),
-        in_specs=[
+    in_specs = ([
             whole((rows, width)), whole((rows, 1)), whole((1, width)), whole((1, width)),
             pl.BlockSpec((width, width), lambda i: (0, part(i))),
             pl.BlockSpec((1, width), lambda i: (0, jnp.minimum(part(i), 2))),
             whole((2 * rows, 1)), whole((1, width)),
-        ],
-        out_specs=[whole((rows, width))] + [block] * 4
-        + [pl.BlockSpec((2, rows, PAIR), lambda i: (pair(i), 0, 0)), block, whole((rows, width))],
-        out_shape=[full] + [saved] * 4 + [
+        ])
+    out_specs = ([whole((rows, width))] + [block] * 4
+        + [pl.BlockSpec((2, rows, PAIR), lambda i: (pair(i), 0, 0)), block, whole((rows, width))])
+    out_shape = ([full] + [saved] * 4 + [
             jax.ShapeDtypeStruct((2 * pairs, rows, PAIR), BF16),
             jax.ShapeDtypeStruct((pairs, rows, PAIR), F32), full,
-        ],
-        scratch_shapes=[
+        ])
+    scratch = ([
             pltpu.VMEM((rows, width), BF16), pltpu.VMEM((3, pairs, rows, PAIR), BF16),
             pltpu.VMEM((2, pairs, rows, PAIR), BF16), pltpu.VMEM((pairs, rows, PAIR), BF16),
             pltpu.VMEM((2, 2 * rows, PAIR), BF16), pltpu.VMEM((2, 2 * rows, PAIR), BF16),
             pltpu.SemaphoreType.DMA((2,)), pltpu.SemaphoreType.DMA((2,)),
-        ],
-        compiler_params=pltpu.CompilerParams(
-            vmem_limit_bytes=KERNEL_VMEM, collective_id=collective_id, has_side_effects=True
-        ),
-        name="attention_forward",
-    )(hidden, mask, gain, shift, weight, bias, key_bias, out_bias)
+        ])
+    return hosted(
+        attention_forward_body, pairs + 4, list(zip((hidden, mask, gain, shift, weight, bias, key_bias, out_bias), in_specs)), list(zip(out_shape, out_specs)), scratch,
+        guests, collective_id, "attention_forward",
+    )
 
 
 def pair_backward(query_of, grad_of, out_of, keys, values, key_sums, value_sums, rows, save):
@@ -878,7 +1178,7 @@
 
 
 def attention_backward_body(
-    incoming_ref, mask_ref, hidden_ref, normed_ref, key_ref, value_ref, key_far_ref, value_far_ref,
+    spot, incoming_ref, mask_ref, hidden_ref, normed_ref, key_ref, value_ref, key_far_ref, value_far_ref,
     extended_ref, attended_ref, weight_ref, gain_ref, key_bias_ref,
     weight_grad, out_ref, gain_grad, shift_grad, query_bias_grad, value_bias_grad, out_bias_grad,
     grad, grad_out, attended, normed_t, total, grads, sent, arrived, keys, values, key_sums, value_sums,
@@ -887,14 +1187,12 @@
     step, last = pl.program_id(0), pl.num_programs(0) - 1
     rows, width = grad.shape
     pairs = width // PAIR
-    spot = Spot()
 
     def swap_of(p):
         return swap_with_mate(spot, sent.at[p], arrived.at[p], send.at[p], recv.at[p])
 
     @pl.when(step == 0)
     def _():
-        spot.greet_mate()
         grad_rows = mask_ref[...] * incoming_ref[...].astype(F32)
         grad[...] = grad_rows.astype(BF16)
         out_bias_grad[...] = jnp.sum(grad_rows, axis=0, keepdims=True)
@@ -961,31 +1259,28 @@
 
 def attention_backward(
     incoming, mask, hidden, normed, key, value, key_far, value_far, extended, attended, weight, gain, key_bias,
-    collective_id,
+    guests, collective_id,
 ):
     rows, width = hidden.shape
     pairs = width // PAIR
     pair = lambda i: jnp.minimum(i, pairs - 1)
     block = pl.BlockSpec((1, rows, PAIR), lambda i: (pair(i), 0, 0))
     vector = jax.ShapeDtypeStruct((1, width), F32)
-    return pl.pallas_call(
-        attention_backward_body,
-        grid=(pairs + 4,),
-        in_specs=[whole((rows, width)), whole((rows, 1)), whole((rows, width)), whole((rows, width))]
+    in_specs = ([whole((rows, width)), whole((rows, 1)), whole((rows, width)), whole((rows, width))]
         + [block] * 4
         + [
             pl.BlockSpec((2, rows, PAIR), lambda i: (pair(i), 0, 0)), block,
             pl.BlockSpec((width, width), lambda i: (0, jnp.where(i < pairs, 3, jnp.minimum(i - pairs, 2)))),
             whole((1, width)), whole((2 * rows, 1)),
-        ],
-        out_specs=[
+        ])
+    out_specs = ([
             pl.BlockSpec((16, width // 16, width), lambda i: (0, 0, jnp.maximum(i - pairs, 0))),
             whole((rows, width)),
-        ] + [whole((1, width))] * 5,
-        out_shape=[
+        ] + [whole((1, width))] * 5)
+    out_shape = ([
             jax.ShapeDtypeStruct((16, width // 16, 4 * width), BF16), jax.ShapeDtypeStruct((rows, width), BF16),
-        ] + [vector] * 5,
-        scratch_shapes=[
+        ] + [vector] * 5)
+    scratch = ([
             pltpu.VMEM((rows, width), BF16), pltpu.VMEM((pairs, rows, PAIR), BF16),
             pltpu.VMEM((pairs, rows, PAIR), BF16), pltpu.VMEM((width, rows), BF16),
             pltpu.VMEM((rows, width), F32), pltpu.VMEM((3, pairs, rows, PAIR), BF16),
@@ -993,13 +1288,10 @@
             pltpu.VMEM((2, 2 * rows, PAIR), BF16), pltpu.VMEM((2, 2 * rows, PAIR), BF16),
             pltpu.VMEM((2, 2 * rows, PAIR), F32), pltpu.VMEM((2, 2 * rows, PAIR), F32),
             pltpu.SemaphoreType.DMA((pairs,)), pltpu.SemaphoreType.DMA((pairs,)),
-        ],
-        compiler_params=pltpu.CompilerParams(
-            vmem_limit_bytes=KERNEL_VMEM, collective_id=collective_id, has_side_effects=True
-        ),
-        name="attention_backward",
-    )(
-        incoming, mask, hidden, normed, key, value, key_far, value_far, extended, attended, weight, gain, key_bias
+        ])
+    return hosted(
+        attention_backward_body, pairs + 4, list(zip((incoming, mask, hidden, normed, key, value, key_far, value_far, extended, attended, weight, gain, key_bias), in_specs)), list(zip(out_shape, out_specs)), scratch,
+        guests, collective_id, "attention_backward",
     )
 
 
@@ -1029,64 +1321,141 @@
     key_bias = jnp.where(jnp.concatenate([own_rows, far_rows]), 0.0, MASKED)[:, None]
 
     norms = jnp.concatenate([norm_gain, norm_shift, jnp.zeros((6, width), F32)], axis=0)
-    fronts, downs, norm_all = gather_weights(w_front[0], w_back[0], norms)
+    first_front, norm_all, owns = first_weights(w_front[0], w_back[0], norms)
+    fronts, downs = [first_front.reshape(width, -1)] + [None] * (sections - 1), [None] * 2
+    front_shape = first_front.shape
+    down_shape = (32, w_back.shape[1] // 16, width)
     gains, shifts = norm_all[:, 0], norm_all[:, 1]
 
     hidden = (clip_pair[0].astype(F32) * row_mask).astype(BF16)
     row = lambda a: a.reshape(1, -1)
-    saved, delivered = [], []
+    acts_home = jnp.zeros((clip_inputs.shape[0], padded, width), BF16)
+    grads_home = jnp.zeros((clip_inputs.shape[0], 2 * rows, width), BF16)
+    saved, acts = [], []
+    acts_beside = {
+        ("f", 1): [(0, 0, 112)], ("f", 2): [(0, 112, 496), (1, 0, 128)], ("f", 3): [(1, 128, 320), (2, 0, 288)],
+        ("b", 3): [(1, 448, 160), (2, 288, 320), (3, 0, 192)], ("b", 2): [(3, 192, 416)],
+    }
+    grads_beside = {("b", 1): [(3, 0, 400)], ("b", 0): [(3, 400, 208), (1, 0, rows), (2, 0, 192)]}
+
+    def travel(where, held, plan, home):
+        steps = 9 if where[1] % 2 == 0 else 3
+        return deliver_guest([(held[s], s, start, size) for s, start, size in plan[where]], home, steps)
+
     for s in range(sections):
         layer = s // 2
         gain, shift = row(gains[s]), row(shifts[s])
+        guests = []
+        if s == 0:
+            guests.append(plane_gather_guest([(owns["front", 1], 0, 0)], [front_shape], [(0, 5, 7)]))
+            guests.append(spread_gather_guest(
+                [(owns["back", 0], 0, (0, 4), (6, 9, 9), 0), (owns["back", 1], 1, (0,), (4, 8, 9), 16)], down_shape
+            ))
+        elif s == 2:
+            parts = [(owns["front", 3], 0, 0), (owns["back", 2], 1, 0), (owns["back", 3], 1, 16)]
+            guests.append(plane_gather_guest(parts, [front_shape, down_shape], [(0, 5, 8), (0, 7, 9), (0, 8, 9)]))
+        elif s == 1:
+            guests.append(plane_gather_guest([(owns["front", 2], 0, 0)], [front_shape], [(0, 3, 3)]))
+        onward = {0: [("front", 2), ("front", 3), ("back", 2), ("back", 3)], 1: [("front", 3), ("back", 3)]}.get(s, [])
+        if onward:
+            hops = [(i, key[1], 2 + s, "both") for i, key in enumerate(onward)]
+            if s == 0:
+                hops.insert(0, (0, 2, 1, "up"))
+            guests.append(spread_hop_guest([owns[key] for key in onward], hops))
+        if s:
+            guests.append(travel(("f", s), acts, acts_beside, acts_home))
         if s % 2 == 0:
             pair = bias_query_value[layer]
             bias = jnp.concatenate([pair[:width], jnp.zeros((width,), F32), pair[width:]])
-            *kept, leaving = attention_forward(
-                hidden, row_mask, gain, shift, fronts[s], row(bias), key_bias, row(bias_attn_out[layer]), 2 + s
+            (*kept, leaving), carried = attention_forward(
+                hidden, row_mask, gain, shift, fronts[s], row(bias), key_bias, row(bias_attn_out[layer]),
+                guests, 2 + s,
             )
         else:
-            *kept, leaving = ff_forward(
-                hidden, row_mask, gain, shift, fronts[s], row(bias_up[layer]), downs[layer], row(bias_down[layer])
+            (*kept, leaving), carried = ff_forward(
+                hidden, row_mask, gain, shift, fronts[s], row(bias_up[layer]), downs[layer], row(bias_down[layer]),
+                guests, 2 + s,
             )
+        if s:
+            (acts_home,) = carried[-1]
+        if s == 0:
+            fronts[1], downs[0] = carried[0][0].reshape(width, -1), carried[1][-1].reshape(-1, width)
+        elif s == 2:
+            fronts[3], downs[1] = carried[0][0].reshape(width, -1), carried[0][1].reshape(-1, width)
+        elif s == 1:
+            fronts[2] = carried[0][0].reshape(width, -1)
+        if onward:
+            owns.update(zip(onward, carried[2 - s]))
         saved.append((hidden, *kept))
         hidden = leaving
-        delivered.append(leaving)
+        acts.append(leaving)
 
     incoming = clip_pair[1]
-    sent_grads, grad_fronts, grad_downs = [None] * sections, [None] * sections, [None] * 2
+    input_grads, grad_fronts, grad_downs = [None] * sections, [None] * sections, [None] * 2
     grad_gain, grad_shift = [None] * sections, [None] * sections
     query_sums, value_sums, out_sums, up_sums, down_sums = ([None] * 2 for _ in range(5))
+    plane_stages = {
+        2: ((0, 1, 4, 8), (0, 2, 6, 9), (0, 2, 7, 9)), 1: ((0, 1, 3, 3),), 0: ((0, 1, 4, 8), (0, 2, 6, 9), (0, 2, 7, 9)),
+    }
     for s in reversed(range(sections)):
         layer, gain = s // 2, row(gains[s])
+        guests = []
+        if s < 3:
+            jobs = [(grad_fronts[s + 1], 0)]
+            if s % 2 == 0:
+                jobs += [(grad_downs[layer], 0), (grad_downs[layer], 16)]
+            guests.append(plane_sum_guest(jobs, plane_stages[s]))
+        if s < 2:
+            hops = {1: [(3, 0), (2, 0), (3, 0)], 0: [(3, 1), (2, 1), (3, 1), (2, 0)]}[s]
+            guests.append(section_hop_guest([(part, target, done + 1) for part, (target, done) in zip(passing, hops)]))
+        if ("b", s) in acts_beside:
+            guests.append(travel(("b", s), acts, acts_beside, acts_home))
+        else:
+            guests.append(travel(("b", s), input_grads, grads_beside, grads_home))
         if s % 2 == 0:
             entered, normed, key, value, key_far, value_far, extended, attended = saved[s]
             (
                 grad_fronts[s], incoming, grad_gain[s], grad_shift[s],
                 query_sums[layer], value_sums[layer], out_sums[layer],
-            ) = attention_backward(
+            ), carried = attention_backward(
                 incoming, row_mask, entered, normed, key, value, key_far, value_far, extended, attended,
-                fronts[s], gain, key_bias, 3 + s,
+                fronts[s], gain, key_bias, guests, 6 + s,
             )
         else:
             entered, act, slope, normed = saved[s]
             (
                 grad_fronts[s], grad_downs[layer], incoming, grad_gain[s], grad_shift[s],
                 up_sums[layer], down_sums[layer],
-            ) = ff_backward(incoming, row_mask, entered, normed, act, slope, fronts[s], downs[layer], gain)
-        sent_grads[s] = incoming
+            ), carried = ff_backward(
+                incoming, row_mask, entered, normed, act, slope, fronts[s], downs[layer], gain, guests, 6 + s
+            )
+        input_grads[s] = incoming
+        if ("b", s) in acts_beside:
+            (acts_home,) = carried[-1]
+        else:
+            (grads_home,) = carried[-1]
+        if s == 2:
+            passing = carried[0]
+        elif s == 1:
+            passing = [*carried[1], *carried[0]]
+        elif s == 0:
+            (front_3, back_2, back_3, front_2), (front_1, back_0, back_1) = carried[1], carried[0]
 
     pair_sums = [jnp.concatenate([q, v], axis=1) for q, v in zip(query_sums, value_sums)]
     small = jnp.concatenate(
         [v.reshape(-1) for v in grad_gain + grad_shift + pair_sums + out_sums + up_sums + down_sums]
     )
-    acts_out, grads_out, front_out, back_out, small = collect(
-        delivered, sent_grads, grad_fronts, grad_downs, small.reshape(-1, 128), padded
-    )
+    grads_home, front_out, back_out, small = collect(
+        input_grads[0], input_grads[2], grads_home, grad_fronts[0],
+        [front_3, back_3, front_2, back_2, front_1, back_0, back_1], small.reshape(-1, 128),
+    )
+    front_out = front_out.reshape(width, -1)
+    back_out = back_out.reshape(-1, width)
     small = small.reshape(-1)
     for bit in spot.spare_bits:
         small = small + swap(small, bit)
         front_out, back_out = add(front_out, swap(front_out, bit)), add(back_out, swap(back_out, bit))
-    grads_out = jnp.pad(grads_out.astype(F32), ((0, 0), (0, padded - 2 * rows), (0, 0)))
+    grads_out = jnp.pad(grads_home.astype(F32), ((0, 0), (0, padded - 2 * rows), (0, 0)))
     parts, place_at = [], 0
     layers, hidden_units = bias_up.shape
     for count, size in (
@@ -1096,7 +1465,7 @@
         parts.append(small[place_at : place_at + count * size].reshape(count, size))
         place_at += count * size
     return (
-        acts_out[None],
+        acts_home[None],
         grads_out[None],
         front_out.astype(F32)[None],
         back_out.astype(F32)[None],

time: 774 us -> 639 us (0.83)
  Pallas kernels: 721 us -> 576 us
  local copies, waits for them, and re-layouts: 22 us -> 32 us
    pallas_call x10, Pallas kernels: 721 us -> 576 us  [the longest x8 405 us: hosted(): pl.pallas_call(kernel, grid=(grid,), in_specs=[s for _, s in operands + g...]
  transfers between devices with their start and end apart: 2 -> 2, of which waited for: 0 -> 0; matrix products, arithmetic and copies ran while one was open for 1% -> 2% of each run, Pallas kernels for 22% -> 5%
where the time goes in v4:
time: 639 us; the launch traced here: 635 us
  Pallas kernels  576 us (90%)
  local copies, waits for them, and re-layouts  32 us (5%)
  other arithmetic  23.4 us (4%)
    pallas_call x8, Pallas kernels, hosted(): pl.pallas_call(kernel, grid=(grid,), in_specs=[s for _, s in operands + g...  405 us
    pallas_call x1, Pallas kernels, collect(): pl.pallas_call(collect_body, in_specs=[hbm] * 3 + [vmem] * (len(parts) +...  141 us
    pallas_call x1, Pallas kernels, first_weights(): pl.pallas_call(first_weights_body, in_specs=[hbm] * (2 + len(begun)), out...  30.3 us
  transfers between devices with their start and end apart: 2, of which 0 were waited for; matrix products, arithmetic and copies ran while one was open for 2% of the time, Pallas kernels for 5%

profile of v4, /device:TPU:0, one launch (start us, length us, event | category | flops | bytes accessed | tf_op | source)
XLA Modules:
  0.0 635.1 jit_solution(7017560206269474762)
XLA Ops:
  0.6 0.0 copy-start
  0.7 2.5 constant_dynamic-slice_fusion.4
  3.2 0.0 copy-start.3
  3.3 0.0 copy-start.29
  3.3 1.2 copy-done.3
  4.5 1.4 fusion
  5.9 0.5 collective-permute-start
  6.3 0.6 dynamic_slice.33
  7.6 0.1 collective-permute-start.1
  7.7 1.1 constant_dynamic-slice_fusion.3.refs_0_
  8.9 0.9 copy.47.refs_2_
  9.7 0.8 copy.50.refs_5_
  10.6 0.8 copy.51.refs_6_
  11.4 0.0 copy-start.4
  11.4 0.7 copy.49.refs_4_
  12.2 0.7 copy.52.refs_7_
  12.9 0.7 copy.53.refs_8_
  13.6 0.1 pad.20.clone
  13.7 0.7 maximum_maximum_fusion.refs_1_
  14.3 30.3 %first_weights.1 = (bf16[16,48,3072]{2,1,0:T(8,128)(2,1)}, f32[4,8,768]{2,1,0:T(8,128)}, bf16[2,48,3072]{2,1,0:T(8,128)(2,1)}, bf16[2,96,768]{2,1,0:T(8,128)(2,1...) custom-call(bf16[2,48,3072]{2,1,0:T(8,128)(2,1)} %copy-done.6, ...), custom_call_target="tpu_custom_call", output_to_operand_aliasing={{2}: (2, {}), {3}: (3, {}), {4}: (4, {}), {5}: (5, {}), {6}... | custom-call | tf_op jit(solution)/shard_map/first_weights/pallas_call | solution.py:297
  44.7 1.5 slice_bitcast_fusion.2
  46.2 0.6 fusion.12
  46.8 0.6 fusion.11
  47.5 0.6 fusion.10
  48.1 0.6 reshape.212.refs_5_
  48.7 0.6 reshape.216.refs_5_
  49.4 0.5 slice.144
  50.6 0.1 pad_add_fusion
  50.7 0.3 copy.46
  51.0 0.8 fusion.4.refs_1_
  51.8 0.9 broadcast_select_fusion.refs_6_.refs_12_
  52.7 1.6 fusion.2
  54.3 1.0 slice_bitcast_fusion.1.refs_0_
  55.3 1.1 fusion.3.refs_0_.refs_2_
  56.4 74.1 %attention_forward.2 = (bf16[608,768]{1,0:T(8,128)(2,1)}, bf16[6,608,128]{2,1,0:T(8,128)(2,1)}, bf16[6,608,128]{2,1,0:T(8,128)(2,1)}, bf16[6,608,128]{2,1,0:T(8,...) custom-call(bf16[608,768]{1,0:T(8,128)(2,1)} %fusion.3.refs_0_.refs_, ...), custom_call_target="tpu_custom_call", output_to_operand_aliasing={{9}: (9, {}), {10}: (10, {}), {12}: (11, {}), {13}: (12, {}... | custom-call | tf_op jit(solution)/shard_map/attention_forward/pallas_call | solution.py:402
  130.5 2.1 broadcast_in_dim.37.refs_12_
  132.6 39.5 %ff_forward.2 = (bf16[608,3072]{1,0:T(8,128)(2,1)}, bf16[608,3072]{1,0:T(8,128)(2,1)}, bf16[608,768]{1,0:T(8,128)(2,1)}, bf16[608,768]{1,0:T(8,128)(2,1)}, bf16[...) custom-call(bf16[608,768]{1,0:T(8,128)(2,1)} %get-tuple-element.116., ...), custom_call_target="tpu_custom_call", output_to_operand_aliasing={{5}: (9, {}), {6}: (10, {}), {7}: (12, {})} | custom-call | tf_op jit(solution)/shard_map/ff_forward/pallas_call | solution.py:402
  172.1 57.5 %attention_forward.3 = (bf16[608,768]{1,0:T(8,128)(2,1)}, bf16[6,608,128]{2,1,0:T(8,128)(2,1)}, bf16[6,608,128]{2,1,0:T(8,128)(2,1)}, bf16[6,608,128]{2,1,0:T(8,...) custom-call(bf16[608,768]{1,0:T(8,128)(2,1)} %get-tuple-element.122., ...), custom_call_target="tpu_custom_call", output_to_operand_aliasing={{10}: (13, {})} | custom-call | tf_op jit(solution)/shard_map/attention_forward/pallas_call | solution.py:402
  229.6 25.6 %ff_forward.3 = (bf16[608,3072]{1,0:T(8,128)(2,1)}, bf16[608,3072]{1,0:T(8,128)(2,1)}, bf16[608,768]{1,0:T(8,128)(2,1)}, bf16[608,768]{1,0:T(8,128)(2,1)}, bf16[2,1280,768]{2,1,0:T(8,128)(2,1)}) custom-call(bf16[608,768]{1,0:T(8,128)(2,1)} %get-tuple-element.128.refs_0_.refs_9_.refs_2_.refs_10_, ...), custom_call_target="tpu_custom_call", output_to_operand_aliasing={{4}: (10, {})} | custom-call | tf_op jit(solution)/shard_map/ff_forward/pallas_call | solution.py:402
  255.1 32.6 %ff_backward.2 = (bf16[16,48,3072]{2,1,0:T(8,128)(2,1)}, bf16[32,96,768]{2,1,0:T(8,128)(2,1)}, bf16[608,768]{1,0:T(8,128)(2,1)}, f32[1,768]{1,0:T(1,128)}, f32[1...) custom-call(bf16[608,768]{1,0:T(8,128)(2,1)} %slice_bitcast_fusion.1, ...), custom_call_target="tpu_custom_call", output_to_operand_aliasing={{7}: (12, {})} | custom-call | tf_op jit(solution)/shard_map/ff_backward/pallas_call | solution.py:402
  287.8 69.1 %attention_backward.2 = (bf16[16,48,3072]{2,1,0:T(8,128)(2,1)}, bf16[608,768]{1,0:T(8,128)(2,1)}, f32[1,768]{1,0:T(1,128)}, f32[1,768]{1,0:T(1,128)}, f32[1,768]...) custom-call(bf16[608,768]{1,0:T(8,128)(2,1)} %get-tuple-element.137., ...), custom_call_target="tpu_custom_call", output_to_operand_aliasing={{10}: (16, {})} | custom-call | tf_op jit(solution)/shard_map/attention_backward/pallas_call | solution.py:402
  356.8 2.1 broadcast_in_dim.39.refs_14_
  359.0 46.2 %ff_backward.3 = (bf16[16,48,3072]{2,1,0:T(8,128)(2,1)}, bf16[32,96,768]{2,1,0:T(8,128)(2,1)}, bf16[608,768]{1,0:T(8,128)(2,1)}, f32[1,768]{1,0:T(1,128)}, f32[1...) custom-call(bf16[608,768]{1,0:T(8,128)(2,1)} %get-tuple-element.149., ...), custom_call_target="tpu_custom_call", output_to_operand_aliasing={{11}: (14, {})} | custom-call | tf_op jit(solution)/shard_map/ff_backward/pallas_call | solution.py:402
  405.3 60.4 %attention_backward.3 = (bf16[16,48,3072]{2,1,0:T(8,128)(2,1)}, bf16[608,768]{1,0:T(8,128)(2,1)}, f32[1,768]{1,0:T(1,128)}, f32[1,768]{1,0:T(1,128)}, f32[1,768]...) custom-call(bf16[608,768]{1,0:T(8,128)(2,1)} %get-tuple-element.157., ...), custom_call_target="tpu_custom_call", output_to_operand_aliasing={{14}: (22, {})} | custom-call | tf_op jit(solution)/shard_map/attention_backward/pallas_call | solution.py:402
  465.7 0.7 reduce.4
  466.5 0.7 reduce.8
  467.3 0.7 reduce.14
  468.2 0.7 maximum_reduce_fusion
  469.1 0.0 copy-start.9
  469.1 0.6 copy-done.9
  469.8 140.7 %collect.1 = (bf16[2,1216,768]{2,1,0:T(8,128)(2,1)}, bf16[16,48,3072]{2,1,0:T(8,128)(2,1)}, bf16[16,96,768]{2,1,0:T(8,128)(2,1)}, f32[144,128]{1,0:T(8,128)}) custom-call(bf16[608,768]{1,0:T(8,128)(2,1)} %get-tuple-element.172.refs_0_, bf16[608,768]{1,0:T(8,128)(2,1)} %get-tuple-element.149.refs_0_.refs_21_.refs_1_, ...), custom_call_target="tpu_custom_call", output_to_operand_aliasing={{0}: (11, {})} | custom-call | tf_op jit(solution)/shard_map/collect/pallas_call | solution.py:830
  610.4 0.7 fusion.9
  611.2 0.8 slice.180
  611.9 0.7 fusion.8
  612.6 7.5 %bitcast_convert_fusion = f32[1,768,3072]{2,1,0:T(8,128)} fusion(bf16[1,768,3072]{2,1,0:T(8,128)(2,1)} %bitcast.62), kind=kLoop, calls=%fused_computation | loop fusion | flops 2359296 | bytes 14155776 | tf_op jit(solution)/shard_map/convert_element_type | solution.py:1470
  620.2 3.8 bitcast_convert_fusion.1
  624.0 2.5 bitcast_convert_fusion.2
  626.6 0.6 constant_dynamic-slice_fusion
  627.2 0.6 constant_dynamic-slice_fusion.1
  627.7 0.6 reshape.238
  628.3 0.6 reshape.240
  629.0 0.6 reshape.239
  629.6 0.6 reshape.241
  630.2 4.4 copy.87
  (95 shorter events, 0.5 us)
Async XLA Ops:
  0.6 10.7 %copy-start = (bf16[1,1536,768]{2,1,0:T(8,128)(2,1)S(1)}, bf16[1,1536,768]{2,1,0:T(8,128)(2,1)}, u32[]{:S(2)}) copy-start(bf16[1,1536,768]{2,1,0:T(8,128)(2,1)} %param.15) | copy-start | bytes 7077892
  3.2 1.3 copy-start.3
  3.3 2.6 copy-start.5
  3.3 3.1 copy-start.29
  5.9 7.8 %copy-start.27 = (f32[1,768]{1,0:T(1,128)S(1)}, f32[1,768]{1,0:T(1,128)}, u32[]{:S(2)}) copy-start(f32[1,768]{1,0:T(1,128)} %param.17) | copy-start | bytes 9220
  5.9 7.8 %copy-start.28 = (f32[1,768]{1,0:T(1,128)S(1)}, f32[1,768]{1,0:T(1,128)}, u32[]{:S(2)}) copy-start(f32[1,768]{1,0:T(1,128)} %param.16) | copy-start | bytes 9220
  5.9 46.8 %collective-permute-start = (bf16[2,608,768]{2,1,0:T(8,128)(2,1)}, bf16[2,608,768]{2,1,0:T(8,128)(2,1)}, u32[]{:S(2)}, u32[]{:S(2)}) collective-permute-start(bf16[2,608,768]{2,1,0:T(8,128)(2,1)} %fusion), channel_id=1, source_target_pairs={{0,1},{1,0},{2,3},{3,2},{4,5},{5,4},{6,7},{7,6},{8,9},{9,8},{10,11... | collective-permute-start | bytes 5603336 | tf_op jit(solution)/shard_map/ppermute | solution.py:37
  7.6 41.8 %collective-permute-start.1 = (f32[8,128]{1,0:T(8,128)S(1)}, f32[8,128]{1,0:T(8,128)S(1)}, u32[]{:S(2)}, u32[]{:S(2)}) collective-permute-start(f32[8,128]{1,0:T(8,128)S(1)} %broadcast_in_dim.33), channel_id=1, source_target_pairs={{0,1},{1,0},{2,3},{3,2},{4,5},{5,4},{6,7},{7,6},{8,9},{9,8},{10,11... | collective-permute-start | bytes 12296 | tf_op jit(solution)/shard_map/ppermute | solution.py:37
  8.8 5.5 copy-start.6
  10.6 35.6 %copy-start.11 = (f32[2,1536]{1,0:T(2,128)S(1)}, f32[2,1536]{1,0:T(2,128)}, u32[]{:S(2)}) copy-start(f32[2,1536]{1,0:T(2,128)} %param.18) | copy-start | bytes 36868
  10.6 35.7 %copy-start.14 = (f32[2,768]{1,0:T(2,128)S(1)}, f32[2,768]{1,0:T(2,128)}, u32[]{:S(2)}) copy-start(f32[2,768]{1,0:T(2,128)} %param.19) | copy-start | bytes 18436
  10.6 36.3 %copy-start.15 = (f32[2,768]{1,0:T(2,128)S(1)}, f32[2,768]{1,0:T(2,128)}, u32[]{:S(2)}) copy-start(f32[2,768]{1,0:T(2,128)} %param.21) | copy-start | bytes 18436
  10.6 36.9 %copy-start.10 = (f32[2,3072]{1,0:T(2,128)S(1)}, f32[2,3072]{1,0:T(2,128)}, u32[]{:S(2)}) copy-start(f32[2,3072]{1,0:T(2,128)} %param.20) | copy-start | bytes 73732
  11.4 2.9 copy-start.7
  11.4 41.3 %copy-start.4 = (bf16[1,1280,768]{2,1,0:T(8,128)(2,1)S(1)}, bf16[1,1280,768]{2,1,0:T(8,128)(2,1)}, u32[]{:S(2)}) copy-start(bf16[1,1280,768]{2,1,0:T(8,128)(2,1)} %copy-done.3) | copy-start | bytes 5898244
  405.2 61.3 %copy-start.26 = (f32[1,768]{1,0:T(1,128)S(1)}, f32[1,768]{1,0:T(1,128)}, u32[]{:S(2)}) copy-start(f32[1,768]{1,0:T(1,128)} %get-tuple-element.182) | copy-start | bytes 9220
  405.2 61.3 %copy-start.23 = (f32[1,768]{1,0:T(1,128)S(1)}, f32[1,768]{1,0:T(1,128)}, u32[]{:S(2)}) copy-start(f32[1,768]{1,0:T(1,128)} %get-tuple-element.183) | copy-start | bytes 9220
  405.2 61.3 %copy-start.20 = (f32[1,768]{1,0:T(1,128)S(1)}, f32[1,768]{1,0:T(1,128)}, u32[]{:S(2)}) copy-start(f32[1,768]{1,0:T(1,128)} %get-tuple-element.184) | copy-start | bytes 9220
  405.2 62.0 %copy-start.25 = (f32[1,768]{1,0:T(1,128)S(1)}, f32[1,768]{1,0:T(1,128)}, u32[]{:S(2)}) copy-start(f32[1,768]{1,0:T(1,128)} %get-tuple-element.186) | copy-start | bytes 9220
  405.2 62.0 %copy-start.22 = (f32[1,768]{1,0:T(1,128)S(1)}, f32[1,768]{1,0:T(1,128)}, u32[]{:S(2)}) copy-start(f32[1,768]{1,0:T(1,128)} %get-tuple-element.187) | copy-start | bytes 9220
  405.2 62.1 %copy-start.19 = (f32[1,768]{1,0:T(1,128)S(1)}, f32[1,768]{1,0:T(1,128)}, u32[]{:S(2)}) copy-start(f32[1,768]{1,0:T(1,128)} %get-tuple-element.188) | copy-start | bytes 9220
  405.2 62.8 %copy-start.21 = (f32[1,768]{1,0:T(1,128)S(1)}, f32[1,768]{1,0:T(1,128)}, u32[]{:S(2)}) copy-start(f32[1,768]{1,0:T(1,128)} %get-tuple-element.194) | copy-start | bytes 9220
  405.2 62.8 %copy-start.24 = (f32[1,768]{1,0:T(1,128)S(1)}, f32[1,768]{1,0:T(1,128)}, u32[]{:S(2)}) copy-start(f32[1,768]{1,0:T(1,128)} %get-tuple-element.197) | copy-start | bytes 9220
  405.3 62.8 %copy-start.18 = (f32[1,768]{1,0:T(1,128)S(1)}, f32[1,768]{1,0:T(1,128)}, u32[]{:S(2)}) copy-start(f32[1,768]{1,0:T(1,128)} %get-tuple-element.198) | copy-start | bytes 9220
  405.3 62.9 %copy-start.16 = (f32[1,768]{1,0:T(1,128)S(1)}, f32[1,768]{1,0:T(1,128)}, u32[]{:S(2)}) copy-start(f32[1,768]{1,0:T(1,128)} %get-tuple-element.191) | copy-start | bytes 9220
  405.3 62.9 %copy-start.17 = (f32[1,768]{1,0:T(1,128)S(1)}, f32[1,768]{1,0:T(1,128)}, u32[]{:S(2)}) copy-start(f32[1,768]{1,0:T(1,128)} %get-tuple-element.192) | copy-start | bytes 9220
  405.3 63.8 %copy-start.13 = (f32[1,3072]{1,0:T(1,128)S(1)}, f32[1,3072]{1,0:T(1,128)}, u32[]{:S(2)}) copy-start(f32[1,3072]{1,0:T(1,128)} %get-tuple-element.195) | copy-start | bytes 36868
  405.3 63.8 %copy-start.12 = (f32[1,3072]{1,0:T(1,128)S(1)}, f32[1,3072]{1,0:T(1,128)}, u32[]{:S(2)}) copy-start(f32[1,3072]{1,0:T(1,128)} %get-tuple-element.196) | copy-start | bytes 36868
  469.1 0.6 copy-start.9
  612.6 7.5 %copy-start.2 = (bf16[2,1216,768]{2,1,0:T(8,128)(2,1)S(1)}, bf16[2,1216,768]{2,1,0:T(8,128)(2,1)}, u32[]{:S(2)}) copy-start(bf16[2,1216,768]{2,1,0:T(8,128)(2,1)} %get-tuple-element.200) | copy-start | bytes 11206660
  620.2 3.8 copy-start.8
  630.2 4.4 copy-start.1

commit v5 on v4

--- a/solution.py
+++ b/solution.py
@@ -150,164 +150,6 @@
             copies[name].wait_send()
         for name in ("m", "mx", "my", "md0", "md1"):
             arrivals[name].wait_recv()
-
-
-class SpreadHop:
-    def __init__(self, spot, own, source, hop, send, recv, ways="both"):
-        self.spot, self.own, self.send, self.recv = spot, own, send, recv
-        self.up_from = source + hop - 1 if source + hop < spot.sections and ways != "down" else None
-        self.down_from = source - hop + 1 if source - hop >= 0 and ways != "up" else None
-
-    def copies(self):
-        s, spot = self, self.spot
-        return (
-            remote(s.own, s.own, s.send.at[0], s.recv, spot.above),
-            remote(s.own, s.own, s.send.at[1], s.recv, spot.below),
-        )
-
-    def start(self, upwards=True, downwards=True):
-        up, down = self.copies()
-        if upwards and self.up_from is not None:
-            pl.when(self.spot.z == self.up_from)(up.start)
-        if downwards and self.down_from is not None:
-            pl.when(self.spot.z == self.down_from)(down.start)
-
-    def arrive(self):
-        up, _ = self.copies()
-        if self.up_from is not None:
-            pl.when(self.spot.z == self.up_from + 1)(up.wait_recv)
-        if self.down_from is not None:
-            pl.when(self.spot.z == self.down_from - 1)(up.wait_recv)
-
-    def leave(self):
-        up, down = self.copies()
-        if self.up_from is not None:
-            pl.when(self.spot.z == self.up_from)(up.wait_send)
-        if self.down_from is not None:
-            pl.when(self.spot.z == self.down_from)(down.wait_send)
-
-    def finish(self):
-        self.arrive()
-        self.leave()
-
-
-def hops_from(source, sections):
-    return max(source, sections - 1 - source)
-
-
-COLUMN_CHUNKS = 4
-BEGUN = (
-    ("front", 1, 2, "both"), ("back", 0, 1, "both"), ("back", 1, 1, "both"), ("front", 2, 1, "down"),
-    ("front", 3, 1, "both"), ("back", 2, 1, "both"), ("back", 3, 1, "both"),
-)
-
-
-def first_weights_body(*refs):
-    refs_list = list(refs)
-    take = lambda n: [refs_list.pop(0) for _ in range(n)]
-    own_in, norms, _ = take(1)[0], take(1)[0], take(len(BEGUN))
-    front, norm_all, owns = take(1)[0], take(1)[0], take(len(BEGUN))
-    own, own_sem, norm_send, norm_recv, zsend, zrecv, psend, precv, stay_sem, bsend, brecv = take(11)
-    spot = Spot()
-    load = pltpu.make_async_copy(own_in, own, own_sem)
-    load.start()
-    load.wait()
-    spot.greet()
-    size = own.shape[2] // COLUMN_CHUNKS
-    hops, gathers, stays = [], [], []
-    for j in range(COLUMN_CHUNKS):
-        at = pl.ds((j + 1) % COLUMN_CHUNKS * size, size)
-        piece = own.at[:, :, at]
-        hops.append([SpreadHop(spot, piece, 0, hop, zsend.at[j, hop - 1], zrecv.at[j, hop - 1]) for hop in (1, 2, 3)])
-        gathers.append(PlaneGather(spot, front.at[:, :, at], psend.at[j], precv.at[j]))
-        stays.append(
-            pltpu.make_async_copy(piece, gathers[j].dst.at[gathers[j].blocks(spot.core, spot.c)], stay_sem.at[j])
-        )
-        hops[j][0].start()
-        if j == 0:
-            norm_copies = [
-                remote(
-                    norms, norm_all.at[spot.z], norm_send.at[step], norm_recv.at[step],
-                    {"section": (spot.z + step) % spot.sections},
-                )
-                for step in range(1, spot.sections)
-            ]
-            norm_copies.append(pltpu.make_async_copy(norms, norm_all.at[spot.z], norm_send.at[0]))
-            for copy in norm_copies:
-                copy.start()
-    begun, count = [], 0
-    for held, (_, source, made, ways) in zip(owns, BEGUN):
-        begun.append([
-            SpreadHop(
-                spot, held, source, hop + 1, bsend.at[count + hop], brecv.at[count + hop], "both" if hop else ways
-            )
-            for hop in range(made)
-        ])
-        count += made
-    for chain in begun:
-        chain[0].start(upwards=False)
-    begun[5][0].start(downwards=False)
-    for j in range(COLUMN_CHUNKS):
-        for hop in range(3):
-            hops[j][hop].arrive()
-            if hop < 2:
-                hops[j][hop + 1].start()
-        gathers[j].begin(own.at[:, :, pl.ds((j + 1) % COLUMN_CHUNKS * size, size)])
-        stays[j].start()
-    for chain in begun[:5] + begun[6:]:
-        chain[0].start(downwards=False)
-    for j in range(COLUMN_CHUNKS):
-        gathers[j].second()
-    begun[0][0].arrive()
-    begun[0][1].start()
-    for gather in gathers:
-        gather.third()
-    for chain in begun[1:]:
-        chain[0].arrive()
-    begun[0][1].arrive()
-    for chain in begun:
-        for hop in chain:
-            hop.leave()
-    for j in range(COLUMN_CHUNKS):
-        for hop in hops[j]:
-            hop.leave()
-        gathers[j].finish()
-        stays[j].wait()
-    norm_copies[-1].wait()
-    for step, copy in enumerate(norm_copies[:-1], 1):
-        copy.wait_send()
-        block = norm_all.at[(spot.z + spot.sections - step) % spot.sections]
-        remote(block, block, norm_send.at[step], norm_recv.at[step], spot.mate).wait_recv()
-
-
-def first_weights(front, back, norms):
-    sections = lax.axis_size("section")
-    spot = Spot()
-    at = spot.core * 8 + spot.c * 2
-    owns = {}
-    for kind, weight in (("front", front), ("back", back)):
-        blocks = weight.reshape(16, weight.shape[0] // 16, weight.shape[1])
-        owns[kind] = lax.dynamic_slice_in_dim(blocks, at, 2, 0)
-    hbm = hbm_spec()
-    sems = pltpu.SemaphoreType.DMA
-    begun = [owns[kind] for kind, _, _, _ in BEGUN]
-    made = sum(hops for _, _, hops, _ in BEGUN)
-    shape = lambda a: jax.ShapeDtypeStruct(a.shape, a.dtype)
-    full = jax.ShapeDtypeStruct((16,) + owns["front"].shape[1:], BF16)
-    out = pl.pallas_call(
-        first_weights_body,
-        in_specs=[hbm] * (2 + len(begun)), out_specs=[hbm] * (2 + len(begun)),
-        out_shape=[full, jax.ShapeDtypeStruct((sections,) + norms.shape, F32)] + [shape(a) for a in begun],
-        scratch_shapes=[
-            pltpu.VMEM(owns["front"].shape, BF16), sems, sems((sections,)), sems((sections,)),
-            sems((COLUMN_CHUNKS, 3, 2)), sems((COLUMN_CHUNKS, 3)), sems((COLUMN_CHUNKS, 9)), sems((COLUMN_CHUNKS, 9)),
-            sems((COLUMN_CHUNKS,)), sems((made, 2)), sems((made,)),
-        ],
-        input_output_aliases={2 + i: 2 + i for i in range(len(begun))},
-        compiler_params=pltpu.CompilerParams(collective_id=0, has_side_effects=True),
-        name="first_weights",
-    )(owns["front"], norms, *begun)
-    return out[0], out[1], {(kind, source): held for (kind, source, _, _), held in zip(BEGUN, out[2:])}
 
 
 class Deliver:
@@ -443,86 +285,6 @@
         [(jax.ShapeDtypeStruct(home.shape, home.dtype), hbm_spec())],
         [sems((count, 2)), sems((count, 4))],
         [(count, 0)], plan,
-    )
-
-
-def plane_gather_guest(parts, shapes, stages):
-    sems = pltpu.SemaphoreType.DMA
-
-    def plan(spot, ins, outs, held):
-        send, recv, stay_sem = held
-        hooks = {}
-        for i, (_, result, first) in enumerate(parts):
-            job = PlaneGather(spot, outs[result].at[pl.ds(first, 16)], send.at[i], recv.at[i])
-            stay = pltpu.make_async_copy(ins[i], job.dst.at[job.blocks(spot.core, spot.c)], stay_sem.at[i])
-            actions = (functools.partial(job.begin, ins[i]), job.second, job.third)
-            for at, action in zip(stages[i], actions):
-                hooks.setdefault(at, []).append(action)
-            hooks.setdefault(stages[i][0], []).append(stay.start)
-            hooks.setdefault("end", []).extend([job.finish, stay.wait])
-        return hooks
-
-    return Guest(
-        [(a, vmem_spec()) for a, _, _ in parts],
-        [(jax.ShapeDtypeStruct(shape, BF16), hbm_spec()) for shape in shapes],
-        [sems((len(parts), 9)), sems((len(parts), 9)), sems((len(parts),))],
-        (), plan,
-    )
-
-
-def spread_gather_guest(jobs, shape):
-    sems = pltpu.SemaphoreType.DMA
-    made = sum(len(job[2]) for job in jobs)
-
-    def plan(spot, ins, outs, held):
-        hsend, hrecv, send, recv, stay_sem = held
-        hooks, count = {}, 0
-        for i, (_, source, hop_steps, stages, first) in enumerate(jobs):
-            own, before = outs[i], None
-            for back, at in enumerate(hop_steps):
-                hop = SpreadHop(
-                    spot, own, source, hops_from(source, spot.sections) - len(hop_steps) + 1 + back,
-                    hsend.at[count], hrecv.at[count],
-                )
-                count += 1
-                if before is not None:
-                    hooks.setdefault(at, []).append(before.arrive)
-                hooks.setdefault(at, []).append(hop.start)
-                hooks.setdefault("end", []).append(hop.leave)
-                before = hop
-            job = PlaneGather(spot, outs[-1].at[pl.ds(first, 16)], send.at[i], recv.at[i])
-            stay = pltpu.make_async_copy(own, job.dst.at[job.blocks(spot.core, spot.c)], stay_sem.at[i])
-            hooks.setdefault(stages[0], []).extend([before.arrive, functools.partial(job.begin, own), stay.start])
-            hooks.setdefault(stages[1], []).append(job.second)
-            hooks.setdefault(stages[2], []).append(job.third)
-            hooks.setdefault("end", []).extend([job.finish, stay.wait])
-        return hooks
-
-    return Guest(
-        [(job[0], hbm_spec()) for job in jobs],
-        [(jax.ShapeDtypeStruct(job[0].shape, BF16), hbm_spec()) for job in jobs]
-        + [(jax.ShapeDtypeStruct(shape, BF16), hbm_spec())],
-        [sems((made, 2)), sems((made,)), sems((len(jobs), 9)), sems((len(jobs), 9)), sems((len(jobs),))],
-        [(i, i) for i in range(len(jobs))], plan,
-    )
-
-
-def spread_hop_guest(arrays, jobs, start=0):
-    sems = pltpu.SemaphoreType.DMA
-
-    def plan(spot, ins, outs, held):
-        send, recv = held
-        hops = [
-            SpreadHop(spot, outs[i], source, hop, send.at[n], recv.at[n], ways)
-            for n, (i, source, hop, ways) in enumerate(jobs)
-        ]
-        return {start: [h.start for h in hops], "end": [h.finish for h in hops]}
-
-    return Guest(
-        [(a, hbm_spec()) for a in arrays],
-        [(jax.ShapeDtypeStruct(a.shape, a.dtype), hbm_spec()) for a in arrays],
-        [sems((len(jobs), 2)), sems((len(jobs),))],
-        [(i, i) for i in range(len(arrays))], plan,
     )
 
 
@@ -896,57 +658,14 @@
     return remote(src, dst, send, recv, spot.mate)
 
 
-def ff_forward_body(
-    spot, hidden_ref, mask_ref, gain_ref, shift_ref, up_ref, bias_up_ref, down_ref, bias_down_ref,
-    act_ref, slope_ref, normed_out, out_ref, normed, total,
-):
-    step, last = pl.program_id(0), pl.num_programs(0) - 1
-
-    @pl.when(step == 0)
-    def _():
-        unit, _ = norm_rows(hidden_ref[...].astype(F32))
-        normed[...] = (unit * gain_ref[...] + shift_ref[...]).astype(BF16)
-        normed_out[...] = normed[...]
-
-    rows = normed.shape[0]
-    for span in (slice(0, rows // 2), slice(rows // 2, rows)):
-        pre = mm(normed[span, :], up_ref[...]) + bias_up_ref[...]
-        act, slope = gelu_and_slope(pre)
-        act_ref[span, :] = act.astype(BF16)
-        slope_ref[span, :] = slope.astype(BF16)
-        part = mm(act.astype(BF16), down_ref[...])
-        total[span, :] = jnp.where(step == 0, part, total[span, :] + part)
-
-    @pl.when(step == last)
-    def _():
-        hidden = hidden_ref[...].astype(F32)
-        out_ref[...] = (mask_ref[...] * (hidden + total[...] + bias_down_ref[...])).astype(BF16)
-
-
-def ff_forward(hidden, mask, gain, shift, up, bias_up, down, bias_down, guests, collective_id):
-    rows, width = hidden.shape
-    units = up.shape[1]
-    size = width
-    columns = pl.BlockSpec((rows, size), lambda i: (0, i))
-    in_specs = ([
-            whole((rows, width)), whole((rows, 1)), whole((1, width)), whole((1, width)),
-            pl.BlockSpec((width, size), lambda i: (0, i)), pl.BlockSpec((1, size), lambda i: (0, i)),
-            pl.BlockSpec((size, width), lambda i: (i, 0)), whole((1, width)),
-        ])
-    out_specs = ([columns, columns, whole((rows, width)), whole((rows, width))])
-    out_shape = ([
-            jax.ShapeDtypeStruct((rows, units), BF16), jax.ShapeDtypeStruct((rows, units), BF16),
-            jax.ShapeDtypeStruct((rows, width), BF16), jax.ShapeDtypeStruct((rows, width), BF16),
-        ])
-    scratch = ([pltpu.VMEM((rows, width), BF16), pltpu.VMEM((rows, width), F32)])
-    return hosted(
-        ff_forward_body, units // size, list(zip((hidden, mask, gain, shift, up, bias_up, down, bias_down), in_specs)), list(zip(out_shape, out_specs)), scratch,
-        guests, collective_id, "ff_forward",
-    )
+def transposed_norm(hidden_ref, norm_ref):
+    unit, _ = norm_rows(hidden_ref[0].astype(F32))
+    normed = (unit * norm_ref[0, 0:1, :] + norm_ref[0, 1:2, :]).astype(BF16)
+    return normed.astype(F32).T.astype(BF16)
 
 
 def ff_backward_body(
-    spot, incoming_ref, mask_ref, hidden_ref, normed_ref, act_ref, slope_ref, up_ref, down_ref, gain_ref,
+    spot, incoming_ref, mask_ref, hidden_ref, act_ref, slope_ref, up_ref, down_ref, norm_ref,
     up_grad, down_grad, out_ref, gain_grad, shift_grad, up_bias_grad, down_bias_grad,
     grad, normed_t, total,
 ):
@@ -957,33 +676,36 @@
         grad_rows = mask_ref[...] * incoming_ref[...].astype(F32)
         grad[...] = grad_rows.astype(BF16)
         down_bias_grad[...] = jnp.sum(grad_rows, axis=0, keepdims=True)
-        normed_t[...] = normed_ref[...].astype(F32).T.astype(BF16)
-
-    grad_pre = (contract_cols(grad[...], down_ref[...]) * slope_ref[...].astype(F32)).astype(BF16)
-    down_grad[...] = contract_rows(act_ref[...], grad[...]).astype(BF16).reshape(down_grad.shape)
+        normed_t[...] = transposed_norm(hidden_ref, norm_ref)
+
+    width = grad.shape[1]
+    up, down = up_ref[0].reshape(width, width), down_ref[0].reshape(width, width)
+    grad_pre = (contract_cols(grad[...], down) * slope_ref[0].astype(F32)).astype(BF16)
+    down_grad[...] = contract_rows(act_ref[0], grad[...]).astype(BF16).reshape(down_grad.shape)
     up_bias_grad[...] = jnp.sum(grad_pre.astype(F32), axis=0, keepdims=True)
     up_grad[...] = mm(normed_t[...], grad_pre).astype(BF16).reshape(up_grad.shape)
-    part = contract_cols(grad_pre, up_ref[...])
+    part = contract_cols(grad_pre, up)
     total[...] = jnp.where(step == 0, part, total[...] + part)
 
     @pl.when(step == last)
     def _():
         grad_hidden, gain_grad[...], shift_grad[...] = norm_backward(
-            hidden_ref[...].astype(F32), total[...], gain_ref[...]
+            hidden_ref[0].astype(F32), total[...], norm_ref[0, 0:1, :]
         )
         out_ref[...] = (grad[...].astype(F32) + grad_hidden).astype(BF16)
 
 
-def ff_backward(incoming, mask, hidden, normed, act, slope, up, down, gain, guests, collective_id):
-    rows, width = hidden.shape
-    units, size = up.shape[1], width
-    columns = pl.BlockSpec((rows, size), lambda i: (0, i))
+def ff_backward(incoming, mask, hidden, act, slope, fronts, downs, norms, s, guests, collective_id):
+    rows, width = incoming.shape
+    units, size, layer = fronts.shape[3], width, s // 2
+    columns = pl.BlockSpec((1, rows, size), lambda i: (layer, 0, i))
     vector = jax.ShapeDtypeStruct((1, width), F32)
-    in_specs = ([
-            whole((rows, width)), whole((rows, 1)), whole((rows, width)), whole((rows, width)), columns, columns,
-            pl.BlockSpec((width, size), lambda i: (0, i)), pl.BlockSpec((size, width), lambda i: (i, 0)),
-            whole((1, width)),
-        ])
+    in_specs = [
+        whole((rows, width)), whole((rows, 1)), pl.BlockSpec((1, rows, width), lambda i: (s, 0, 0)), columns, columns,
+        pl.BlockSpec((1, 16, width // 16, size), lambda i: (s, 0, 0, i)),
+        pl.BlockSpec((1, size * 32 // units, units // 32, width), lambda i: (layer, i, 0, 0)),
+        pl.BlockSpec((1,) + norms.shape[1:], lambda i: (s, 0, 0)),
+    ]
     out_specs = ([
             pl.BlockSpec((16, width // 16, size), lambda i: (0, 0, i)),
             pl.BlockSpec((size * 32 // units, units // 32, width), lambda i: (i, 0, 0)),
@@ -999,7 +721,7 @@
             pltpu.VMEM((rows, width), BF16), pltpu.VMEM((width, rows), BF16), pltpu.VMEM((rows, width), F32),
         ])
     return hosted(
-        ff_backward_body, units // size, list(zip((incoming, mask, hidden, normed, act, slope, up, down, gain), in_specs)), list(zip(out_shape, out_specs)), scratch,
+        ff_backward_body, units // size, list(zip((incoming, mask, hidden, act, slope, fronts, downs, norms), in_specs)), list(zip(out_shape, out_specs)), scratch,
         guests, collective_id, "ff_backward",
     )
 
@@ -1057,104 +779,6 @@
         for lane, part in enumerate(three_parts(-(top + jnp.log(total))), aux + 1):
             query = jnp.where(lanes == lane, part, query)
         save(head, slice(start, start + chunk), query.astype(BF16), summed / total)
-
-
-def attention_forward_body(
-    spot, hidden_ref, mask_ref, gain_ref, shift_ref, weight_ref, bias_ref, key_bias_ref, out_bias_ref,
-    normed_out, key_out, value_out, key_far_out, value_far_out, extended_out, attended_out, out_ref,
-    normed, own, far, attended, keys, values, send, recv,
-):
-    step, last = pl.program_id(0), pl.num_programs(0) - 1
-    rows, width = normed.shape
-    pairs = width // PAIR
-
-    def swaps():
-        return [swap_with_mate(spot, own.at[j], far.at[j], send.at[j], recv.at[j]) for j in (0, 1)]
-
-    @pl.when(step == 0)
-    def _():
-        unit, _ = norm_rows(hidden_ref[...].astype(F32))
-        normed[...] = (unit * gain_ref[...] + shift_ref[...]).astype(BF16)
-        normed_out[...] = normed[...]
-
-    for j, scale in ((0, 1.0), (1, 1.0), (2, HEAD_DIM**-0.5)):
-        @pl.when(step == j)
-        def _(j=j, scale=scale):
-            block = (mm(normed[...], weight_ref[...]) + bias_ref[...]).astype(BF16)
-            if scale != 1.0:
-                block = (block.astype(F32) * scale).astype(BF16)
-            for p, part in enumerate(pairs_of(block)):
-                own[j, p] = part
-            if j < 2:
-                swaps()[j].start()
-            else:
-                for copy in swaps():
-                    copy.wait()
-
-    @pl.when((step >= 3) & (step < 3 + pairs))
-    def _():
-        p = step - 3
-        for head in (0, 1):
-            extend_keys(
-                keys.at[head], values.at[head], [(own[0, p], own[1, p]), (far[0, p], far[1, p])],
-                key_bias_ref, head,
-            )
-        for j, out in enumerate((key_out, value_out)):
-            out[0] = own[j, p]
-        for j, out in enumerate((key_far_out, value_far_out)):
-            out[0] = far[j, p]
-        lanes = lane_ids((rows // 2, PAIR))
-        firsts = {}
-
-        def save(head, span, query, out):
-            extended_out[head, span, :] = query
-            if head == 0:
-                firsts[span.start] = out
-            else:
-                both = jnp.where(lanes < HEAD_DIM, firsts[span.start], out)
-                attended_out[0, span, :] = both
-                attended[p, span, :] = both.astype(BF16)
-
-        pair_forward(lambda span: own[2, p, span, :], keys, values, rows, rows // 2, save)
-
-    @pl.when(step == last)
-    def _():
-        branch = contract_cols(joined(attended), weight_ref[...]) + out_bias_ref[...]
-        out_ref[...] = (mask_ref[...] * (hidden_ref[...].astype(F32) + branch)).astype(BF16)
-
-
-def attention_forward(
-    hidden, mask, gain, shift, weight, bias, key_bias, out_bias, guests, collective_id
-):
-    rows, width = hidden.shape
-    pairs = width // PAIR
-    pair = lambda i: jnp.clip(i - 3, 0, pairs - 1)
-    part = lambda i: jnp.where(i < 3, (i + 1) % 3, 3)
-    block = pl.BlockSpec((1, rows, PAIR), lambda i: (pair(i), 0, 0))
-    saved = jax.ShapeDtypeStruct((pairs, rows, PAIR), BF16)
-    full = jax.ShapeDtypeStruct((rows, width), BF16)
-    in_specs = ([
-            whole((rows, width)), whole((rows, 1)), whole((1, width)), whole((1, width)),
-            pl.BlockSpec((width, width), lambda i: (0, part(i))),
-            pl.BlockSpec((1, width), lambda i: (0, jnp.minimum(part(i), 2))),
-            whole((2 * rows, 1)), whole((1, width)),
-        ])
-    out_specs = ([whole((rows, width))] + [block] * 4
-        + [pl.BlockSpec((2, rows, PAIR), lambda i: (pair(i), 0, 0)), block, whole((rows, width))])
-    out_shape = ([full] + [saved] * 4 + [
-            jax.ShapeDtypeStruct((2 * pairs, rows, PAIR), BF16),
-            jax.ShapeDtypeStruct((pairs, rows, PAIR), F32), full,
-        ])
-    scratch = ([
-            pltpu.VMEM((rows, width), BF16), pltpu.VMEM((3, pairs, rows, PAIR), BF16),
-            pltpu.VMEM((2, pairs, rows, PAIR), BF16), pltpu.VMEM((pairs, rows, PAIR), BF16),
-            pltpu.VMEM((2, 2 * rows, PAIR), BF16), pltpu.VMEM((2, 2 * rows, PAIR), BF16),
-            pltpu.SemaphoreType.DMA((2,)), pltpu.SemaphoreType.DMA((2,)),
-        ])
-    return hosted(
-        attention_forward_body, pairs + 4, list(zip((hidden, mask, gain, shift, weight, bias, key_bias, out_bias), in_specs)), list(zip(out_shape, out_specs)), scratch,
-        guests, collective_id, "attention_forward",
-    )
 
 
 def pair_backward(query_of, grad_of, out_of, keys, values, key_sums, value_sums, rows, save):
@@ -1178,8 +802,8 @@
 
 
 def attention_backward_body(
-    spot, incoming_ref, mask_ref, hidden_ref, normed_ref, key_ref, value_ref, key_far_ref, value_far_ref,
-    extended_ref, attended_ref, weight_ref, gain_ref, key_bias_ref,
+    spot, incoming_ref, mask_ref, hidden_ref, key_ref, value_ref, key_far_ref, value_far_ref,
+    extended_ref, attended_ref, weight_ref, norm_ref, key_bias_ref,
     weight_grad, out_ref, gain_grad, shift_grad, query_bias_grad, value_bias_grad, out_bias_grad,
     grad, grad_out, attended, normed_t, total, grads, sent, arrived, keys, values, key_sums, value_sums,
     send, recv,
@@ -1196,7 +820,7 @@
         grad_rows = mask_ref[...] * incoming_ref[...].astype(F32)
         grad[...] = grad_rows.astype(BF16)
         out_bias_grad[...] = jnp.sum(grad_rows, axis=0, keepdims=True)
-        for p, part in enumerate(pairs_of(mm(grad[...], weight_ref[...]).astype(BF16))):
+        for p, part in enumerate(pairs_of(mm(grad[...], weight_ref[0].reshape(width, width)).astype(BF16))):
             grad_out[p] = part
 
     @pl.when(step < pairs)
@@ -1205,15 +829,15 @@
         for head in (0, 1):
             extend_keys(
                 keys.at[head], values.at[head],
-                [(key_ref[0], value_ref[0]), (key_far_ref[0], value_far_ref[0])], key_bias_ref, head,
+                [(key_ref[0, 0], value_ref[0, 0]), (key_far_ref[0, 0], value_far_ref[0, 0])], key_bias_ref, head,
             )
-        attended[p] = attended_ref[0].astype(BF16)
+        attended[p] = attended_ref[0, 0].astype(BF16)
 
         def save(value):
             grads[0, p] = value
 
         pair_backward(
-            lambda head: extended_ref[head], lambda: grad_out[p], lambda: attended_ref[0],
+            lambda head: extended_ref[0, head], lambda: grad_out[p], lambda: attended_ref[0, 0],
             keys, values, key_sums, value_sums, rows, save,
         )
         first = lane_ids((rows, PAIR)) < HEAD_DIM
@@ -1224,7 +848,7 @@
 
     @pl.when(step == pairs)
     def _():
-        normed_t[...] = normed_ref[...].astype(F32).T.astype(BF16)
+        normed_t[...] = transposed_norm(hidden_ref, norm_ref)
         for p in range(pairs):
             swap_of(p).wait()
             for j in (0, 1):
@@ -1245,34 +869,35 @@
             value_bias_grad[...] = sums
 
         weight_grad[...] = mm(normed_t[...], part).astype(BF16).reshape(weight_grad.shape)
-        product = contract_cols(part, weight_ref[...])
+        product = contract_cols(part, weight_ref[0].reshape(width, width))
         total[...] = jnp.where(j == 0, product, total[...] + product)
 
     @pl.when(step == last)
     def _():
         weight_grad[...] = contract_rows(grad[...], joined(attended)).astype(BF16).reshape(weight_grad.shape)
         grad_hidden, gain_grad[...], shift_grad[...] = norm_backward(
-            hidden_ref[...].astype(F32), total[...], gain_ref[...]
+            hidden_ref[0].astype(F32), total[...], norm_ref[0, 0:1, :]
         )
         out_ref[...] = (grad[...].astype(F32) + grad_hidden).astype(BF16)
 
 
 def attention_backward(
-    incoming, mask, hidden, normed, key, value, key_far, value_far, extended, attended, weight, gain, key_bias,
+    incoming, mask, hidden, key, value, key_far, value_far, extended, attended, fronts, norms, key_bias, s,
     guests, collective_id,
 ):
-    rows, width = hidden.shape
+    rows, width = incoming.shape
+    layer = s // 2
     pairs = width // PAIR
     pair = lambda i: jnp.minimum(i, pairs - 1)
-    block = pl.BlockSpec((1, rows, PAIR), lambda i: (pair(i), 0, 0))
+    block = pl.BlockSpec((1, 1, rows, PAIR), lambda i: (layer, pair(i), 0, 0))
     vector = jax.ShapeDtypeStruct((1, width), F32)
-    in_specs = ([whole((rows, width)), whole((rows, 1)), whole((rows, width)), whole((rows, width))]
-        + [block] * 4
-        + [
-            pl.BlockSpec((2, rows, PAIR), lambda i: (pair(i), 0, 0)), block,
-            pl.BlockSpec((width, width), lambda i: (0, jnp.where(i < pairs, 3, jnp.minimum(i - pairs, 2)))),
-            whole((1, width)), whole((2 * rows, 1)),
-        ])
+    part = lambda i: jnp.where(i < pairs, 3, jnp.minimum(i - pairs, 2))
+    in_specs = [whole((rows, width)), whole((rows, 1)), pl.BlockSpec((1, rows, width), lambda i: (s, 0, 0))]
+    in_specs += [block] * 4 + [
+        pl.BlockSpec((1, 2, rows, PAIR), lambda i: (layer, pair(i), 0, 0)), block,
+        pl.BlockSpec((1, 16, width // 16, width), lambda i: (s, 0, 0, part(i))),
+        pl.BlockSpec((1,) + norms.shape[1:], lambda i: (s, 0, 0)), whole((2 * rows, 1)),
+    ]
     out_specs = ([
             pl.BlockSpec((16, width // 16, width), lambda i: (0, 0, jnp.maximum(i - pairs, 0))),
             whole((rows, width)),
@@ -1290,9 +915,421 @@
             pltpu.SemaphoreType.DMA((pairs,)), pltpu.SemaphoreType.DMA((pairs,)),
         ])
     return hosted(
-        attention_backward_body, pairs + 4, list(zip((incoming, mask, hidden, normed, key, value, key_far, value_far, extended, attended, weight, gain, key_bias), in_specs)), list(zip(out_shape, out_specs)), scratch,
+        attention_backward_body, pairs + 4, list(zip((incoming, mask, hidden, key, value, key_far, value_far, extended, attended, fronts, norms, key_bias), in_specs)), list(zip(out_shape, out_specs)), scratch,
         guests, collective_id, "attention_backward",
     )
+
+
+class Weight(PlaneGather):
+    SENDS, RECEIVES = 13, 10
+
+    def __init__(self, spot, src, dst, source, send, recv):
+        super().__init__(spot, dst, send, recv)
+        self.src, self.source = src, source
+        self.own = self.blocks(spot.core, spot.c)
+
+    def along(self, src):
+        s = self.spot
+        return (
+            remote(src.at[self.own], self.dst.at[self.own], self.send.at[9], self.recv.at[9], s.above),
+            remote(src.at[self.own], self.dst.at[self.own], self.send.at[10], self.recv.at[9], s.below),
+        )
+
+    def load(self):
+        return pltpu.make_async_copy(self.src, self.dst, self.send.at[11])
+
+    def open(self, up=True, down=True, load=True):
+        rise, fall = self.along(self.src)
+
+        @pl.when(self.spot.z == self.source)
+        def _():
+            if up and self.source + 1 < self.spot.sections:
+                rise.start()
+            if down and self.source:
+                fall.start()
+            if load:
+                self.load().start()
+
+    def pass_on(self, hop, begin=True):
+        rise, fall = self.along(self.dst)
+        last = self.spot.sections - 1
+        for at, further, copy in ((self.source + hop, last, rise), (self.source - hop, 0, fall)):
+            if not 0 <= at <= last:
+                continue
+
+            @pl.when(self.spot.z == at)
+            def _(at=at, further=further, copy=copy):
+                rise.wait_recv()
+                if at != further:
+                    copy.start()
+                if begin:
+                    self.begin(self.dst.at[self.own])
+
+    def away(self, action):
+        pl.when(self.spot.z != self.source)(action)
+
+    def enter(self):
+        self.away(lambda: self.begin(self.dst.at[self.own]))
+
+    def middle(self):
+        self.away(self.second)
+
+    def late(self):
+        self.away(self.third)
+
+    def ready(self):
+        rise, fall = self.along(self.src)
+        last = self.spot.sections - 1
+        if self.source < last:
+            pl.when((self.spot.z >= self.source) & (self.spot.z < last))(rise.wait_send)
+        if self.source:
+            pl.when((self.spot.z <= self.source) & (self.spot.z > 0))(fall.wait_send)
+        pl.when(self.spot.z == self.source)(self.load().wait)
+        self.away(self.finish)
+
+
+QKV_ORDER = (1, 2, 0, 3)
+FORWARD_STEPS = 14
+
+
+def forward_body(*refs):
+    refs_list = list(refs)
+    take = lambda n: [refs_list.pop(0) for _ in range(n)]
+    clips, grads, front, back, norms, kind_in, bias_qv, bias_attn, bias_up, bias_down = take(10)
+    key_out, value_out, key_far_out, value_far_out, extended_out, attended_out, act_out, slope_out = take(8)
+    fronts_out, downs_out, hidden_out, grad_out, acts_home, mask_out, key_bias_out, norm_out = take(8)
+    fronts, downs, hidden, own, far, attended, keys, values, normed, total, norm_all, kind, blank = take(13)
+    wsend, wrecv, nsend, nrecv, csend, crecv, ksend, krecv, dsend, drecv, lsem = take(11)
+    step = pl.program_id(0)
+    layer, turn = step // FORWARD_STEPS, step % FORWARD_STEPS
+    rows, width = normed.shape
+    pairs = width // PAIR
+    spot = Spot()
+    owner, slot = spot.z // 2, spot.z % 2
+    holds = spot.core == owner
+
+    weights, count = {}, 0
+
+    def weight(name, src, dst, source):
+        nonlocal count
+        weights[name] = Weight(spot, src, dst, source, wsend.at[count], wrecv.at[count])
+        count += 1
+
+    for j, block in enumerate(QKV_ORDER):
+        at = pl.ds(block * width, width)
+        weight(("first", j), front.at[:, :, at], fronts.at[0, :, :, at], 0)
+    for s in range(1, 4):
+        weight(("front", s), front, fronts.at[s], s)
+    for s in range(4):
+        weight(("back", s), back, downs.at[s // 2, pl.ds(16 * (s % 2), 16)], s)
+    first = [weights["first", j] for j in range(4)]
+    front_1, front_2, front_3 = (weights["front", s] for s in (1, 2, 3))
+    back_0, back_1, back_2, back_3 = (weights["back", s] for s in range(4))
+
+    norm_copies = [
+        remote(norms, norm_all.at[spot.z], nsend.at[i], nrecv.at[i], {"section": (spot.z + i) % spot.sections})
+        for i in range(1, spot.sections)
+    ]
+
+    def clip_copies():
+        mine, other = (pl.ds(pl.multiple_of(c * rows, 16), rows) for c in (spot.core, 1 - spot.core))
+        away = [
+            remote(clips.at[slot, other], hidden.at[0], csend.at[0], crecv.at[0], spot.mate),
+            remote(grads.at[slot, other], grad_out, csend.at[1], crecv.at[1], spot.mate),
+            remote(kind_in, kind, csend.at[2], crecv.at[2], spot.mate),
+        ]
+        stay = [
+            pltpu.make_async_copy(clips.at[slot, mine], hidden.at[0], csend.at[3]),
+            pltpu.make_async_copy(grads.at[slot, mine], grad_out, csend.at[4]),
+        ]
+        return away, stay
+
+    def pads():
+        pad = acts_home.shape[1] - 2 * rows
+        return [
+            pltpu.make_async_copy(blank, acts_home.at[i, pl.ds(2 * rows, pad)], lsem.at[i]) for i in (0, 1)
+        ]
+
+    def enter():
+        blank[...] = jnp.zeros_like(blank)
+        spot.greet()
+        for w in first:
+            w.open()
+        away, stay = clip_copies()
+
+        @pl.when(holds)
+        def _():
+            for copy in (away[2], away[0], stay[0], away[1]):
+                copy.start()
+            kind[...] = kind_in[...]
+        for copy in norm_copies:
+            copy.start()
+        norm_all[spot.z] = norms[...]
+        for w in (front_1, back_1, front_2, back_2, front_3, back_3):
+            w.open(up=False)
+        back_2.open(down=False, load=False)
+        for w in first:
+            for hop in (1, 2, 3):
+                w.pass_on(hop)
+        for w in (front_1, back_1, front_2):
+            w.open(down=False, load=False)
+        back_0.open()
+
+        @pl.when(holds)
+        def _():
+            stay[1].start()
+            stay[0].wait()
+
+        @pl.when(jnp.logical_not(holds))
+        def _():
+            away[0].wait_recv()
+            away[2].wait_recv()
+        for i, copy in enumerate(norm_copies, 1):
+            block = norm_all.at[(spot.z + spot.sections - i) % spot.sections]
+            remote(block, block, nsend.at[i], nrecv.at[i], spot.mate).wait_recv()
+        norm_out[...] = norm_all[...]
+        for copy in pads():
+            copy.start()
+        length = SHORT + (LONG - SHORT) * kind[0:1, 0:1]
+        place = lax.broadcasted_iota(jnp.int32, (rows, 1), 0)
+        near, there = ((place + c * rows).astype(F32) < length for c in (spot.core, 1 - spot.core))
+        mask_out[...] = near.astype(F32)
+        key_bias_out[:rows, :] = jnp.where(near, 0.0, MASKED)
+        key_bias_out[rows:, :] = jnp.where(there, 0.0, MASKED)
+        for w in first:
+            w.middle()
+        front_1.pass_on(1)
+        back_1.pass_on(1)
+        for w in first:
+            w.late()
+        front_1.pass_on(2)
+        first[0].ready()
+
+    plan = {
+        0: [enter], 1: [first[1].ready, lambda: back_1.pass_on(2), lambda: back_0.pass_on(1)],
+        2: [first[2].ready, lambda: back_0.pass_on(2), lambda: front_2.pass_on(1, False),
+            lambda: back_2.pass_on(1, False)],
+        3: [first[3].ready, lambda: back_0.pass_on(3), lambda: front_3.pass_on(1, False)],
+        4: [front_1.middle, lambda: back_3.pass_on(1, False), lambda: front_2.pass_on(2, False)],
+        5: [lambda: back_2.pass_on(2, False)],
+        6: [back_1.middle, lambda: front_3.pass_on(2, False)],
+        7: [back_0.middle, front_1.late, lambda: back_3.pass_on(2, False)],
+        8: [front_2.enter],
+        9: [back_1.late, lambda: front_3.pass_on(3, False)],
+        10: [back_0.late, lambda: back_3.pass_on(3, False), front_1.ready, back_1.ready, back_0.ready],
+        11: [front_3.enter],
+        12: [front_2.middle],
+        13: [front_2.late, back_2.enter, back_3.enter],
+        14: [front_2.ready],
+        16: [front_3.middle],
+        18: [back_2.middle],
+        19: [back_3.middle, front_3.late],
+        21: [back_2.late],
+        22: [back_3.late],
+        24: [front_3.ready, back_2.ready, back_3.ready],
+    }
+    ends = []
+
+    def keep(at, src, dst, index):
+        copy = pltpu.make_async_copy(src, dst, lsem.at[2 + index])
+        plan.setdefault(at, []).append(copy.start)
+        ends.append(copy.wait)
+
+    for s, at in ((0, 10), (1, 12), (2, 20), (3, 25)):
+        keep(at, fronts.at[s], fronts_out.at[s], s)
+    for layer_id, at in ((0, 15), (1, 26)):
+        keep(at, downs.at[layer_id], downs_out.at[layer_id], 4 + layer_id)
+    for s, at in ((0, 4), (1, 11), (2, 16), (3, 25)):
+        keep(at, hidden.at[s], hidden_out.at[s], 6 + s)
+
+    for n, (s, first_row, size, begin, stop) in enumerate(FORWARD_DELIVERIES):
+        size = size or rows - first_row
+        blocks = size // 16
+        for i in range(stop - begin):
+            low, high = blocks * i // (stop - begin), blocks * (i + 1) // (stop - begin)
+            part = Deliver(
+                spot, hidden.at[s + 1], acts_home, s, dsend.at[n], drecv.at[n], first_row + 16 * low, 16 * (high - low)
+            )
+            plan.setdefault(begin + i, []).append(part.start)
+        ends.append(Deliver(spot, hidden.at[s + 1], acts_home, s, dsend.at[n], drecv.at[n], first_row, size).finish)
+
+    for at, actions in sorted(plan.items()):
+        @pl.when(step == at)
+        def _(actions=actions):
+            for action in actions:
+                action()
+
+    def norms_of(s):
+        return norm_all[s, 0:1, :], norm_all[s, 1:2, :]
+
+    def start_sub_layer(s):
+        gain, shift = norms_of(s)
+        unit, _ = norm_rows(hidden[s].astype(F32))
+        normed[...] = (unit * gain + shift).astype(BF16)
+
+    def front_block(s, block):
+        return fronts[s, :, :, pl.ds(pl.multiple_of(block * width, width), width)].reshape(width, width)
+
+    def swaps():
+        return [
+            remote(own.at[j], far.at[layer, j], ksend.at[layer, j], krecv.at[layer, j], spot.mate) for j in (0, 1)
+        ]
+
+    @pl.when(turn == 0)
+    def _():
+        start_sub_layer(2 * layer)
+
+    for j, scale in ((0, 1.0), (1, 1.0), (2, HEAD_DIM**-0.5)):
+        @pl.when(turn == j)
+        def _(j=j, scale=scale):
+            block = mm(normed[...], front_block(2 * layer, QKV_ORDER[j]))
+            if j == 1:
+                block = block + bias_qv[pl.ds(layer, 1), width:]
+            elif j == 2:
+                block = block + bias_qv[pl.ds(layer, 1), :width]
+            block = block.astype(BF16)
+            if scale != 1.0:
+                block = (block.astype(F32) * scale).astype(BF16)
+            for p, part in enumerate(pairs_of(block)):
+                own[j, p] = part
+            if j < 2:
+                swaps()[j].start()
+            else:
+                for copy in swaps():
+                    copy.wait()
+
+    @pl.when((turn >= 3) & (turn < 3 + pairs))
+    def _():
+        p = turn - 3
+        for head in (0, 1):
+            extend_keys(
+                keys.at[head], values.at[head], [(own[0, p], own[1, p]), (far[layer, 0, p], far[layer, 1, p])],
+                key_bias_out, head,
+            )
+        for j, out in enumerate((key_out, value_out)):
+            out[0, 0] = own[j, p]
+        for j, out in enumerate((key_far_out, value_far_out)):
+            out[0, 0] = far[layer, j, p]
+        lanes = lane_ids((rows // 2, PAIR))
+        firsts = {}
+
+        def save(head, span, query, out):
+            extended_out[0, head, span, :] = query
+            if head == 0:
+                firsts[span.start] = out
+            else:
+                both = jnp.where(lanes < HEAD_DIM, firsts[span.start], out)
+                attended_out[0, 0, span, :] = both
+                attended[p, span, :] = both.astype(BF16)
+
+        pair_forward(lambda span: own[2, p, span, :], keys, values, rows, rows // 2, save)
+
+    @pl.when(turn == 3 + pairs)
+    def _():
+        s = 2 * layer
+        branch = contract_cols(joined(attended), front_block(s, 3)) + bias_attn[pl.ds(layer, 1), :]
+        hidden[s + 1] = (mask_out[...] * (hidden[s].astype(F32) + branch)).astype(BF16)
+
+    @pl.when(turn == 4 + pairs)
+    def _():
+        start_sub_layer(2 * layer + 1)
+
+    @pl.when(turn >= 4 + pairs)
+    def _():
+        i = turn - 4 - pairs
+        columns = pl.ds(pl.multiple_of(i * width, width), width)
+        up = fronts[2 * layer + 1, :, :, columns].reshape(width, width)
+        down_blocks = width * 32 // (width * 4)
+        down = downs[layer, pl.ds(i * down_blocks, down_blocks)].reshape(width, width)
+        bias = bias_up[pl.ds(layer, 1), columns]
+        for span in (slice(0, rows // 2), slice(rows // 2, rows)):
+            act, slope = gelu_and_slope(mm(normed[span, :], up) + bias)
+            act_out[0, span, :] = act.astype(BF16)
+            slope_out[0, span, :] = slope.astype(BF16)
+            part = mm(act.astype(BF16), down)
+            total[span, :] = jnp.where(i == 0, part, total[span, :] + part)
+
+    @pl.when(turn == FORWARD_STEPS - 1)
+    def _():
+        s = 2 * layer + 1
+        branch = total[...] + bias_down[pl.ds(layer, 1), :]
+        hidden[s + 1] = (mask_out[...] * (hidden[s].astype(F32) + branch)).astype(BF16)
+
+    @pl.when(step == 2 * FORWARD_STEPS - 1)
+    def _():
+        copy = pltpu.make_async_copy(hidden.at[4], hidden_out.at[4], lsem.at[12])
+        copy.start()
+        for end in ends:
+            end()
+        copy.wait()
+        for pad in pads():
+            pad.wait()
+        for sent in norm_copies:
+            sent.wait_send()
+        away, stay = clip_copies()
+
+        @pl.when(holds)
+        def _():
+            for sent in away:
+                sent.wait_send()
+            stay[1].wait()
+
+        pl.when(jnp.logical_not(holds))(away[1].wait_recv)
+
+
+FORWARD_DELIVERIES = ((0, 0, None, 10, 24), (1, 0, None, 14, 27), (2, 0, 160, 24, 27))
+
+
+def forward(clips, grads, kind, front, back, norms, bias_qv, bias_attn, bias_up, bias_down, rows):
+    sections = lax.axis_size("section")
+    padded, width = clips.shape[1:]
+    units, pairs = front.shape[1], width // PAIR
+    front_b = front.reshape(16, width // 16, units)
+    back_b = back.reshape(16, back.shape[0] // 16, width)
+    layers = sections // 2
+    layer = lambda i: i // FORWARD_STEPS
+    pair = lambda i: jnp.clip(i % FORWARD_STEPS - 3, 0, pairs - 1)
+    unit = lambda i: jnp.maximum(i % FORWARD_STEPS - 4 - pairs, 0)
+    hbm, vmem = hbm_spec(), vmem_spec()
+    per_pair = pl.BlockSpec((1, 1, rows, PAIR), lambda i: (layer(i), pair(i), 0, 0))
+    per_unit = pl.BlockSpec((1, rows, width), lambda i: (layer(i), 0, unit(i)))
+    shape = jax.ShapeDtypeStruct
+    saved = shape((layers, pairs, rows, PAIR), BF16)
+    sems = pltpu.SemaphoreType.DMA
+    jobs = 4 + 3 + 4
+    sent = len(FORWARD_DELIVERIES)
+    return pl.pallas_call(
+        forward_body,
+        grid=(2 * FORWARD_STEPS,),
+        in_specs=[hbm] * 4 + [vmem] * 6,
+        out_specs=[per_pair] * 4
+        + [pl.BlockSpec((1, 2, rows, PAIR), lambda i: (layer(i), pair(i), 0, 0)), per_pair, per_unit, per_unit]
+        + [hbm] * 5 + [vmem] * 3,
+        out_shape=[saved] * 4
+        + [
+            shape((layers, 2 * pairs, rows, PAIR), BF16), shape((layers, pairs, rows, PAIR), F32),
+            shape((layers, rows, units), BF16), shape((layers, rows, units), BF16),
+            shape((sections,) + front_b.shape, BF16), shape((layers, 32) + back_b.shape[1:], BF16),
+            shape((sections + 1, rows, width), BF16), shape((rows, width), BF16),
+            shape((clips.shape[0], padded, width), BF16),
+            shape((rows, 1), F32), shape((2 * rows, 1), F32), shape((sections,) + norms.shape, F32),
+        ],
+        scratch_shapes=[
+            pltpu.VMEM((sections,) + front_b.shape, BF16), pltpu.VMEM((layers, 32) + back_b.shape[1:], BF16),
+            pltpu.VMEM((sections + 1, rows, width), BF16), pltpu.VMEM((3, pairs, rows, PAIR), BF16),
+            pltpu.VMEM((layers, 2, pairs, rows, PAIR), BF16), pltpu.VMEM((pairs, rows, PAIR), BF16),
+            pltpu.VMEM((2, 2 * rows, PAIR), BF16), pltpu.VMEM((2, 2 * rows, PAIR), BF16),
+            pltpu.VMEM((rows, width), BF16), pltpu.VMEM((rows, width), F32),
+            pltpu.VMEM((sections,) + norms.shape, F32), pltpu.VMEM(kind.shape, F32),
+            pltpu.VMEM((padded - 2 * rows, width), BF16),
+            sems((jobs, Weight.SENDS)), sems((jobs, Weight.RECEIVES)), sems((sections,)), sems((sections,)),
+            sems((5,)), sems((3,)), sems((layers, 2)), sems((layers, 2)), sems((sent, 2)), sems((sent, 4)), sems((13,)),
+        ],
+        compiler_params=pltpu.CompilerParams(
+            vmem_limit_bytes=63 * 2**20, collective_id=0, has_side_effects=True
+        ),
+        name="forward",
+    )(clips, grads, front_b, back_b, norms, kind, bias_qv, bias_attn, bias_up, bias_down)
 
 
 def per_device(
@@ -1303,94 +1340,26 @@
     sections = lax.axis_size("section")
     padded, width = clip_inputs.shape[1:]
     rows = -(-LONG // 32) * 16
-    core, section = spot.core, spot.z
-
-    owner, slot = section // 2, section % 2
-    mine = jnp.stack([lax.dynamic_index_in_dim(a, slot, 0, False) for a in (clip_inputs, out_grad)])
-    far = swap(lax.dynamic_slice_in_dim(mine, (1 - core) * rows, rows, 1), 1)
-    near = lax.dynamic_slice_in_dim(mine, core * rows, rows, 1)
-    clip_pair = jnp.where(core == owner, near, far)
-    own_class = lax.dynamic_index_in_dim(clip_class, slot, 0, False).astype(F32)
-    own_class = jnp.broadcast_to(own_class, (8, 128))
-    clip_kind = jnp.where(core == owner, own_class, swap(own_class, 1))[0, 0]
-    length = SHORT + (LONG - SHORT) * clip_kind
-    positions = jnp.arange(rows, dtype=jnp.int32)
-    own_rows = (positions + core * rows).astype(F32) < length
-    far_rows = (positions + (1 - core) * rows).astype(F32) < length
-    row_mask = own_rows.astype(F32)[:, None]
-    key_bias = jnp.where(jnp.concatenate([own_rows, far_rows]), 0.0, MASKED)[:, None]
-
+    section = spot.z
+
+    kind = lax.dynamic_index_in_dim(clip_class, section % 2, 0, False).astype(F32)
     norms = jnp.concatenate([norm_gain, norm_shift, jnp.zeros((6, width), F32)], axis=0)
-    first_front, norm_all, owns = first_weights(w_front[0], w_back[0], norms)
-    fronts, downs = [first_front.reshape(width, -1)] + [None] * (sections - 1), [None] * 2
-    front_shape = first_front.shape
-    down_shape = (32, w_back.shape[1] // 16, width)
-    gains, shifts = norm_all[:, 0], norm_all[:, 1]
-
-    hidden = (clip_pair[0].astype(F32) * row_mask).astype(BF16)
-    row = lambda a: a.reshape(1, -1)
-    acts_home = jnp.zeros((clip_inputs.shape[0], padded, width), BF16)
+    (
+        key, value, key_far, value_far, extended, attended, act, slope,
+        fronts, downs, hidden, incoming, acts_home, row_mask, key_bias, norm_all,
+    ) = forward(
+        clip_inputs, out_grad, jnp.broadcast_to(kind, (8, 128)), w_front[0], w_back[0], norms,
+        bias_query_value, bias_attn_out, bias_up, bias_down, rows,
+    )
+    acts = [hidden[s + 1] for s in range(sections)]
     grads_home = jnp.zeros((clip_inputs.shape[0], 2 * rows, width), BF16)
-    saved, acts = [], []
-    acts_beside = {
-        ("f", 1): [(0, 0, 112)], ("f", 2): [(0, 112, 496), (1, 0, 128)], ("f", 3): [(1, 128, 320), (2, 0, 288)],
-        ("b", 3): [(1, 448, 160), (2, 288, 320), (3, 0, 192)], ("b", 2): [(3, 192, 416)],
-    }
+    acts_beside = {("b", 3): [(2, 160, 448), (3, 0, 192)], ("b", 2): [(3, 192, 416)]}
     grads_beside = {("b", 1): [(3, 0, 400)], ("b", 0): [(3, 400, 208), (1, 0, rows), (2, 0, 192)]}
 
     def travel(where, held, plan, home):
         steps = 9 if where[1] % 2 == 0 else 3
         return deliver_guest([(held[s], s, start, size) for s, start, size in plan[where]], home, steps)
 
-    for s in range(sections):
-        layer = s // 2
-        gain, shift = row(gains[s]), row(shifts[s])
-        guests = []
-        if s == 0:
-            guests.append(plane_gather_guest([(owns["front", 1], 0, 0)], [front_shape], [(0, 5, 7)]))
-            guests.append(spread_gather_guest(
-                [(owns["back", 0], 0, (0, 4), (6, 9, 9), 0), (owns["back", 1], 1, (0,), (4, 8, 9), 16)], down_shape
-            ))
-        elif s == 2:
-            parts = [(owns["front", 3], 0, 0), (owns["back", 2], 1, 0), (owns["back", 3], 1, 16)]
-            guests.append(plane_gather_guest(parts, [front_shape, down_shape], [(0, 5, 8), (0, 7, 9), (0, 8, 9)]))
-        elif s == 1:
-            guests.append(plane_gather_guest([(owns["front", 2], 0, 0)], [front_shape], [(0, 3, 3)]))
-        onward = {0: [("front", 2), ("front", 3), ("back", 2), ("back", 3)], 1: [("front", 3), ("back", 3)]}.get(s, [])
-        if onward:
-            hops = [(i, key[1], 2 + s, "both") for i, key in enumerate(onward)]
-            if s == 0:
-                hops.insert(0, (0, 2, 1, "up"))
-            guests.append(spread_hop_guest([owns[key] for key in onward], hops))
-        if s:
-            guests.append(travel(("f", s), acts, acts_beside, acts_home))
-        if s % 2 == 0:
-            pair = bias_query_value[layer]
-            bias = jnp.concatenate([pair[:width], jnp.zeros((width,), F32), pair[width:]])
-            (*kept, leaving), carried = attention_forward(
-                hidden, row_mask, gain, shift, fronts[s], row(bias), key_bias, row(bias_attn_out[layer]),
-                guests, 2 + s,
-            )
-        else:
-            (*kept, leaving), carried = ff_forward(
-                hidden, row_mask, gain, shift, fronts[s], row(bias_up[layer]), downs[layer], row(bias_down[layer]),
-                guests, 2 + s,
-            )
-        if s:
-            (acts_home,) = carried[-1]
-        if s == 0:
-            fronts[1], downs[0] = carried[0][0].reshape(width, -1), carried[1][-1].reshape(-1, width)
-        elif s == 2:
-            fronts[3], downs[1] = carried[0][0].reshape(width, -1), carried[0][1].reshape(-1, width)
-        elif s == 1:
-            fronts[2] = carried[0][0].reshape(width, -1)
-        if onward:
-            owns.update(zip(onward, carried[2 - s]))
-        saved.append((hidden, *kept))
-        hidden = leaving
-        acts.append(leaving)
-
-    incoming = clip_pair[1]
     input_grads, grad_fronts, grad_downs = [None] * sections, [None] * sections, [None] * 2
     grad_gain, grad_shift = [None] * sections, [None] * sections
     query_sums, value_sums, out_sums, up_sums, down_sums = ([None] * 2 for _ in range(5))
@@ -1398,7 +1367,7 @@
         2: ((0, 1, 4, 8), (0, 2, 6, 9), (0, 2, 7, 9)), 1: ((0, 1, 3, 3),), 0: ((0, 1, 4, 8), (0, 2, 6, 9), (0, 2, 7, 9)),
     }
     for s in reversed(range(sections)):
-        layer, gain = s // 2, row(gains[s])
+        layer = s // 2
         guests = []
         if s < 3:
             jobs = [(grad_fronts[s + 1], 0)]
@@ -1413,21 +1382,19 @@
         else:
             guests.append(travel(("b", s), input_grads, grads_beside, grads_home))
         if s % 2 == 0:
-            entered, normed, key, value, key_far, value_far, extended, attended = saved[s]
             (
                 grad_fronts[s], incoming, grad_gain[s], grad_shift[s],
                 query_sums[layer], value_sums[layer], out_sums[layer],
             ), carried = attention_backward(
-                incoming, row_mask, entered, normed, key, value, key_far, value_far, extended, attended,
-                fronts[s], gain, key_bias, guests, 6 + s,
+                incoming, row_mask, hidden, key, value, key_far, value_far, extended, attended,
+                fronts, norm_all, key_bias, s, guests, 6 + s,
             )
         else:
-            entered, act, slope, normed = saved[s]
             (
                 grad_fronts[s], grad_downs[layer], incoming, grad_gain[s], grad_shift[s],
                 up_sums[layer], down_sums[layer],
             ), carried = ff_backward(
-                incoming, row_mask, entered, normed, act, slope, fronts[s], downs[layer], gain, guests, 6 + s
+                incoming, row_mask, hidden, act, slope, fronts, downs, norm_all, s, guests, 6 + s
             )
         input_grads[s] = incoming
         if ("b", s) in acts_beside:

time: 639 us -> 578 us (0.905)
  Pallas kernels: 576 us -> 534 us
  local copies, waits for them, and re-layouts: 32 us -> 15 us
    pallas_call x8 -> x4, Pallas kernels: 405 us -> 227 us  [hosted(): pl.pallas_call(kernel, grid=(grid,), in_specs=[s for _, s in operands + g...]
    pallas_call x1, Pallas kernels: 30.3 us -> 165 us  [forward(): pl.pallas_call(forward_body, grid=(2 * FORWARD_STEPS,), in_specs=[hbm] *...]
  transfers between devices with their start and end apart: 2 -> 0, of which waited for: 0 -> 0; matrix products, arithmetic and copies ran while one was open for 2% -> 0% of each run, Pallas kernels for 5% -> 0%
where the time goes in v5:
time: 578 us; the launch traced here: 569 us
  Pallas kernels  534 us (92%)
  other arithmetic  18 us (3%)
  local copies, waits for them, and re-layouts  15 us (3%)
    pallas_call x4, Pallas kernels, hosted(): pl.pallas_call(kernel, grid=(grid,), in_specs=[s for _, s in operands + g...  227 us
    pallas_call x1, Pallas kernels, forward(): pl.pallas_call(forward_body, grid=(2 * FORWARD_STEPS,), in_specs=[hbm] *...  165 us
    pallas_call x1, Pallas kernels, collect(): pl.pallas_call(collect_body, in_specs=[hbm] * 3 + [vmem] * (len(parts) +...  142 us

profile of v5, /device:TPU:0, one launch (start us, length us, event | category | flops | bytes accessed | tf_op | source)
XLA Modules:
  0.0 569.1 jit_solution(14547931795516526412)
XLA Ops:
  0.7 0.1 pad.12.clone
  0.7 1.4 maximum_maximum_fusion.refs_4_
  2.1 1.2 dynamic_slice.10
  4.0 0.6 broadcast_in_dim.21.refs_5_
  4.6 164.9 %forward.1 = (bf16[2,6,608,128]{3,2,1,0:T(8,128)(2,1)}, bf16[2,6,608,128]{3,2,1,0:T(8,128)(2,1)}, bf16[2,6,608,128]{3,2,1,0:T(8,128)(2,1)}, bf16[2,6,608,128]{3,...) custom-call(bf16[2,1280,768]{2,1,0:T(8,128)(2,1)} %refs_0_.1, ...), custom_call_target="tpu_custom_call" | custom-call | tf_op jit(solution)/shard_map/forward/pallas_call | solution.py:1301
  169.5 2.8 slice_bitcast_fusion
  172.4 43.1 %ff_backward.2 = (bf16[16,48,3072]{2,1,0:T(8,128)(2,1)}, bf16[32,96,768]{2,1,0:T(8,128)(2,1)}, bf16[608,768]{1,0:T(8,128)(2,1)}, f32[1,768]{1,0:T(1,128)}, f32[1...) custom-call(bf16[608,768]{1,0:T(8,128)(2,1)} %get-tuple-element.76.r, ...), custom_call_target="tpu_custom_call", output_to_operand_aliasing={{7}: (10, {})} | custom-call | tf_op jit(solution)/shard_map/ff_backward/pallas_call | solution.py:244
  215.4 78.1 %attention_backward.2 = (bf16[16,48,3072]{2,1,0:T(8,128)(2,1)}, bf16[608,768]{1,0:T(8,128)(2,1)}, f32[1,768]{1,0:T(1,128)}, f32[1,768]{1,0:T(1,128)}, f32[1,768]...) custom-call(bf16[608,768]{1,0:T(8,128)(2,1)} %get-tuple-element.85.r, ...), custom_call_target="tpu_custom_call", output_to_operand_aliasing={{10}: (15, {})} | custom-call | tf_op jit(solution)/shard_map/attention_backward/pallas_call | solution.py:244
  293.5 2.1 broadcast_in_dim.23.refs_13_
  295.6 45.9 %ff_backward.3 = (bf16[16,48,3072]{2,1,0:T(8,128)(2,1)}, bf16[32,96,768]{2,1,0:T(8,128)(2,1)}, bf16[608,768]{1,0:T(8,128)(2,1)}, f32[1,768]{1,0:T(1,128)}, f32[1...) custom-call(bf16[608,768]{1,0:T(8,128)(2,1)} %get-tuple-element.97.r, ...), custom_call_target="tpu_custom_call", output_to_operand_aliasing={{11}: (13, {})} | custom-call | tf_op jit(solution)/shard_map/ff_backward/pallas_call | solution.py:244
  341.5 0.0 copy-start.16
  341.5 0.0 copy-start.14
  341.6 0.0 copy-start.13
  341.6 0.0 copy-start.15
  341.6 0.0 copy-start.12
  341.6 0.0 copy-start.10
  341.6 0.0 copy-start.6
  341.6 0.0 copy-start.7
  341.6 0.0 copy-start.9
  341.6 0.0 copy-start.5
  341.6 0.0 copy-start.4
  341.6 0.0 copy-start.11
  341.7 0.0 copy-start.8
  341.7 60.4 %attention_backward.3 = (bf16[16,48,3072]{2,1,0:T(8,128)(2,1)}, bf16[608,768]{1,0:T(8,128)(2,1)}, f32[1,768]{1,0:T(1,128)}, f32[1,768]{1,0:T(1,128)}, f32[1,768]...) custom-call(bf16[608,768]{1,0:T(8,128)(2,1)} %get-tuple-element.102., ...), custom_call_target="tpu_custom_call", output_to_operand_aliasing={{14}: (21, {})} | custom-call | tf_op jit(solution)/shard_map/attention_backward/pallas_call | solution.py:244
  402.1 0.7 reduce
  402.8 0.0 copy-done.16
  402.9 0.0 copy-done.14
  402.9 0.0 copy-done.13
  402.9 0.7 reduce.4
  403.7 0.0 copy-done.15
  403.7 0.0 copy-done.12
  403.7 0.0 copy-done.10
  403.8 0.7 maximum_reduce_fusion
  404.5 0.0 copy-done.6
  404.5 0.0 copy-done.7
  404.6 0.7 reduce.10
  405.3 0.0 copy-done.9
  405.3 0.0 copy-done.5
  405.4 0.0 copy-done.4
  405.4 0.0 copy-done.11
  405.4 0.0 copy-done.8
  405.5 0.0 copy-start.3
  405.5 0.6 copy-done.3
  406.1 141.5 %collect.1 = (bf16[2,1216,768]{2,1,0:T(8,128)(2,1)}, bf16[16,48,3072]{2,1,0:T(8,128)(2,1)}, bf16[16,96,768]{2,1,0:T(8,128)(2,1)}, f32[144,128]{1,0:T(8,128)}) custom-call(bf16[608,768]{1,0:T(8,128)(2,1)} %get-tuple-element.110.refs_0_, bf16[608,768]{1,0:T(8,128)(2,1)} %get-tuple-element.97.refs_0_.refs_20_.refs_1_, ...), custom_call_target="tpu_custom_call", output_to_operand_aliasing={{0}: (11, {})} | custom-call | tf_op jit(solution)/shard_map/collect/pallas_call | solution.py:592
  547.6 0.0 copy-start
  547.6 6.0 %bitcast_convert_fusion.1 = f32[1,2,1280,768]{3,2,1,0:T(8,128)} fusion(bf16[2,1216,768]{2,1,0:T(8,128)(2,1)} %get-tuple-element.138), kind=kLoop, calls=%fused_computation.1 | loop fusion | flops 1966080 | bytes 11599872 | tf_op jit(solution)/shard_map/broadcast_in_dim | solution.py:1436
  553.7 0.0 copy-done
  553.7 0.0 copy-start.1
  553.7 5.0 bitcast_convert_fusion
  558.7 0.0 copy-start.2
  558.7 0.0 copy-done.1
  558.7 2.5 bitcast_convert_fusion.2
  561.3 0.0 copy-done.2
  561.3 0.6 constant_dynamic-slice_fusion
  561.9 0.6 reshape.148
  562.5 0.6 reshape.149
  563.1 0.6 reshape.150
  563.8 0.6 reshape.151
  564.4 4.3 copy.48
  (33 shorter events, 0.3 us)
Async XLA Ops:
  341.5 61.3 %copy-start.16 = (f32[1,768]{1,0:T(1,128)S(1)}, f32[1,768]{1,0:T(1,128)}, u32[]{:S(2)}) copy-start(f32[1,768]{1,0:T(1,128)} %get-tuple-element.120) | copy-start | bytes 9220
  341.5 61.3 %copy-start.14 = (f32[1,768]{1,0:T(1,128)S(1)}, f32[1,768]{1,0:T(1,128)}, u32[]{:S(2)}) copy-start(f32[1,768]{1,0:T(1,128)} %get-tuple-element.121) | copy-start | bytes 9220
  341.6 61.3 %copy-start.13 = (f32[1,768]{1,0:T(1,128)S(1)}, f32[1,768]{1,0:T(1,128)}, u32[]{:S(2)}) copy-start(f32[1,768]{1,0:T(1,128)} %get-tuple-element.122) | copy-start | bytes 9220
  341.6 62.1 %copy-start.15 = (f32[1,768]{1,0:T(1,128)S(1)}, f32[1,768]{1,0:T(1,128)}, u32[]{:S(2)}) copy-start(f32[1,768]{1,0:T(1,128)} %get-tuple-element.124) | copy-start | bytes 9220
  341.6 62.1 %copy-start.12 = (f32[1,768]{1,0:T(1,128)S(1)}, f32[1,768]{1,0:T(1,128)}, u32[]{:S(2)}) copy-start(f32[1,768]{1,0:T(1,128)} %get-tuple-element.125) | copy-start | bytes 9220
  341.6 62.2 %copy-start.10 = (f32[1,768]{1,0:T(1,128)S(1)}, f32[1,768]{1,0:T(1,128)}, u32[]{:S(2)}) copy-start(f32[1,768]{1,0:T(1,128)} %get-tuple-element.126) | copy-start | bytes 9220
  341.6 62.9 %copy-start.6 = (f32[1,768]{1,0:T(1,128)S(1)}, f32[1,768]{1,0:T(1,128)}, u32[]{:S(2)}) copy-start(f32[1,768]{1,0:T(1,128)} %get-tuple-element.129) | copy-start | bytes 9220
  341.6 62.9 %copy-start.7 = (f32[1,768]{1,0:T(1,128)S(1)}, f32[1,768]{1,0:T(1,128)}, u32[]{:S(2)}) copy-start(f32[1,768]{1,0:T(1,128)} %get-tuple-element.130) | copy-start | bytes 9220
  341.6 63.7 %copy-start.9 = (f32[1,768]{1,0:T(1,128)S(1)}, f32[1,768]{1,0:T(1,128)}, u32[]{:S(2)}) copy-start(f32[1,768]{1,0:T(1,128)} %get-tuple-element.132) | copy-start | bytes 9220
  341.6 63.7 %copy-start.5 = (f32[1,3072]{1,0:T(1,128)S(1)}, f32[1,3072]{1,0:T(1,128)}, u32[]{:S(2)}) copy-start(f32[1,3072]{1,0:T(1,128)} %get-tuple-element.133) | copy-start | bytes 36868
  341.6 63.7 %copy-start.4 = (f32[1,3072]{1,0:T(1,128)S(1)}, f32[1,3072]{1,0:T(1,128)}, u32[]{:S(2)}) copy-start(f32[1,3072]{1,0:T(1,128)} %get-tuple-element.134) | copy-start | bytes 36868
  341.6 63.7 %copy-start.11 = (f32[1,768]{1,0:T(1,128)S(1)}, f32[1,768]{1,0:T(1,128)}, u32[]{:S(2)}) copy-start(f32[1,768]{1,0:T(1,128)} %get-tuple-element.135) | copy-start | bytes 9220
  341.7 63.8 %copy-start.8 = (f32[1,768]{1,0:T(1,128)S(1)}, f32[1,768]{1,0:T(1,128)}, u32[]{:S(2)}) copy-start(f32[1,768]{1,0:T(1,128)} %get-tuple-element.136) | copy-start | bytes 9220
  405.5 0.6 copy-start.3
  547.6 6.1 %copy-start = (bf16[16,48,3072]{2,1,0:T(8,128)(2,1)S(1)}, bf16[16,48,3072]{2,1,0:T(8,128)(2,1)}, u32[]{:S(2)}) copy-start(bf16[16,48,3072]{2,1,0:T(8,128)(2,1)} %get-tuple-element.139) | copy-start | bytes 14155780
  553.7 5.1 copy-start.1
  558.7 2.6 copy-start.2

commit v6 on v5

--- a/solution.py
+++ b/solution.py
@@ -228,7 +228,7 @@
             parts = [[r.pop(0) for _ in range(n)] for r, n in (
                 (gins, len(g.inputs)), (gouts, len(g.outputs)), (gheld, len(g.scratch))
             )]
-            for at, actions in g.plan(spot, *parts).items():
+            for at, actions in g.plan(spot, *parts, held).items():
                 hooks.setdefault(at, []).extend(actions)
 
         def run(actions):
@@ -260,80 +260,33 @@
     return own, per_guest
 
 
-def deliver_guest(pieces, home, steps):
+def deliver_guest(pieces, home):
     sems = pltpu.SemaphoreType.DMA
     count = len(pieces)
-
-    def plan(spot, ins, outs, held):
+    arrays = [i for i, piece in enumerate(pieces) if not isinstance(piece[0], int)]
+
+    def plan(spot, ins, outs, held, body):
         send, recv = held
         hooks = {}
-        for i, (_, target, first, size) in enumerate(pieces):
+        sources = [body[p[0]] if isinstance(p[0], int) else ins[arrays.index(i)] for i, p in enumerate(pieces)]
+        for i, (_, target, first, size, steps) in enumerate(pieces):
             blocks = size // 16
-            for step in range(steps):
-                low, high = blocks * step // steps, blocks * (step + 1) // steps
+            for turn, step in enumerate(steps):
+                low, high = blocks * turn // len(steps), blocks * (turn + 1) // len(steps)
                 if high > low:
                     part = Deliver(
-                        spot, ins[i], outs[0], target, send.at[i], recv.at[i], first + 16 * low, 16 * (high - low)
+                        spot, sources[i], outs[0], target, send.at[i], recv.at[i], first + 16 * low, 16 * (high - low)
                     )
                     hooks.setdefault(step, []).append(part.start)
-            every = Deliver(spot, ins[i], outs[0], target, send.at[i], recv.at[i], first, size)
+            every = Deliver(spot, sources[i], outs[0], target, send.at[i], recv.at[i], first, size)
             hooks.setdefault("end", []).append(every.finish)
         return hooks
 
     return Guest(
-        [(piece[0], hbm_spec()) for piece in pieces] + [(home, hbm_spec())],
+        [(pieces[i][0], hbm_spec()) for i in arrays] + [(home, hbm_spec())],
         [(jax.ShapeDtypeStruct(home.shape, home.dtype), hbm_spec())],
         [sems((count, 2)), sems((count, 4))],
-        [(count, 0)], plan,
-    )
-
-
-def plane_sum_guest(jobs, stages):
-    sems = pltpu.SemaphoreType.DMA
-    shapes = [(a.shape[1], a.shape[2]) for a, _ in jobs]
-    arrays = []
-    for a, _ in jobs:
-        if not any(a is b for b in arrays):
-            arrays.append(a)
-    index = [next(i for i, b in enumerate(arrays) if b is a) for a, _ in jobs]
-
-    def plan(spot, ins, outs, held):
-        send, recv = held[-2:]
-        hooks = {}
-        for i, (_, first) in enumerate(jobs):
-            src = ins[index[i]].at[pl.ds(first, 16)]
-            job = PlaneSum(spot, src, held[6 * i : 6 * i + 6], send.at[i], recv.at[i])
-            actions = (job.start, job.first, job.second, functools.partial(job.third, outs[i]))
-            for at, action in zip(stages[i], actions):
-                hooks.setdefault(at, []).append(action)
-            hooks.setdefault("end", []).append(job.finish)
-        return hooks
-
-    return Guest(
-        [(a, hbm_spec()) for a in arrays],
-        [(jax.ShapeDtypeStruct((2,) + s, BF16), vmem_spec()) for s in shapes],
-        [b for s in shapes for b in PlaneSum.scratch(*s)] + [sems((len(jobs), 8)), sems((len(jobs), 8))],
-        (), plan,
-    )
-
-
-def section_hop_guest(jobs, start=0):
-    sems = pltpu.SemaphoreType.DMA
-
-    def plan(spot, ins, outs, held):
-        send, recv = held[-2:]
-        hops = [
-            SectionHop(spot, ins[i], outs[i], held[i], target, hop, send.at[i], recv.at[i])
-            for i, (_, target, hop) in enumerate(jobs)
-        ]
-        return {start: [h.start for h in hops], "end": [h.finish for h in hops]}
-
-    return Guest(
-        [(a, vmem_spec()) for a, _, _ in jobs],
-        [(jax.ShapeDtypeStruct(a.shape, BF16), vmem_spec()) for a, _, _ in jobs],
-        [pltpu.VMEM((2 * a.shape[0],) + a.shape[1:], BF16) for a, _, _ in jobs]
-        + [sems((len(jobs),)), sems((len(jobs), 2))],
-        (), plan,
+        [(len(arrays), 0)], plan,
     )
 
 
@@ -349,8 +302,8 @@
 
 
 class PlaneSum:
-    def __init__(self, spot, src, bufs, send, recv):
-        self.spot, self.src, self.send, self.recv = spot, src, send, recv
+    def __init__(self, spot, src, bufs, send, recv, in_place=False):
+        self.spot, self.src, self.send, self.recv, self.in_place = spot, src, send, recv, in_place
         self.half, self.from_mate, self.in_x, self.in_y, self.in_yx, self.in_xy = bufs
 
     @staticmethod
@@ -359,10 +312,10 @@
 
     def mate_copies(self):
         s, spot = self, self.spot
-        return (
-            pltpu.make_async_copy(s.src.at[pl.ds(spot.core * 8, 8)], s.half, s.send.at[0]),
-            remote(s.src.at[pl.ds((1 - spot.core) * 8, 8)], s.from_mate, s.send.at[1], s.recv.at[1], spot.mate),
-        )
+        away = remote(s.src.at[pl.ds((1 - spot.core) * 8, 8)], s.from_mate, s.send.at[1], s.recv.at[1], spot.mate)
+        if s.in_place:
+            return (away,)
+        return (pltpu.make_async_copy(s.src.at[pl.ds(spot.core * 8, 8)], s.half, s.send.at[0]), away)
 
     def start(self):
         for copy in self.mate_copies():
@@ -412,206 +365,190 @@
         first = pl.ds(0, 1)
         add_into(s.block(spot.c, 0), s.in_x.at[first], s.in_xy)
         add_into(s.block(spot.c, 1), s.in_y.at[first], s.in_yx)
-        out[...] = s.half[pl.ds(spot.c * 2, 2)]
+        for half in (0, 1):
+            out[half] = s.half[spot.c * 2 + half]
 
     def finish(self):
         for copy in self.first_copies() + self.second_copies():
             copy.wait_send()
 
 
-class SectionHop:
-    def __init__(self, spot, src, total, bufs, target, hop, send, recv):
-        self.spot, self.src, self.total, self.bufs, self.send, self.recv = spot, src, total, bufs, send, recv
-        last = spot.sections - 1
-        self.below = hop - 1 if hop <= target else None
-        self.above = last - hop + 1 if last - hop >= target else None
-
-    def copies(self):
-        s, spot, n = self, self.spot, self.src.shape[0]
-        up = remote(s.src, s.bufs.at[pl.ds(n, n)], s.send, s.recv.at[1], spot.above)
-        down = remote(s.src, s.bufs.at[pl.ds(0, n)], s.send, s.recv.at[0], spot.below)
-        return up, down
-
-    def start(self):
-        up, down = self.copies()
-        if self.below is not None:
-            pl.when(self.spot.z == self.below)(up.start)
-        if self.above is not None:
-            pl.when(self.spot.z == self.above)(down.start)
-        self.total[...] = self.src[...]
-
-    def finish(self):
-        up, down = self.copies()
-        n = self.src.shape[0]
-        if self.below is not None:
-            pl.when(self.spot.z == self.below)(up.wait_send)
-
-            @pl.when(self.spot.z == self.below + 1)
-            def _():
-                up.wait_recv()
-                add_into(self.total, self.bufs.at[pl.ds(n, n)])
-        if self.above is not None:
-            pl.when(self.spot.z == self.above)(down.wait_send)
-
-            @pl.when(self.spot.z == self.above - 1)
-            def _():
-                down.wait_recv()
-                add_into(self.total, self.bufs.at[pl.ds(0, n)])
-
-
-LEFT = (("front", 3, 2), ("back", 3, 2), ("front", 2, 1), ("back", 2, 2), ("front", 1, 0), ("back", 0, 0), ("back", 1, 0))
+LEFT = (
+    ("front", 0, 3, 2), ("back", None, 2, 2), ("front", 1, 3, 2), ("back", None, 3, 2),
+    ("front", 0, 1, 1), ("back", None, 0, 1), ("front", 1, 1, 1), ("back", None, 1, 1),
+)
 
 
 def collect_body(*refs):
     sections = lax.axis_size("section")
     refs_list = list(refs)
     take = lambda n: [refs_list.pop(0) for _ in range(n)]
-    last, second, first_front = take(3)
+    last, second, first_front, third_front = take(4)
     parts = take(len(LEFT))
     small, _ = take(2)
     home, front_out, back_out, small_out = take(4)
-    plane_bufs, own, (sums, arriving) = take(6), take(1)[0], take(2)
-    psend, precv, dsend, drecv, asend, arecv, ssend, srecv, stay_sem, zsend, zrecv = take(11)
-    hop_refs = refs_list
+    plane_bufs, own, third_bufs, third_own, (sums, arriving) = take(6), take(1)[0], take(6), take(1)[0], take(2)
+    totals = take(len(LEFT))
+    psend, precv, tsend, trecv, dsend, drecv, asend, arecv, ssend, srecv, stay_sem, zsend, zrecv, lsem = take(14)
     spot = Spot()
+    loads = [pltpu.make_async_copy(a, b, lsem.at[i]) for i, (a, b) in enumerate(zip(parts, totals))]
+    for load in loads:
+        load.start()
     spot.greet()
-    delivers = [
-        Deliver(spot, piece, home, target, dsend.at[target // 2], drecv.at[target // 2], *rows)
-        for piece, target, rows in ((last, 0, ()), (second, 2, (192, second.shape[0] - 192)))
-    ]
     plane = PlaneSum(spot, first_front, plane_bufs, psend, precv)
-    count = 0
-
-    def chain(src, target, done):
-        nonlocal count
-        hops = []
-        for hop in range(done + 1, max(target, sections - 1 - target) + 1):
-            total, bufs = hop_refs.pop(0), hop_refs.pop(0)
-            hops.append(SectionHop(spot, src, total, bufs, target, hop, zsend.at[count], zrecv.at[count]))
-            src, count = total, count + 1
-        return hops, src
-
-    chains = [chain(part, target, done) for part, (_, target, done) in zip(parts, LEFT)]
-    first_chains = [chain(own.at[pl.ds(i, 1)], 0, 0) for i in (0, 1)]
-
-    def turn(which, i):
-        for hops, _ in which:
-            if 0 < i <= len(hops):
-                hops[i - 1].finish()
-        for hops, _ in which:
-            if i < len(hops):
-                hops[i].start()
-
+    third_plane = PlaneSum(spot, third_front, third_bufs, tsend, trecv)
     plane.start()
-    turn(chains, 0)
+    third_plane.start()
+    rows = last.shape[0]
+    ahead = rows * 2 // 5 // 16 * 16
+    early, late, every = (
+        Deliver(spot, last, home, 0, dsend.at[0], drecv.at[0], *r) for r in ((0, ahead), (ahead, rows - ahead), ())
+    )
+    other = Deliver(spot, second, home, 2, dsend.at[1], drecv.at[1])
+
+    sequences = []
+
+    def sequence(total, target, done):
+        n = len(sequences)
+        chain = Chain(spot, total, take(len(sides(target))), target, zsend.at[n], zrecv.at[n])
+        sequences.append((chain, range(done + 1, hops_of(target) + 1)))
+        return sequences[-1]
+
+    chains = [sequence(total, target, done) for total, (_, _, target, done) in zip(totals, LEFT)]
+    first_chains = [sequence(own.at[pl.ds(i, 1)], 0, 0) for i in (0, 1)]
+    third_chain = [sequence(third_own, 2, 0)]
+
+    def advance(which, turn):
+        for chain, hops in which:
+            if 0 < turn <= len(hops):
+                chain.take(hops[turn - 1])
+            if turn < len(hops):
+                chain.give(hops[turn])
+
+    for load in loads:
+        load.wait()
+    advance(chains, 0)
+    early.start()
+    other.start()
     sums[0] = small[...]
     partners = [spot.mate, spot.x, spot.y] + [
         {"section": spot.z + bit * (1 - 2 * ((spot.z // bit) % 2))}
         for bit in (1 << i for i in range((sections - 1).bit_length()))
     ]
+    steps = len(partners)
+
+    def small_copy(i):
+        return remote(sums.at[i], arriving.at[i], ssend.at[i], srecv.at[i], partners[i])
 
     def small_step(i):
-        copy = remote(sums.at[i], arriving.at[i], ssend.at[i], srecv.at[i], partners[i])
-        copy.start()
-        copy.wait()
-        sums[i + 1] = sums[i] + arriving[i]
+        if 0 < i <= steps:
+            small_copy(i - 1).wait()
+            sums[i] = sums[i - 1] + arriving[i - 1]
+        if i < steps:
+            small_copy(i).start()
 
     small_step(0)
     plane.first()
-    for deliver in delivers:
-        deliver.start()
-    turn(chains, 1)
-    for i in range(1, len(partners)):
-        small_step(i)
-    small_out[...] = sums[len(partners)]
+    small_step(1)
     plane.second()
-    turn(chains, 2)
+    third_plane.first()
+    small_step(2)
     plane.third(own)
-    turn(first_chains[:1], 0)
-    turn(first_chains[1:], 0)
-    turn(chains, 3)
+    advance(first_chains, 0)
+    advance(chains, 1)
+    third_plane.second()
+    small_step(3)
+    advance(first_chains, 1)
+    advance(chains, 2)
+    third_plane.third(third_own)
+    advance(third_chain, 0)
+    advance(first_chains, 2)
+    late.start()
+    small_step(4)
     gathers = [
         PlaneGather(spot, out, asend.at[i], arecv.at[i]) for i, out in enumerate((front_out, back_out))
     ]
-    ends = {(kind, target): end for (kind, target, _), (_, end) in zip(LEFT, chains)}
-    stays = []
 
     def begin(i, kind):
         gather = gathers[i]
+        blocks = gather.blocks(spot.core, spot.c)
         for z in range(sections):
-            blocks = gather.blocks(spot.core, spot.c)
-            if kind == "front" and z == 0:
-                pieces = [
-                    (end, gather.dst.at[gather.blocks(spot.core, spot.c, half)], stay_sem.at[half])
-                    for half, (_, end) in enumerate(first_chains)
-                ]
+            if kind == "back":
+                held = [t for t, (name, _, target, _) in zip(totals, LEFT) if name == kind and target == z]
+                pieces = [(held[0], gather.dst.at[blocks])]
+            elif z in (1, 3):
+                held = [t for t, (name, _, target, _) in zip(totals, LEFT) if name == kind and target == z]
+                size = held[0].shape[2]
+                pieces = [(t, gather.dst.at[blocks, :, pl.ds(n * size, size)]) for n, t in enumerate(held)]
             else:
-                pieces = [(ends[kind, z], gather.dst.at[blocks], stay_sem.at[2 + i])]
-            copies = [pltpu.make_async_copy(*piece) for piece in pieces]
+                pieces = [(own if z == 0 else third_own, gather.dst.at[blocks])]
+            copies = [pltpu.make_async_copy(a, b, stay_sem.at[i, n]) for n, (a, b) in enumerate(pieces)]
 
             @pl.when(spot.z == z)
-            def _(gather=gather, copies=copies):
+            def _(gather=gather, copies=copies, blocks=blocks):
                 for copy in copies:
                     copy.start()
                 for copy in copies:
                     copy.wait()
-                gather.begin(gather.dst.at[gather.blocks(spot.core, spot.c)])
+                gather.begin(gather.dst.at[blocks])
 
     begin(1, "back")
-    turn(first_chains[:1], 1)
-    turn(first_chains[1:], 1)
+    advance(third_chain, 1)
+    small_step(5)
+    small_out[...] = sums[steps]
     gathers[1].second()
-    turn(first_chains[:1], 2)
-    turn(first_chains[1:], 2)
+    advance(first_chains, 3)
+    advance(third_chain, 2)
+    begin(0, "front")
     gathers[1].third()
-    turn(first_chains[:1], 3)
-    turn(first_chains[1:], 3)
-    begin(0, "front")
     gathers[0].second()
     gathers[0].third()
     for gather in gathers:
         gather.finish()
-    for deliver in delivers:
+    for deliver in (every, other):
         deliver.finish()
     plane.finish()
-
-
-def collect(last, second, home, first_front, parts, small):
+    third_plane.finish()
+    for chain, hops in sequences:
+        for hop in hops:
+            chain.leave(hop)
+
+
+def collect(last, second, home, first_front, third_front, parts, small):
     sections = lax.axis_size("section")
     hbm, vmem = hbm_spec(), vmem_spec()
     steps = 3 + (sections - 1).bit_length()
     sems = pltpu.SemaphoreType.DMA
     front_shape = first_front.shape
     back_shape = (16,) + parts[1].shape[1:]
-    hop_scratch, hops = [], 0
-    jobs = [(p.shape, target, done) for p, (_, target, done) in zip(parts, LEFT)]
-    for shape, target, done in jobs + [((1,) + front_shape[1:], 0, 0)] * 2:
-        for _ in range(done, max(target, sections - 1 - target)):
-            hop_scratch += [pltpu.VMEM(shape, BF16), pltpu.VMEM((2 * shape[0],) + shape[1:], BF16)]
-            hops += 1
+    buffers = []
+    jobs = [(p.shape, left[2]) for p, left in zip(parts, LEFT)]
+    jobs += [((1,) + front_shape[1:], 0)] * 2 + [((2,) + front_shape[1:], 2)]
+    for shape, target in jobs:
+        buffers += [pltpu.VMEM(shape, BF16)] * len(sides(target))
     return pl.pallas_call(
         collect_body,
-        in_specs=[hbm] * 3 + [vmem] * (len(parts) + 1) + [hbm],
+        in_specs=[hbm] * (4 + len(parts)) + [vmem, hbm],
         out_specs=[hbm] * 3 + [vmem],
         out_shape=[
             jax.ShapeDtypeStruct(home.shape, BF16), jax.ShapeDtypeStruct(front_shape, BF16),
             jax.ShapeDtypeStruct(back_shape, BF16), jax.ShapeDtypeStruct(small.shape, F32),
         ],
-        scratch_shapes=PlaneSum.scratch(*front_shape[1:])
+        scratch_shapes=(PlaneSum.scratch(*front_shape[1:]) + [pltpu.VMEM((2,) + front_shape[1:], BF16)]) * 2
+        + [pltpu.VMEM((steps + 1,) + small.shape, F32), pltpu.VMEM((steps,) + small.shape, F32)]
+        + [pltpu.VMEM(p.shape, BF16) for p in parts]
         + [
-            pltpu.VMEM((2,) + front_shape[1:], BF16),
-            pltpu.VMEM((steps + 1,) + small.shape, F32), pltpu.VMEM((steps,) + small.shape, F32),
-            sems((8,)), sems((8,)), sems((2, 2)), sems((2, 4)),
-            sems((2, 9)), sems((2, 9)), sems((steps,)), sems((steps,)), sems((4,)),
-            sems((hops,)), sems((hops, 2)),
+            sems((8,)), sems((8,)), sems((8,)), sems((8,)), sems((2, 2)), sems((2, 4)),
+            sems((2, 9)), sems((2, 9)), sems((steps,)), sems((steps,)), sems((2, 2)),
+            sems((len(jobs),)), sems((len(jobs), 2)), sems((len(parts),)),
         ]
-        + hop_scratch,
-        input_output_aliases={4 + len(parts): 0},
+        + buffers,
+        input_output_aliases={5 + len(parts): 0},
         compiler_params=pltpu.CompilerParams(
             collective_id=1, has_side_effects=True, vmem_limit_bytes=KERNEL_VMEM
         ),
         name="collect",
-    )(last, second, first_front, *parts, small, home)
+    )(last, second, first_front, third_front, *parts, small, home)
 
 
 def norm_rows(hidden):
@@ -662,68 +599,6 @@
     unit, _ = norm_rows(hidden_ref[0].astype(F32))
     normed = (unit * norm_ref[0, 0:1, :] + norm_ref[0, 1:2, :]).astype(BF16)
     return normed.astype(F32).T.astype(BF16)
-
-
-def ff_backward_body(
-    spot, incoming_ref, mask_ref, hidden_ref, act_ref, slope_ref, up_ref, down_ref, norm_ref,
-    up_grad, down_grad, out_ref, gain_grad, shift_grad, up_bias_grad, down_bias_grad,
-    grad, normed_t, total,
-):
-    step, last = pl.program_id(0), pl.num_programs(0) - 1
-
-    @pl.when(step == 0)
-    def _():
-        grad_rows = mask_ref[...] * incoming_ref[...].astype(F32)
-        grad[...] = grad_rows.astype(BF16)
-        down_bias_grad[...] = jnp.sum(grad_rows, axis=0, keepdims=True)
-        normed_t[...] = transposed_norm(hidden_ref, norm_ref)
-
-    width = grad.shape[1]
-    up, down = up_ref[0].reshape(width, width), down_ref[0].reshape(width, width)
-    grad_pre = (contract_cols(grad[...], down) * slope_ref[0].astype(F32)).astype(BF16)
-    down_grad[...] = contract_rows(act_ref[0], grad[...]).astype(BF16).reshape(down_grad.shape)
-    up_bias_grad[...] = jnp.sum(grad_pre.astype(F32), axis=0, keepdims=True)
-    up_grad[...] = mm(normed_t[...], grad_pre).astype(BF16).reshape(up_grad.shape)
-    part = contract_cols(grad_pre, up)
-    total[...] = jnp.where(step == 0, part, total[...] + part)
-
-    @pl.when(step == last)
-    def _():
-        grad_hidden, gain_grad[...], shift_grad[...] = norm_backward(
-            hidden_ref[0].astype(F32), total[...], norm_ref[0, 0:1, :]
-        )
-        out_ref[...] = (grad[...].astype(F32) + grad_hidden).astype(BF16)
-
-
-def ff_backward(incoming, mask, hidden, act, slope, fronts, downs, norms, s, guests, collective_id):
-    rows, width = incoming.shape
-    units, size, layer = fronts.shape[3], width, s // 2
-    columns = pl.BlockSpec((1, rows, size), lambda i: (layer, 0, i))
-    vector = jax.ShapeDtypeStruct((1, width), F32)
-    in_specs = [
-        whole((rows, width)), whole((rows, 1)), pl.BlockSpec((1, rows, width), lambda i: (s, 0, 0)), columns, columns,
-        pl.BlockSpec((1, 16, width // 16, size), lambda i: (s, 0, 0, i)),
-        pl.BlockSpec((1, size * 32 // units, units // 32, width), lambda i: (layer, i, 0, 0)),
-        pl.BlockSpec((1,) + norms.shape[1:], lambda i: (s, 0, 0)),
-    ]
-    out_specs = ([
-            pl.BlockSpec((16, width // 16, size), lambda i: (0, 0, i)),
-            pl.BlockSpec((size * 32 // units, units // 32, width), lambda i: (i, 0, 0)),
-            whole((rows, width)), whole((1, width)), whole((1, width)),
-            pl.BlockSpec((1, size), lambda i: (0, i)), whole((1, width)),
-        ])
-    out_shape = ([
-            jax.ShapeDtypeStruct((16, width // 16, units), BF16), jax.ShapeDtypeStruct((32, units // 32, width), BF16),
-            jax.ShapeDtypeStruct((rows, width), BF16), vector, vector,
-            jax.ShapeDtypeStruct((1, units), F32), vector,
-        ])
-    scratch = ([
-            pltpu.VMEM((rows, width), BF16), pltpu.VMEM((width, rows), BF16), pltpu.VMEM((rows, width), F32),
-        ])
-    return hosted(
-        ff_backward_body, units // size, list(zip((incoming, mask, hidden, act, slope, fronts, downs, norms), in_specs)), list(zip(out_shape, out_specs)), scratch,
-        guests, collective_id, "ff_backward",
-    )
 
 
 def lane_ids(shape):
@@ -782,142 +657,27 @@
 
 
 def pair_backward(query_of, grad_of, out_of, keys, values, key_sums, value_sums, rows, save):
-    lanes = lane_ids((rows, PAIR))
-    parts = []
-    for head in (0, 1):
-        aux = HEAD_DIM * (1 - head)
-        inside = (lanes // HEAD_DIM) == head
-        query = query_of(head)
-        grad = jnp.where(inside, grad_of().astype(F32), 0.0)
-        dots = jnp.sum(grad * out_of(), axis=1, keepdims=True)
-        for lane, part in enumerate(three_parts(-dots), aux):
-            grad = jnp.where(lanes == lane, part, grad)
-        probs = jnp.exp(contract_cols(query, keys[head]))
-        shifted = contract_cols(grad.astype(BF16), values[head])
-        grad_scores = (probs * shifted).astype(BF16)
-        parts.append(mm(grad_scores, keys[head]) * HEAD_DIM**-0.5)
-        value_sums[head] = mm(grad.T.astype(BF16), probs.astype(BF16)).T
-        key_sums[head] = mm(query.astype(F32).T.astype(BF16), grad_scores).T
-    save(jnp.where(lanes < HEAD_DIM, parts[0], parts[1]).astype(BF16))
-
-
-def attention_backward_body(
-    spot, incoming_ref, mask_ref, hidden_ref, key_ref, value_ref, key_far_ref, value_far_ref,
-    extended_ref, attended_ref, weight_ref, norm_ref, key_bias_ref,
-    weight_grad, out_ref, gain_grad, shift_grad, query_bias_grad, value_bias_grad, out_bias_grad,
-    grad, grad_out, attended, normed_t, total, grads, sent, arrived, keys, values, key_sums, value_sums,
-    send, recv,
-):
-    step, last = pl.program_id(0), pl.num_programs(0) - 1
-    rows, width = grad.shape
-    pairs = width // PAIR
-
-    def swap_of(p):
-        return swap_with_mate(spot, sent.at[p], arrived.at[p], send.at[p], recv.at[p])
-
-    @pl.when(step == 0)
-    def _():
-        grad_rows = mask_ref[...] * incoming_ref[...].astype(F32)
-        grad[...] = grad_rows.astype(BF16)
-        out_bias_grad[...] = jnp.sum(grad_rows, axis=0, keepdims=True)
-        for p, part in enumerate(pairs_of(mm(grad[...], weight_ref[0].reshape(width, width)).astype(BF16))):
-            grad_out[p] = part
-
-    @pl.when(step < pairs)
-    def _():
-        p = step
+    for start, size in ((0, 256), (256, rows - 256)):
+        span = slice(start, start + size)
+        lanes = lane_ids((size, PAIR))
+        parts = []
         for head in (0, 1):
-            extend_keys(
-                keys.at[head], values.at[head],
-                [(key_ref[0, 0], value_ref[0, 0]), (key_far_ref[0, 0], value_far_ref[0, 0])], key_bias_ref, head,
-            )
-        attended[p] = attended_ref[0, 0].astype(BF16)
-
-        def save(value):
-            grads[0, p] = value
-
-        pair_backward(
-            lambda head: extended_ref[0, head], lambda: grad_out[p], lambda: attended_ref[0, 0],
-            keys, values, key_sums, value_sums, rows, save,
-        )
-        first = lane_ids((rows, PAIR)) < HEAD_DIM
-        for j, sums in enumerate((key_sums, value_sums)):
-            grads[1 + j, p] = jnp.where(first, sums[0, :rows, :], sums[1, :rows, :]).astype(BF16)
-            sent[p, j] = jnp.where(first, sums[0, rows:, :], sums[1, rows:, :]).astype(BF16)
-        swap_of(p).start()
-
-    @pl.when(step == pairs)
-    def _():
-        normed_t[...] = transposed_norm(hidden_ref, norm_ref)
-        for p in range(pairs):
-            swap_of(p).wait()
-            for j in (0, 1):
-                grads[1 + j, p] = (grads[1 + j, p].astype(F32) + arrived[p, j].astype(F32)).astype(BF16)
-
-    @pl.when((step >= pairs) & (step < last))
-    def _():
-        j = step - pairs
-        part = joined(grads, (j,))
-        sums = jnp.sum(part.astype(F32), axis=0, keepdims=True)
-
-        @pl.when(j == 0)
-        def _():
-            query_bias_grad[...] = sums
-
-        @pl.when(j == 2)
-        def _():
-            value_bias_grad[...] = sums
-
-        weight_grad[...] = mm(normed_t[...], part).astype(BF16).reshape(weight_grad.shape)
-        product = contract_cols(part, weight_ref[0].reshape(width, width))
-        total[...] = jnp.where(j == 0, product, total[...] + product)
-
-    @pl.when(step == last)
-    def _():
-        weight_grad[...] = contract_rows(grad[...], joined(attended)).astype(BF16).reshape(weight_grad.shape)
-        grad_hidden, gain_grad[...], shift_grad[...] = norm_backward(
-            hidden_ref[0].astype(F32), total[...], norm_ref[0, 0:1, :]
-        )
-        out_ref[...] = (grad[...].astype(F32) + grad_hidden).astype(BF16)
-
-
-def attention_backward(
-    incoming, mask, hidden, key, value, key_far, value_far, extended, attended, fronts, norms, key_bias, s,
-    guests, collective_id,
-):
-    rows, width = incoming.shape
-    layer = s // 2
-    pairs = width // PAIR
-    pair = lambda i: jnp.minimum(i, pairs - 1)
-    block = pl.BlockSpec((1, 1, rows, PAIR), lambda i: (layer, pair(i), 0, 0))
-    vector = jax.ShapeDtypeStruct((1, width), F32)
-    part = lambda i: jnp.where(i < pairs, 3, jnp.minimum(i - pairs, 2))
-    in_specs = [whole((rows, width)), whole((rows, 1)), pl.BlockSpec((1, rows, width), lambda i: (s, 0, 0))]
-    in_specs += [block] * 4 + [
-        pl.BlockSpec((1, 2, rows, PAIR), lambda i: (layer, pair(i), 0, 0)), block,
-        pl.BlockSpec((1, 16, width // 16, width), lambda i: (s, 0, 0, part(i))),
-        pl.BlockSpec((1,) + norms.shape[1:], lambda i: (s, 0, 0)), whole((2 * rows, 1)),
-    ]
-    out_specs = ([
-            pl.BlockSpec((16, width // 16, width), lambda i: (0, 0, jnp.maximum(i - pairs, 0))),
-            whole((rows, width)),
-        ] + [whole((1, width))] * 5)
-    out_shape = ([
-            jax.ShapeDtypeStruct((16, width // 16, 4 * width), BF16), jax.ShapeDtypeStruct((rows, width), BF16),
-        ] + [vector] * 5)
-    scratch = ([
-            pltpu.VMEM((rows, width), BF16), pltpu.VMEM((pairs, rows, PAIR), BF16),
-            pltpu.VMEM((pairs, rows, PAIR), BF16), pltpu.VMEM((width, rows), BF16),
-            pltpu.VMEM((rows, width), F32), pltpu.VMEM((3, pairs, rows, PAIR), BF16),
-            pltpu.VMEM((pairs, 2, rows, PAIR), BF16), pltpu.VMEM((pairs, 2, rows, PAIR), BF16),
-            pltpu.VMEM((2, 2 * rows, PAIR), BF16), pltpu.VMEM((2, 2 * rows, PAIR), BF16),
-            pltpu.VMEM((2, 2 * rows, PAIR), F32), pltpu.VMEM((2, 2 * rows, PAIR), F32),
-            pltpu.SemaphoreType.DMA((pairs,)), pltpu.SemaphoreType.DMA((pairs,)),
-        ])
-    return hosted(
-        attention_backward_body, pairs + 4, list(zip((incoming, mask, hidden, key, value, key_far, value_far, extended, attended, fronts, norms, key_bias), in_specs)), list(zip(out_shape, out_specs)), scratch,
-        guests, collective_id, "attention_backward",
-    )
+            aux = HEAD_DIM * (1 - head)
+            inside = (lanes // HEAD_DIM) == head
+            query = query_of(head, span)
+            grad = jnp.where(inside, grad_of(span).astype(F32), 0.0)
+            dots = jnp.sum(grad * out_of(span), axis=1, keepdims=True)
+            for lane, part in enumerate(three_parts(-dots), aux):
+                grad = jnp.where(lanes == lane, part, grad)
+            probs = jnp.exp(contract_cols(query, keys[head]))
+            shifted = contract_cols(grad.astype(BF16), values[head])
+            grad_scores = (probs * shifted).astype(BF16)
+            parts.append(mm(grad_scores, keys[head]) * HEAD_DIM**-0.5)
+            to_values = mm(grad.T.astype(BF16), probs.astype(BF16)).T
+            to_keys = mm(query.astype(F32).T.astype(BF16), grad_scores).T
+            value_sums[head] = to_values if start == 0 else value_sums[head] + to_values
+            key_sums[head] = to_keys if start == 0 else key_sums[head] + to_keys
+        save(span, jnp.where(lanes < HEAD_DIM, parts[0], parts[1]).astype(BF16))
 
 
 class Weight(PlaneGather):
@@ -1332,6 +1092,279 @@
     )(clips, grads, front_b, back_b, norms, kind, bias_qv, bias_attn, bias_up, bias_down)
 
 
+FF_STEPS = 4
+
+
+def backward_body(
+    spot, incoming_ref, mask_ref, hidden_ref, act_ref, slope_ref, front_ref, down_ref, norm_ref,
+    key_ref, value_ref, key_far_ref, value_far_ref, extended_ref, attended_ref, key_bias_ref,
+    weight_grad, mid_out, out_ref, ff_gain_grad, ff_shift_grad, up_bias_grad, down_bias_grad,
+    gain_grad, shift_grad, query_bias_grad, value_bias_grad, out_bias_grad,
+    mid, front_grad, down_grad, grad, normed_t, total, grad_out, attended, grads, sent, arrived,
+    keys, values, key_sums, value_sums, send, recv,
+):
+    step, last = pl.program_id(0), pl.num_programs(0) - 1
+    rows, width = grad.shape
+    pairs = width // PAIR
+    first_pair, first_part = FF_STEPS, FF_STEPS + pairs
+    weight = front_ref[0].reshape(width, width)
+
+    def swap_of(p):
+        return remote(sent.at[p], arrived.at[p], send.at[p], recv.at[p], spot.mate)
+
+    def start(source, bias_sums):
+        grad_rows = mask_ref[...] * source.astype(F32)
+        grad[...] = grad_rows.astype(BF16)
+        bias_sums[...] = jnp.sum(grad_rows, axis=0, keepdims=True)
+
+    def norm_grads(gain_sums, shift_sums):
+        grad_hidden, gain_sums[...], shift_sums[...] = norm_backward(
+            hidden_ref[0].astype(F32), total[...], norm_ref[0, 0:1, :]
+        )
+        return (grad[...].astype(F32) + grad_hidden).astype(BF16)
+
+    @pl.when(step == 0)
+    def _():
+        start(incoming_ref[...], down_bias_grad)
+        normed_t[...] = transposed_norm(hidden_ref, norm_ref)
+
+    @pl.when(step < FF_STEPS)
+    def _():
+        down = down_ref[0].reshape(width, width)
+        blocks = down_ref.shape[1]
+        grad_pre = (contract_cols(grad[...], down) * slope_ref[0].astype(F32)).astype(BF16)
+        down_part = contract_rows(act_ref[0], grad[...]).astype(BF16)
+        down_grad[pl.ds(step * blocks, blocks)] = down_part.reshape(down_ref.shape[1:])
+        up_bias_grad[...] = jnp.sum(grad_pre.astype(F32), axis=0, keepdims=True)
+        up_part = mm(normed_t[...], grad_pre).astype(BF16)
+        columns = pl.ds(pl.multiple_of(step * width, width), width)
+        front_grad[:, :, columns] = up_part.reshape(16, width // 16, width)
+        part = contract_cols(grad_pre, weight)
+        total[...] = jnp.where(step == 0, part, total[...] + part)
+
+    @pl.when(step == FF_STEPS - 1)
+    def _():
+        mid[...] = norm_grads(ff_gain_grad, ff_shift_grad)
+        mid_out[...] = mid[...]
+
+    @pl.when(step == first_pair)
+    def _():
+        start(mid[...], out_bias_grad)
+        for p, part in enumerate(pairs_of(mm(grad[...], weight).astype(BF16))):
+            grad_out[p] = part
+
+    @pl.when((step >= first_pair) & (step < first_part))
+    def _():
+        p = step - first_pair
+        for head in (0, 1):
+            extend_keys(
+                keys.at[head], values.at[head],
+                [(key_ref[0, 0], value_ref[0, 0]), (key_far_ref[0, 0], value_far_ref[0, 0])], key_bias_ref, head,
+            )
+        attended[p] = attended_ref[0, 0].astype(BF16)
+
+        def save(span, value):
+            grads[0, p, span, :] = value
+
+        pair_backward(
+            lambda head, span: extended_ref[0, head, span, :], lambda span: grad_out[p, span, :],
+            lambda span: attended_ref[0, 0, span, :], keys, values, key_sums, value_sums, rows, save,
+        )
+        first = lane_ids((rows, PAIR)) < HEAD_DIM
+        for j, sums in enumerate((key_sums, value_sums)):
+            grads[1 + j, p] = jnp.where(first, sums[0, :rows, :], sums[1, :rows, :]).astype(BF16)
+            sent[p, j] = jnp.where(first, sums[0, rows:, :], sums[1, rows:, :]).astype(BF16)
+        swap_of(p).start()
+
+    @pl.when(step == first_part)
+    def _():
+        normed_t[...] = transposed_norm(hidden_ref, norm_ref)
+        for p in range(pairs):
+            swap_of(p).wait()
+            for j in (0, 1):
+                grads[1 + j, p] = (grads[1 + j, p].astype(F32) + arrived[p, j].astype(F32)).astype(BF16)
+
+    @pl.when((step >= first_part) & (step < last))
+    def _():
+        j = step - first_part
+        part = joined(grads, (j,))
+        sums = jnp.sum(part.astype(F32), axis=0, keepdims=True)
+
+        @pl.when(j == 0)
+        def _():
+            query_bias_grad[...] = sums
+
+        @pl.when(j == 2)
+        def _():
+            value_bias_grad[...] = sums
+
+        weight_grad[...] = mm(normed_t[...], part).astype(BF16).reshape(weight_grad.shape)
+        product = contract_cols(part, weight)
+        total[...] = jnp.where(j == 0, product, total[...] + product)
+
+    @pl.when(step == last)
+    def _():
+        weight_grad[...] = contract_rows(grad[...], joined(attended)).astype(BF16).reshape(weight_grad.shape)
+        out_ref[...] = norm_grads(gain_grad, shift_grad)
+
+
+def backward(incoming, mask, hidden, act, slope, fronts, downs, norms, heads, key_bias, layer, guests, collective_id):
+    rows, width = incoming.shape
+    units, pairs = fronts.shape[3], width // PAIR
+    first_part = FF_STEPS + pairs
+    once = lambda shape: pl.BlockSpec(shape, lambda i: (0,) * len(shape), pipeline_mode=pl.Buffered(1))
+    sub = lambda i: 2 * layer + jnp.where(i < FF_STEPS, 1, 0)
+    unit = lambda i: jnp.minimum(i, FF_STEPS - 1)
+    pair = lambda i: jnp.clip(i - FF_STEPS, 0, pairs - 1)
+    column = lambda i: jnp.where(i < FF_STEPS, i, jnp.where(i < first_part, 3, jnp.minimum(i - first_part, 2)))
+    per_unit = pl.BlockSpec((1, rows, width), lambda i: (layer, 0, unit(i)))
+    per_pair = pl.BlockSpec((1, 1, rows, PAIR), lambda i: (layer, pair(i), 0, 0))
+    down_blocks = 32 // FF_STEPS
+    in_specs = [
+        once((rows, width)), once((rows, 1)),
+        pl.BlockSpec((1, rows, width), lambda i: (sub(i), 0, 0)), per_unit, per_unit,
+        pl.BlockSpec((1, 16, width // 16, width), lambda i: (sub(i), 0, 0, column(i))),
+        pl.BlockSpec((1, down_blocks) + downs.shape[2:], lambda i: (layer, unit(i), 0, 0)),
+        pl.BlockSpec((1,) + norms.shape[1:], lambda i: (sub(i), 0, 0)),
+        per_pair, per_pair, per_pair, per_pair,
+        pl.BlockSpec((1, 2, rows, PAIR), lambda i: (layer, pair(i), 0, 0)), per_pair, once((2 * rows, 1)),
+    ]
+    full, vector = jax.ShapeDtypeStruct((rows, width), BF16), jax.ShapeDtypeStruct((1, width), F32)
+    out_specs = [
+        pl.BlockSpec((16, width // 16, width), lambda i: (0, 0, jnp.maximum(i - first_part, 0))),
+        whole((rows, width)), whole((rows, width)), whole((1, width)), whole((1, width)),
+        pl.BlockSpec((1, width), lambda i: (0, unit(i))),
+    ] + [whole((1, width))] * 6
+    out_shape = [
+        jax.ShapeDtypeStruct((16, width // 16, units), BF16), full, full, vector, vector,
+        jax.ShapeDtypeStruct((1, units), F32),
+    ] + [vector] * 6
+    vmem = pltpu.VMEM
+    scratch = [
+        vmem((rows, width), BF16), vmem((16, width // 16, units), BF16), vmem(downs.shape[1:], BF16),
+        vmem((rows, width), BF16), vmem((width, rows), BF16), vmem((rows, width), F32),
+        vmem((pairs, rows, PAIR), BF16), vmem((pairs, rows, PAIR), BF16), vmem((3, pairs, rows, PAIR), BF16),
+        vmem((pairs, 2, rows, PAIR), BF16), vmem((pairs, 2, rows, PAIR), BF16),
+        vmem((2, 2 * rows, PAIR), BF16), vmem((2, 2 * rows, PAIR), BF16),
+        vmem((2, 2 * rows, PAIR), F32), vmem((2, 2 * rows, PAIR), F32),
+        pltpu.SemaphoreType.DMA((pairs,)), pltpu.SemaphoreType.DMA((pairs,)),
+    ]
+    args = (incoming, mask, hidden, act, slope, fronts, downs, norms, *heads, key_bias)
+    return hosted(
+        backward_body, first_part + 4, list(zip(args, in_specs)), list(zip(out_shape, out_specs)), scratch,
+        guests, collective_id, f"backward_{layer}", 63 * 2**20,
+    )
+
+
+def held_sum_guest(shapes, views, stages, targets, hop_steps):
+    sems = pltpu.SemaphoreType.DMA
+    sizes = [5 + len(sides(target)) for target in targets]
+
+    def plan(spot, ins, outs, held, body):
+        held = list(held)
+        send, recv, csend, crecv = held[-4:]
+        hooks = {}
+        for i, (number, index) in enumerate(views):
+            bufs, held = held[: sizes[i]], held[sizes[i] :]
+            src = body[number].at[index]
+            job = PlaneSum(
+                spot, src, [src.at[pl.ds(spot.core * 8, 8)]] + bufs[:5], send.at[i], recv.at[i], in_place=True
+            )
+            chain = Chain(spot, outs[i], bufs[5:], targets[i], csend.at[i], crecv.at[i])
+            actions = (job.start, job.first, job.second, functools.partial(job.third, outs[i]))
+            for at, action in zip(stages[i], actions):
+                hooks.setdefault(at, []).append(action)
+            hooks.setdefault(hop_steps[i], []).append(functools.partial(chain.give, 1))
+            hooks.setdefault("end", []).extend(
+                [job.finish, functools.partial(chain.take, 1), functools.partial(chain.leave, 1)]
+            )
+        return hooks
+
+    buffers = []
+    for shape, target in zip(shapes, targets):
+        buffers += PlaneSum.scratch(*shape)[1:] + [pltpu.VMEM((2,) + shape, BF16)] * len(sides(target))
+    count = len(shapes)
+    return Guest(
+        (), [(jax.ShapeDtypeStruct((2,) + s, BF16), vmem_spec()) for s in shapes],
+        buffers + [sems((count, 8)), sems((count, 8)), sems((count,)), sems((count, 2))], (), plan,
+    )
+
+
+def sides(target):
+    return [name for name, any_there in (("below", target > 0), ("above", target < 3)) if any_there]
+
+
+def hops_of(target):
+    return max(target, 3 - target)
+
+
+class Chain:
+    def __init__(self, spot, total, bufs, target, send, recv):
+        self.spot, self.total, self.target, self.send, self.recv = spot, total, target, send, recv
+        self.from_below, self.from_above = bufs[0], bufs[-1]
+
+    def ends(self, hop):
+        last = self.spot.sections - 1
+        return hop - 1 if hop <= self.target else None, last - hop + 1 if last - hop >= self.target else None
+
+    def rise(self):
+        return remote(self.total, self.from_below, self.send, self.recv.at[0], self.spot.above)
+
+    def fall(self):
+        return remote(self.total, self.from_above, self.send, self.recv.at[1], self.spot.below)
+
+    def give(self, hop):
+        below, above = self.ends(hop)
+        if below is not None:
+            pl.when(self.spot.z == below)(self.rise().start)
+        if above is not None:
+            pl.when(self.spot.z == above)(self.fall().start)
+
+    def take(self, hop):
+        below, above = self.ends(hop)
+        if below is not None:
+            @pl.when(self.spot.z == below + 1)
+            def _():
+                self.rise().wait_recv()
+                add_into(self.total, self.from_below)
+        if above is not None:
+            @pl.when(self.spot.z == above - 1)
+            def _():
+                self.fall().wait_recv()
+                add_into(self.total, self.from_above)
+
+    def leave(self, hop):
+        below, above = self.ends(hop)
+        if below is not None:
+            pl.when(self.spot.z == below)(self.rise().wait_send)
+        if above is not None:
+            pl.when(self.spot.z == above)(self.fall().wait_send)
+
+
+def chain_guest(jobs, hop):
+    sems = pltpu.SemaphoreType.DMA
+
+    def plan(spot, ins, outs, held, body):
+        held = list(held)
+        send, recv, loads = held[-3:]
+        begin, end = [], []
+        for i, (_, target) in enumerate(jobs):
+            bufs, held = held[: len(sides(target))], held[len(sides(target)) :]
+            chain = Chain(spot, outs[i], bufs, target, send.at[i], recv.at[i])
+            load = pltpu.make_async_copy(ins[i], outs[i], loads.at[i])
+            begin.extend([load.start, load.wait, functools.partial(chain.give, hop)])
+            end.extend([functools.partial(chain.take, hop), functools.partial(chain.leave, hop)])
+        return {0: begin, "end": end}
+
+    buffers = []
+    for a, target in jobs:
+        buffers += [pltpu.VMEM(a.shape, BF16)] * len(sides(target))
+    return Guest(
+        [(a, hbm_spec()) for a, _ in jobs], [(jax.ShapeDtypeStruct(a.shape, BF16), vmem_spec()) for a, _ in jobs],
+        buffers + [sems((len(jobs),)), sems((len(jobs), 2)), sems((len(jobs),))], (), plan,
+    )
+
+
 def per_device(
     clip_inputs, out_grad, clip_class, w_front, w_back, norm_gain, norm_shift,
     bias_query_value, bias_attn_out, bias_up, bias_down,
@@ -1352,61 +1385,46 @@
         bias_query_value, bias_attn_out, bias_up, bias_down, rows,
     )
     acts = [hidden[s + 1] for s in range(sections)]
+    acts = [hidden[s + 1] for s in range(sections)]
     grads_home = jnp.zeros((clip_inputs.shape[0], 2 * rows, width), BF16)
-    acts_beside = {("b", 3): [(2, 160, 448), (3, 0, 192)], ("b", 2): [(3, 192, 416)]}
-    grads_beside = {("b", 1): [(3, 0, 400)], ("b", 0): [(3, 400, 208), (1, 0, rows), (2, 0, 192)]}
-
-    def travel(where, held, plan, home):
-        steps = 9 if where[1] % 2 == 0 else 3
-        return deliver_guest([(held[s], s, start, size) for s, start, size in plan[where]], home, steps)
-
-    input_grads, grad_fronts, grad_downs = [None] * sections, [None] * sections, [None] * 2
+    heads = (key, value, key_far, value_far, extended, attended)
+    input_grads, grad_fronts = [None] * sections, [None] * sections
     grad_gain, grad_shift = [None] * sections, [None] * sections
     query_sums, value_sums, out_sums, up_sums, down_sums = ([None] * 2 for _ in range(5))
-    plane_stages = {
-        2: ((0, 1, 4, 8), (0, 2, 6, 9), (0, 2, 7, 9)), 1: ((0, 1, 3, 3),), 0: ((0, 1, 4, 8), (0, 2, 6, 9), (0, 2, 7, 9)),
-    }
-    for s in reversed(range(sections)):
-        layer = s // 2
-        guests = []
-        if s < 3:
-            jobs = [(grad_fronts[s + 1], 0)]
-            if s % 2 == 0:
-                jobs += [(grad_downs[layer], 0), (grad_downs[layer], 16)]
-            guests.append(plane_sum_guest(jobs, plane_stages[s]))
-        if s < 2:
-            hops = {1: [(3, 0), (2, 0), (3, 0)], 0: [(3, 1), (2, 1), (3, 1), (2, 0)]}[s]
-            guests.append(section_hop_guest([(part, target, done + 1) for part, (target, done) in zip(passing, hops)]))
-        if ("b", s) in acts_beside:
-            guests.append(travel(("b", s), acts, acts_beside, acts_home))
+    units = fronts.shape[3] // 2
+    halves = [pl.ds(0, units), pl.ds(units, units)]
+    views = []
+    for i in (0, 1):
+        views += [(1, (slice(None), slice(None), halves[i])), (2, pl.ds(16 * i, 16))]
+    shapes = [(width // 16, units), downs.shape[2:]] * 2
+    stages = ((2, 3, 6, 8), (2, 3, 7, 9), (4, 5, 9, 11), (4, 5, 10, 12))
+    hop_steps = (8, 9, 11, 12)
+    early, late = range(0, 4), range(4, 8)
+    for layer in (1, 0):
+        targets = (2 * layer + 1, 2 * layer, 2 * layer + 1, 2 * layer + 1)
+        guests = [held_sum_guest(shapes, views, stages, targets, hop_steps)]
+        if layer == 1:
+            guests.append(deliver_guest(
+                [(acts[2], 2, 160, rows - 160, early), (acts[3], 3, 0, 528, early)], acts_home
+            ))
         else:
-            guests.append(travel(("b", s), input_grads, grads_beside, grads_home))
-        if s % 2 == 0:
-            (
-                grad_fronts[s], incoming, grad_gain[s], grad_shift[s],
-                query_sums[layer], value_sums[layer], out_sums[layer],
-            ), carried = attention_backward(
-                incoming, row_mask, hidden, key, value, key_far, value_far, extended, attended,
-                fronts, norm_all, key_bias, s, guests, 6 + s,
-            )
+            guests.append(chain_guest(list(zip(passing, (3, 2, 3, 3))), 2))
+            guests.append(deliver_guest(
+                [(input_grads[3], 3, 0, rows, early), (0, 1, 0, rows, late)], grads_home
+            ))
+            guests.append(deliver_guest([(acts[3], 3, 528, rows - 528, (0,))], acts_home))
+        (
+            grad_fronts[2 * layer], input_grads[2 * layer + 1], input_grads[2 * layer],
+            grad_gain[2 * layer + 1], grad_shift[2 * layer + 1], up_sums[layer], down_sums[layer],
+            grad_gain[2 * layer], grad_shift[2 * layer], query_sums[layer], value_sums[layer], out_sums[layer],
+        ), carried = backward(
+            incoming, row_mask, hidden, act, slope, fronts, downs, norm_all, heads, key_bias, layer, guests, 2 + layer
+        )
+        incoming = input_grads[2 * layer]
+        if layer == 1:
+            passing, (acts_home,) = carried
         else:
-            (
-                grad_fronts[s], grad_downs[layer], incoming, grad_gain[s], grad_shift[s],
-                up_sums[layer], down_sums[layer],
-            ), carried = ff_backward(
-                incoming, row_mask, hidden, act, slope, fronts, downs, norm_all, s, guests, 6 + s
-            )
-        input_grads[s] = incoming
-        if ("b", s) in acts_beside:
-            (acts_home,) = carried[-1]
-        else:
-            (grads_home,) = carried[-1]
-        if s == 2:
-            passing = carried[0]
-        elif s == 1:
-            passing = [*carried[1], *carried[0]]
-        elif s == 0:
-            (front_3, back_2, back_3, front_2), (front_1, back_0, back_1) = carried[1], carried[0]
+            later, earlier, (grads_home,), (acts_home,) = carried
 
     pair_sums = [jnp.concatenate([q, v], axis=1) for q, v in zip(query_sums, value_sums)]
     small = jnp.concatenate(
@@ -1414,7 +1432,7 @@
     )
     grads_home, front_out, back_out, small = collect(
         input_grads[0], input_grads[2], grads_home, grad_fronts[0],
-        [front_3, back_3, front_2, back_2, front_1, back_0, back_1], small.reshape(-1, 128),
+        grad_fronts[2], [*earlier, *later], small.reshape(-1, 128),
     )
     front_out = front_out.reshape(width, -1)
     back_out = back_out.reshape(-1, width)

time: 578 us -> 516 us (0.89); the launches traced: 569 us -> 513 us
  Pallas kernels: 534 us -> 476 us
    pallas_call x4 -> x2, Pallas kernels: 227 us -> 191 us  [hosted(): pl.pallas_call(kernel, grid=(grid,), in_specs=[s for _, s in operands + g...]
    pallas_call x1, Pallas kernels: 142 us -> 120 us  [collect(): pl.pallas_call(collect_body, in_specs=[hbm] * (4 + len(parts)) + [vmem, h...]
where the time goes in v6:
time: 516 us; the launch traced here: 513 us
  Pallas kernels  476 us (92%)
  other arithmetic  20 us (4%)
  local copies, waits for them, and re-layouts  15.7 us (3%)
    pallas_call x2, Pallas kernels, hosted(): pl.pallas_call(kernel, grid=(grid,), in_specs=[s for _, s in operands + g...  191 us
    pallas_call x1, Pallas kernels, forward(): pl.pallas_call(forward_body, grid=(2 * FORWARD_STEPS,), in_specs=[hbm] *...  165 us
    pallas_call x1, Pallas kernels, collect(): pl.pallas_call(collect_body, in_specs=[hbm] * (4 + len(parts)) + [vmem, h...  120 us

profile of v6, /device:TPU:0, one launch (start us, length us, event | category | flops | bytes accessed | tf_op | source)
XLA Modules:
  0.0 513.3 jit_solution(17715933667587318673)
XLA Ops:
  0.7 0.1 pad.12.clone
  0.7 1.4 maximum_maximum_fusion.refs_4_
  2.1 1.2 dynamic_slice.10
  4.0 0.6 broadcast_in_dim.21.refs_5_
  4.6 165.0 %forward.1 = (bf16[2,6,608,128]{3,2,1,0:T(8,128)(2,1)}, bf16[2,6,608,128]{3,2,1,0:T(8,128)(2,1)}, bf16[2,6,608,128]{3,2,1,0:T(8,128)(2,1)}, bf16[2,6,608,128]{3,...) custom-call(bf16[2,1280,768]{2,1,0:T(8,128)(2,1)} %refs_0_.1, ...), custom_call_target="tpu_custom_call" | custom-call | tf_op jit(solution)/shard_map/forward/pallas_call | solution.py:1061
  169.6 2.8 slice_bitcast_fusion
  172.5 105.9 %backward_1.1 = (bf16[16,48,3072]{2,1,0:T(8,128)(2,1)}, bf16[608,768]{1,0:T(8,128)(2,1)}, bf16[608,768]{1,0:T(8,128)(2,1)}, f32[1,768]{1,0:T(1,128)}, f32[1,768]...) custom-call(bf16[608,768]{1,0:T(8,128)(2,1)} %get-tuple-element.68.r, ...), custom_call_target="tpu_custom_call", output_to_operand_aliasing={{16}: (17, {})} | custom-call | tf_op jit(solution)/shard_map/backward_1/pallas_call | solution.py:244
  278.4 2.1 broadcast_in_dim.22.refs_20_
  280.5 0.0 copy-start.12
  280.5 0.0 copy-start.11
  280.5 0.0 copy-start.10
  280.5 0.0 copy-start.9
  280.5 0.0 copy-start.5
  280.5 0.0 copy-start.6
  280.5 0.0 copy-start.8
  280.5 0.0 copy-start.4
  280.5 0.0 copy-start.7
  280.6 85.2 %backward_0.1 = (bf16[16,48,3072]{2,1,0:T(8,128)(2,1)}, bf16[608,768]{1,0:T(8,128)(2,1)}, bf16[608,768]{1,0:T(8,128)(2,1)}, f32[1,768]{1,0:T(1,128)}, f32[1,768]...) custom-call(bf16[608,768]{1,0:T(8,128)(2,1)} %get-tuple-element.84.r, ...), custom_call_target="tpu_custom_call", output_to_operand_aliasing={{20}: (20, {}), {21}: (22, {})} | custom-call | tf_op jit(solution)/shard_map/backward_0/pallas_call | solution.py:244
  365.8 0.7 reduce
  366.5 0.7 reduce.1
  367.2 0.0 copy-done.12
  367.3 0.0 copy-done.11
  367.3 0.7 reduce.4
  368.0 0.7 reduce.5
  368.7 0.0 copy-done.10
  368.8 0.0 copy-done.9
  368.8 0.7 maximum_reduce_fusion
  369.5 0.0 copy-done.5
  369.5 0.0 copy-done.6
  369.6 0.7 reduce.10
  370.3 0.0 copy-done.8
  370.4 0.7 constant_dynamic-update-slice_fusion.3
  371.1 0.0 copy-done.4
  371.1 0.7 reduce.12
  371.8 0.0 copy-done.7
  371.8 0.0 copy-start.3
  371.8 0.6 copy-done.3
  372.5 119.7 %collect.1 = (bf16[2,1216,768]{2,1,0:T(8,128)(2,1)}, bf16[16,48,3072]{2,1,0:T(8,128)(2,1)}, bf16[16,96,768]{2,1,0:T(8,128)(2,1)}, f32[144,128]{1,0:T(8,128)}) custom-call(bf16[608,768]{1,0:T(8,128)(2,1)} %get-tuple-element.92.refs_0_, bf16[608,768]{1,0:T(8,128)(2,1)} %get-tuple-element.84.refs_0_.refs_1_, ...), custom_call_target="tpu_custom_call", output_to_operand_aliasing={{0}: (13, {})} | custom-call | tf_op jit(solution)/shard_map/collect/pallas_call | solution.py:529
  492.1 0.0 copy-start
  492.1 6.0 %bitcast_convert_fusion.1 = f32[1,2,1280,768]{3,2,1,0:T(8,128)} fusion(bf16[2,1216,768]{2,1,0:T(8,128)(2,1)} %get-tuple-element.122), kind=kLoop, calls=%fused_computation.1 | loop fusion | flops 1966080 | bytes 11599872 | tf_op jit(solution)/shard_map/broadcast_in_dim | solution.py:1454
  498.2 0.0 copy-done
  498.2 0.0 copy-start.1
  498.2 5.0 bitcast_convert_fusion
  503.2 0.0 copy-start.2
  503.2 0.0 copy-done.1
  503.2 2.5 bitcast_convert_fusion.2
  505.8 0.0 copy-done.2
  505.8 0.6 constant_dynamic-slice_fusion
  506.4 0.6 reshape.148
  507.0 0.6 reshape.149
  507.6 0.6 reshape.150
  508.3 0.6 reshape.151
  508.9 4.3 copy.46
  (29 shorter events, 0.2 us)
Async XLA Ops:
  280.5 86.7 %copy-start.12 = (f32[1,768]{1,0:T(1,128)S(1)}, f32[1,768]{1,0:T(1,128)}, u32[]{:S(2)}) copy-start(f32[1,768]{1,0:T(1,128)} %get-tuple-element.105) | copy-start | bytes 9220
  280.5 86.8 %copy-start.11 = (f32[1,768]{1,0:T(1,128)S(1)}, f32[1,768]{1,0:T(1,128)}, u32[]{:S(2)}) copy-start(f32[1,768]{1,0:T(1,128)} %get-tuple-element.106) | copy-start | bytes 9220
  280.5 88.2 %copy-start.10 = (f32[1,768]{1,0:T(1,128)S(1)}, f32[1,768]{1,0:T(1,128)}, u32[]{:S(2)}) copy-start(f32[1,768]{1,0:T(1,128)} %get-tuple-element.109) | copy-start | bytes 9220
  280.5 88.3 %copy-start.9 = (f32[1,768]{1,0:T(1,128)S(1)}, f32[1,768]{1,0:T(1,128)}, u32[]{:S(2)}) copy-start(f32[1,768]{1,0:T(1,128)} %get-tuple-element.110) | copy-start | bytes 9220
  280.5 89.0 %copy-start.5 = (f32[1,768]{1,0:T(1,128)S(1)}, f32[1,768]{1,0:T(1,128)}, u32[]{:S(2)}) copy-start(f32[1,768]{1,0:T(1,128)} %get-tuple-element.113) | copy-start | bytes 9220
  280.5 89.0 %copy-start.6 = (f32[1,768]{1,0:T(1,128)S(1)}, f32[1,768]{1,0:T(1,128)}, u32[]{:S(2)}) copy-start(f32[1,768]{1,0:T(1,128)} %get-tuple-element.114) | copy-start | bytes 9220
  280.5 89.8 %copy-start.8 = (f32[1,768]{1,0:T(1,128)S(1)}, f32[1,768]{1,0:T(1,128)}, u32[]{:S(2)}) copy-start(f32[1,768]{1,0:T(1,128)} %get-tuple-element.116) | copy-start | bytes 9220
  280.5 90.5 %copy-start.4 = (f32[1,3072]{1,0:T(1,128)S(1)}, f32[1,3072]{1,0:T(1,128)}, u32[]{:S(2)}) copy-start(f32[1,3072]{1,0:T(1,128)} %get-tuple-element.118) | copy-start | bytes 36868
  280.5 91.2 %copy-start.7 = (f32[1,768]{1,0:T(1,128)S(1)}, f32[1,768]{1,0:T(1,128)}, u32[]{:S(2)}) copy-start(f32[1,768]{1,0:T(1,128)} %get-tuple-element.120) | copy-start | bytes 9220
  371.8 0.6 copy-start.3
  492.1 6.1 %copy-start = (bf16[16,48,3072]{2,1,0:T(8,128)(2,1)S(1)}, bf16[16,48,3072]{2,1,0:T(8,128)(2,1)}, u32[]{:S(2)}) copy-start(bf16[16,48,3072]{2,1,0:T(8,128)(2,1)} %get-tuple-element.123) | copy-start | bytes 14155780
  498.2 5.1 copy-start.1
  503.2 2.6 copy-start.2

commit v7 on v6

--- a/solution.py
+++ b/solution.py
@@ -153,7 +153,8 @@
 
 
 class Deliver:
-    def __init__(self, spot, src, dst, target, send, recv, start=0, size=None):
+    def __init__(self, spot, src, dst, target, send, recv, start=0, size=None, sources=None):
+        self.sources = range(spot.sections) if sources is None else sources
         self.spot, self.src, self.dst, self.target, self.send, self.recv = spot, src, dst, target, send, recv
         self.rows, self.start_row = src.shape[0], start
         self.size = size or src.shape[0]
@@ -175,20 +176,27 @@
 
     def start(self):
         away, stay = self.copies()
-        pl.when(self.home)(stay.start)
-        pl.when(jnp.logical_not(self.home))(away.start)
+        chosen = self.chosen()
+        pl.when(chosen & self.home)(stay.start)
+        pl.when(chosen & jnp.logical_not(self.home))(away.start)
+
+    def chosen(self):
+        return (self.spot.z >= min(self.sources)) & (self.spot.z <= max(self.sources))
 
     def finish(self):
         away, stay = self.copies()
-        pl.when(self.home)(stay.wait)
-        pl.when(jnp.logical_not(self.home))(away.wait_send)
+        chosen = self.chosen()
+        pl.when(chosen & self.home)(stay.wait)
+        pl.when(chosen & jnp.logical_not(self.home))(away.wait_send)
         spot = self.spot
         for slot in (0, 1):
             for core in (0, 1):
-                here = (spot.core * 2 + slot == spot.z) & (spot.core == core)
+                source = spot.core * 2 + slot
+                here = (source == spot.z) & (spot.core == core)
+                sent = (source >= min(self.sources)) & (source <= max(self.sources))
                 block = self.place(slot, core)
                 landing = remote(block, block, self.send.at[0], self.recv.at[slot * 2 + core], spot.mate)
-                pl.when((spot.z == self.target) & jnp.logical_not(here))(landing.wait_recv)
+                pl.when((spot.z == self.target) & jnp.logical_not(here) & sent)(landing.wait_recv)
 
 
 class Guest:
@@ -268,17 +276,18 @@
     def plan(spot, ins, outs, held, body):
         send, recv = held
         hooks = {}
-        sources = [body[p[0]] if isinstance(p[0], int) else ins[arrays.index(i)] for i, p in enumerate(pieces)]
-        for i, (_, target, first, size, steps) in enumerate(pieces):
+        held_by = [body[p[0]] if isinstance(p[0], int) else ins[arrays.index(i)] for i, p in enumerate(pieces)]
+        for i, (_, target, first, size, steps, *sources) in enumerate(pieces):
             blocks = size // 16
             for turn, step in enumerate(steps):
                 low, high = blocks * turn // len(steps), blocks * (turn + 1) // len(steps)
                 if high > low:
                     part = Deliver(
-                        spot, sources[i], outs[0], target, send.at[i], recv.at[i], first + 16 * low, 16 * (high - low)
+                        spot, held_by[i], outs[0], target, send.at[i], recv.at[i], first + 16 * low, 16 * (high - low),
+                        *sources,
                     )
                     hooks.setdefault(step, []).append(part.start)
-            every = Deliver(spot, sources[i], outs[0], target, send.at[i], recv.at[i], first, size)
+            every = Deliver(spot, held_by[i], outs[0], target, send.at[i], recv.at[i], first, size, *sources)
             hooks.setdefault("end", []).append(every.finish)
         return hooks
 
@@ -375,37 +384,32 @@
 
 LEFT = (
     ("front", 0, 3, 2), ("back", None, 2, 2), ("front", 1, 3, 2), ("back", None, 3, 2),
-    ("front", 0, 1, 1), ("back", None, 0, 1), ("front", 1, 1, 1), ("back", None, 1, 1),
+    ("front", 0, 1, 1), ("back", None, 0, 1), ("front", 1, 1, 1), ("back", None, 1, 0),
 )
+
+
+TAIL_CHUNKS = 4
 
 
 def collect_body(*refs):
     sections = lax.axis_size("section")
     refs_list = list(refs)
     take = lambda n: [refs_list.pop(0) for _ in range(n)]
-    last, second, first_front, third_front = take(4)
+    last, second, third, first_front, third_front = take(5)
     parts = take(len(LEFT))
-    small, _ = take(2)
+    vectors = take(2 * sections + 5 * (sections // 2))
+    take(1)
     home, front_out, back_out, small_out = take(4)
-    plane_bufs, own, third_bufs, third_own, (sums, arriving) = take(6), take(1)[0], take(6), take(1)[0], take(2)
+    sums, arriving = take(2)
     totals = take(len(LEFT))
-    psend, precv, tsend, trecv, dsend, drecv, asend, arecv, ssend, srecv, stay_sem, zsend, zrecv, lsem = take(14)
+    psend, precv, dsend, drecv, asend, arecv, ssend, srecv, stay_sem, zsend, zrecv, lsem = take(12)
     spot = Spot()
     loads = [pltpu.make_async_copy(a, b, lsem.at[i]) for i, (a, b) in enumerate(zip(parts, totals))]
     for load in loads:
         load.start()
     spot.greet()
-    plane = PlaneSum(spot, first_front, plane_bufs, psend, precv)
-    third_plane = PlaneSum(spot, third_front, third_bufs, tsend, trecv)
-    plane.start()
-    third_plane.start()
-    rows = last.shape[0]
-    ahead = rows * 2 // 5 // 16 * 16
-    early, late, every = (
-        Deliver(spot, last, home, 0, dsend.at[0], drecv.at[0], *r) for r in ((0, ahead), (ahead, rows - ahead), ())
-    )
-    other = Deliver(spot, second, home, 2, dsend.at[1], drecv.at[1])
-
+    size = first_front.shape[2] // TAIL_CHUNKS
+    columns = [pl.ds(c * size, size) for c in range(TAIL_CHUNKS)]
     sequences = []
 
     def sequence(total, target, done):
@@ -413,10 +417,6 @@
         chain = Chain(spot, total, take(len(sides(target))), target, zsend.at[n], zrecv.at[n])
         sequences.append((chain, range(done + 1, hops_of(target) + 1)))
         return sequences[-1]
-
-    chains = [sequence(total, target, done) for total, (_, _, target, done) in zip(totals, LEFT)]
-    first_chains = [sequence(own.at[pl.ds(i, 1)], 0, 0) for i in (0, 1)]
-    third_chain = [sequence(third_own, 2, 0)]
 
     def advance(which, turn):
         for chain, hops in which:
@@ -425,12 +425,32 @@
             if turn < len(hops):
                 chain.give(hops[turn])
 
-    for load in loads:
-        load.wait()
-    advance(chains, 0)
-    early.start()
-    other.start()
-    sums[0] = small[...]
+    chains = [sequence(total, target, done) for total, (_, _, target, done) in zip(totals, LEFT)]
+    planes, owns, chunk_chains = {}, {}, {}
+    for n, (z, grad) in enumerate(((0, first_front), (2, third_front))):
+        for c in range(TAIL_CHUNKS):
+            at = n * TAIL_CHUNKS + c
+            planes[z, c] = PlaneSum(spot, grad.at[:, :, columns[c]], take(6), psend.at[at], precv.at[at])
+            owns[z, c] = take(1)[0]
+            chunk_chains[z, c] = sequence(owns[z, c], z, 0)
+    every_chunk = range(TAIL_CHUNKS)
+    for z in (0, 2):
+        for c in every_chunk:
+            planes[z, c].start()
+    rows = last.shape[0]
+    ahead = rows * 3 // 4 // 16 * 16
+    early, late, every = (
+        Deliver(spot, last, home, 0, dsend.at[0], drecv.at[0], *r) for r in ((0, ahead), (ahead, rows - ahead), ())
+    )
+    other = [
+        Deliver(spot, second, home, 2, dsend.at[1], drecv.at[1], 0, rows, (0, 1)),
+        Deliver(spot, third, home, 3, dsend.at[2], drecv.at[2], 400, rows - 400),
+    ]
+    at = 0
+    for vector in vectors:
+        for first in range(0, vector.shape[1], sums.shape[2]):
+            sums[0, at : at + 1, :] = vector[:, first : first + sums.shape[2]]
+            at += 1
     partners = [spot.mate, spot.x, spot.y] + [
         {"section": spot.z + bit * (1 - 2 * ((spot.z // bit) % 2))}
         for bit in (1 << i for i in range((sections - 1).bit_length()))
@@ -448,107 +468,140 @@
             small_copy(i).start()
 
     small_step(0)
-    plane.first()
+    for c in every_chunk:
+        planes[0, c].first()
+    for load in loads:
+        load.wait()
+    advance(chains, 0)
+    early.start()
+    for deliver in other:
+        deliver.start()
     small_step(1)
-    plane.second()
-    third_plane.first()
+    for c in every_chunk:
+        planes[0, c].second()
+        if c:
+            planes[0, c - 1].third(owns[0, c - 1])
+            advance([chunk_chains[0, c - 1]], 0)
+        planes[2, c].first()
+    planes[0, TAIL_CHUNKS - 1].third(owns[0, TAIL_CHUNKS - 1])
+    advance([chunk_chains[0, TAIL_CHUNKS - 1]], 0)
     small_step(2)
-    plane.third(own)
-    advance(first_chains, 0)
+    late.start()
+    for c in every_chunk:
+        advance([chunk_chains[0, c]], 1)
     advance(chains, 1)
-    third_plane.second()
     small_step(3)
-    advance(first_chains, 1)
+    for c in every_chunk:
+        advance([chunk_chains[0, c]], 2)
+        planes[2, c].second()
+        if c:
+            planes[2, c - 1].third(owns[2, c - 1])
+            advance([chunk_chains[2, c - 1]], 0)
+    planes[2, TAIL_CHUNKS - 1].third(owns[2, TAIL_CHUNKS - 1])
+    advance([chunk_chains[2, TAIL_CHUNKS - 1]], 0)
+    small_step(4)
     advance(chains, 2)
-    third_plane.third(third_own)
-    advance(third_chain, 0)
-    advance(first_chains, 2)
-    late.start()
-    small_step(4)
-    gathers = [
-        PlaneGather(spot, out, asend.at[i], arecv.at[i]) for i, out in enumerate((front_out, back_out))
-    ]
-
-    def begin(i, kind):
-        gather = gathers[i]
-        blocks = gather.blocks(spot.core, spot.c)
-        for z in range(sections):
-            if kind == "back":
-                held = [t for t, (name, _, target, _) in zip(totals, LEFT) if name == kind and target == z]
-                pieces = [(held[0], gather.dst.at[blocks])]
-            elif z in (1, 3):
-                held = [t for t, (name, _, target, _) in zip(totals, LEFT) if name == kind and target == z]
-                size = held[0].shape[2]
-                pieces = [(t, gather.dst.at[blocks, :, pl.ds(n * size, size)]) for n, t in enumerate(held)]
-            else:
-                pieces = [(own if z == 0 else third_own, gather.dst.at[blocks])]
-            copies = [pltpu.make_async_copy(a, b, stay_sem.at[i, n]) for n, (a, b) in enumerate(pieces)]
+    fronts = [PlaneGather(spot, front_out.at[:, :, columns[c]], asend.at[c], arecv.at[c]) for c in every_chunk]
+    back = PlaneGather(spot, back_out, asend.at[TAIL_CHUNKS], arecv.at[TAIL_CHUNKS])
+
+    def held(kind, z, c):
+        if kind == "front" and z in (0, 2):
+            return owns[z, c]
+        found = [t for t, (name, _, target, _) in zip(totals, LEFT) if name == kind and target == z]
+        if kind == "back":
+            return found[0]
+        half, at = divmod(c * size, found[0].shape[2])
+        return found[half].at[:, :, pl.ds(at, size)]
+
+    def begin(gather, kind, sections_now, c=0):
+        for z in sections_now:
+            stay = pltpu.make_async_copy(
+                held(kind, z, c), gather.dst.at[gather.blocks(spot.core, spot.c)],
+                stay_sem.at[TAIL_CHUNKS if kind == "back" else c],
+            )
 
             @pl.when(spot.z == z)
-            def _(gather=gather, copies=copies, blocks=blocks):
-                for copy in copies:
-                    copy.start()
-                for copy in copies:
-                    copy.wait()
-                gather.begin(gather.dst.at[blocks])
-
-    begin(1, "back")
-    advance(third_chain, 1)
+            def _(z=z, stay=stay):
+                stay.start()
+                gather.begin(held(kind, z, c))
+
+    def stayed():
+        for c in range(TAIL_CHUNKS + 1):
+            kind, gather = ("front", fronts[c]) if c < TAIL_CHUNKS else ("back", back)
+            pltpu.make_async_copy(
+                held(kind, 1, 0 if kind == "back" else c), gather.dst.at[gather.blocks(spot.core, spot.c)],
+                stay_sem.at[c],
+            ).wait()
+
+    for c in every_chunk:
+        begin(fronts[c], "front", (1, 3), c)
+    for c in every_chunk:
+        advance([chunk_chains[0, c]], 3)
+        begin(fronts[c], "front", (0,), c)
+    for c in every_chunk:
+        advance([chunk_chains[2, c]], 1)
     small_step(5)
     small_out[...] = sums[steps]
-    gathers[1].second()
-    advance(first_chains, 3)
-    advance(third_chain, 2)
-    begin(0, "front")
-    gathers[1].third()
-    gathers[0].second()
-    gathers[0].third()
-    for gather in gathers:
+    for c in every_chunk:
+        advance([chunk_chains[2, c]], 2)
+        begin(fronts[c], "front", (2,), c)
+    begin(back, "back", range(sections))
+    for gather in fronts:
+        gather.second()
+    back.second()
+    for gather in (*fronts, back):
+        gather.third()
+    for gather in (*fronts, back):
         gather.finish()
-    for deliver in (every, other):
+    stayed()
+    for deliver in (every, *other):
         deliver.finish()
-    plane.finish()
-    third_plane.finish()
+    for plane in planes.values():
+        plane.finish()
     for chain, hops in sequences:
         for hop in hops:
             chain.leave(hop)
 
 
-def collect(last, second, home, first_front, third_front, parts, small):
+def collect(last, second, third, home, first_front, third_front, parts, vectors):
     sections = lax.axis_size("section")
+    width = last.shape[1]
+    small = jax.ShapeDtypeStruct((sum(v.shape[1] // width for v in vectors), width), F32)
     hbm, vmem = hbm_spec(), vmem_spec()
     steps = 3 + (sections - 1).bit_length()
     sems = pltpu.SemaphoreType.DMA
     front_shape = first_front.shape
+    chunk = (front_shape[1], front_shape[2] // TAIL_CHUNKS)
     back_shape = (16,) + parts[1].shape[1:]
     buffers = []
-    jobs = [(p.shape, left[2]) for p, left in zip(parts, LEFT)]
-    jobs += [((1,) + front_shape[1:], 0)] * 2 + [((2,) + front_shape[1:], 2)]
-    for shape, target in jobs:
-        buffers += [pltpu.VMEM(shape, BF16)] * len(sides(target))
+    for part, left in zip(parts, LEFT):
+        buffers += [pltpu.VMEM(part.shape, BF16)] * len(sides(left[2]))
+    for target in (0, 2):
+        for _ in range(TAIL_CHUNKS):
+            buffers += PlaneSum.scratch(*chunk) + [pltpu.VMEM((2,) + chunk, BF16)] * (1 + len(sides(target)))
+    jobs = len(parts) + 2 * TAIL_CHUNKS
     return pl.pallas_call(
         collect_body,
-        in_specs=[hbm] * (4 + len(parts)) + [vmem, hbm],
+        in_specs=[hbm] * (5 + len(parts)) + [vmem] * len(vectors) + [hbm],
         out_specs=[hbm] * 3 + [vmem],
         out_shape=[
             jax.ShapeDtypeStruct(home.shape, BF16), jax.ShapeDtypeStruct(front_shape, BF16),
             jax.ShapeDtypeStruct(back_shape, BF16), jax.ShapeDtypeStruct(small.shape, F32),
         ],
-        scratch_shapes=(PlaneSum.scratch(*front_shape[1:]) + [pltpu.VMEM((2,) + front_shape[1:], BF16)]) * 2
-        + [pltpu.VMEM((steps + 1,) + small.shape, F32), pltpu.VMEM((steps,) + small.shape, F32)]
+        scratch_shapes=[pltpu.VMEM((steps + 1,) + small.shape, F32), pltpu.VMEM((steps,) + small.shape, F32)]
         + [pltpu.VMEM(p.shape, BF16) for p in parts]
         + [
-            sems((8,)), sems((8,)), sems((8,)), sems((8,)), sems((2, 2)), sems((2, 4)),
-            sems((2, 9)), sems((2, 9)), sems((steps,)), sems((steps,)), sems((2, 2)),
-            sems((len(jobs),)), sems((len(jobs), 2)), sems((len(parts),)),
+            sems((2 * TAIL_CHUNKS, 8)), sems((2 * TAIL_CHUNKS, 8)), sems((3, 2)), sems((3, 4)),
+            sems((TAIL_CHUNKS + 1, 9)), sems((TAIL_CHUNKS + 1, 9)), sems((steps,)), sems((steps,)),
+            sems((TAIL_CHUNKS + 1,)), sems((jobs,)), sems((jobs, 2)), sems((len(parts),)),
         ]
         + buffers,
-        input_output_aliases={5 + len(parts): 0},
+        input_output_aliases={5 + len(parts) + len(vectors): 0},
         compiler_params=pltpu.CompilerParams(
             collective_id=1, has_side_effects=True, vmem_limit_bytes=KERNEL_VMEM
         ),
         name="collect",
-    )(last, second, first_front, third_front, *parts, small, home)
+    )(last, second, third, first_front, third_front, *parts, *vectors, home)
 
 
 def norm_rows(hidden):
@@ -779,11 +832,15 @@
         at = pl.ds(block * width, width)
         weight(("first", j), front.at[:, :, at], fronts.at[0, :, :, at], 0)
     for s in range(1, 4):
-        weight(("front", s), front, fronts.at[s], s)
+        for n in range(1 + s % 2):
+            size = fronts.shape[3] // (1 + s % 2)
+            at = pl.ds(n * size, size)
+            weight(("front", s, n), front.at[:, :, at], fronts.at[s, :, :, at], s)
     for s in range(4):
         weight(("back", s), back, downs.at[s // 2, pl.ds(16 * (s % 2), 16)], s)
     first = [weights["first", j] for j in range(4)]
-    front_1, front_2, front_3 = (weights["front", s] for s in (1, 2, 3))
+    front_1, front_2, front_3 = ([weights["front", s, n] for n in range(1 + s % 2)] for s in (1, 2, 3))
+    (front_2,) = front_2
     back_0, back_1, back_2, back_3 = (weights["back", s] for s in range(4))
 
     norm_copies = [
@@ -825,13 +882,13 @@
         for copy in norm_copies:
             copy.start()
         norm_all[spot.z] = norms[...]
-        for w in (front_1, back_1, front_2, back_2, front_3, back_3):
+        for w in (*front_1, back_1, front_2, back_2, *front_3, back_3):
             w.open(up=False)
         back_2.open(down=False, load=False)
         for w in first:
             for hop in (1, 2, 3):
                 w.pass_on(hop)
-        for w in (front_1, back_1, front_2):
+        for w in (front_1[0], front_1[1], back_1, front_2):
             w.open(down=False, load=False)
         back_0.open()
 
@@ -858,35 +915,40 @@
         key_bias_out[rows:, :] = jnp.where(there, 0.0, MASKED)
         for w in first:
             w.middle()
-        front_1.pass_on(1)
+        for w in front_1:
+            w.pass_on(1)
         back_1.pass_on(1)
         for w in first:
             w.late()
-        front_1.pass_on(2)
+        for w in front_1:
+            w.pass_on(2)
         first[0].ready()
 
+    early, late = functools.partial, False
     plan = {
-        0: [enter], 1: [first[1].ready, lambda: back_1.pass_on(2), lambda: back_0.pass_on(1)],
-        2: [first[2].ready, lambda: back_0.pass_on(2), lambda: front_2.pass_on(1, False),
-            lambda: back_2.pass_on(1, False)],
-        3: [first[3].ready, lambda: back_0.pass_on(3), lambda: front_3.pass_on(1, False)],
-        4: [front_1.middle, lambda: back_3.pass_on(1, False), lambda: front_2.pass_on(2, False)],
-        5: [lambda: back_2.pass_on(2, False)],
-        6: [back_1.middle, lambda: front_3.pass_on(2, False)],
-        7: [back_0.middle, front_1.late, lambda: back_3.pass_on(2, False)],
+        0: [enter],
+        1: [first[1].ready, early(back_1.pass_on, 2), early(back_0.pass_on, 1)],
+        2: [first[2].ready, early(back_0.pass_on, 2), early(front_2.pass_on, 1, late), early(back_2.pass_on, 1, late)],
+        3: [first[3].ready, early(back_0.pass_on, 3), *(early(w.pass_on, 1, late) for w in front_3)],
+        4: [front_1[0].middle, early(back_3.pass_on, 1, late), early(front_2.pass_on, 2, late)],
+        5: [front_1[1].middle, early(back_2.pass_on, 2, late)],
+        6: [back_1.middle, *(early(w.pass_on, 2, late) for w in front_3), front_1[0].late],
+        7: [back_0.middle, front_1[1].late, early(back_3.pass_on, 2, late)],
         8: [front_2.enter],
-        9: [back_1.late, lambda: front_3.pass_on(3, False)],
-        10: [back_0.late, lambda: back_3.pass_on(3, False), front_1.ready, back_1.ready, back_0.ready],
-        11: [front_3.enter],
-        12: [front_2.middle],
-        13: [front_2.late, back_2.enter, back_3.enter],
+        9: [back_1.late, *(early(w.pass_on, 3, late) for w in front_3)],
+        10: [back_0.late, early(back_3.pass_on, 3, late), front_1[0].ready, back_0.ready],
+        11: [front_3[0].enter, back_2.enter],
+        12: [front_1[1].ready, back_1.ready, front_2.middle],
+        13: [front_2.late, front_3[1].enter, back_3.enter],
         14: [front_2.ready],
-        16: [front_3.middle],
-        18: [back_2.middle],
-        19: [back_3.middle, front_3.late],
-        21: [back_2.late],
+        15: [front_3[0].middle],
+        17: [back_2.middle, front_3[0].late],
+        18: [front_3[1].middle],
+        19: [back_3.middle, back_2.late],
+        20: [front_3[1].late],
         22: [back_3.late],
-        24: [front_3.ready, back_2.ready, back_3.ready],
+        24: [front_3[0].ready, back_2.ready],
+        26: [front_3[1].ready, back_3.ready],
     }
     ends = []
 
@@ -895,9 +957,9 @@
         plan.setdefault(at, []).append(copy.start)
         ends.append(copy.wait)
 
-    for s, at in ((0, 10), (1, 12), (2, 20), (3, 25)):
+    for s, at in ((0, 10), (1, 13), (2, 20), (3, 27)):
         keep(at, fronts.at[s], fronts_out.at[s], s)
-    for layer_id, at in ((0, 15), (1, 26)):
+    for layer_id, at in ((0, 15), (1, 27)):
         keep(at, downs.at[layer_id], downs_out.at[layer_id], 4 + layer_id)
     for s, at in ((0, 4), (1, 11), (2, 16), (3, 25)):
         keep(at, hidden.at[s], hidden_out.at[s], 6 + s)
@@ -1037,7 +1099,7 @@
         pl.when(jnp.logical_not(holds))(away[1].wait_recv)
 
 
-FORWARD_DELIVERIES = ((0, 0, None, 10, 24), (1, 0, None, 14, 27), (2, 0, 160, 24, 27))
+FORWARD_DELIVERIES = ((0, 0, None, 10, 18), (1, 0, None, 14, 20))
 
 
 def forward(clips, grads, kind, front, back, norms, bias_qv, bias_attn, bias_up, bias_down, rows):
@@ -1056,7 +1118,7 @@
     shape = jax.ShapeDtypeStruct
     saved = shape((layers, pairs, rows, PAIR), BF16)
     sems = pltpu.SemaphoreType.DMA
-    jobs = 4 + 3 + 4
+    jobs = 4 + 5 + 4
     sent = len(FORWARD_DELIVERIES)
     return pl.pallas_call(
         forward_body,
@@ -1258,7 +1320,8 @@
 
 def held_sum_guest(shapes, views, stages, targets, hop_steps):
     sems = pltpu.SemaphoreType.DMA
-    sizes = [5 + len(sides(target)) for target in targets]
+    hopping = [sides(target) if at is not None else [] for target, at in zip(targets, hop_steps)]
+    sizes = [5 + len(names) for names in hopping]
 
     def plan(spot, ins, outs, held, body):
         held = list(held)
@@ -1270,19 +1333,19 @@
             job = PlaneSum(
                 spot, src, [src.at[pl.ds(spot.core * 8, 8)]] + bufs[:5], send.at[i], recv.at[i], in_place=True
             )
-            chain = Chain(spot, outs[i], bufs[5:], targets[i], csend.at[i], crecv.at[i])
             actions = (job.start, job.first, job.second, functools.partial(job.third, outs[i]))
             for at, action in zip(stages[i], actions):
                 hooks.setdefault(at, []).append(action)
-            hooks.setdefault(hop_steps[i], []).append(functools.partial(chain.give, 1))
-            hooks.setdefault("end", []).extend(
-                [job.finish, functools.partial(chain.take, 1), functools.partial(chain.leave, 1)]
-            )
+            hooks.setdefault("end", []).append(job.finish)
+            if hop_steps[i] is not None:
+                chain = Chain(spot, outs[i], bufs[5:], targets[i], csend.at[i], crecv.at[i])
+                hooks.setdefault(hop_steps[i], []).append(functools.partial(chain.give, 1))
+                hooks["end"].extend([functools.partial(chain.take, 1), functools.partial(chain.leave, 1)])
         return hooks
 
     buffers = []
-    for shape, target in zip(shapes, targets):
-        buffers += PlaneSum.scratch(*shape)[1:] + [pltpu.VMEM((2,) + shape, BF16)] * len(sides(target))
+    for shape, names in zip(shapes, hopping):
+        buffers += PlaneSum.scratch(*shape)[1:] + [pltpu.VMEM((2,) + shape, BF16)] * len(names)
     count = len(shapes)
     return Guest(
         (), [(jax.ShapeDtypeStruct((2,) + s, BF16), vmem_spec()) for s in shapes],
@@ -1341,26 +1404,34 @@
             pl.when(self.spot.z == above)(self.fall().wait_send)
 
 
-def chain_guest(jobs, hop):
+def chain_guest(jobs):
     sems = pltpu.SemaphoreType.DMA
 
     def plan(spot, ins, outs, held, body):
         held = list(held)
         send, recv, loads = held[-3:]
-        begin, end = [], []
-        for i, (_, target) in enumerate(jobs):
+        hooks, ends = {}, []
+        for i, (_, target, first, steps) in enumerate(jobs):
             bufs, held = held[: len(sides(target))], held[len(sides(target)) :]
             chain = Chain(spot, outs[i], bufs, target, send.at[i], recv.at[i])
             load = pltpu.make_async_copy(ins[i], outs[i], loads.at[i])
-            begin.extend([load.start, load.wait, functools.partial(chain.give, hop)])
-            end.extend([functools.partial(chain.take, hop), functools.partial(chain.leave, hop)])
-        return {0: begin, "end": end}
+            hooks.setdefault(0, []).extend([load.start, load.wait])
+            for n, at in enumerate(steps):
+                hop = first + n
+                if n:
+                    hooks.setdefault(at, []).append(functools.partial(chain.take, hop - 1))
+                hooks.setdefault(at, []).append(functools.partial(chain.give, hop))
+                ends.append(functools.partial(chain.leave, hop))
+            ends.append(functools.partial(chain.take, first + len(steps) - 1))
+        hooks["end"] = ends
+        return hooks
 
     buffers = []
-    for a, target in jobs:
+    for a, target, _, _ in jobs:
         buffers += [pltpu.VMEM(a.shape, BF16)] * len(sides(target))
     return Guest(
-        [(a, hbm_spec()) for a, _ in jobs], [(jax.ShapeDtypeStruct(a.shape, BF16), vmem_spec()) for a, _ in jobs],
+        [(job[0], hbm_spec()) for job in jobs],
+        [(jax.ShapeDtypeStruct(job[0].shape, BF16), vmem_spec()) for job in jobs],
         buffers + [sems((len(jobs),)), sems((len(jobs), 2)), sems((len(jobs),))], (), plan,
     )
 
@@ -1397,22 +1468,24 @@
     for i in (0, 1):
         views += [(1, (slice(None), slice(None), halves[i])), (2, pl.ds(16 * i, 16))]
     shapes = [(width // 16, units), downs.shape[2:]] * 2
-    stages = ((2, 3, 6, 8), (2, 3, 7, 9), (4, 5, 9, 11), (4, 5, 10, 12))
-    hop_steps = (8, 9, 11, 12)
+    stages = ((2, 3, 6, 8), (2, 3, 7, 9), (4, 5, 9, 12), (4, 5, 11, "end"))
+    hop_steps = {1: (8, 9, None, None), 0: (8, 9, 12, None)}
     early, late = range(0, 4), range(4, 8)
     for layer in (1, 0):
         targets = (2 * layer + 1, 2 * layer, 2 * layer + 1, 2 * layer + 1)
-        guests = [held_sum_guest(shapes, views, stages, targets, hop_steps)]
+        guests = [held_sum_guest(shapes, views, stages, targets, hop_steps[layer])]
         if layer == 1:
             guests.append(deliver_guest(
-                [(acts[2], 2, 160, rows - 160, early), (acts[3], 3, 0, 528, early)], acts_home
+                [(acts[2], 2, 0, rows, early), (acts[3], 3, 0, 400, early)], acts_home
             ))
         else:
-            guests.append(chain_guest(list(zip(passing, (3, 2, 3, 3))), 2))
+            done = ((3, 2, (1,)), (2, 2, (1,)), (3, 1, (0, 5)), (3, 1, (0, 5)))
+            guests.append(chain_guest([(part, *hops) for part, hops in zip(passing, done)]))
             guests.append(deliver_guest(
-                [(input_grads[3], 3, 0, rows, early), (0, 1, 0, rows, late)], grads_home
+                [(input_grads[3], 3, 0, 400, early), (0, 1, 0, rows, late), (input_grads[2], 2, 0, rows, early, (2, 3))],
+                grads_home
             ))
-            guests.append(deliver_guest([(acts[3], 3, 528, rows - 528, (0,))], acts_home))
+            guests.append(deliver_guest([(acts[3], 3, 400, rows - 400, early)], acts_home))
         (
             grad_fronts[2 * layer], input_grads[2 * layer + 1], input_grads[2 * layer],
             grad_gain[2 * layer + 1], grad_shift[2 * layer + 1], up_sums[layer], down_sums[layer],
@@ -1426,17 +1499,14 @@
         else:
             later, earlier, (grads_home,), (acts_home,) = carried
 
-    pair_sums = [jnp.concatenate([q, v], axis=1) for q, v in zip(query_sums, value_sums)]
-    small = jnp.concatenate(
-        [v.reshape(-1) for v in grad_gain + grad_shift + pair_sums + out_sums + up_sums + down_sums]
-    )
+    pair_sums = [v for both in zip(query_sums, value_sums) for v in both]
+    vectors = grad_gain + grad_shift + pair_sums + out_sums + up_sums + down_sums
     grads_home, front_out, back_out, small = collect(
-        input_grads[0], input_grads[2], grads_home, grad_fronts[0],
-        grad_fronts[2], [*earlier, *later], small.reshape(-1, 128),
+        input_grads[0], input_grads[2], input_grads[3], grads_home, grad_fronts[0],
+        grad_fronts[2], [*earlier, *later], vectors,
     )
     front_out = front_out.reshape(width, -1)
     back_out = back_out.reshape(-1, width)
-    small = small.reshape(-1)
     for bit in spot.spare_bits:
         small = small + swap(small, bit)
         front_out, back_out = add(front_out, swap(front_out, bit)), add(back_out, swap(back_out, bit))
@@ -1447,8 +1517,9 @@
         (sections, width), (sections, width), (layers, 2 * width), (layers, width),
         (layers, hidden_units), (layers, width),
     ):
-        parts.append(small[place_at : place_at + count * size].reshape(count, size))
-        place_at += count * size
+        taken = count * size // width
+        parts.append(small[place_at : place_at + taken].reshape(count, size))
+        place_at += taken
     return (
         acts_home[None],
         grads_out[None],

time: 516 us -> 505 us (0.979)
  the two profiles are of different devices: /device:TPU:0 before, /device:TPU:17 now
where the time goes in v7:
time: 505 us; the launch traced here: 502 us
  Pallas kernels  470 us (93%)
  other arithmetic  15.2 us (3%)
  local copies, waits for them, and re-layouts  14.7 us (3%)
    pallas_call x2, Pallas kernels, hosted(): pl.pallas_call(kernel, grid=(grid,), in_specs=[s for _, s in operands + g...  171 us
    pallas_call x1, Pallas kernels, forward(): pl.pallas_call(forward_body, grid=(2 * FORWARD_STEPS,), in_specs=[hbm] *...  168 us
    pallas_call x1, Pallas kernels, collect(): pl.pallas_call(collect_body, in_specs=[hbm] * (5 + len(parts)) + [vmem] *...  132 us

profile of v7, /device:TPU:17, one launch (start us, length us, event | category | flops | bytes accessed | tf_op | source)
XLA Modules:
  0.0 501.9 jit_solution(13717985056099156151)
XLA Ops:
  0.7 1.2 dynamic_slice.10
  2.6 0.1 pad.8.clone
  2.6 0.6 broadcast_in_dim.21.refs_5_
  3.2 1.4 maximum_maximum_fusion.refs_4_
  4.6 168.0 %forward.1 = (bf16[2,6,608,128]{3,2,1,0:T(8,128)(2,1)}, bf16[2,6,608,128]{3,2,1,0:T(8,128)(2,1)}, bf16[2,6,608,128]{3,2,1,0:T(8,128)(2,1)}, bf16[2,6,608,128]{3,...) custom-call(bf16[2,1280,768]{2,1,0:T(8,128)(2,1)} %refs_0_.1, ...), custom_call_target="tpu_custom_call" | custom-call | tf_op jit(solution)/shard_map/forward/pallas_call | solution.py:1123
  172.6 2.8 slice_bitcast_fusion
  175.4 86.4 %backward_1.1 = (bf16[16,48,3072]{2,1,0:T(8,128)(2,1)}, bf16[608,768]{1,0:T(8,128)(2,1)}, bf16[608,768]{1,0:T(8,128)(2,1)}, f32[1,768]{1,0:T(1,128)}, f32[1,768]...) custom-call(bf16[608,768]{1,0:T(8,128)(2,1)} %get-tuple-element.68.r, ...), custom_call_target="tpu_custom_call", output_to_operand_aliasing={{16}: (17, {})} | custom-call | tf_op jit(solution)/shard_map/backward_1/pallas_call | solution.py:252
  261.8 2.2 broadcast_in_dim.22.refs_21_
  264.0 84.6 %backward_0.1 = (bf16[16,48,3072]{2,1,0:T(8,128)(2,1)}, bf16[608,768]{1,0:T(8,128)(2,1)}, bf16[608,768]{1,0:T(8,128)(2,1)}, f32[1,768]{1,0:T(1,128)}, f32[1,768]...) custom-call(bf16[608,768]{1,0:T(8,128)(2,1)} %get-tuple-element.84.r, ...), custom_call_target="tpu_custom_call", output_to_operand_aliasing={{20}: (21, {}), {21}: (23, {})} | custom-call | tf_op jit(solution)/shard_map/backward_0/pallas_call | solution.py:252
  348.5 131.5 %collect.1 = (bf16[2,1216,768]{2,1,0:T(8,128)(2,1)}, bf16[16,48,3072]{2,1,0:T(8,128)(2,1)}, bf16[16,96,768]{2,1,0:T(8,128)(2,1)}, f32[24,768]{1,0:T(8,128)}) custom-call(bf16[608,768]{1,0:T(8,128)(2,1)} %get-tuple-element.92.refs_0_, bf16[608,768]{1,0:T(8,128)(2,1)} %get-tuple-element.84.refs_0_.refs_20_.refs_1_, ...), custom_call_target="tpu_custom_call", output_to_operand_aliasing={{0}: (31, {})} | custom-call | tf_op jit(solution)/shard_map/collect/pallas_call | solution.py:583
  480.1 1.4 fusion
  481.4 0.8 slice.30
  482.2 0.0 slice-start
  482.2 0.8 fusion.1
  483.1 0.6 reshape.53
  483.7 0.6 reshape.54
  484.3 0.6 constant_dynamic-slice_fusion
  484.9 0.0 slice-start.1
  484.9 6.0 %bitcast_convert_fusion.1 = f32[1,2,1280,768]{3,2,1,0:T(8,128)} fusion(bf16[2,1216,768]{2,1,0:T(8,128)(2,1)} %get-tuple-element.122), kind=kLoop, calls=%fused_computation.1 | loop fusion | flops 1966080 | bytes 11599872 | tf_op jit(solution)/shard_map/broadcast_in_dim | solution.py:1525
  490.9 0.0 slice-done
  490.9 0.0 slice-done.1
  490.9 0.0 copy-start.1
  490.9 5.0 %bitcast_convert_fusion = f32[1,768,3072]{2,1,0:T(8,128)} fusion(bf16[1,768,3072]{2,1,0:T(8,128)(2,1)S(1)} %bitcast.22), kind=kLoop, calls=%fused_computation | loop fusion | flops 2359296 | bytes 14155776 | tf_op jit(solution)/shard_map/convert_element_type | solution.py:1526
  496.0 0.0 copy-done.1
  496.0 0.0 copy-start
  496.0 2.8 bitcast_convert_fusion.2
  498.7 1.1 copy-done
  499.8 1.9 copy.30
  (2 shorter events, 0.0 us)
Async XLA Ops:
  482.2 8.7 %slice-start = ((s8[4718592]{0:T(1024)(128)(4,1)}), s8[524288]{0:T(1024)(128)(4,1)S(1)}, s32[]{:S(2)}) async-start(s8[4718592]{0:T(1024)(128)(4,1)} %bitcast.20), calls=%async_computation | async-start | bytes 1048576
  484.9 6.0 %slice-start.1 = ((s8[4718592]{0:T(1024)(128)(4,1)}), s8[4194304]{0:T(1024)(128)(4,1)S(1)}, s32[]{:S(2)}) async-start(s8[4718592]{0:T(1024)(128)(4,1)} %bitcast.20), calls=%async_computation.1 | async-start | bytes 8388608
  490.9 5.0 %copy-start.1 = (bf16[16,96,768]{2,1,0:T(8,128)(2,1)S(1)}, bf16[16,96,768]{2,1,0:T(8,128)(2,1)}, u32[]{:S(2)}) copy-start(bf16[16,96,768]{2,1,0:T(8,128)(2,1)} %get-tuple-element.124) | copy-start | bytes 7077892
  496.0 3.8 copy-start

commit v8 on v7

--- a/solution.py
+++ b/solution.py
@@ -271,12 +271,20 @@
 def deliver_guest(pieces, home):
     sems = pltpu.SemaphoreType.DMA
     count = len(pieces)
+    fresh = isinstance(home, jax.ShapeDtypeStruct)
     arrays = [i for i, piece in enumerate(pieces) if not isinstance(piece[0], int)]
 
     def plan(spot, ins, outs, held, body):
         send, recv = held
         hooks = {}
-        held_by = [body[p[0]] if isinstance(p[0], int) else ins[arrays.index(i)] for i, p in enumerate(pieces)]
+        held_by = []
+        for i, piece in enumerate(pieces):
+            if isinstance(piece[0], int):
+                held_by.append(body[piece[0]])
+            elif isinstance(piece[0], tuple):
+                held_by.append(ins[arrays.index(i)].at[piece[0][1]])
+            else:
+                held_by.append(ins[arrays.index(i)])
         for i, (_, target, first, size, steps, *sources) in enumerate(pieces):
             blocks = size // 16
             for turn, step in enumerate(steps):
@@ -292,10 +300,11 @@
         return hooks
 
     return Guest(
-        [(pieces[i][0], hbm_spec()) for i in arrays] + [(home, hbm_spec())],
+        [(pieces[i][0][0] if isinstance(pieces[i][0], tuple) else pieces[i][0], hbm_spec()) for i in arrays]
+        + ([] if fresh else [(home, hbm_spec())]),
         [(jax.ShapeDtypeStruct(home.shape, home.dtype), hbm_spec())],
         [sems((count, 2)), sems((count, 4))],
-        [(len(arrays), 0)], plan,
+        [] if fresh else [(len(arrays), 0)], plan,
     )
 
 
@@ -485,6 +494,38 @@
         planes[2, c].first()
     planes[0, TAIL_CHUNKS - 1].third(owns[0, TAIL_CHUNKS - 1])
     advance([chunk_chains[0, TAIL_CHUNKS - 1]], 0)
+    fronts = [PlaneGather(spot, front_out.at[:, :, columns[c]], asend.at[c], arecv.at[c]) for c in every_chunk]
+    back = PlaneGather(spot, back_out, asend.at[TAIL_CHUNKS], arecv.at[TAIL_CHUNKS])
+
+    def held(kind, z, c):
+        if kind == "front" and z in (0, 2):
+            return owns[z, c]
+        found = [t for t, (name, _, target, _) in zip(totals, LEFT) if name == kind and target == z]
+        if kind == "back":
+            return found[0]
+        half, at = divmod(c * size, found[0].shape[2])
+        return found[half].at[:, :, pl.ds(at, size)]
+
+    def begin(gather, kind, sections_now, c=0):
+        for z in sections_now:
+            stay = pltpu.make_async_copy(
+                held(kind, z, c), gather.dst.at[gather.blocks(spot.core, spot.c)],
+                stay_sem.at[TAIL_CHUNKS if kind == "back" else c],
+            )
+
+            @pl.when(spot.z == z)
+            def _(z=z, stay=stay):
+                stay.start()
+                gather.begin(held(kind, z, c))
+
+    def stayed():
+        for c in range(TAIL_CHUNKS + 1):
+            kind, gather = ("front", fronts[c]) if c < TAIL_CHUNKS else ("back", back)
+            pltpu.make_async_copy(
+                held(kind, 1, 0 if kind == "back" else c), gather.dst.at[gather.blocks(spot.core, spot.c)],
+                stay_sem.at[c],
+            ).wait()
+
     small_step(2)
     late.start()
     for c in every_chunk:
@@ -499,42 +540,12 @@
             advance([chunk_chains[2, c - 1]], 0)
     planes[2, TAIL_CHUNKS - 1].third(owns[2, TAIL_CHUNKS - 1])
     advance([chunk_chains[2, TAIL_CHUNKS - 1]], 0)
+    for c in every_chunk:
+        begin(fronts[c], "front", (1, 3), c)
+    begin(back, "back", (2, 3))
     small_step(4)
     advance(chains, 2)
-    fronts = [PlaneGather(spot, front_out.at[:, :, columns[c]], asend.at[c], arecv.at[c]) for c in every_chunk]
-    back = PlaneGather(spot, back_out, asend.at[TAIL_CHUNKS], arecv.at[TAIL_CHUNKS])
-
-    def held(kind, z, c):
-        if kind == "front" and z in (0, 2):
-            return owns[z, c]
-        found = [t for t, (name, _, target, _) in zip(totals, LEFT) if name == kind and target == z]
-        if kind == "back":
-            return found[0]
-        half, at = divmod(c * size, found[0].shape[2])
-        return found[half].at[:, :, pl.ds(at, size)]
-
-    def begin(gather, kind, sections_now, c=0):
-        for z in sections_now:
-            stay = pltpu.make_async_copy(
-                held(kind, z, c), gather.dst.at[gather.blocks(spot.core, spot.c)],
-                stay_sem.at[TAIL_CHUNKS if kind == "back" else c],
-            )
-
-            @pl.when(spot.z == z)
-            def _(z=z, stay=stay):
-                stay.start()
-                gather.begin(held(kind, z, c))
-
-    def stayed():
-        for c in range(TAIL_CHUNKS + 1):
-            kind, gather = ("front", fronts[c]) if c < TAIL_CHUNKS else ("back", back)
-            pltpu.make_async_copy(
-                held(kind, 1, 0 if kind == "back" else c), gather.dst.at[gather.blocks(spot.core, spot.c)],
-                stay_sem.at[c],
-            ).wait()
-
-    for c in every_chunk:
-        begin(fronts[c], "front", (1, 3), c)
+    begin(back, "back", (0, 1))
     for c in every_chunk:
         advance([chunk_chains[0, c]], 3)
         begin(fronts[c], "front", (0,), c)
@@ -545,7 +556,6 @@
     for c in every_chunk:
         advance([chunk_chains[2, c]], 2)
         begin(fronts[c], "front", (2,), c)
-    begin(back, "back", range(sections))
     for gather in fronts:
         gather.second()
     back.second()
@@ -1455,9 +1465,8 @@
         clip_inputs, out_grad, jnp.broadcast_to(kind, (8, 128)), w_front[0], w_back[0], norms,
         bias_query_value, bias_attn_out, bias_up, bias_down, rows,
     )
-    acts = [hidden[s + 1] for s in range(sections)]
-    acts = [hidden[s + 1] for s in range(sections)]
-    grads_home = jnp.zeros((clip_inputs.shape[0], 2 * rows, width), BF16)
+    acts = [(hidden, s + 1) for s in range(sections)]
+    grads_home = jax.ShapeDtypeStruct((clip_inputs.shape[0], 2 * rows, width), BF16)
     heads = (key, value, key_far, value_far, extended, attended)
     input_grads, grad_fronts = [None] * sections, [None] * sections
     grad_gain, grad_shift = [None] * sections, [None] * sections

time: 505 us -> 488 us (0.966); the launches traced: 502 us -> 479 us
  Pallas kernels: 470 us -> 452 us
    pallas_call x2, Pallas kernels: 171 us -> 159 us  [hosted(): pl.pallas_call(kernel, grid=(grid,), in_specs=[s for _, s in operands + g...]
    pallas_call x1, Pallas kernels: 132 us -> 125 us  [collect(): pl.pallas_call(collect_body, in_specs=[hbm] * (5 + len(parts)) + [vmem] *...]
where the time goes in v8:
time: 488 us; the launch traced here: 479 us
  Pallas kernels  452 us (93%)
  other arithmetic  15.2 us (3%)
  local copies, waits for them, and re-layouts  9.73 us (2%)
    pallas_call x1, Pallas kernels, forward(): pl.pallas_call(forward_body, grid=(2 * FORWARD_STEPS,), in_specs=[hbm] *...  168 us
    pallas_call x2, Pallas kernels, hosted(): pl.pallas_call(kernel, grid=(grid,), in_specs=[s for _, s in operands + g...  159 us
    pallas_call x1, Pallas kernels, collect(): pl.pallas_call(collect_body, in_specs=[hbm] * (5 + len(parts)) + [vmem] *...  125 us

profile of v8, /device:TPU:17, one launch (start us, length us, event | category | flops | bytes accessed | tf_op | source)
XLA Modules:
  0.0 478.5 jit_solution(7841052483371000513)
XLA Ops:
  0.7 1.2 dynamic_slice.10
  2.6 0.1 pad.8.clone
  2.6 0.6 broadcast_in_dim.18.refs_5_
  3.2 1.4 maximum_maximum_fusion.refs_4_
  4.6 168.0 %forward.1 = (bf16[2,6,608,128]{3,2,1,0:T(8,128)(2,1)}, bf16[2,6,608,128]{3,2,1,0:T(8,128)(2,1)}, bf16[2,6,608,128]{3,2,1,0:T(8,128)(2,1)}, bf16[2,6,608,128]{3,...) custom-call(bf16[2,1280,768]{2,1,0:T(8,128)(2,1)} %refs_0_.1, ...), custom_call_target="tpu_custom_call" | custom-call | tf_op jit(solution)/shard_map/forward/pallas_call | solution.py:1133
  172.6 74.5 %backward_1.1 = (bf16[16,48,3072]{2,1,0:T(8,128)(2,1)}, bf16[608,768]{1,0:T(8,128)(2,1)}, bf16[608,768]{1,0:T(8,128)(2,1)}, f32[1,768]{1,0:T(1,128)}, f32[1,768]...) custom-call(bf16[608,768]{1,0:T(8,128)(2,1)} %get-tuple-element.68.r, ...), custom_call_target="tpu_custom_call", output_to_operand_aliasing={{16}: (17, {})} | custom-call | tf_op jit(solution)/shard_map/backward_1/pallas_call | solution.py:252
  247.1 84.4 %backward_0.1 = (bf16[16,48,3072]{2,1,0:T(8,128)(2,1)}, bf16[608,768]{1,0:T(8,128)(2,1)}, bf16[608,768]{1,0:T(8,128)(2,1)}, f32[1,768]{1,0:T(1,128)}, f32[1,768]...) custom-call(bf16[608,768]{1,0:T(8,128)(2,1)} %get-tuple-element.84.r, ...), custom_call_target="tpu_custom_call", output_to_operand_aliasing={{21}: (22, {})} | custom-call | tf_op jit(solution)/shard_map/backward_0/pallas_call | solution.py:252
  331.5 125.1 %collect.1 = (bf16[2,1216,768]{2,1,0:T(8,128)(2,1)}, bf16[16,48,3072]{2,1,0:T(8,128)(2,1)}, bf16[16,96,768]{2,1,0:T(8,128)(2,1)}, f32[24,768]{1,0:T(8,128)}) custom-call(bf16[608,768]{1,0:T(8,128)(2,1)} %get-tuple-element.92.refs_0_, bf16[608,768]{1,0:T(8,128)(2,1)} %get-tuple-element.84.refs_0_.refs_20_.refs_1_, ...), custom_call_target="tpu_custom_call", output_to_operand_aliasing={{0}: (31, {})} | custom-call | tf_op jit(solution)/shard_map/collect/pallas_call | solution.py:593
  456.6 1.4 fusion
  458.0 0.8 slice.22
  458.8 0.0 slice-start
  458.8 0.8 fusion.1
  459.6 0.6 reshape.53
  460.3 0.6 reshape.54
  460.9 0.6 constant_dynamic-slice_fusion
  461.5 0.0 slice-start.1
  461.5 6.0 %bitcast_convert_fusion.1 = f32[1,2,1280,768]{3,2,1,0:T(8,128)} fusion(bf16[2,1216,768]{2,1,0:T(8,128)(2,1)} %get-tuple-element.122), kind=kLoop, calls=%fused_computation.1 | loop fusion | flops 1966080 | bytes 11599872 | tf_op jit(solution)/shard_map/broadcast_in_dim | solution.py:1534
  467.5 0.0 slice-done
  467.5 0.0 slice-done.1
  467.5 0.0 copy-start.1
  467.5 5.0 %bitcast_convert_fusion = f32[1,768,3072]{2,1,0:T(8,128)} fusion(bf16[1,768,3072]{2,1,0:T(8,128)(2,1)S(1)} %bitcast.18), kind=kLoop, calls=%fused_computation | loop fusion | flops 2359296 | bytes 14155776 | tf_op jit(solution)/shard_map/convert_element_type | solution.py:1535
  472.6 0.0 copy-done.1
  472.6 0.0 copy-start
  472.6 2.8 bitcast_convert_fusion.2
  475.3 1.1 copy-done
  476.4 1.9 copy.28
  (2 shorter events, 0.0 us)
Async XLA Ops:
  458.8 8.7 %slice-start = ((s8[4718592]{0:T(1024)(128)(4,1)}), s8[524288]{0:T(1024)(128)(4,1)S(1)}, s32[]{:S(2)}) async-start(s8[4718592]{0:T(1024)(128)(4,1)} %bitcast.16), calls=%async_computation | async-start | bytes 1048576
  461.5 6.0 %slice-start.1 = ((s8[4718592]{0:T(1024)(128)(4,1)}), s8[4194304]{0:T(1024)(128)(4,1)S(1)}, s32[]{:S(2)}) async-start(s8[4718592]{0:T(1024)(128)(4,1)} %bitcast.16), calls=%async_computation.1 | async-start | bytes 8388608
  467.5 5.0 %copy-start.1 = (bf16[16,96,768]{2,1,0:T(8,128)(2,1)S(1)}, bf16[16,96,768]{2,1,0:T(8,128)(2,1)}, u32[]{:S(2)}) copy-start(bf16[16,96,768]{2,1,0:T(8,128)(2,1)} %get-tuple-element.124) | copy-start | bytes 7077892
  472.6 3.8 copy-start

commit v9 on v8

--- a/solution.py
+++ b/solution.py
@@ -946,8 +946,7 @@
         7: [back_0.middle, front_1[1].late, early(back_3.pass_on, 2, late)],
         8: [front_2.enter],
         9: [back_1.late, *(early(w.pass_on, 3, late) for w in front_3)],
-        10: [back_0.late, early(back_3.pass_on, 3, late), front_1[0].ready, back_0.ready],
-        11: [front_3[0].enter, back_2.enter],
+        10: [back_0.late, early(back_3.pass_on, 3, late), front_3[0].enter, back_2.enter, front_1[0].ready, back_0.ready],
         12: [front_1[1].ready, back_1.ready, front_2.middle],
         13: [front_2.late, front_3[1].enter, back_3.enter],
         14: [front_2.ready],
@@ -967,10 +966,14 @@
         plan.setdefault(at, []).append(copy.start)
         ends.append(copy.wait)
 
-    for s, at in ((0, 10), (1, 13), (2, 20), (3, 27)):
+    for s, at in ((0, 10), (1, 13), (2, 20)):
         keep(at, fronts.at[s], fronts_out.at[s], s)
-    for layer_id, at in ((0, 15), (1, 27)):
-        keep(at, downs.at[layer_id], downs_out.at[layer_id], 4 + layer_id)
+    keep(15, downs.at[0], downs_out.at[0], 4)
+    half = fronts.shape[3] // 2
+    for n, at in ((0, 24), (1, 26)):
+        columns, blocks = pl.ds(n * half, half), pl.ds(16 * n, 16)
+        keep(at, fronts.at[3, :, :, columns], fronts_out.at[3, :, :, columns], (3, 11)[n])
+        keep(at, downs.at[1, blocks], downs_out.at[1, blocks], (5, 12)[n])
     for s, at in ((0, 4), (1, 11), (2, 16), (3, 25)):
         keep(at, hidden.at[s], hidden_out.at[s], 6 + s)
 
@@ -1155,7 +1158,7 @@
             pltpu.VMEM((sections,) + norms.shape, F32), pltpu.VMEM(kind.shape, F32),
             pltpu.VMEM((padded - 2 * rows, width), BF16),
             sems((jobs, Weight.SENDS)), sems((jobs, Weight.RECEIVES)), sems((sections,)), sems((sections,)),
-            sems((5,)), sems((3,)), sems((layers, 2)), sems((layers, 2)), sems((sent, 2)), sems((sent, 4)), sems((13,)),
+            sems((5,)), sems((3,)), sems((layers, 2)), sems((layers, 2)), sems((sent, 2)), sems((sent, 4)), sems((15,)),
         ],
         compiler_params=pltpu.CompilerParams(
             vmem_limit_bytes=63 * 2**20, collective_id=0, has_side_effects=True

time: 488 us -> 488 us (level)
  no operation moved by 1% of the time
where the time goes in v9:
time: 488 us; the launch traced here: 479 us
  Pallas kernels  452 us (93%)
  other arithmetic  15.2 us (3%)
  local copies, waits for them, and re-layouts  9.73 us (2%)
    pallas_call x1, Pallas kernels, forward(): pl.pallas_call(forward_body, grid=(2 * FORWARD_STEPS,), in_specs=[hbm] *...  168 us
    pallas_call x2, Pallas kernels, hosted(): pl.pallas_call(kernel, grid=(grid,), in_specs=[s for _, s in operands + g...  159 us
    pallas_call x1, Pallas kernels, collect(): pl.pallas_call(collect_body, in_specs=[hbm] * (5 + len(parts)) + [vmem] *...  125 us

profile of v9, /device:TPU:17, one launch (start us, length us, event | category | flops | bytes accessed | tf_op | source)
XLA Modules:
  0.0 478.5 jit_solution(9746689146461252165)
XLA Ops:
  0.7 1.2 dynamic_slice.10
  2.6 0.1 pad.8.clone
  2.6 0.6 broadcast_in_dim.18.refs_5_
  3.2 1.4 maximum_maximum_fusion.refs_4_
  4.6 168.0 %forward.1 = (bf16[2,6,608,128]{3,2,1,0:T(8,128)(2,1)}, bf16[2,6,608,128]{3,2,1,0:T(8,128)(2,1)}, bf16[2,6,608,128]{3,2,1,0:T(8,128)(2,1)}, bf16[2,6,608,128]{3,...) custom-call(bf16[2,1280,768]{2,1,0:T(8,128)(2,1)} %refs_0_.1, ...), custom_call_target="tpu_custom_call" | custom-call | tf_op jit(solution)/shard_map/forward/pallas_call | solution.py:1136
  172.6 74.5 %backward_1.1 = (bf16[16,48,3072]{2,1,0:T(8,128)(2,1)}, bf16[608,768]{1,0:T(8,128)(2,1)}, bf16[608,768]{1,0:T(8,128)(2,1)}, f32[1,768]{1,0:T(1,128)}, f32[1,768]...) custom-call(bf16[608,768]{1,0:T(8,128)(2,1)} %get-tuple-element.68.r, ...), custom_call_target="tpu_custom_call", output_to_operand_aliasing={{16}: (17, {})} | custom-call | tf_op jit(solution)/shard_map/backward_1/pallas_call | solution.py:252
  247.1 84.4 %backward_0.1 = (bf16[16,48,3072]{2,1,0:T(8,128)(2,1)}, bf16[608,768]{1,0:T(8,128)(2,1)}, bf16[608,768]{1,0:T(8,128)(2,1)}, f32[1,768]{1,0:T(1,128)}, f32[1,768]...) custom-call(bf16[608,768]{1,0:T(8,128)(2,1)} %get-tuple-element.84.r, ...), custom_call_target="tpu_custom_call", output_to_operand_aliasing={{21}: (22, {})} | custom-call | tf_op jit(solution)/shard_map/backward_0/pallas_call | solution.py:252
  331.5 125.1 %collect.1 = (bf16[2,1216,768]{2,1,0:T(8,128)(2,1)}, bf16[16,48,3072]{2,1,0:T(8,128)(2,1)}, bf16[16,96,768]{2,1,0:T(8,128)(2,1)}, f32[24,768]{1,0:T(8,128)}) custom-call(bf16[608,768]{1,0:T(8,128)(2,1)} %get-tuple-element.92.refs_0_, bf16[608,768]{1,0:T(8,128)(2,1)} %get-tuple-element.84.refs_0_.refs_20_.refs_1_, ...), custom_call_target="tpu_custom_call", output_to_operand_aliasing={{0}: (31, {})} | custom-call | tf_op jit(solution)/shard_map/collect/pallas_call | solution.py:593
  456.6 1.4 fusion
  458.0 0.8 slice.22
  458.8 0.0 slice-start
  458.8 0.8 fusion.1
  459.6 0.6 reshape.53
  460.3 0.6 reshape.54
  460.9 0.6 constant_dynamic-slice_fusion
  461.5 0.0 slice-start.1
  461.5 6.0 %bitcast_convert_fusion.1 = f32[1,2,1280,768]{3,2,1,0:T(8,128)} fusion(bf16[2,1216,768]{2,1,0:T(8,128)(2,1)} %get-tuple-element.122), kind=kLoop, calls=%fused_computation.1 | loop fusion | flops 1966080 | bytes 11599872 | tf_op jit(solution)/shard_map/broadcast_in_dim | solution.py:1537
  467.5 0.0 slice-done
  467.5 0.0 slice-done.1
  467.5 0.0 copy-start.1
  467.5 5.0 %bitcast_convert_fusion = f32[1,768,3072]{2,1,0:T(8,128)} fusion(bf16[1,768,3072]{2,1,0:T(8,128)(2,1)S(1)} %bitcast.18), kind=kLoop, calls=%fused_computation | loop fusion | flops 2359296 | bytes 14155776 | tf_op jit(solution)/shard_map/convert_element_type | solution.py:1538
  472.6 0.0 copy-done.1
  472.6 0.0 copy-start
  472.6 2.8 bitcast_convert_fusion.2
  475.3 1.1 copy-done
  476.4 1.9 copy.28
  (2 shorter events, 0.0 us)
Async XLA Ops:
  458.8 8.7 %slice-start = ((s8[4718592]{0:T(1024)(128)(4,1)}), s8[524288]{0:T(1024)(128)(4,1)S(1)}, s32[]{:S(2)}) async-start(s8[4718592]{0:T(1024)(128)(4,1)} %bitcast.16), calls=%async_computation | async-start | bytes 1048576
  461.5 6.0 %slice-start.1 = ((s8[4718592]{0:T(1024)(128)(4,1)}), s8[4194304]{0:T(1024)(128)(4,1)S(1)}, s32[]{:S(2)}) async-start(s8[4718592]{0:T(1024)(128)(4,1)} %bitcast.16), calls=%async_computation.1 | async-start | bytes 8388608
  467.5 5.0 %copy-start.1 = (bf16[16,96,768]{2,1,0:T(8,128)(2,1)S(1)}, bf16[16,96,768]{2,1,0:T(8,128)(2,1)}, u32[]{:S(2)}) copy-start(bf16[16,96,768]{2,1,0:T(8,128)(2,1)} %get-tuple-element.124) | copy-start | bytes 7077892
  472.6 3.8 copy-start
